TPU v7x, 32 devices: a whole 2x2x4 slice. The times are simulated.
32 devices in a mesh: seq: 4 (over y, x), fsdp: 8 (over z, core).
Axes of the slice: x: 2, y: 2, z: 4, core: 2. Of those that a mesh axis runs over, the one named last changes fastest.
Arguments:
- tokens: bfloat16 [16, 1024, 1536], P('fsdp', 'seq'), may hold values from -6 to 6
- joined_input_weight: bfloat16 [1536, 3072], P('fsdp'), may hold values from -0.15625 to 0.15625
- out_projection: bfloat16 [1536, 1536], P('fsdp'), may hold values from -1.25 to 1.25
- gate_weight: bfloat16 [1536, 4096], P('fsdp'), may hold values from -0.15625 to 0.15625
- up_weight: bfloat16 [1536, 4096], P('fsdp'), may hold values from -0.15625 to 0.15625
- down_weight: bfloat16 [4096, 1536], P('fsdp'), may hold values from -0.09375 to 0.09375
- norm_first: float32 [1536], replicated, may hold values from 0.25 to 1.75
- norm_second: float32 [1536], replicated, may hold values from 0.25 to 1.75
- positions: int32 [16, 1024], P('fsdp'), may hold values from 0 to 767, as said below
- cotangent: bfloat16 [16, 1024, 1536], P('fsdp', 'seq'), may hold values from -6 to 6
Outputs:
- block_out: bfloat16 [16, 1024, 1536], P('fsdp', 'seq')
- tokens_grad: bfloat16 [16, 1024, 1536], P('fsdp', 'seq')
- in_projection_grad: float32 [1536, 3072], P('fsdp')
- out_projection_grad: float32 [1536, 1536], P('fsdp')
- gate_grad: float32 [1536, 4096], P('fsdp')
- up_grad: float32 [1536, 4096], P('fsdp')
- down_grad: float32 [4096, 1536], P('fsdp')
- norm_first_grad: float32 [1536], replicated
- norm_second_grad: float32 [1536], replicated
Inputs may be any that keep to these rules, and one draw needn't show every extreme that they name: `positions`: in every sequence row 0 has position 0, and each later row has the position of the row before plus one, or 0 where a new document starts; every sequence holds three documents, the middle one of exactly 768 rows, the others shorter than 256 rows.
All inputs are finite; a program needn't handle non-finite values.
Results may differ from a plain program's by a relative error of at most 0.02.
Values may be sent and summed in bfloat16 or wider, within the bound.
No kernel may reach another device: no remote copies, remote signals or barrier semaphores. Data moves between devices by JAX's collectives and lax.ppermute only.
A program may use at most 384 MiB of HBM per device.

v0:
```python
import math

import jax
import jax.numpy as jnp
from jax import lax
from jax.sharding import PartitionSpec as P

FF = 4096
QUERY_HEAD_COUNT = 16
KEY_VALUE_HEADS = 8
HEAD_DIMENSION = 96


epsilon = 1e-05
rope_base = 100000.0
block_limit = 512


def norm_parts(inputs, gain_row):
    factor = lax.rsqrt(jnp.mean(inputs * inputs, axis=-1, keepdims=True) + epsilon)
    unit_rows = inputs * factor
    return (unit_rows, factor, (unit_rows * gain_row).astype(jnp.bfloat16))


def norm_back(grad_rows, unit_rows, factor, gain_row):
    scaled = grad_rows * gain_row
    mean_dot = jnp.mean(scaled * unit_rows, axis=-1, keepdims=True)
    return (factor * (scaled - unit_rows * mean_dot), jnp.sum(grad_rows * unit_rows, axis=0))


def turning(flat_positions, head_size):
    halves = head_size // 2
    frequency = jnp.exp(
        jnp.arange(halves, dtype=jnp.float32) * (-2.0 * math.log(rope_base) / head_size)
    )
    angles = flat_positions.astype(jnp.float32)[:, None] * frequency[None, :]
    return (jnp.cos(angles)[:, None, :], jnp.sin(angles)[:, None, :])


def apply_rotary(values, cosine_lookup, sine_lookup):
    halves = values.shape[-1] // 2
    first_half = values[..., :halves]
    second_half = values[..., halves:]
    return jnp.concatenate(
        [
            first_half * cosine_lookup - second_half * sine_lookup,
            second_half * cosine_lookup + first_half * sine_lookup,
        ],
        axis=-1,
    )


def row_adder(operand, shard_part):
    summed = jnp.dot(operand, shard_part, preferred_element_type=jnp.float32)
    return (summed,)


def pair_adder(operand, shard_parts):
    gate_sum = jnp.dot(operand, shard_parts[0], preferred_element_type=jnp.float32)
    up_sum = jnp.dot(operand, shard_parts[1], preferred_element_type=jnp.float32)
    return (gate_sum, up_sum)


def block_scores(query_block, key_block, begin_row, doc_starts, scaling):
    scores = (
        jnp.einsum("sqkgd,stkd->skgqt", query_block, key_block, preferred_element_type=jnp.float32)
        * scaling
    )
    query_count = query_block.shape[1]
    query_index = begin_row + jnp.arange(query_count, dtype=jnp.int32)
    key_index = jnp.arange(key_block.shape[1], dtype=jnp.int32)
    doc_first = doc_starts[:, begin_row : begin_row + query_count]
    allowed = (key_index[None, None, :] <= query_index[None, :, None]) & (
        key_index[None, None, :] >= doc_first[:, :, None]
    )
    return jnp.where(allowed[:, None, None], scores, -1e30)


def body(
    tokens,
    joined_input_weight,
    out_projection,
    gate_weight,
    up_weight,
    down_weight,
    norm_first,
    norm_second,
    positions,
    cotangent,
):
    seq_count, shard_len, model_width = tokens.shape
    sequence_splits = lax.axis_size("seq")
    total_rows = seq_count * shard_len
    full_len = positions.shape[1]
    query_columns = QUERY_HEAD_COUNT * HEAD_DIMENSION
    paired_width = KEY_VALUE_HEADS * HEAD_DIMENSION
    query_heads = QUERY_HEAD_COUNT // sequence_splits
    paired_heads = KEY_VALUE_HEADS // sequence_splits
    repeat_count = QUERY_HEAD_COUNT // KEY_VALUE_HEADS
    query_slab = query_heads * HEAD_DIMENSION
    pair_slab = paired_heads * HEAD_DIMENSION
    scaling = 1.0 / math.sqrt(HEAD_DIMENSION)
    step_rows = min(block_limit, full_len)
    local_pos = lax.dynamic_slice_in_dim(positions, lax.axis_index("seq") * shard_len, shard_len, 1)
    cosine_lookup, sine_lookup = turning(local_pos.reshape(total_rows), HEAD_DIMENSION)
    inputs = tokens.reshape(total_rows, model_width).astype(jnp.float32)
    unit_in, factor_in, normed_in = norm_parts(inputs, norm_first)
    in_fold = row_adder(normed_in, lax.all_gather(joined_input_weight, "fsdp", axis=0, tiled=True))
    projected_tokens = in_fold[0]
    query_turned = apply_rotary(
        projected_tokens[:, :query_columns].reshape(total_rows, QUERY_HEAD_COUNT, HEAD_DIMENSION),
        cosine_lookup,
        sine_lookup,
    ).astype(jnp.bfloat16)
    key_turned = apply_rotary(
        projected_tokens[:, query_columns : query_columns + paired_width].reshape(
            total_rows, KEY_VALUE_HEADS, HEAD_DIMENSION
        ),
        cosine_lookup,
        sine_lookup,
    ).astype(jnp.bfloat16)
    value_low = projected_tokens[:, query_columns + paired_width :].astype(jnp.bfloat16)
    packed = jnp.concatenate(
        [
            query_turned.reshape(seq_count, shard_len, sequence_splits, query_slab),
            key_turned.reshape(seq_count, shard_len, sequence_splits, pair_slab),
            value_low.reshape(seq_count, shard_len, sequence_splits, pair_slab),
        ],
        axis=3,
    )
    by_heads = lax.all_to_all(packed, "seq", split_axis=2, concat_axis=1, tiled=True)
    head_query = by_heads[:, :, 0, :query_slab].reshape(
        seq_count, full_len, paired_heads, repeat_count, HEAD_DIMENSION
    )
    head_key = by_heads[:, :, 0, query_slab : query_slab + pair_slab].reshape(
        seq_count, full_len, paired_heads, HEAD_DIMENSION
    )
    head_value = by_heads[:, :, 0, query_slab + pair_slab :].reshape(
        seq_count, full_len, paired_heads, HEAD_DIMENSION
    )
    doc_starts = jnp.arange(full_len, dtype=jnp.int32)[None, :] - positions
    out_blocks = []
    log_blocks = []
    for block_index in range(full_len // step_rows):
        begin_row = block_index * step_rows
        end_row = begin_row + step_rows
        scores = block_scores(
            head_query[:, begin_row:end_row], head_key[:, :end_row], begin_row, doc_starts, scaling
        )
        row_max = jnp.max(scores, axis=-1, keepdims=True)
        raised = jnp.exp(scores - row_max)
        row_total = jnp.sum(raised, axis=-1, keepdims=True)
        shares = (raised / row_total).astype(jnp.bfloat16)
        out_blocks.append(
            jnp.einsum(
                "skgqt,stkd->sqkgd",
                shares,
                head_value[:, :end_row],
                preferred_element_type=jnp.float32,
            )
        )
        log_blocks.append(row_max + jnp.log(row_total))
    log_sums = jnp.concatenate(log_blocks, axis=3)
    mixed_heads = (
        jnp.concatenate(out_blocks, axis=1)
        .astype(jnp.bfloat16)
        .reshape(seq_count, full_len, 1, query_slab)
    )
    mixed_rows = lax.all_to_all(
        mixed_heads, "seq", split_axis=1, concat_axis=2, tiled=True
    ).reshape(total_rows, query_columns)
    out_fold = row_adder(mixed_rows, lax.all_gather(out_projection, "fsdp", axis=0, tiled=True))
    residual = inputs + out_fold[0]
    unit_mid, factor_mid, normed_mid = norm_parts(residual, norm_second)
    feed_fold = pair_adder(
        normed_mid,
        (
            lax.all_gather(gate_weight, "fsdp", axis=0, tiled=True),
            lax.all_gather(up_weight, "fsdp", axis=0, tiled=True),
        ),
    )
    gate_pre = feed_fold[0]
    up_pre = feed_fold[1]
    gate_sig = jax.nn.sigmoid(gate_pre)
    gate_act = gate_pre * gate_sig
    hidden = (gate_act * up_pre).astype(jnp.bfloat16)
    down_fold = row_adder(hidden, lax.all_gather(down_weight, "fsdp", axis=0, tiled=True))
    block_out = (
        (residual + down_fold[0]).astype(jnp.bfloat16).reshape(seq_count, shard_len, model_width)
    )
    full_in, full_out, full_gate, full_up, full_down = (
        lax.all_gather(joined_input_weight, "fsdp", axis=0, tiled=True),
        lax.all_gather(out_projection, "fsdp", axis=0, tiled=True),
        lax.all_gather(gate_weight, "fsdp", axis=0, tiled=True),
        lax.all_gather(up_weight, "fsdp", axis=0, tiled=True),
        lax.all_gather(down_weight, "fsdp", axis=0, tiled=True),
    )
    grad_out = cotangent.reshape(total_rows, model_width).astype(jnp.float32)
    grad_low = cotangent.reshape(total_rows, model_width)
    grad_hidden = jnp.einsum("rd,fd->rf", grad_low, full_down, preferred_element_type=jnp.float32)
    grad_gate = (grad_hidden * up_pre * (gate_sig * (1.0 + gate_pre * (1.0 - gate_sig)))).astype(
        jnp.bfloat16
    )
    grad_up = (grad_hidden * gate_act).astype(jnp.bfloat16)
    grad_mid = jnp.einsum(
        "rf,df->rd", grad_gate, full_gate, preferred_element_type=jnp.float32
    ) + jnp.einsum("rf,df->rd", grad_up, full_up, preferred_element_type=jnp.float32)
    grad_norm_mid, gain_second = norm_back(grad_mid, unit_mid, factor_mid, norm_second)
    grad_resid = grad_out + grad_norm_mid
    grad_branch = grad_resid.astype(jnp.bfloat16)
    grad_mixed = jnp.einsum(
        "rd,ed->re", grad_branch, full_out, preferred_element_type=jnp.float32
    ).astype(jnp.bfloat16)
    head_grad = lax.all_to_all(
        grad_mixed.reshape(seq_count, shard_len, sequence_splits, query_slab),
        "seq",
        split_axis=2,
        concat_axis=1,
        tiled=True,
    )
    head_grad = head_grad.reshape(seq_count, full_len, paired_heads, repeat_count, HEAD_DIMENSION)
    query_grads = []
    key_grad = jnp.zeros((seq_count, full_len, paired_heads, HEAD_DIMENSION), jnp.float32)
    value_grad = jnp.zeros((seq_count, full_len, paired_heads, HEAD_DIMENSION), jnp.float32)
    for block_index in range(full_len // step_rows):
        begin_row = block_index * step_rows
        end_row = begin_row + step_rows
        query_block = head_query[:, begin_row:end_row]
        grad_block = head_grad[:, begin_row:end_row]
        scores = block_scores(query_block, head_key[:, :end_row], begin_row, doc_starts, scaling)
        shares = jnp.exp(scores - log_sums[:, :, :, begin_row:end_row])
        prob_grad = jnp.einsum(
            "sqkgd,stkd->skgqt",
            grad_block,
            head_value[:, :end_row],
            preferred_element_type=jnp.float32,
        )
        mean_dot = jnp.sum(shares * prob_grad, axis=-1, keepdims=True)
        score_grad = (scaling * (shares * (prob_grad - mean_dot))).astype(jnp.bfloat16)
        query_grads.append(
            jnp.einsum(
                "skgqt,stkd->sqkgd",
                score_grad,
                head_key[:, :end_row],
                preferred_element_type=jnp.float32,
            )
        )
        key_grad = key_grad.at[:, :end_row].add(
            jnp.einsum(
                "skgqt,sqkgd->stkd", score_grad, query_block, preferred_element_type=jnp.float32
            )
        )
        value_grad = value_grad.at[:, :end_row].add(
            jnp.einsum(
                "skgqt,sqkgd->stkd",
                shares.astype(jnp.bfloat16),
                grad_block,
                preferred_element_type=jnp.float32,
            )
        )
    packed_back = jnp.concatenate(
        [
            jnp.concatenate(query_grads, axis=1)
            .astype(jnp.bfloat16)
            .reshape(seq_count, full_len, 1, query_slab),
            key_grad.astype(jnp.bfloat16).reshape(seq_count, full_len, 1, pair_slab),
            value_grad.astype(jnp.bfloat16).reshape(seq_count, full_len, 1, pair_slab),
        ],
        axis=3,
    )
    on_tokens = lax.all_to_all(packed_back, "seq", split_axis=1, concat_axis=2, tiled=True)
    query_back = (
        on_tokens[..., :query_slab]
        .reshape(total_rows, QUERY_HEAD_COUNT, HEAD_DIMENSION)
        .astype(jnp.float32)
    )
    key_back = (
        on_tokens[..., query_slab : query_slab + pair_slab]
        .reshape(total_rows, KEY_VALUE_HEADS, HEAD_DIMENSION)
        .astype(jnp.float32)
    )
    value_back = on_tokens[..., query_slab + pair_slab :].reshape(total_rows, paired_width)
    proj_grad = jnp.concatenate(
        [
            apply_rotary(query_back, cosine_lookup, -sine_lookup)
            .reshape(total_rows, query_columns)
            .astype(jnp.bfloat16),
            apply_rotary(key_back, cosine_lookup, -sine_lookup)
            .reshape(total_rows, paired_width)
            .astype(jnp.bfloat16),
            value_back,
        ],
        axis=1,
    )
    grad_in = jnp.einsum("re,de->rd", proj_grad, full_in, preferred_element_type=jnp.float32)
    grad_norm_in, gain_first = norm_back(grad_in, unit_in, factor_in, norm_first)
    tokens_grad = (
        (grad_resid + grad_norm_in).astype(jnp.bfloat16).reshape(seq_count, shard_len, model_width)
    )

    def product_of(operand, right_side):
        return jnp.einsum("rd,re->de", operand, right_side, preferred_element_type=jnp.float32)

    owner_part = lax.psum_scatter(
        jnp.concatenate(
            [
                product_of(normed_in, proj_grad),
                product_of(normed_mid, grad_gate),
                product_of(normed_mid, grad_up),
                product_of(mixed_rows, grad_branch),
            ],
            axis=1,
        ).astype(jnp.bfloat16),
        "fsdp",
        scatter_dimension=0,
        tiled=True,
    ).astype(jnp.float32)
    down_part = lax.psum_scatter(
        jnp.einsum("rf,rd->fd", hidden, grad_low, preferred_element_type=jnp.float32).astype(
            jnp.bfloat16
        ),
        "fsdp",
        scatter_dimension=0,
        tiled=True,
    ).astype(jnp.float32)
    owner_part, down_part = (
        lax.psum(owner_part.astype(jnp.bfloat16), "seq").astype(jnp.float32),
        lax.psum(down_part.astype(jnp.bfloat16), "seq").astype(jnp.float32),
    )
    gain_totals = lax.psum((gain_first, gain_second), ("seq", "fsdp"))
    input_columns = (QUERY_HEAD_COUNT + 2 * KEY_VALUE_HEADS) * HEAD_DIMENSION
    in_grad = owner_part[:, :input_columns]
    gate_grad = owner_part[:, input_columns : input_columns + FF]
    up_grad = owner_part[:, input_columns + FF : input_columns + 2 * FF]
    out_grad = owner_part[:, input_columns + 2 * FF :]
    return (
        block_out,
        tokens_grad,
        in_grad,
        out_grad,
        gate_grad,
        up_grad,
        down_part,
        gain_totals[0],
        gain_totals[1],
    )


def solution(mesh):
    return jax.shard_map(
        body,
        mesh=mesh,
        in_specs=(
            P("fsdp", "seq", None),
            P("fsdp", None),
            P("fsdp", None),
            P("fsdp", None),
            P("fsdp", None),
            P("fsdp", None),
            P(),
            P(),
            P("fsdp", None),
            P("fsdp", "seq", None),
        ),
        out_specs=(
            P("fsdp", "seq", None),
            P("fsdp", "seq", None),
            P("fsdp", None),
            P("fsdp", None),
            P("fsdp", None),
            P("fsdp", None),
            P("fsdp", None),
            P(),
            P(),
        ),
        check_vma=False,
    )
```

profile of v0, /device:TPU:0, one launch (start us, length us, event | category | flops | bytes accessed | tf_op | source)
XLA Modules:
  0.0 1375.9 jit_solution(15492844296058917122)
XLA Ops:
  12.6 90.6 %all-gather.6.cloned.1.call-done = bf16[1536,3072]{1,0:T(8,128)(2,1)} async-done(((bf16[192,3072]{1,0:T(8,128)(2,1)}), bf16[1536,3072]{1,0:T(8,128)(2,1)}) %all-gather.6.cloned.1.call-update) | async-done | bytes 9437200 | tf_op jit(solution)/shard_map/all_gather | solution.py:108
  103.2 7.6 fusion.71
  113.3 2.3 copy.103
  115.6 2.9 reshape.480
  118.5 2.4 copy.101
  120.8 2.4 subtract_convert_fusion.1
  127.2 17.2 %pad_maximum_fusion.1 = bf16[2,256,4,768]{1,0,3,2:T(2,128)(2,1)} fusion(bf16[2,256,4,192]{1,0,3,2:T(2,128)(2,1)} %reshape.480, bf16[2,256,4,192]{1,0,3,2:T(2,128)(2,1)S(1)} %convert_element_type.141, bf16[2,256,4,384]{1,0,3,2:T(2,128)(2,1)S(1)} %copy-done.13), kind=kLoop, calls=%fused_computation.49 | loop fusion | flops 3145728 | bytes 6291456 | tf_op jit(solution)/shard_map/concatenate | solution.py:123
  144.3 3.7 all-to-all-start
  151.6 33.3 %all-to-all-done = bf16[2,256,4,768]{1,0,3,2:T(2,128)(2,1)S(1)} async-done(((bf16[2,256,4,768]{1,0,3,2:T(2,128)(2,1)}), bf16[2,256,4,768]{1,0,3,2:T(2,128)(2,1)S(1)}, u32[]{:S(2)}, u32[]{:S(2)}) %all-to-all-start) | async-done | bytes 3145760 | tf_op jit(solution)/shard_map/all_to_all | solution.py:131
  186.5 7.4 copy.104
  197.0 2.3 copy.106
  201.5 3.3 fusion.70
  208.2 2.5 fusion.35
  210.7 2.6 copy.110
  213.3 8.9 fusion.69
  222.2 8.1 fusion.5
  230.4 7.6 fusion.37
  241.3 22.2 %all_to_all.66 = bf16[2,1024,1,384]{3,0,2,1:T(2,128)(2,1)S(1)} all-to-all(bf16[2,1024,1,384]{3,0,2,1:T(2,128)(2,1)S(1)} %pad_maximum_fusion.5), channel_id=1, replica_groups=mesh['seq'=4,'fsdp'=8] {'seq'}, dimensions={1} | all-to-all | bytes 3145728 | tf_op jit(solution)/shard_map/all_to_all | solution.py:169
  265.3 5.2 multiply_reduce_fusion.4
  272.6 12.1 fusion.73
  284.7 104.0 %all-gather.10.cloned.1.call-done = bf16[1536,4096]{1,0:T(8,128)(2,1)} async-done(((bf16[192,4096]{1,0:T(8,128)(2,1)}), bf16[1536,4096]{1,0:T(8,128)(2,1)}) %all-gather.10.cloned.1.call-update) | async-done | bytes 12582928 | tf_op jit(solution)/shard_map/all_gather | solution.py:178
  388.7 11.7 fusion.72
  400.4 104.8 %all-gather.14.cloned.1.call-done = bf16[4096,1536]{1,0:T(8,128)(2,1)} async-done(((bf16[512,1536]{1,0:T(8,128)(2,1)}), bf16[4096,1536]{1,0:T(8,128)(2,1)}) %all-gather.14.cloned.1.call-update) | async-done | bytes 12582928 | tf_op jit(solution)/shard_map/all_gather | solution.py:187
  505.2 21.9 %multiply_convert_fusion = (bf16[512,4096]{1,0:T(8,128)(2,1)}, bf16[512,4096]{1,0:T(8,128)(2,1)}, bf16[512,4096]{1,0:T(8,128)(2,1)}) fusion(f32[512,4096]{1,0:T(8,128)} %fusion.72, f32[512,4096]{1,0:T(8,128)} %fusion.73, bf16[512,1536]{1,0:T(8,128)(2,1)S(1)} %bitcast.239, bf16[4096,1536]{1,0:T(8,128)(2,1)} %all-gather.14.cloned.1.call-done), kind=kOutput, calls=%fused_computation.27 | convolution fusion | flops 6473908224 | bytes 43515904 | tf_op jit(solution)/shard_map/rd,fd->rf/dot_general | solution.py:200
  527.1 12.3 convolution_convert_fusion
  539.4 11.3 fusion.74
  550.7 12.0 multiply_reduce_fusion
  565.3 2.7 convolution_convert_fusion.5
  569.8 4.1 all-to-all-start.2
  574.0 19.6 %all-to-all-done.2 = bf16[2,256,4,384]{3,1,0,2:T(8,128)(2,1)S(1)} async-done(((bf16[2,256,4,384]{3,1,0,2:T(8,128)(2,1)}), bf16[2,256,4,384]{3,1,0,2:T(8,128)(2,1)S(1)}, u32[]{:S(2)}, u32[]{:S(2)}) %all-to-all-start.2) | async-done | bytes 1572896 | tf_op jit(solution)/shard_map/all_to_all | solution.py:214
  595.9 4.8 fusion.39
  600.7 9.6 fusion.30
  610.4 2.5 copy.125
  612.8 4.6 fusion.49
  617.4 15.8 %fusion.34 = bf16[2,2,96,2,512]{4,2,3,1,0:T(8,128)(2,1)} fusion(f32[2,2,512,512,2]{3,2,4,1,0:T(8,128)} %fusion.49, f32[2,2,2,512,512]{3,4,2,1,0:T(8,128)} %copy-done, f32[2,2,2,512]{3,2,1,0:T(2,128)S(1)} %log_add_fusion.1, bf16[2,1024,2,96]{1,3,2,0:T(8,128)(2,1)} %bitcast.243), kind=kOutput, calls=%fused_computation.84 | convolution fusion | flops 417731072 | bytes 34766848 | tf_op jit(solution)/shard_map/skgqt,stkd->sqkgd/dot_general | solution.py:241
  633.2 3.1 copy.118
  636.3 8.1 fusion.46
  644.4 23.4 %fusion.36 = bf16[2,2,96,2,512]{4,2,3,1,0:T(8,128)(2,1)S(1)} fusion(bf16[2,1024,2,96,1]{1,3,4,2,0:T(8,128)(2,1)} %bitcast.244, f32[2,2,1024,512,2]{3,2,4,1,0:T(8,128)} %fusion.46, f32[2,2,2,512,1024]{3,4,2,1,0:T(8,128)} %get-tuple-element.104, f32[2,2,2,512]{3,2,1,0:T(2,128)S(1)} %log_add_fusion), kind=kOutput, calls=%fused_computation.86 | convolution fusion | flops 835064832 | bytes 35143680 | tf_op jit(solution)/shard_map/skgqt,stkd->sqkgd/dot_general | solution.py:241
  669.7 13.4 fusion.38
  683.2 24.5 %fusion.31 = bf16[2,1024,2,96]{1,3,2,0:T(8,128)(2,1)} fusion(f32[2,512,2,96]{1,3,2,0:T(8,128)} %fusion.38, f32[2,2,1024,512,2]{3,2,4,1,0:T(8,128)} %fusion.46, f32[2,2,2,512,1024]{3,4,2,1,0:T(8,128)} %get-tuple-element.104, f32[2,2,2,512]{3,2,1,0:T(2,128)S(1)} %log_add_fusion, bf16[2,1024,2,2,96]{1,4,3,2,0:T(8,128)(2,1)} %bitcast.233), kind=kOutput, calls=%fused_computation.79 | convolution fusion | flops 835458048 | bytes 69500928 | tf_op jit(solution)/shard_map/skgqt,sqkgd->stkd/dot_general | solution.py:249
  707.7 2.5 copy.124
  710.1 14.5 %pad_maximum_fusion.2 = bf16[2,1024,1,768]{3,0,2,1:T(2,128)(2,1)} fusion(bf16[2,1024,1,192]{3,0,2,1:T(2,128)(2,1)S(1)} %copy.125, bf16[2,1024,1,192]{3,0,2,1:T(2,128)(2,1)S(1)} %copy.124, bf16[2,512,1,384]{3,0,2,1:T(2,128)(2,1)} %copy.119, bf16[2,512,1,384]{3,0,2,1:T(2,128)(2,1)S(1)} %copy-done.17), kind=kLoop, calls=%fused_computation.50 | loop fusion | flops 12582912 | bytes 6291456 | tf_op jit(solution)/shard_map/concatenate | solution.py:261
  724.6 4.9 all-to-all-start.3
  729.7 6.1 convolution_convert_fusion.4
  735.7 9.6 convolution_convert_fusion.1
  745.3 9.6 convolution_convert_fusion.2
  754.9 10.7 all-to-all-done.3
  765.6 6.9 copy.127
  774.2 4.1 copy.128
  778.2 4.5 reshape.491
  782.8 2.5 slice_convert_fusion.2
  785.2 2.4 copy.129
  787.6 3.3 reshape.492
  795.3 9.6 convolution_convert_fusion.3
  804.8 29.4 %pad_maximum_fusion = bf16[1536,12800]{1,0:T(8,128)(2,1)} fusion(bf16[1536,1536]{1,0:T(8,128)(2,1)} %convolution_convert_fusion.4, bf16[1536,4096]{1,0:T(8,128)(2,1)} %convolution_convert_fusion.1, bf16[1536,4096]{1,0:T(8,128)(2,1)} %convolution_convert_fusion.2, bf16[1536,3072]{1,0:T(8,128)(2,1)} %convolution_convert_fusion.3), kind=kLoop, calls=%fused_computation.2 | loop fusion | flops 157286400 | bytes 78643200 | tf_op jit(solution)/shard_map/concatenate | solution.py:305
  834.3 377.9 %reduce-scatter.3.cloned.1.call-done = bf16[192,12800]{1,0:T(8,128)(2,1)} async-done(((bf16[1536,12800]{1,0:T(8,128)(2,1)}), bf16[192,12800]{1,0:T(8,128)(2,1)}) %reduce-scatter.3.cloned.1.call-update) | async-done | bytes 4915216 | tf_op jit(solution)/shard_map/reduce_scatter | solution.py:304
  1212.3 12.5 fusion.25
  1224.8 11.2 multiply_reduce_fusion.1
  1236.0 38.7 %all-reduce.2 = (f32[1536]{0:T(1024)}, f32[1536]{0:T(1024)}) all-reduce(f32[1536]{0:T(1024)S(1)} %get-tuple-element.75, f32[1536]{0:T(1024)S(1)} %copy-done.44), channel_id=1, replica_groups=mesh['seq'=4,'fsdp'=8] {'seq','fsdp'}, use_global_device_ids=true, to_apply=%region_15.16 | all-reduce | flops 3072 | bytes 24576 | tf_op jit(solution)/shard_map/psum | solution.py:330
  1274.7 4.8 add_convert_fusion
  1279.6 78.4 %all-reduce.6.cloned.1.call-done = (bf16[192,12800]{1,0:T(8,128)(2,1)}, bf16[512,1536]{1,0:T(8,128)(2,1)}) async-done(((bf16[192,12800]{1,0:T(8,128)(2,1)}, bf16[512,1536]{1,0:T(8,128)(2,1)}), (bf16[192,12800]{1,0:T(8,128)(2,1)}, bf16[512,1536]{1,0:T(8,128)(2,1)})) %all-reduce.6.cloned.1.call-update) | async-done | bytes 6488080 | tf_op jit(solution)/shard_map/psum | solution.py:327
  1358.0 2.4 slice.250
  1360.3 2.9 slice.249
  1363.3 3.5 fusion.66
  (172 shorter events, 49.3 us)
Async XLA Ops:
  7.2 3.4 copy-start.43
  7.2 3.5 copy-start.2
  7.2 4.9 copy-start.38
  7.2 95.9 %all-gather.6.cloned.1.call-start = ((), (), s32[]{:S(2)}) async-start(), calls=%async_computation.6 | async-start | bytes 10616832 | tf_op jit(solution)/shard_map/all_gather | solution.py:108
  7.9 257.4 %all-gather.8.cloned.1.call-start = ((), (), s32[]{:S(2)}) async-start(), calls=%async_computation.7 | async-start | bytes 5308416 | tf_op jit(solution)/shard_map/all_gather | solution.py:172
  8.7 263.9 %all-gather.12.cloned.1.call-start = ((), (), s32[]{:S(2)}) async-start(), calls=%async_computation.9 | async-start | bytes 14155776 | tf_op jit(solution)/shard_map/all_gather | solution.py:179
  9.4 379.3 %all-gather.10.cloned.1.call-start = ((), (), s32[]{:S(2)}) async-start(), calls=%async_computation.8 | async-start | bytes 14155776 | tf_op jit(solution)/shard_map/all_gather | solution.py:178
  10.0 495.2 %all-gather.14.cloned.1.call-start = ((), (), s32[]{:S(2)}) async-start(), calls=%async_computation.10 | async-start | bytes 14155776 | tf_op jit(solution)/shard_map/all_gather | solution.py:187
  11.0 1.1 copy-start.41
  12.1 113.6 %copy-start.18 = (f32[512,48]{0,1:T(8,128)}, f32[512,48]{0,1:T(8,128)S(1)}, u32[]{:S(2)}) copy-start(f32[512,48]{0,1:T(8,128)S(1)} %get-tuple-element.102) | copy-start | bytes 294916
  12.6 98.2 %copy-start.23 = (bf16[512,1536]{1,0:T(8,128)(2,1)}, bf16[512,1536]{1,0:T(8,128)(2,1)S(1)}, u32[]{:S(2)}) copy-start(bf16[512,1536]{1,0:T(8,128)(2,1)S(1)} %multiply_convert_fusion.4) | copy-start | bytes 4718596
  123.2 2.0 copy-start.11
  125.7 1.4 copy-start.13
  144.3 40.5 %all-to-all-start = ((bf16[2,256,4,768]{1,0,3,2:T(2,128)(2,1)}), bf16[2,256,4,768]{1,0,3,2:T(2,128)(2,1)S(1)}, u32[]{:S(2)}, u32[]{:S(2)}) async-start(bf16[2,256,4,768]{1,0,3,2:T(2,128)(2,1)} %pad_maximum_fusion.1), calls=%async_computation | async-start | bytes 6291456 | tf_op jit(solution)/shard_map/all_to_all | solution.py:131
  148.1 686.3 %reduce-scatter.5.cloned.1.call-start = ((), (), s32[]{:S(2)}) async-start(), calls=%async_computation.12 | async-start | bytes 14155776 | tf_op jit(solution)/shard_map/reduce_scatter | solution.py:318
  184.9 1.7 copy-start.7
  197.0 4.0 copy-start.16
  201.0 12.3 copy-start.20
  201.5 28.9 %copy-start.14 = (bf16[2,1024,1,192]{1,3,0,2:T(8,128)(2,1)}, bf16[2,1024,1,192]{1,3,0,2:T(8,128)(2,1)S(1)}, u32[]{:S(2)}) copy-start(bf16[2,1024,1,192]{1,3,0,2:T(8,128)(2,1)S(1)} %copy.105) | copy-start | bytes 2359300
  204.8 3.4 copy-start
  204.8 3.4 copy-start.34
  206.1 4.6 copy-start.36
  263.6 1.7 copy-start.3
  265.3 5.2 copy-start.22
  265.3 6.9 copy-start.40
  270.5 1.7 copy-start.9
  272.5 116.2 %copy-start.25 = (bf16[512,1536]{1,0:T(8,128)(2,1)}, bf16[512,1536]{1,0:T(8,128)(2,1)S(1)}, u32[]{:S(2)}) copy-start(bf16[512,1536]{1,0:T(8,128)(2,1)S(1)} %multiply_convert_fusion.3) | copy-start | bytes 4718596
  284.7 220.5 %copy-start.28 = (bf16[2,256,1536]{2,1,0:T(8,128)(2,1)S(1)}, bf16[2,256,1536]{2,1,0:T(8,128)(2,1)}, u32[]{:S(2)}) copy-start(bf16[2,256,1536]{2,1,0:T(8,128)(2,1)} %param.31) | copy-start | bytes 4718596
  539.4 11.3 copy-start.10
  539.4 25.9 %slice-start = ((s8[4718592]{0:T(1024)(128)(4,1)}), s8[4194304]{0:T(1024)(128)(4,1)S(1)}, s32[]{:S(2)}) async-start(s8[4718592]{0:T(1024)(128)(4,1)} %bitcast.258), calls=%async_computation.14 | async-start | bytes 8388608
  550.7 14.6 %slice-start.1 = ((s8[4718592]{0:T(1024)(128)(4,1)}), s8[524288]{0:T(1024)(128)(4,1)S(1)}, s32[]{:S(2)}) async-start(s8[4718592]{0:T(1024)(128)(4,1)} %bitcast.258), calls=%async_computation.15 | async-start | bytes 1048576
  563.7 1.7 copy-start.5
  568.0 5.9 copy-start.35
  568.0 5.9 copy-start.37
  569.8 23.7 %all-to-all-start.2 = ((bf16[2,256,4,384]{3,1,0,2:T(8,128)(2,1)}), bf16[2,256,4,384]{3,1,0,2:T(8,128)(2,1)S(1)}, u32[]{:S(2)}, u32[]{:S(2)}) async-start(bf16[2,256,4,384]{3,1,0,2:T(8,128)(2,1)} %copy.114), calls=%async_computation.2 | async-start | bytes 3145728 | tf_op jit(solution)/shard_map/all_to_all | solution.py:214
  600.7 12.1 copy-start.15
  644.4 25.3 %copy-start.21 = (bf16[2,1024,1,384]{1,3,0,2:T(8,128)(2,1)S(1)}, bf16[2,1024,1,384]{1,3,0,2:T(8,128)(2,1)}, u32[]{:S(2)}) copy-start(bf16[2,1024,1,384]{1,3,0,2:T(8,128)(2,1)} %copy-done.20) | copy-start | bytes 4718596
  683.2 27.0 %copy-start.17 = (bf16[2,512,1,384]{3,0,2,1:T(2,128)(2,1)S(1)}, bf16[2,512,1,384]{3,0,2,1:T(2,128)(2,1)}, u32[]{:S(2)}) copy-start(bf16[2,512,1,384]{3,0,2,1:T(2,128)(2,1)} %copy.118) | copy-start | bytes 2359300
  724.6 5.0 copy-start.6
  724.6 40.9 %all-to-all-start.3 = ((bf16[2,1024,1,768]{3,0,2,1:T(2,128)(2,1)}), bf16[2,1024,1,768]{3,0,2,1:T(2,128)(2,1)}, u32[]{:S(2)}, u32[]{:S(2)}) async-start(bf16[2,1024,1,768]{3,0,2,1:T(2,128)(2,1)} %pad_maximum_fusion.2), calls=%async_computation.3 | async-start | bytes 6291456 | tf_op jit(solution)/shard_map/all_to_all | solution.py:271
  729.6 482.6 %reduce-scatter.3.cloned.1.call-start = ((), (), s32[]{:S(2)}) async-start(), calls=%async_computation.11 | async-start | bytes 44236800 | tf_op jit(solution)/shard_map/reduce_scatter | solution.py:304
  729.6 6.1 copy-start.26
  729.6 6.1 copy-start.46
  735.7 9.6 copy-start.45
  772.5 1.7 copy-start.8
  785.2 7.9 copy-start.19
  785.2 7.9 copy-start.29
  790.9 2.3 copy-start.12
  793.2 1.1 copy-start.30
  793.6 1.0 copy-start.32
  793.6 1.7 copy-start.24
  834.3 523.7 %all-reduce.6.cloned.1.call-start = ((), (), s32[]{:S(2)}) async-start(), calls=%async_computation.13 | async-start | bytes 12976128 | tf_op jit(solution)/shard_map/psum | solution.py:327
  1212.2 12.6 copy-start.4
  1212.2 12.6 copy-start.31
  1212.2 12.6 copy-start.33
  1212.3 12.6 copy-start.39
  1212.3 12.6 copy-start.42
  1224.8 11.2 copy-start.44
  1358.0 5.3 copy-start.1
  1363.3 3.5 copy-start.27
Sparse Core Ops, SparseCore 0:
  9.7 93.4 all-gather.5
  104.8 50.1 all-gather.7
  156.6 115.5 all-gather.11
  273.7 114.9 all-gather.9
  390.2 114.9 all-gather.13
  539.5 127.4 reduce-scatter.4
  834.4 377.7 reduce-scatter.2
  1216.2 141.7 all-reduce.5
where the time goes:
time: 1390 us; the launch traced here: 1380 us
  waiting for transfers between devices  822 us (59%)
  matrix products  282 us (20%)
  other arithmetic  92.6 us (7%)
  local copies, waits for them, and re-layouts  89.9 us (6%)
  blocking collectives  60.9 us (4%)
  between operations  15.3 us (1%)
    reduce_scatter x1, waiting for transfers between devices, body(): lax.psum_scatter(jnp.concatenate([product_of(normed_in, proj_grad), produ...  378 us
    all_gather x1, waiting for transfers between devices, body(): lax.all_gather(down_weight, 'fsdp', axis=0, tiled=True)  105 us
    all_gather x1, waiting for transfers between devices, body(): lax.all_gather(gate_weight, 'fsdp', axis=0, tiled=True)  104 us
    all_gather x1, waiting for transfers between devices, body(): lax.all_gather(joined_input_weight, 'fsdp', axis=0, tiled=True)  90.6 us
    psum x1, waiting for transfers between devices, body(): lax.psum(owner_part.astype(jnp.bfloat16), 'seq').astype(jnp.float32)  78.4 us
    dot_general x2, matrix products, body(): jnp.einsum('skgqt,stkd->sqkgd', score_grad, head_key[:, :end_row], prefer...  39.2 us
    psum x1, blocking collectives, body(): gain_totals = lax.psum((gain_first, gain_second), ('seq', 'fsdp'))  38.7 us
    dot_general x2, matrix products, body(): jnp.einsum('skgqt,sqkgd->stkd', score_grad, query_block, preferred_elemen...  37.9 us
  transfers between devices with their start and end apart: 11, of which 8 were waited for; matrix products, arithmetic and copies ran while one was open for 30% of the time, Pallas kernels for 0%

commit v1 on v0

v1 whole, which is shorter than its diff:
```python
import functools
import math

import jax
import jax.numpy as jnp
import numpy as np
from jax import lax
from jax.experimental import pallas as pl
from jax.experimental.pallas import tpu as pltpu
from jax.sharding import PartitionSpec as P

FF = 4096
QUERY_HEAD_COUNT = 16
KEY_VALUE_HEADS = 8
HEAD_DIMENSION = 96
HALF = HEAD_DIMENSION // 2
LANES = 128

epsilon = 1e-05
rope_base = 100000.0
SCALING = 1.0 / math.sqrt(HEAD_DIMENSION)
LOG2E = 1.4426950408889634
BF16 = jnp.bfloat16
F32 = jnp.float32
MIB = 1024 * 1024


def dot(a, b, ca, cb):
    return lax.dot_general(a, b, (((ca,), (cb,)), ((), ())), preferred_element_type=F32)


def params(limit):
    return pltpu.CompilerParams(
        vmem_limit_bytes=limit * MIB,
    )


def cost(flops, moved, trans=0):
    return pl.CostEstimate(flops=int(flops), bytes_accessed=int(moved), transcendentals=int(trans))


def pad_matrix(pairs, repeat):
    unit = repeat + 2
    out = np.zeros((pairs * unit * HEAD_DIMENSION, pairs * unit * LANES), np.float32)
    for g in range(pairs):
        for r in range(unit):
            if r < repeat:
                src = (g * repeat + r) * HEAD_DIMENSION
            else:
                src = (pairs * repeat + (r - repeat) * pairs + g) * HEAD_DIMENSION
            dst = (g * unit + r) * LANES
            for j in range(HEAD_DIMENSION):
                lane = j if (r == unit - 1 or j < HALF) else 64 + j - HALF
                out[src + j, dst + lane] = 1.0
    return out


def place_matrix(pairs, repeat):
    out = np.zeros((pairs, repeat * LANES, pairs * repeat * HEAD_DIMENSION), np.float32)
    for g in range(pairs):
        for r in range(repeat):
            for j in range(HEAD_DIMENSION):
                out[g, r * LANES + j, (g * repeat + r) * HEAD_DIMENSION + j] = 1.0
    return out


def in_kernel(unit, x_ref, w_ref, pad_ref, cos_ref, sin_ref, out_ref, wide):
    @pl.when((pl.program_id(0) == 0) & (pl.program_id(1) == 0))
    def _():
        wide[...] = dot(w_ref[...], pad_ref[...], 1, 0).astype(BF16)

    rows = dot(x_ref[...], wide[...], 1, 0)
    cosine, sine = cos_ref[...], sin_ref[...]
    for part in range(rows.shape[1] // LANES):
        piece = rows[:, part * LANES : (part + 1) * LANES]
        if part % unit != unit - 1:
            piece = piece * cosine + pltpu.roll(piece, 64, 1) * sine
        out_ref[:, part * LANES : (part + 1) * LANES] = piece.astype(BF16)


def project_in(normed, w_slice, pad, cosine, sine, unit):
    spans, seqs, span, width = normed.shape
    narrow, wide = pad.shape
    rows = spans * seqs * span
    return pl.pallas_call(
        functools.partial(in_kernel, unit),
        out_shape=jax.ShapeDtypeStruct((spans, seqs, span, wide), BF16),
        grid=(spans, seqs),
        in_specs=[
            pl.BlockSpec((None, None, span, width), lambda i, j: (i, j, 0, 0)),
            pl.BlockSpec((width, narrow), lambda i, j: (0, 0)),
            pl.BlockSpec((narrow, wide), lambda i, j: (0, 0)),
            pl.BlockSpec((None, None, span, LANES), lambda i, j: (i, j, 0, 0)),
            pl.BlockSpec((None, None, span, LANES), lambda i, j: (i, j, 0, 0)),
        ],
        out_specs=pl.BlockSpec((None, None, span, wide), lambda i, j: (i, j, 0, 0)),
        scratch_shapes=[pltpu.VMEM((width, wide), BF16)],
        compiler_params=params(40),
        cost_estimate=cost(2 * rows * width * wide, 2 * rows * (width + wide) + 2 * width * narrow),
        name="project_in",
    )(normed, w_slice, pad, cosine, sine)


def mask_of(scores, first_key, first_row, starts, repeat, diagonal):
    keys = lax.broadcasted_iota(jnp.int32, scores.shape, 0) + first_key
    allowed = keys >= starts
    if diagonal:
        step = scores.shape[1] // repeat
        rows = lax.broadcasted_iota(jnp.int32, scores.shape, 1) % step + first_row
        allowed = allowed & (keys <= rows)
    return jnp.where(allowed, scores, -1e30)


def forward_kernel(step, repeat, proj_ref, start_ref, place_ref, out_ref, lse_ref):
    spans, span, _ = proj_ref.shape
    full = spans * span
    pair = pl.program_id(1)
    key = proj_ref[:, :, repeat * LANES : (repeat + 1) * LANES].reshape(full, LANES)
    value = proj_ref[:, :, (repeat + 1) * LANES :].reshape(full, LANES)
    value_t = value.T
    starts = start_ref[...]
    for block in range(full // step):
        begin, end = block * step, (block + 1) * step
        rows = slice(begin, end)
        query = jnp.concatenate(
            [
                proj_ref[:, :, r * LANES : (r + 1) * LANES].reshape(full, LANES)[rows]
                for r in range(repeat)
            ],
            axis=0,
        )
        starts_now = jnp.concatenate([starts[:, rows]] * repeat, axis=1)
        pieces = []
        for key_block in range(block + 1):
            first = key_block * step
            scores = dot(key[first : first + step], query, 1, 1) * (SCALING * LOG2E)
            pieces.append(
                mask_of(scores, first, begin, starts_now, repeat, key_block == block)
            )
        top = functools.reduce(
            jnp.maximum, [jnp.max(p, axis=0, keepdims=True) for p in pieces]
        )
        total = None
        summed = None
        for key_block in range(block + 1):
            first = key_block * step
            raised = jnp.exp2(pieces[key_block] - top)
            part = jnp.sum(raised, axis=0, keepdims=True)
            mixed = dot(value_t[:, first : first + step], raised.astype(BF16), 1, 0)
            total = part if total is None else total + part
            summed = mixed if summed is None else summed + mixed
        mixed_t = (summed * (1.0 / total)).astype(BF16)
        lse_ref[block : block + 1, :] = top + jnp.log2(total)
        wide = None
        for r in range(repeat):
            term = dot(
                mixed_t[:, r * step : (r + 1) * step],
                place_ref[r * LANES : (r + 1) * LANES, :],
                0,
                0,
            )
            wide = term if wide is None else wide + term
        wide = wide.astype(BF16)
        for piece in range(step // span):
            at = block * (step // span) + piece
            rows_now = wide[piece * span : (piece + 1) * span]

            @pl.when(pair == 0)
            def _():
                out_ref[at] = rows_now

            @pl.when(pair != 0)
            def _():
                out_ref[at] = out_ref[at] + rows_now


def attention_forward(proj, starts, place, repeat, step):
    spans, seqs, span, wide = proj.shape
    pairs, _, narrow = place.shape
    full = spans * span
    group = wide // pairs
    work = seqs * pairs * repeat * full * full
    return pl.pallas_call(
        functools.partial(forward_kernel, step, repeat),
        out_shape=(
            jax.ShapeDtypeStruct((spans, seqs, span, narrow), BF16),
            jax.ShapeDtypeStruct((seqs, pairs, full // step, repeat * step), F32),
        ),
        grid=(seqs, pairs),
        in_specs=[
            pl.BlockSpec((spans, None, span, group), lambda i, j: (0, i, 0, j)),
            pl.BlockSpec((None, 1, full), lambda i, j: (i, 0, 0)),
            pl.BlockSpec((None, repeat * LANES, narrow), lambda i, j: (j, 0, 0)),
        ],
        out_specs=(
            pl.BlockSpec((spans, None, span, narrow), lambda i, j: (0, i, 0, 0)),
            pl.BlockSpec((None, None, full // step, repeat * step), lambda i, j: (i, j, 0, 0)),
        ),
        compiler_params=params(48),
        cost_estimate=cost(2 * work * 256, 2 * proj.size * 2, work),
        name="attention_forward",
    )(proj, starts, place)


def backward_kernel(
    step,
    repeat,
    proj_ref,
    start_ref,
    place_ref,
    grad_ref,
    lse_ref,
    cos_ref,
    sin_ref,
    pad_ref,
    out_ref,
    key_acc,
    value_acc,
):
    spans, span, _ = proj_ref.shape
    full = spans * span
    pair = pl.program_id(1)
    key = proj_ref[:, :, repeat * LANES : (repeat + 1) * LANES].reshape(full, LANES)
    value = proj_ref[:, :, (repeat + 1) * LANES :].reshape(full, LANES)
    key_t = key.T
    starts = start_ref[...]
    cosine = cos_ref[...].reshape(full, LANES)
    sine = sin_ref[...].reshape(full, LANES)
    key_acc[...] = jnp.zeros_like(key_acc)
    value_acc[...] = jnp.zeros_like(value_acc)

    def turn_back(grad, rows):
        grad = grad.astype(BF16).astype(F32)
        return (grad * cosine[rows] - pltpu.roll(grad, 64, 1) * sine[rows]).astype(BF16)

    def put(at, rows_now):
        @pl.when(pair == 0)
        def _():
            out_ref[at] = rows_now

        @pl.when(pair != 0)
        def _():
            out_ref[at] = out_ref[at] + rows_now

    for block in range(full // step):
        begin, end = block * step, (block + 1) * step
        rows = slice(begin, end)
        query = jnp.concatenate(
            [
                proj_ref[:, :, r * LANES : (r + 1) * LANES].reshape(full, LANES)[rows]
                for r in range(repeat)
            ],
            axis=0,
        )
        grad_rows = grad_ref[...].reshape(full, grad_ref.shape[2])[rows]
        grad = jnp.concatenate(
            [
                dot(grad_rows, place_ref[r * LANES : (r + 1) * LANES, :], 1, 1).astype(BF16)
                for r in range(repeat)
            ],
            axis=0,
        )
        starts_now = jnp.concatenate([starts[:, rows]] * repeat, axis=1)
        lse = lse_ref[block : block + 1, :]
        kept = []
        mean_dot = None
        for key_block in range(block + 1):
            first = key_block * step
            keys = slice(first, first + step)
            scores = dot(key[keys], query, 1, 1) * (SCALING * LOG2E)
            scores = mask_of(scores, first, begin, starts_now, repeat, key_block == block)
            shares = jnp.exp2(scores - lse)
            value_acc[keys, :] += dot(shares.astype(BF16), grad, 1, 0)
            prob_grad = dot(value[keys], grad, 1, 1)
            product = shares * prob_grad
            part = jnp.sum(product, axis=0, keepdims=True)
            mean_dot = part if mean_dot is None else mean_dot + part
            kept.append((shares, product))
        query_grad_t = None
        for key_block in range(block + 1):
            first = key_block * step
            keys = slice(first, first + step)
            shares, product = kept[key_block]
            score_grad = (SCALING * (product - shares * mean_dot)).astype(BF16)
            key_acc[keys, :] += dot(score_grad, query, 1, 0)
            term = dot(key_t[:, keys], score_grad, 1, 0)
            query_grad_t = term if query_grad_t is None else query_grad_t + term
        query_grad = query_grad_t.T
        wide = None
        for r in range(repeat):
            turned = turn_back(query_grad[r * step : (r + 1) * step], rows)
            term = dot(turned, pad_ref[:, r * LANES : (r + 1) * LANES], 1, 1)
            wide = term if wide is None else wide + term
        wide = wide.astype(BF16)
        for piece in range(step // span):
            put(block * (step // span) + piece, wide[piece * span : (piece + 1) * span])
    for at in range(spans):
        rows = slice(at * span, (at + 1) * span)
        turned = turn_back(key_acc[rows, :], rows)
        wide = dot(turned, pad_ref[:, repeat * LANES : (repeat + 1) * LANES], 1, 1)
        wide += dot(value_acc[rows, :].astype(BF16), pad_ref[:, (repeat + 1) * LANES :], 1, 1)
        out_ref[at] = out_ref[at] + wide.astype(BF16)


def attention_backward(proj, starts, place, grad, lse, cosine, sine, pad, repeat, step):
    spans, seqs, span, wide = proj.shape
    pairs, _, narrow = place.shape
    full = spans * span
    group = wide // pairs
    work = seqs * pairs * repeat * full * full
    return pl.pallas_call(
        functools.partial(backward_kernel, step, repeat),
        out_shape=jax.ShapeDtypeStruct((spans, seqs, span, pad.shape[0]), BF16),
        grid=(seqs, pairs),
        in_specs=[
            pl.BlockSpec((spans, None, span, group), lambda i, j: (0, i, 0, j)),
            pl.BlockSpec((None, 1, full), lambda i, j: (i, 0, 0)),
            pl.BlockSpec((None, repeat * LANES, narrow), lambda i, j: (j, 0, 0)),
            pl.BlockSpec((spans, None, span, narrow), lambda i, j: (0, i, 0, 0)),
            pl.BlockSpec((None, None, full // step, repeat * step), lambda i, j: (i, j, 0, 0)),
            pl.BlockSpec((spans, None, span, LANES), lambda i, j: (0, i, 0, 0)),
            pl.BlockSpec((spans, None, span, LANES), lambda i, j: (0, i, 0, 0)),
            pl.BlockSpec((pad.shape[0], group), lambda i, j: (0, j)),
        ],
        out_specs=pl.BlockSpec((spans, None, span, pad.shape[0]), lambda i, j: (0, i, 0, 0)),
        scratch_shapes=[pltpu.VMEM((full, LANES), F32), pltpu.VMEM((full, LANES), F32)],
        compiler_params=params(56),
        cost_estimate=cost(2 * work * 640, 2 * proj.size * 4, work),
        name="attention_backward",
    )(proj, starts, place, grad, lse, cosine, sine, pad)


def out_kernel(mixed_ref, w_ref, tokens_ref, gain_ref, resid_ref, normed_ref):
    summed = tokens_ref[...].astype(F32)
    depth = mixed_ref.shape[2]
    for at in range(mixed_ref.shape[0]):
        summed += dot(mixed_ref[at], w_ref[at * depth : (at + 1) * depth, :], 1, 0)
    resid_ref[...] = summed
    factor = lax.rsqrt(jnp.mean(summed * summed, axis=-1, keepdims=True) + epsilon)
    normed_ref[...] = (summed * factor * gain_ref[...]).astype(BF16)


def project_out(mixed, w_out, tokens, gain, block):
    spans, rows, depth = mixed.shape
    width = w_out.shape[1]
    return pl.pallas_call(
        out_kernel,
        out_shape=(
            jax.ShapeDtypeStruct((rows, width), F32),
            jax.ShapeDtypeStruct((rows, width), BF16),
        ),
        grid=(rows // block,),
        in_specs=[
            pl.BlockSpec((spans, block, depth), lambda i: (0, i, 0)),
            pl.BlockSpec(w_out.shape, lambda i: (0, 0)),
            pl.BlockSpec((block, width), lambda i: (i, 0)),
            pl.BlockSpec((1, width), lambda i: (0, 0)),
        ],
        out_specs=(
            pl.BlockSpec((block, width), lambda i: (i, 0)),
            pl.BlockSpec((block, width), lambda i: (i, 0)),
        ),
        compiler_params=params(40),
        cost_estimate=cost(2 * rows * width * width, rows * width * 10 + width * width * 2),
        name="project_out",
    )(mixed, w_out, tokens, gain)


def feed_kernel(
    x_ref, c_ref, gate_ref, up_ref, down_ref, out_ref, dx_ref, hid_ref, dgate_ref, dup_ref
):
    x = x_ref[...]
    gate = dot(x, gate_ref[...], 1, 0)
    up = dot(x, up_ref[...], 1, 0)
    sig = jax.nn.sigmoid(gate)
    act = gate * sig
    hidden = (act * up).astype(BF16)
    hid_ref[...] = hidden
    out_ref[...] = dot(hidden, down_ref[...], 1, 0).astype(BF16)
    grad_hidden = dot(c_ref[...], down_ref[...], 1, 1)
    grad_gate = (grad_hidden * up * (sig * (1.0 + gate * (1.0 - sig)))).astype(BF16)
    grad_up = (grad_hidden * act).astype(BF16)
    dgate_ref[...] = grad_gate
    dup_ref[...] = grad_up
    dx_ref[...] = (dot(grad_gate, gate_ref[...], 1, 1) + dot(grad_up, up_ref[...], 1, 1)).astype(
        BF16
    )


def feed_forward(x, c, gate_w, up_w, down_w, block):
    rows, width = x.shape
    inner = gate_w.shape[1]
    one = pl.Buffered(1)
    row_spec = pl.BlockSpec((block, width), lambda i: (i, 0))
    hid_spec = pl.BlockSpec((block, inner), lambda i: (i, 0))
    return pl.pallas_call(
        feed_kernel,
        out_shape=(
            jax.ShapeDtypeStruct((rows, width), BF16),
            jax.ShapeDtypeStruct((rows, width), BF16),
            jax.ShapeDtypeStruct((rows, inner), BF16),
            jax.ShapeDtypeStruct((rows, inner), BF16),
            jax.ShapeDtypeStruct((rows, inner), BF16),
        ),
        grid=(rows // block,),
        in_specs=[
            row_spec,
            row_spec,
            pl.BlockSpec(gate_w.shape, lambda i: (0, 0), pipeline_mode=one),
            pl.BlockSpec(up_w.shape, lambda i: (0, 0), pipeline_mode=one),
            pl.BlockSpec(down_w.shape, lambda i: (0, 0), pipeline_mode=one),
        ],
        out_specs=(row_spec, row_spec, hid_spec, hid_spec, hid_spec),
        compiler_params=params(56),
        cost_estimate=cost(
            12 * rows * width * inner, rows * (8 * width + 6 * inner) + 6 * width * inner
        ),
        name="feed_forward",
    )(x, c, gate_w, up_w, down_w)


def back_kernel(grad_ref, resid_ref, cot_ref, gain_ref, w_ref, resid_grad_ref, branch_ref, mixed_ref):
    rows = resid_ref[...]
    factor = lax.rsqrt(jnp.mean(rows * rows, axis=-1, keepdims=True) + epsilon)
    unit_rows = rows * factor
    scaled = grad_ref[...].astype(F32) * gain_ref[...]
    mean_dot = jnp.mean(scaled * unit_rows, axis=-1, keepdims=True)
    grad = cot_ref[...].astype(F32) + factor * (scaled - unit_rows * mean_dot)
    resid_grad_ref[...] = grad
    branch = grad.astype(BF16)
    branch_ref[...] = branch
    depth = mixed_ref.shape[2]
    for at in range(mixed_ref.shape[0]):
        mixed_ref[at] = dot(branch, w_ref[at * depth : (at + 1) * depth, :], 1, 1).astype(BF16)


def norm_out_back(grad_mid, resid, cot, gain, w_out, spans, block):
    rows, width = resid.shape
    depth = w_out.shape[0] // spans
    row_spec = pl.BlockSpec((block, width), lambda i: (i, 0))
    return pl.pallas_call(
        back_kernel,
        out_shape=(
            jax.ShapeDtypeStruct((rows, width), F32),
            jax.ShapeDtypeStruct((rows, width), BF16),
            jax.ShapeDtypeStruct((spans, rows, depth), BF16),
        ),
        grid=(rows // block,),
        in_specs=[
            row_spec,
            row_spec,
            row_spec,
            pl.BlockSpec((1, width), lambda i: (0, 0)),
            pl.BlockSpec(w_out.shape, lambda i: (0, 0)),
        ],
        out_specs=(row_spec, row_spec, pl.BlockSpec((spans, block, depth), lambda i: (0, i, 0))),
        compiler_params=params(40),
        cost_estimate=cost(2 * rows * width * width, rows * width * 16 + width * width * 2),
        name="norm_out_back",
    )(grad_mid, resid, cot, gain, w_out)


def turning_tables(positions, spans):
    seqs, full = positions.shape
    frequency = jnp.exp(
        jnp.arange(HALF, dtype=F32) * (-2.0 * math.log(rope_base) / HEAD_DIMENSION)
    )
    angles = positions.astype(F32)[:, :, None] * frequency
    cosine, sine = jnp.cos(angles), jnp.sin(angles)
    empty = jnp.zeros((seqs, full, 64 - HALF), F32)

    def spread(first, second):
        table = jnp.concatenate([first, empty, second, empty], axis=-1)
        return table.reshape(seqs, spans, full // spans, LANES).transpose(1, 0, 2, 3)

    return spread(cosine, cosine), spread(-sine, sine)


def after(value, *others):
    return lax.optimization_barrier((value, *others))[0]


def body(
    tokens,
    joined_input_weight,
    out_projection,
    gate_weight,
    up_weight,
    down_weight,
    norm_first,
    norm_second,
    positions,
    cotangent,
):
    seqs, span, width = tokens.shape
    spans = lax.axis_size("seq")
    shards = lax.axis_size("fsdp")
    me = lax.axis_index("seq")
    rows = seqs * span
    full = positions.shape[1]
    pairs = KEY_VALUE_HEADS // spans
    repeat = QUERY_HEAD_COUNT // KEY_VALUE_HEADS
    unit = repeat + 2
    query_columns = QUERY_HEAD_COUNT * HEAD_DIMENSION
    pair_columns = KEY_VALUE_HEADS * HEAD_DIMENSION
    query_slab = query_columns // spans
    pair_slab = pair_columns // spans
    own_rows = joined_input_weight.shape[0]
    piece = FF // (shards * spans)
    step = span
    pad = jnp.asarray(pad_matrix(pairs, repeat), BF16)
    place = jnp.asarray(place_matrix(pairs, repeat), BF16)

    def columns(begin, size):
        return lax.dynamic_slice_in_dim(joined_input_weight, begin + me * size, size, 1)

    in_shard = jnp.concatenate(
        [
            columns(0, query_slab),
            columns(query_columns, pair_slab),
            columns(query_columns + pair_columns, pair_slab),
        ],
        axis=1,
    )

    def inner_columns(weight):
        cut = weight.reshape(own_rows, shards, spans, piece)
        return lax.dynamic_index_in_dim(cut, me, 2, keepdims=False).reshape(
            own_rows, shards * piece
        )

    def gather(shard):
        return lax.all_gather(shard, "fsdp", axis=0, tiled=True)

    w_in = gather(in_shard)
    w_out = gather(out_projection)
    w_gate = gather(inner_columns(gate_weight))
    w_up = gather(inner_columns(up_weight))
    w_down = gather(lax.dynamic_slice_in_dim(down_weight, me * piece, piece, 0))

    inputs = tokens.reshape(rows, width).astype(F32)
    factor_in = lax.rsqrt(jnp.mean(inputs * inputs, axis=-1, keepdims=True) + epsilon)
    unit_in = inputs * factor_in
    normed_in = (unit_in * norm_first).astype(BF16)
    x_in = lax.all_gather(normed_in.reshape(seqs, span, width), "seq", axis=0)
    cosine, sine = turning_tables(positions, spans)
    starts = (jnp.arange(full, dtype=jnp.int32)[None, :] - positions)[:, None, :]

    proj = project_in(x_in, w_in, pad, cosine, sine, unit)
    grad_all = lax.all_gather(after(cotangent, proj), "seq", axis=0).reshape(spans * rows, width)
    mixed, lse = attention_forward(proj, starts, place, repeat, step)
    mixed_rows = lax.all_to_all(
        mixed, "seq", split_axis=0, concat_axis=0, tiled=True
    ).reshape(spans, rows, query_slab)
    resid, normed_mid = project_out(
        mixed_rows, w_out, tokens.reshape(rows, width), norm_second[None, :], min(256, rows)
    )
    x_mid = lax.all_gather(normed_mid, "seq", axis=0).reshape(spans * rows, width)
    down_part, grad_mid_part, hidden, grad_gate, grad_up = feed_forward(
        x_mid, grad_all, w_gate, w_up, w_down, 256
    )

    def scatter(value):
        return lax.psum_scatter(
            value.reshape(spans, rows, width), "seq", scatter_dimension=0, tiled=False
        )

    grad_mid = scatter(grad_mid_part)
    down_sum = scatter(after(down_part, grad_mid))
    block_out = (resid + down_sum.astype(F32)).astype(BF16).reshape(seqs, span, width)

    def product_of(left, right):
        return jnp.einsum("rd,re->de", left, right, preferred_element_type=F32)

    gate_part = product_of(x_mid, grad_gate)
    up_part = product_of(x_mid, grad_up)
    down_grad_part = product_of(hidden, grad_all)
    gain_second = (
        jnp.sum(gate_part * w_gate.astype(F32), axis=1) + jnp.sum(up_part * w_up.astype(F32), axis=1)
    ) / norm_second

    def owned(value):
        return lax.psum_scatter(value.astype(BF16), "fsdp", scatter_dimension=0, tiled=True)

    def inner_whole(value):
        every = lax.all_gather(value, "seq", axis=0).astype(F32)
        return (
            every.reshape(spans, own_rows, shards, piece)
            .transpose(1, 2, 0, 3)
            .reshape(own_rows, FF)
        )

    gate_grad = inner_whole(owned(gate_part))
    up_grad = inner_whole(owned(up_part))
    down_grad = lax.all_gather(owned(down_grad_part), "seq", axis=0, tiled=True).astype(F32)

    grad_resid, grad_branch, grad_mixed = norm_out_back(
        grad_mid,
        resid,
        cotangent.reshape(rows, width),
        norm_second[None, :],
        w_out,
        spans,
        min(256, rows),
    )
    head_grad = lax.all_to_all(
        grad_mixed.reshape(spans, seqs, span, query_slab),
        "seq",
        split_axis=0,
        concat_axis=0,
        tiled=True,
    )
    out_part = jnp.einsum(
        "srd,re->sde", mixed_rows, grad_branch, preferred_element_type=F32
    ).reshape(query_columns, width)
    out_own = lax.psum_scatter(
        out_part.astype(BF16), ("fsdp", "seq"), scatter_dimension=0, tiled=True
    )
    out_grad = lax.all_gather(out_own, "seq", axis=0, tiled=True).astype(F32)

    grad_proj = attention_backward(
        proj, starts, place, head_grad, lse, cosine, sine, pad, repeat, step
    ).reshape(spans * rows, pad.shape[0])
    grad_in_part = jnp.einsum(
        "re,de->rd", grad_proj, w_in, preferred_element_type=F32
    ).astype(BF16)
    grad_in = scatter(grad_in_part).astype(F32)
    in_part = product_of(x_in.reshape(spans * rows, width), grad_proj)
    gain_first = jnp.sum(in_part * w_in.astype(F32), axis=1) / norm_first
    in_every = lax.all_gather(owned(in_part), "seq", axis=0).astype(F32)
    in_grad = jnp.concatenate(
        [
            part.transpose(1, 0, 2).reshape(own_rows, -1)
            for part in (
                in_every[:, :, :query_slab],
                in_every[:, :, query_slab : query_slab + pair_slab],
                in_every[:, :, query_slab + pair_slab :],
            )
        ],
        axis=1,
    )
    scaled = grad_in * norm_first
    mean_dot = jnp.mean(scaled * unit_in, axis=-1, keepdims=True)
    tokens_grad = (
        (grad_resid + factor_in * (scaled - unit_in * mean_dot))
        .astype(BF16)
        .reshape(seqs, span, width)
    )
    gain_totals = lax.psum((gain_first, gain_second), ("seq", "fsdp"))
    return (
        block_out,
        tokens_grad,
        in_grad,
        out_grad,
        gate_grad,
        up_grad,
        down_grad,
        gain_totals[0],
        gain_totals[1],
    )


def solution(mesh):
    return jax.shard_map(
        body,
        mesh=mesh,
        in_specs=(
            P("fsdp", "seq", None),
            P("fsdp", None),
            P("fsdp", None),
            P("fsdp", None),
            P("fsdp", None),
            P("fsdp", None),
            P(),
            P(),
            P("fsdp", None),
            P("fsdp", "seq", None),
        ),
        out_specs=(
            P("fsdp", "seq", None),
            P("fsdp", "seq", None),
            P("fsdp", None),
            P("fsdp", None),
            P("fsdp", None),
            P("fsdp", None),
            P("fsdp", None),
            P(),
            P(),
        ),
        check_vma=False,
    )
```

time: 1390 us -> 1120 us (0.81)
  matrix products: 282 us -> 62.9 us
  waiting for transfers between devices: 822 us -> 673 us
  Pallas kernels: 0 us -> 132 us
  other arithmetic: 92.6 us -> 42.4 us
  local copies, waits for them, and re-layouts: 89.9 us -> 108 us
    reduce_scatter x2 -> x5, waiting for transfers between devices: 378 us -> 122 us  [the longest x4 62.6 us: owned(): lax.psum_scatter(value.astype(BF16), 'fsdp', scatter_dimension=0, tiled=T...]
    dot_general x27 -> x6, matrix products: 282 us -> 62.9 us  [the longest x4 47.1 us: product_of(): return jnp.einsum('rd,re->de', left, right, preferred_element_type=F32)]
    unnamed x8 -> x23, waiting for transfers between devices: 3.16 us -> 154 us
    pallas_call x0 -> x6, Pallas kernels: none -> 132 us  [the longest x1 48.3 us: feed_forward(): pl.pallas_call(feed_kernel, out_shape=(jax.ShapeDtypeStruct((rows, width)...]
    all_gather x5 -> x12, waiting for transfers between devices: 299 us -> 385 us  [the longest x5 111 us: gather(): return lax.all_gather(shard, 'fsdp', axis=0, tiled=True)]
    psum x1 -> x0, waiting for transfers between devices: 78.4 us -> none  [body(): lax.psum(owner_part.astype(jnp.bfloat16), 'seq').astype(jnp.float32)]
    concatenate x8 -> x2, other arithmetic: 63.5 us -> 3.7 us  [the longest x1 2.87 us: body(): jnp.concatenate([part.transpose(1, 0, 2).reshape(own_rows, -1) for part i...]
    all_to_all x3 -> x1, waiting for transfers between devices: 63.5 us -> 11.8 us  [body(): lax.all_to_all(mixed, 'seq', split_axis=0, concat_axis=0, tiled=True)]
  transfers between devices with their start and end apart: 11 -> 21, of which waited for: 8 -> 19; matrix products, arithmetic and copies ran while one was open for 30% -> 16% of each run, Pallas kernels for 0% -> 7%
where the time goes in v1:
time: 1120 us; the launch traced here: 1110 us
  waiting for transfers between devices  673 us (60%)
  Pallas kernels  132 us (12%)
  local copies, waits for them, and re-layouts  108 us (10%)
  blocking collectives  74.7 us (7%)
  matrix products  62.9 us (6%)
  other arithmetic  42.4 us (4%)
  between operations  15.2 us (1%)
    unnamed x23, waiting for transfers between devices  154 us
    all_gather x5, waiting for transfers between devices, gather(): return lax.all_gather(shard, 'fsdp', axis=0, tiled=True)  111 us
    all_gather x1, waiting for transfers between devices, body(): lax.all_gather(normed_mid, 'seq', axis=0).reshape(spans * rows, width)  72.6 us
    all_gather x1, waiting for transfers between devices, body(): x_in = lax.all_gather(normed_in.reshape(seqs, span, width), 'seq', axis=0)  71.7 us
    all_gather x1, waiting for transfers between devices, body(): lax.all_gather(after(cotangent, proj), 'seq', axis=0)  70.9 us
    reduce_scatter x4, waiting for transfers between devices, owned(): lax.psum_scatter(value.astype(BF16), 'fsdp', scatter_dimension=0, tiled=T...  62.6 us
    reduce_scatter x1, waiting for transfers between devices, body(): lax.psum_scatter(out_part.astype(BF16), ('fsdp', 'seq'), scatter_dimensio...  59.2 us
    pallas_call x1, Pallas kernels, feed_forward(): pl.pallas_call(feed_kernel, out_shape=(jax.ShapeDtypeStruct((rows, width)...  48.3 us
  transfers between devices with their start and end apart: 21, of which 19 were waited for; matrix products, arithmetic and copies ran while one was open for 16% of the time, Pallas kernels for 7%

profile of v1, /device:TPU:0, one launch (start us, length us, event | category | flops | bytes accessed | tf_op | source)
XLA Modules:
  0.0 1112.8 jit_solution(6744825878396480220)
XLA Ops:
  10.4 1.8 fusion
  16.0 2.8 reshape.169
  18.9 3.8 reshape.171
  22.7 6.1 dynamic-slice_reduce_fusion
  30.8 3.7 fusion.14
  34.6 2.5 fusion.13
  37.1 7.7 all-gather.19.cloned.1.call-done.w_ref
  44.8 71.7 %all-gather.31.cloned.1.call-done = bf16[8,256,1536]{2,1,0:T(8,128)(2,1)} async-done(((bf16[2,256,1536]{2,1,0:T(8,128)(2,1)}), bf16[8,256,1536]{2,1,0:T(8,128)(2,1)}) %all-gather.31.cloned.1.call-update) | async-done | bytes 6291472 | tf_op jit(solution)/shard_map/all_gather | solution.py:545
  120.6 12.8 %project_in.1.proj_ref = bf16[4,2,256,1024]{3,2,1,0:T(8,128)(2,1)S(1)} custom-call(bf16[4,2,256,1536]{3,2,1,0:T(8,128)(2,1)} %bitcast.110, bf16[1536,768]{1,0:T(8,128)(2,1)S(1)} %copy-done.11, bf16[768,1024]{1,0:T(8,128)(2,1)S(1)} %copy-done.19, f32[4,2,256,128]{3,2,1,0:T(8,128)S(1)} %copy-done.16, f32[4,2,256,128]{3,2,1,0:T(8,128)S(1)} %copy-done.15), custom_call_target="tpu_custom_call" | custom-call | flops 6442450944 | bytes 12845056 | tf_op jit(solution)/shard_map/project_in/pallas_call | solution.py:85
  133.5 1.9 copy-done.21
  135.5 2.2 copy-done.22
  137.7 18.8 %attention_forward.1 = (bf16[4,2,256,384]{3,2,1,0:T(8,128)(2,1)S(1)}, f32[2,2,4,512]{3,2,1,0:T(4,128)S(1)}) custom-call(bf16[4,2,256,1024]{3,2,1,0:T(8,128)(2,1)S(1)} %copy-done.22, s32[2,1,1024]{2,1,0:T(1,128)S(1)} %broadcast_in_dim.7.start_ref, bf16[2,256,384]{2,1,0:T(8,128)(2,1)S(1)} %copy-done.20), custom_call_target="tpu_custom_call" | custom-call | flops 4294967296 | bytes 8388608 | tf_op jit(solution)/shard_map/attention_forward/pallas_call | solution.py:183
  158.2 3.7 all-to-all-start
  162.2 7.7 all-gather.21.cloned.1.call-done.w_ref
  169.9 11.8 %all-to-all-done = bf16[4,2,256,384]{3,2,1,0:T(8,128)(2,1)S(1)} async-done(((bf16[4,2,256,384]{3,2,1,0:T(8,128)(2,1)}), bf16[4,2,256,384]{3,2,1,0:T(8,128)(2,1)S(1)}, u32[]{:S(2)}, u32[]{:S(2)}) %all-to-all-start) | async-done | bytes 1572896 | tf_op jit(solution)/shard_map/all_to_all | solution.py:552
  181.7 2.9 copy-done.8
  184.6 4.1 project_out.1
  191.6 17.5 %all-gather.27.cloned.1.call-done.down_ref = bf16[1024,1536]{1,0:T(8,128)(2,1)} async-done(((bf16[128,1536]{1,0:T(8,128)(2,1)}), bf16[1024,1536]{1,0:T(8,128)(2,1)}) %all-gather.27.cloned.1.call-update) | async-done | bytes 3145744 | tf_op jit(solution)/shard_map/all_gather | solution.py:533
  209.1 39.2 %all-gather.23.cloned.1.call-done.gate_ref = bf16[1536,1024]{1,0:T(8,128)(2,1)} async-done(((bf16[192,1024]{1,0:T(8,128)(2,1)}), bf16[1536,1024]{1,0:T(8,128)(2,1)}) %all-gather.23.cloned.1.call-update) | async-done | bytes 3145744 | tf_op jit(solution)/shard_map/all_gather | solution.py:533
  248.4 39.3 %all-gather.25.cloned.1.call-done.up_ref = bf16[1536,1024]{1,0:T(8,128)(2,1)} async-done(((bf16[192,1024]{1,0:T(8,128)(2,1)}), bf16[1536,1024]{1,0:T(8,128)(2,1)}) %all-gather.25.cloned.1.call-update) | async-done | bytes 3145744 | tf_op jit(solution)/shard_map/all_gather | solution.py:533
  287.6 70.9 %all-gather.35.cloned.1.call-done = bf16[8,256,1536]{2,1,0:T(8,128)(2,1)} async-done(((bf16[2,256,1536]{2,1,0:T(8,128)(2,1)}), bf16[8,256,1536]{2,1,0:T(8,128)(2,1)}) %all-gather.35.cloned.1.call-update) | async-done | bytes 6291472 | tf_op jit(solution)/shard_map/all_gather | solution.py:550
  358.5 72.6 %all-gather.33.cloned.1.call-done.x_ref = bf16[2048,1536]{1,0:T(8,128)(2,1)} async-done(((bf16[512,1536]{1,0:T(8,128)(2,1)}), bf16[2048,1536]{1,0:T(8,128)(2,1)}) %all-gather.33.cloned.1.call-update) | async-done | bytes 6291472 | tf_op jit(solution)/shard_map/all_gather | solution.py:558
  431.1 48.3 %feed_forward.1 = (bf16[2048,1536]{1,0:T(8,128)(2,1)}, bf16[2048,1536]{1,0:T(8,128)(2,1)}, bf16[2048,1024]{1,0:T(8,128)(2,1)}, bf16[2048,1024]{1,0:T(8,128)(2,1)}, bf16[2048,1024]{1,0:T(8,128)(2,1)}) custom-call(bf16[2048,1536]{1,0:T(8,128)(2,1)} %all-gather.33.cloned.1.call-done.x_ref, bf16[2048,1536]{1,0:T(8,128)(2,1)} %bitcast.112, ...), custom_call_target="tpu_custom_call" | custom-call | flops 38654705664 | bytes 47185920 | tf_op jit(solution)/shard_map/feed_forward/pallas_call | solution.py:396
  479.5 12.3 %fusion.18 = (bf16[1536,1024]{0,1:T(8,128)(2,1)}, f32[1536,1024]{0,1:T(8,128)}) fusion(bf16[2048,1536]{1,0:T(8,128)(2,1)} %all-gather.33.cloned.1.call-done.x_ref, bf16[2048,1024]{1,0:T(8,128)(2,1)} %get-tuple-element.35), kind=kOutput, calls=%fused_computation.58 | convolution fusion | flops 6444023808 | bytes 19922944 | tf_op jit(solution)/shard_map/rd,re->de/dot_general | solution.py:573
  491.8 4.7 copy.82
  497.0 12.7 %fusion.17 = (bf16[1536,1024]{0,1:T(8,128)(2,1)}, f32[1536,1024]{0,1:T(8,128)}) fusion(bf16[2048,1536]{1,0:T(8,128)(2,1)} %all-gather.33.cloned.1.call-done.x_ref, bf16[2048,1024]{1,0:T(8,128)(2,1)} %get-tuple-element.34), kind=kOutput, calls=%fused_computation.57 | convolution fusion | flops 6444023808 | bytes 19922944 | tf_op jit(solution)/shard_map/rd,re->de/dot_general | solution.py:573
  509.7 4.6 copy.80
  514.4 11.6 %convolution_convert_fusion.2 = bf16[1024,1536]{1,0:T(8,128)(2,1)} fusion(bf16[2048,1024]{1,0:T(8,128)(2,1)} %get-tuple-element.36, bf16[2048,1536]{1,0:T(8,128)(2,1)} %bitcast.113), kind=kOutput, calls=%fused_computation.7 | convolution fusion | flops 6444023808 | bytes 13631488 | tf_op jit(solution)/shard_map/rd,re->de/dot_general | solution.py:573
  526.1 23.7 %reduce-scatter.31.cloned.1.call-done = bf16[1,512,1536]{2,1,0:T(8,128)(2,1)} async-done(((bf16[4,512,1536]{2,1,0:T(8,128)(2,1)}), bf16[1,512,1536]{2,1,0:T(8,128)(2,1)}) %reduce-scatter.31.cloned.1.call-update) | async-done | bytes 1572880
  549.8 1.9 copy-done.4
  554.5 7.1 norm_out_back.1
  563.2 23.4 %all_to_all.10.grad_ref = bf16[4,2,256,384]{3,2,1,0:T(8,128)(2,1)} all-to-all(bf16[4,2,256,384]{3,2,1,0:T(8,128)(2,1)S(1)} %bitcast.91), channel_id=1, replica_groups=mesh['seq'=4,'fsdp'=8] {'seq'}, dimensions={0} | all-to-all | bytes 3145728 | tf_op jit(solution)/shard_map/all_to_all | solution.py:606
  586.6 40.6 %attention_backward.1 = bf16[4,2,256,768]{3,2,1,0:T(8,128)(2,1)} custom-call(bf16[4,2,256,1024]{3,2,1,0:T(8,128)(2,1)} %copy-done.21, s32[2,1,1024]{2,1,0:T(1,128)} %copy-done.17, bf16[2,256,384]{2,1,0:T(8,128)(2,1)} %constant.48.clone.place_ref, bf16[4,2,256,384]{3,2,1,0:T(8,128)(2,1)} %all_to_all.10.grad_ref, f32[2,2,4,512]{3,2,1,0:T(4,128)} %copy-done.23, ...), custom_call_target="tpu_custom_call" | custom-call | flops 10737418240 | bytes 16777216 | tf_op jit(solution)/shard_map/attention_backward/pallas_call | solution.py:311
  627.3 10.5 fusion.16
  637.7 4.5 copy.78
  643.4 33.3 %reduce-scatter.23.cloned.1.call-done = bf16[128,1536]{1,0:T(8,128)(2,1)} async-done(((bf16[1024,1536]{1,0:T(8,128)(2,1)}), bf16[128,1536]{1,0:T(8,128)(2,1)}) %reduce-scatter.23.cloned.1.call-update) | async-done | bytes 393232 | tf_op jit(solution)/shard_map/reduce_scatter | solution.py:583
  678.5 6.6 convolution_convert_fusion.1
  685.1 29.2 %reduce-scatter.25.cloned.1.call-done = bf16[192,768]{1,0:T(8,128)(2,1)} async-done(((bf16[1536,768]{1,0:T(8,128)(2,1)}), bf16[192,768]{1,0:T(8,128)(2,1)}) %reduce-scatter.25.cloned.1.call-update) | async-done | bytes 294928 | tf_op jit(solution)/shard_map/reduce_scatter | solution.py:583
  715.4 9.2 convolution_convert_fusion
  725.3 6.6 copy.74
  731.8 6.6 copy.75
  738.5 4.5 multiply_reduce_fusion.1
  746.3 1.8 convert_bitcast_fusion
  749.0 3.7 copy.72
  752.7 5.1 reshape.195
  757.8 21.2 %all-gather.39.cloned.1.call-done = bf16[768,1024]{1,0:T(8,128)(2,1)} async-done(((bf16[192,1024]{1,0:T(8,128)(2,1)}), bf16[768,1024]{1,0:T(8,128)(2,1)}) %all-gather.39.cloned.1.call-update) | async-done | bytes 1572880 | tf_op jit(solution)/shard_map/all_gather | solution.py:586
  779.0 1.8 convert_bitcast_fusion.1
  781.7 3.7 copy.70
  785.4 5.1 reshape.193
  790.5 21.2 %all-gather.29.cloned.1.call-done = bf16[512,1536]{1,0:T(8,128)(2,1)} async-done(((bf16[128,1536]{1,0:T(8,128)(2,1)}), bf16[512,1536]{1,0:T(8,128)(2,1)}) %all-gather.29.cloned.1.call-update) | async-done | bytes 1572880 | tf_op jit(solution)/shard_map/all_gather | solution.py:595
  811.7 3.5 convert_element_type.93
  815.2 6.3 copy.73
  821.5 3.8 multiply_reduce_fusion.2
  825.3 39.5 %all-reduce.3 = (f32[1536]{0:T(1024)}, f32[1536]{0:T(1024)}) all-reduce(f32[1536]{0:T(1024)S(1)} %div.14, f32[1536]{0:T(1024)S(1)} %add_divide_fusion), channel_id=1, replica_groups=mesh['seq'=4,'fsdp'=8] {'seq','fsdp'}, use_global_device_ids=true, to_apply=%region_11.12 | all-reduce | flops 3072 | bytes 24576 | tf_op jit(solution)/shard_map/psum | solution.py:649
  864.8 59.2 %reduce-scatter.21.cloned.1.call-done = bf16[48,1536]{1,0:T(8,128)(2,1)} async-done(((bf16[1536,1536]{1,0:T(8,128)(2,1)}), bf16[48,1536]{1,0:T(8,128)(2,1)}) %reduce-scatter.21.cloned.1.call-update) | async-done | bytes 147472 | tf_op jit(solution)/shard_map/reduce_scatter | solution.py:616
  924.0 11.9 %all_gather.66 = bf16[192,1536]{1,0:T(8,128)(2,1)S(1)} all-gather(bf16[48,1536]{1,0:T(8,128)(2,1)} %reduce-scatter.21.cloned.1.call-done), channel_id=1, replica_groups=mesh['seq'=4,'fsdp'=8] {'seq'}, dimensions={0}, use_global_device_ids=true | all-gather | bytes 737280 | tf_op jit(solution)/shard_map/all_gather | solution.py:619
  937.0 15.7 %all-gather.37.cloned.1.call-done = bf16[768,768]{1,0:T(8,128)(2,1)} async-done(((bf16[192,768]{1,0:T(8,128)(2,1)}), bf16[768,768]{1,0:T(8,128)(2,1)}) %all-gather.37.cloned.1.call-update) | async-done | bytes 1179664 | tf_op jit(solution)/shard_map/all_gather | solution.py:630
  962.5 2.7 reshape.183
  965.2 2.9 pad_maximum_fusion
  968.1 58.1 %reduce-scatter.33.cloned.1.call-done = bf16[1,512,1536]{2,1,0:T(8,128)(2,1)} async-done(((bf16[4,512,1536]{2,1,0:T(8,128)(2,1)}), bf16[1,512,1536]{2,1,0:T(8,128)(2,1)}) %reduce-scatter.33.cloned.1.call-update) | async-done | bytes 1572880
  1026.2 4.0 fusion.9
  1030.1 69.4 %reduce-scatter.35.cloned.1.call-done = bf16[1,512,1536]{2,1,0:T(8,128)(2,1)} async-done(((bf16[4,512,1536]{2,1,0:T(8,128)(2,1)}), bf16[1,512,1536]{2,1,0:T(8,128)(2,1)}) %reduce-scatter.35.cloned.1.call-update) | async-done | bytes 1572880
  1099.5 2.3 fusion.5
  1101.8 3.6 fusion.8
  (138 shorter events, 43.9 us)
Async XLA Ops:
  7.2 8.0 copy-start
  7.2 5.6 copy-start.2
  7.2 5.6 copy-start.29
  7.2 37.6 %all-gather.19.cloned.1.call-start = ((), (), s32[]{:S(2)}) async-start(), calls=%async_computation.10 | async-start | bytes 2654208 | tf_op jit(solution)/shard_map/all_gather | solution.py:533
  10.3 106.2 %all-gather.31.cloned.1.call-start = ((), (), s32[]{:S(2)}) async-start(), calls=%async_computation.18 | async-start | bytes 7864320 | tf_op jit(solution)/shard_map/all_gather | solution.py:545
  14.4 155.6 %all-gather.21.cloned.1.call-start = ((), (), s32[]{:S(2)}) async-start(), calls=%async_computation.11 | async-start | bytes 5308416 | tf_op jit(solution)/shard_map/all_gather | solution.py:533
  15.1 194.0 %all-gather.27.cloned.1.call-start = ((), (), s32[]{:S(2)}) async-start(), calls=%async_computation.14 | async-start | bytes 3538944 | tf_op jit(solution)/shard_map/all_gather | solution.py:533
  16.0 232.4 %all-gather.23.cloned.1.call-start = ((), (), s32[]{:S(2)}) async-start(), calls=%async_computation.12 | async-start | bytes 3538944 | tf_op jit(solution)/shard_map/all_gather | solution.py:533
  22.7 8.1 copy-start.32
  29.7 257.9 %all-gather.25.cloned.1.call-start = ((), (), s32[]{:S(2)}) async-start(), calls=%async_computation.13 | async-start | bytes 3538944 | tf_op jit(solution)/shard_map/all_gather | solution.py:533
  30.6 327.9 %all-gather.35.cloned.1.call-start = ((), (), s32[]{:S(2)}) async-start(), calls=%async_computation.20 | async-start | bytes 7864320 | tf_op jit(solution)/shard_map/all_gather | solution.py:550
  34.6 81.9 %copy-start.19 = (bf16[768,1024]{1,0:T(8,128)(2,1)S(1)}, bf16[768,1024]{1,0:T(8,128)(2,1)}, u32[]{:S(2)}) copy-start(bf16[768,1024]{1,0:T(8,128)(2,1)} %constant.47.clone.pad_ref) | copy-start | bytes 4718596
  116.5 1.7 copy-start.11
  118.2 1.2 copy-start.15
  119.4 1.2 copy-start.16
  120.6 14.8 %copy-start.20 = (bf16[2,256,384]{2,1,0:T(8,128)(2,1)S(1)}, bf16[2,256,384]{2,1,0:T(8,128)(2,1)}, u32[]{:S(2)}) copy-start(bf16[2,256,384]{2,1,0:T(8,128)(2,1)} %constant.48.clone.place_ref) | copy-start | bytes 1179652
  133.5 2.0 copy-start.21
  135.5 2.2 copy-start.22
  137.7 18.8 %copy-start.17 = (s32[2,1,1024]{2,1,0:T(1,128)}, s32[2,1,1024]{2,1,0:T(1,128)S(1)}, u32[]{:S(2)}) copy-start(s32[2,1,1024]{2,1,0:T(1,128)S(1)} %broadcast_in_dim.7.start_ref) | copy-start | bytes 24580
  156.5 1.1 copy-start.13
  157.6 0.6 copy-start.23
  158.2 4.0 copy-start.31
  158.2 23.4 %all-to-all-start = ((bf16[4,2,256,384]{3,2,1,0:T(8,128)(2,1)}), bf16[4,2,256,384]{3,2,1,0:T(8,128)(2,1)S(1)}, u32[]{:S(2)}, u32[]{:S(2)}) async-start(bf16[4,2,256,384]{3,2,1,0:T(8,128)(2,1)} %copy-done.13), calls=%async_computation | async-start | bytes 3145728 | tf_op jit(solution)/shard_map/all_to_all | solution.py:552
  161.9 269.2 %all-gather.33.cloned.1.call-start = ((), (), s32[]{:S(2)}) async-start(), calls=%async_computation.19 | async-start | bytes 7864320 | tf_op jit(solution)/shard_map/all_gather | solution.py:558
  181.7 7.0 copy-start.5
  181.7 2.9 copy-start.8
  188.7 1.7 copy-start.3
  190.4 1.1 copy-start.12
  191.6 358.2 %reduce-scatter.31.cloned.1.call-start = ((), (), s32[]{:S(2)}) async-start(), calls=%async_computation.27 | async-start | bytes 7864320
  479.4 162.9 %reduce-scatter.29.cloned.1.call-start = ((), (), s32[]{:S(2)}) async-start(), calls=%async_computation.26 | async-start | bytes 3538944 | tf_op jit(solution)/shard_map/reduce_scatter | solution.py:583
  496.6 146.3 %reduce-scatter.27.cloned.1.call-start = ((), (), s32[]{:S(2)}) async-start(), calls=%async_computation.25 | async-start | bytes 3538944 | tf_op jit(solution)/shard_map/reduce_scatter | solution.py:583
  514.4 162.4 %reduce-scatter.23.cloned.1.call-start = ((), (), s32[]{:S(2)}) async-start(), calls=%async_computation.16 | async-start | bytes 3538944 | tf_op jit(solution)/shard_map/reduce_scatter | solution.py:583
  526.0 188.3 %reduce-scatter.25.cloned.1.call-start = ((), (), s32[]{:S(2)}) async-start(), calls=%async_computation.24 | async-start | bytes 2654208 | tf_op jit(solution)/shard_map/reduce_scatter | solution.py:583
  549.8 1.9 copy-start.4
  551.7 1.4 copy-start.7
  553.1 1.4 copy-start.14
  561.6 1.7 copy-start.9
  563.2 23.4 %copy-start.18 = (bf16[512,1536]{1,0:T(8,128)(2,1)}, bf16[512,1536]{1,0:T(8,128)(2,1)S(1)}, u32[]{:S(2)}) copy-start(bf16[512,1536]{1,0:T(8,128)(2,1)S(1)} %get-tuple-element.33) | copy-start | bytes 4718596
  637.7 39.1 %copy-start.6 = (bf16[4,2,256,384]{3,2,1,0:T(8,128)(2,1)S(1)}, bf16[4,2,256,384]{3,2,1,0:T(8,128)(2,1)}, u32[]{:S(2)}) copy-start(bf16[4,2,256,384]{3,2,1,0:T(8,128)(2,1)} %copy-done.5) | copy-start | bytes 4718596
  642.2 104.1 %all-gather.41.cloned.1.call-start = ((), (), s32[]{:S(2)}) async-start(), calls=%async_computation.23 | async-start | bytes 1966080 | tf_op jit(solution)/shard_map/all_gather | solution.py:586
  642.8 136.2 %all-gather.39.cloned.1.call-start = ((), (), s32[]{:S(2)}) async-start(), calls=%async_computation.22 | async-start | bytes 1966080 | tf_op jit(solution)/shard_map/all_gather | solution.py:586
  643.4 168.3 %all-gather.29.cloned.1.call-start = ((), (), s32[]{:S(2)}) async-start(), calls=%async_computation.17 | async-start | bytes 1966080 | tf_op jit(solution)/shard_map/all_gather | solution.py:595
  676.8 247.2 %reduce-scatter.21.cloned.1.call-start = ((), (), s32[]{:S(2)}) async-start(), calls=%async_computation.15 | async-start | bytes 4866048 | tf_op jit(solution)/shard_map/reduce_scatter | solution.py:616
  685.1 267.6 %all-gather.37.cloned.1.call-start = ((), (), s32[]{:S(2)}) async-start(), calls=%async_computation.21 | async-start | bytes 1474560 | tf_op jit(solution)/shard_map/all_gather | solution.py:630
  714.4 311.8 %reduce-scatter.33.cloned.1.call-start = ((), (), s32[]{:S(2)}) async-start(), calls=%async_computation.28 | async-start | bytes 7864320
  715.1 384.3 %reduce-scatter.35.cloned.1.call-start = ((), (), s32[]{:S(2)}) async-start(), calls=%async_computation.29 | async-start | bytes 7864320
  724.6 0.7 copy-start.33
  738.5 5.5 copy-start.24
  738.5 6.4 copy-start.28
  821.5 3.8 copy-start.30
  954.1 1.4 copy-start.25
  958.6 2.6 copy-start.27
  961.1 4.1 copy-start.26
  1099.5 2.4 copy-start.10
  1101.8 3.7 copy-start.1
Sparse Core Ops, SparseCore 0:
  10.5 34.2 all-gather.18
  47.2 69.2 all-gather.30
  118.2 51.7 all-gather.20
  172.0 37.0 all-gather.26
  211.2 37.1 all-gather.22
  250.4 37.1 all-gather.24
  289.5 69.0 all-gather.34
  360.9 70.1 all-gather.32
  479.5 70.2 reduce-scatter.30
  552.5 40.3 reduce-scatter.28
  595.8 39.3 reduce-scatter.26
  637.3 39.3 reduce-scatter.22
  679.1 35.2 reduce-scatter.24
  716.1 30.1 all-gather.40
  748.0 30.9 all-gather.38
  780.7 30.9 all-gather.28
  817.0 106.9 reduce-scatter.20
  925.8 26.7 all-gather.36
  955.9 70.1 reduce-scatter.32
  1029.3 70.1 reduce-scatter.34

commit v2 on v1

v2 whole, which is shorter than its diff:
```python
import functools
import math

import jax
import jax.numpy as jnp
import numpy as np
from jax import lax
from jax.experimental import pallas as pl
from jax.experimental.pallas import tpu as pltpu
from jax.sharding import PartitionSpec as P

FF = 4096
QUERY_HEAD_COUNT = 16
KEY_VALUE_HEADS = 8
HEAD_DIMENSION = 96
HALF = HEAD_DIMENSION // 2
LANES = 128

epsilon = 1e-05
rope_base = 100000.0
SCALING = 1.0 / math.sqrt(HEAD_DIMENSION)
LOG2E = 1.4426950408889634
BF16 = jnp.bfloat16
F32 = jnp.float32
MIB = 1024 * 1024
VMEM_LIMIT = 60
COST_SCALE = 20


def dot(a, b, ca, cb):
    return lax.dot_general(a, b, (((ca,), (cb,)), ((), ())), preferred_element_type=F32)


def params(limit):
    return pltpu.CompilerParams(vmem_limit_bytes=limit * MIB)


def cost(flops, moved, trans=0):
    return pl.CostEstimate(
        flops=int(flops) * COST_SCALE, bytes_accessed=int(moved) * COST_SCALE, transcendentals=0
    )


CHAIN = []


def call(kernel, *, out_shape, in_specs, out_specs, prefetch=0, grid=(1,), scratch=(), cost_estimate=None, name=None, waits=()):
    count = prefetch + len(in_specs)
    waits = (*waits, *CHAIN[-1:])

    def run(*refs):
        kernel(*refs[:count], *refs[count + len(waits) :])

    inner = pl.pallas_call(
        run,
        out_shape=out_shape,
        grid_spec=pltpu.PrefetchScalarGridSpec(
            num_scalar_prefetch=prefetch,
            grid=grid,
            in_specs=[*in_specs, *[pl.BlockSpec(memory_space=pltpu.HBM)] * len(waits)],
            out_specs=out_specs,
            scratch_shapes=list(scratch),
        ),
        compiler_params=params(VMEM_LIMIT),
        cost_estimate=cost_estimate,
        name=name,
    )

    def made(*args):
        out = inner(*args, *waits)
        CHAIN.append(out[-1] if isinstance(out, (list, tuple)) else out)
        return out

    return made


def pin(*values):
    waits = tuple(CHAIN[-1:])
    count = len(values)
    hbm = pl.BlockSpec(memory_space=pltpu.HBM)
    out = pl.pallas_call(
        lambda *refs: None,
        out_shape=[shape(*x.shape, dtype=x.dtype) for x in values],
        in_specs=[hbm] * (count + len(waits)),
        out_specs=[hbm] * count,
        input_output_aliases={at: at for at in range(count)},
        cost_estimate=cost(0, 0),
        name="pin",
    )(*values, *waits)
    CHAIN.append(out[-1])
    return out


def whole(array, **extra):
    return pl.BlockSpec(array.shape, lambda *_: (0,) * len(array.shape), **extra)


def shape(*sizes, dtype=BF16):
    return jax.ShapeDtypeStruct(sizes, dtype)


def pad_matrix(pairs, repeat):
    unit = repeat + 2
    out = np.zeros((pairs * unit * HEAD_DIMENSION, pairs * unit * LANES), np.float32)
    for g in range(pairs):
        for r in range(unit):
            if r < repeat:
                src = (g * repeat + r) * HEAD_DIMENSION
            else:
                src = (pairs * repeat + (r - repeat) * pairs + g) * HEAD_DIMENSION
            dst = (g * unit + r) * LANES
            for j in range(HEAD_DIMENSION):
                lane = j if (r == unit - 1 or j < HALF) else 64 + j - HALF
                out[src + j, dst + lane] = 1.0
    return out


def place_matrix(pairs, repeat):
    out = np.zeros((pairs, repeat * LANES, pairs * repeat * HEAD_DIMENSION), np.float32)
    for g in range(pairs):
        for r in range(repeat):
            for j in range(HEAD_DIMENSION):
                out[g, r * LANES + j, (g * repeat + r) * HEAD_DIMENSION + j] = 1.0
    return out


def order_of(bits):
    owners = [0]
    for bit in bits:
        owners = owners + [at ^ (1 << bit) for at in owners]
    return owners


def swap(value, bit):
    size = lax.axis_size("seq")
    return lax.ppermute(value, "seq", [(i, i ^ (1 << bit)) for i in range(size)])


def exchange(value, other):
    size = lax.axis_size("seq")
    return lax.ppermute(value, "seq", [(i, i ^ other) for i in range(size)])


def shared(heads):
    return [heads[0]] + [exchange(heads[at], at) for at in range(1, len(heads))]


def around(value):
    size = lax.axis_size("fsdp")
    return lax.ppermute(value, "fsdp", [(i, (i + 2) % size) for i in range(size)])


def beside(value):
    size = lax.axis_size("fsdp")
    return lax.ppermute(value, "fsdp", [(i, i ^ 1) for i in range(size)])


def copy_kernel(source_ref, *outs):
    for at, ref in enumerate(outs):
        ref[...] = source_ref[at]


def split_rows(value, waits=()):
    seqs, span, width = value.shape
    out_shape = [shape(span, width)] * seqs
    return call(
        copy_kernel,
        out_shape=out_shape,
        in_specs=[whole(value)],
        out_specs=[whole(x) for x in out_shape],
        cost_estimate=cost(0, 4 * value.size),
        name="split_rows",
        waits=waits,
    )(value)


def stack_kernel(*refs):
    count = len(refs) // 3
    for at in range(count):
        first, second, out = refs[2 * at], refs[2 * at + 1], refs[2 * count + at]
        rows = first.shape[0]
        out[:rows] = first[...]
        out[rows:] = second[...]


def stack_rows(pairs, name, waits=()):
    out_shape = [shape(2 * a.shape[0], a.shape[1]) for a, _ in pairs]
    flat = [x for pair in pairs for x in pair]
    return call(
        stack_kernel,
        out_shape=out_shape,
        in_specs=[whole(x) for x in flat],
        out_specs=[whole(x) for x in out_shape],
        cost_estimate=cost(0, 4 * sum(x.size for x in flat)),
        name=name,
        waits=waits,
    )(*flat)


def gather_start(blocks, orders):
    return [swap(x, bits[0]) for x, bits in zip(blocks, orders)]


def gather_end(blocks, got, orders, name, waits=()):
    held = list(zip(blocks, got))
    for level in range(1, len(orders[0])):
        joined = stack_rows(held, name, waits if level == 1 else ())
        held = [(x, swap(x, bits[level])) for x, bits in zip(joined, orders)]
    return held


def fold_kernel(*refs):
    count = len(refs) // 4
    for at in range(count):
        near, got, keep, send = refs[at], refs[count + at], refs[2 * count + at], refs[3 * count + at]
        total = near[...].astype(F32) + got[...].astype(F32)
        cut = total.shape[0] // 2
        keep[...] = total[:cut]
        send[...] = total[cut:].astype(BF16)


def fold(near, got, waits=()):
    out_shape = [shape(x.shape[0] // 2, x.shape[1], dtype=F32) for x in near]
    out_shape += [shape(x.shape[0] // 2, x.shape[1]) for x in near]
    out = call(
        fold_kernel,
        out_shape=out_shape,
        in_specs=[whole(x) for x in (*near, *got)],
        out_specs=[whole(x) for x in out_shape],
        cost_estimate=cost(0, 5 * sum(x.size for x in near)),
        name="fold",
        waits=waits,
    )(*near, *got)
    return out[: len(near)], out[len(near) :]


def scatter_start(parts, orders):
    return [near for near, _ in parts], [swap(far, bits[-1]) for (_, far), bits in zip(parts, orders)]


def scatter_end(near, got, orders, waits=()):
    for level in range(len(orders[0]) - 2, -1, -1):
        near, sent = fold(near, got, waits)
        got = [swap(x, bits[level]) for x, bits in zip(sent, orders)]
    return list(zip(near, got))


def norm_kernel(tokens_ref, gain_ref, *outs):
    for seq, out in enumerate(outs):
        rows = tokens_ref[seq].astype(F32)
        factor = lax.rsqrt(jnp.mean(rows * rows, axis=-1, keepdims=True) + epsilon)
        out[...] = (rows * factor * gain_ref[...]).astype(BF16)


def norm_rows(tokens, gain):
    seqs, span, width = tokens.shape
    out_shape = [shape(span, width)] * seqs
    return call(
        norm_kernel,
        out_shape=out_shape,
        in_specs=[whole(tokens), whole(gain)],
        out_specs=[whole(x) for x in out_shape],
        cost_estimate=cost(8 * tokens.size, 4 * tokens.size),
        name="norm_rows",
    )(tokens, gain)


def cut_in_kernel(spans, sizes, me_ref, w_ref, out_ref):
    for own in range(spans):

        @pl.when(me_ref[0] == own)
        def _():
            begin, put = 0, 0
            for size in sizes:
                out_ref[:, put : put + size] = w_ref[:, begin + own * size : begin + (own + 1) * size]
                begin, put = begin + spans * size, put + size


def cut_in(me, weight, spans, sizes):
    out_shape = shape(weight.shape[0], sum(sizes))
    return call(
        functools.partial(cut_in_kernel, spans, sizes),
        out_shape=out_shape,
        prefetch=1,
        in_specs=[whole(weight)],
        out_specs=whole(out_shape),
        cost_estimate=cost(0, 4 * weight.size),
        name="cut_in",
    )(me, weight)


def cut_feed_kernel(spans, shards, piece, me_ref, gate_ref, up_ref, down_ref, both_ref, out_ref):
    inner = shards * piece
    for own in range(spans):

        @pl.when(me_ref[0] == own)
        def _():
            for shard in range(shards):
                begin = (shard * spans + own) * piece
                put = shard * piece
                both_ref[:, put : put + piece] = gate_ref[:, begin : begin + piece]
                both_ref[:, inner + put : inner + put + piece] = up_ref[:, begin : begin + piece]
            out_ref[...] = down_ref[own * piece : (own + 1) * piece, :]


def cut_feed(me, gate, up, down, spans, shards, piece, waits):
    out_shape = (shape(gate.shape[0], 2 * shards * piece), shape(piece, down.shape[1]))
    return call(
        functools.partial(cut_feed_kernel, spans, shards, piece),
        out_shape=out_shape,
        prefetch=1,
        in_specs=[whole(x) for x in (gate, up, down)],
        out_specs=[whole(x) for x in out_shape],
        cost_estimate=cost(0, 4 * gate.size),
        name="cut_feed",
        waits=waits,
    )(me, gate, up, down)


def widen_kernel(w_ref, pad_ref, out_ref):
    out_ref[...] = dot(w_ref[...], pad_ref[...], 1, 0).astype(BF16)


def widen(w_slice, pad, waits=()):
    rows, narrow = w_slice.shape
    wide = pad.shape[1]
    out_shape = shape(rows, wide)
    return call(
        widen_kernel,
        out_shape=out_shape,
        in_specs=[whole(w_slice), whole(pad)],
        out_specs=whole(out_shape),
        cost_estimate=cost(2 * rows * narrow * wide, 2 * rows * (narrow + wide)),
        name="widen",
        waits=waits,
    )(w_slice, pad)


class Walk:
    def __init__(self, spans, span, near_first):
        self.cut, self.span, self.near_first = spans // 2, span, near_first

    def first(self, step):
        return jnp.minimum(step, self.cut - 1)

    def second(self, step):
        return jnp.maximum(step - self.cut, 0)

    def near(self, step, *_):
        return (self.first(step) if self.near_first else self.second(step), 0)

    def far(self, step, *_):
        return (self.second(step) if self.near_first else self.first(step), 0)

    def both(self, step, *_):
        return (step if self.near_first else lax.rem(step + self.cut, 2 * self.cut), 0)

    def specs(self, width):
        return [
            pl.BlockSpec((self.span, width), self.near),
            pl.BlockSpec((self.span, width), self.far),
        ]

    def is_near(self):
        early = pl.program_id(0) < self.cut
        return early if self.near_first else jnp.logical_not(early)

    def load(self, near_ref, far_ref):
        return jnp.where(self.is_near(), near_ref[...], far_ref[...])

    def store(self, near_ref, far_ref, value):
        near = self.is_near()

        @pl.when(near)
        def _():
            near_ref[...] = value

        @pl.when(jnp.logical_not(near))
        def _():
            far_ref[...] = value


def owner_at(order, index):
    owner = 0
    for at, value in enumerate(order):
        owner = jnp.where(index == at, value, owner)
    return owner


class Visits:
    def __init__(self, spans, span):
        self.spans, self.span = spans, span
        self.order = sorted(range(spans), key=lambda at: -bin(at).count("1"))

    def index(self, blocks):
        held = [blocks.get(owner) for owner in self.order]
        known = next(x for x in held if x is not None)
        for at, value in enumerate(held):
            known = held[at] = known if value is None else value
        return lambda step, *_: (owner_at(held, step), 0)

    def parts(self, bits):
        order = order_of(bits)
        cut = self.spans // 2
        near = {owner: at for at, owner in enumerate(order[:cut])}
        far = {owner: at for at, owner in enumerate(order[cut:])}
        return near, far

    def specs(self, bits, width):
        return [pl.BlockSpec((self.span, width), self.index(blocks)) for blocks in self.parts(bits)]

    def rows(self, bits, width):
        order = order_of(bits)
        return pl.BlockSpec(
            (self.span, width), self.index({owner: at for at, owner in enumerate(order)})
        )

    def is_near(self, bits):
        near, _ = self.parts(bits)
        flag = jnp.bool_(False)
        for at, owner in enumerate(self.order):
            if owner in near:
                flag = jnp.logical_or(flag, pl.program_id(0) == at)
        return flag

    def load(self, bits, near_ref, far_ref):
        return jnp.where(self.is_near(bits), near_ref[...], far_ref[...])

    def store(self, bits, near_ref, far_ref, value):
        near = self.is_near(bits)

        @pl.when(near)
        def _():
            near_ref[...] = value

        @pl.when(jnp.logical_not(near))
        def _():
            far_ref[...] = value

    def store_halves(self, ways, refs, value):
        columns = value.shape[1] // len(ways)
        for at, bits in enumerate(ways):
            part = value[:, at * columns : (at + 1) * columns]
            self.store(bits, refs[2 * at], refs[2 * at + 1], part)


def in_kernel(walk, unit, me_ref, w_ref, cos_ref, sin_ref, near_ref, far_ref, out_ref):
    rows = dot(walk.load(near_ref, far_ref), w_ref[...], 1, 0)
    cosine, sine = cos_ref[...], sin_ref[...]
    for part in range(rows.shape[1] // LANES):
        lanes = slice(part * LANES, (part + 1) * LANES)
        piece = rows[:, lanes]
        if part % unit != unit - 1:
            piece = piece * cosine + pltpu.roll(piece, 64, 1) * sine
        out_ref[:, lanes] = piece.astype(BF16)


def project_in(me, rows, bits, w_wide, cosine, sine, unit, waits=()):
    width, wide = w_wide.shape
    order = order_of(bits)
    spans = len(order)
    full = cosine.shape[0]
    span = full // spans
    walk = Walk(spans, span, True)

    def ordered(step, me_ref):
        return (jnp.bitwise_xor(me_ref[0], owner_at(order, step)), 0)

    return call(
        functools.partial(in_kernel, walk, unit),
        out_shape=shape(full, wide),
        prefetch=1,
        grid=(spans,),
        in_specs=[
            whole(w_wide, pipeline_mode=pl.Buffered(1)),
            pl.BlockSpec((span, LANES), ordered),
            pl.BlockSpec((span, LANES), ordered),
            *walk.specs(width),
        ],
        out_specs=pl.BlockSpec((span, wide), ordered),
        cost_estimate=cost(2 * full * width * wide, 2 * full * (width + wide) + 2 * width * wide),
        name="project_in",
        waits=waits,
    )(me, w_wide, cosine, sine, *rows)


def mask_of(scores, first_key, first_row, starts, repeat, diagonal):
    keys = lax.broadcasted_iota(jnp.int32, scores.shape, 0) + first_key
    allowed = keys >= starts
    if diagonal:
        step = scores.shape[1] // repeat
        rows = lax.broadcasted_iota(jnp.int32, scores.shape, 1) % step + first_row
        allowed = allowed & (keys <= rows)
    return jnp.where(allowed, scores, -1e30)


def query_of(proj_ref, rows, repeat):
    return jnp.concatenate(
        [proj_ref[rows, r * LANES : (r + 1) * LANES] for r in range(repeat)], axis=0
    )


def forward_kernel(spans, step, repeat, me_ref, proj_ref, start_ref, place_ref, *rest):
    outs, lse_ref, held = rest[:spans], rest[spans], rest[spans + 1]
    full = proj_ref.shape[0]
    span = full // spans
    pair = pl.program_id(0)
    me = me_ref[0]
    value_t = proj_ref[:, (repeat + 1) * LANES :].T
    starts = start_ref[...]

    @pl.when(pair == 0)
    def _():
        held[...] = jnp.zeros_like(held)

    for block in range(full // step):
        begin, end = block * step, (block + 1) * step
        rows = slice(begin, end)
        query = query_of(proj_ref, rows, repeat)
        starts_now = jnp.concatenate([starts[:, rows]] * repeat, axis=1)
        pieces = []
        for key_block in range(block + 1):
            first = key_block * step
            key = proj_ref[first : first + step, repeat * LANES : (repeat + 1) * LANES]
            scores = dot(key, query, 1, 1) * (SCALING * LOG2E)
            pieces.append(mask_of(scores, first, begin, starts_now, repeat, key_block == block))
        top = functools.reduce(jnp.maximum, [jnp.max(p, axis=0, keepdims=True) for p in pieces])
        total = None
        summed = None
        for key_block in range(block + 1):
            first = key_block * step
            raised = jnp.exp2(pieces[key_block] - top)
            part = jnp.sum(raised, axis=0, keepdims=True)
            mixed = dot(value_t[:, first : first + step], raised.astype(BF16), 1, 0)
            total = part if total is None else total + part
            summed = mixed if summed is None else summed + mixed
        mixed_t = (summed * (1.0 / total)).astype(BF16)
        lse_ref[block : block + 1, :] = top + jnp.log2(total)
        wide = None
        for r in range(repeat):
            term = dot(
                mixed_t[:, r * step : (r + 1) * step],
                place_ref[r * LANES : (r + 1) * LANES, :],
                0,
                0,
            )
            wide = term if wide is None else wide + term
        wide = wide.astype(BF16)
        for piece in range(step // span):
            at = jnp.bitwise_xor(me, block * (step // span) + piece)
            held[at] = held[at] + wide[piece * span : (piece + 1) * span]

    @pl.when(pair == pl.num_programs(0) - 1)
    def _():
        for at in range(spans):
            outs[at][...] = held[at]


def attention_forward(me, proj, starts, place, spans, repeat, step, waits=()):
    full, wide = proj.shape
    pairs, _, narrow = place.shape
    group = wide // pairs
    span = full // spans
    work = pairs * repeat * full * full
    out_shape = [jax.ShapeDtypeStruct((span, narrow), BF16)] * spans
    out_shape.append(jax.ShapeDtypeStruct((pairs, full // step, repeat * step), F32))
    *mixed, lse = call(
        functools.partial(forward_kernel, spans, step, repeat),
        out_shape=out_shape,
        prefetch=1,
        grid=(pairs,),
        in_specs=[
            pl.BlockSpec((full, group), lambda j, _: (0, j)),
            pl.BlockSpec((1, full), lambda j, _: (0, 0)),
            pl.BlockSpec((None, repeat * LANES, narrow), lambda j, _: (j, 0, 0)),
        ],
        out_specs=[whole(x) for x in out_shape[:-1]]
        + [pl.BlockSpec((None, full // step, repeat * step), lambda j, _: (j, 0, 0))],
        scratch=[pltpu.VMEM((spans, span, narrow), BF16)],
        cost_estimate=cost(2 * work * 256, 2 * proj.size * 2, work),
        name="attention_forward",
        waits=waits,
    )(me, proj, starts, place)
    return mixed, lse


def backward_kernel(
    order, step, repeat, me_ref, proj_ref, start_ref, place_ref, lse_ref, cos_ref, sin_ref, pad_ref, *rest
):
    spans = len(order)
    grads, (out_ref, key_acc, value_acc, held) = rest[:spans], rest[spans:]
    full = proj_ref.shape[0]
    span = full // spans
    pair = pl.program_id(0)
    me = me_ref[0]
    key_t = proj_ref[:, repeat * LANES : (repeat + 1) * LANES].T
    starts = start_ref[...]
    key_acc[...] = jnp.zeros_like(key_acc)
    value_acc[...] = jnp.zeros_like(value_acc)

    @pl.when(pair == 0)
    def _():
        for at in range(spans):
            held[jnp.bitwise_xor(me, at)] = grads[at][...]
        out_ref[...] = jnp.zeros_like(out_ref)

    def turn_back(grad, rows):
        grad = grad.astype(BF16).astype(F32)
        return (grad * cos_ref[rows, :] - pltpu.roll(grad, 64, 1) * sin_ref[rows, :]).astype(BF16)

    def put(begin, wide):
        for at in range(0, wide.shape[0], span):
            owner = jnp.bitwise_xor(me, (begin + at) // span)
            where = 0
            for index, value in enumerate(order):
                where = jnp.where(owner == value, index, where)
            here = pl.ds(pl.multiple_of(where * span, span), span)
            out_ref[here, :] = out_ref[here, :] + wide[at : at + span]

    for block in range(full // step):
        begin, end = block * step, (block + 1) * step
        rows = slice(begin, end)
        query = query_of(proj_ref, rows, repeat)
        grad_rows = jnp.concatenate(
            [held[at] for at in range(begin // span, end // span)], axis=0
        )
        grad = jnp.concatenate(
            [
                dot(grad_rows, place_ref[r * LANES : (r + 1) * LANES, :], 1, 1).astype(BF16)
                for r in range(repeat)
            ],
            axis=0,
        )
        starts_now = jnp.concatenate([starts[:, rows]] * repeat, axis=1)
        lse = lse_ref[block : block + 1, :]
        kept = []
        mean_dot = None
        for key_block in range(block + 1):
            first = key_block * step
            keys = slice(first, first + step)
            key = proj_ref[keys, repeat * LANES : (repeat + 1) * LANES]
            value = proj_ref[keys, (repeat + 1) * LANES :]
            scores = dot(key, query, 1, 1) * (SCALING * LOG2E)
            scores = mask_of(scores, first, begin, starts_now, repeat, key_block == block)
            shares = jnp.exp2(scores - lse)
            value_acc[keys, :] += dot(shares.astype(BF16), grad, 1, 0)
            product = shares * dot(value, grad, 1, 1)
            part = jnp.sum(product, axis=0, keepdims=True)
            mean_dot = part if mean_dot is None else mean_dot + part
            kept.append((shares, product))
        query_grad_t = None
        for key_block in range(block + 1):
            first = key_block * step
            keys = slice(first, first + step)
            shares, product = kept[key_block]
            score_grad = (SCALING * (product - shares * mean_dot)).astype(BF16)
            key_acc[keys, :] += dot(score_grad, query, 1, 0)
            term = dot(key_t[:, keys], score_grad, 1, 0)
            query_grad_t = term if query_grad_t is None else query_grad_t + term
        query_grad = query_grad_t.T
        wide = None
        for r in range(repeat):
            turned = turn_back(query_grad[r * step : (r + 1) * step], rows)
            term = dot(turned, pad_ref[:, r * LANES : (r + 1) * LANES], 1, 1)
            wide = term if wide is None else wide + term
        put(begin, wide.astype(BF16))
    for block in range(full // step):
        rows = slice(block * step, (block + 1) * step)
        turned = turn_back(key_acc[rows, :], rows)
        wide = dot(turned, pad_ref[:, repeat * LANES : (repeat + 1) * LANES], 1, 1)
        wide += dot(value_acc[rows, :].astype(BF16), pad_ref[:, (repeat + 1) * LANES :], 1, 1)
        put(block * step, wide.astype(BF16))


def attention_backward(
    me, proj, starts, place, grads, bits, lse, cosine, sine, pad, repeat, step, waits=()):
    full, wide = proj.shape
    pairs, _, narrow = place.shape
    group = wide // pairs
    work = pairs * repeat * full * full
    out_shape = shape(full, pad.shape[0])
    return call(
        functools.partial(backward_kernel, order_of(bits), step, repeat),
        out_shape=out_shape,
        prefetch=1,
        grid=(pairs,),
        in_specs=[
            pl.BlockSpec((full, group), lambda j, _: (0, j)),
            pl.BlockSpec((1, full), lambda j, _: (0, 0)),
            pl.BlockSpec((None, repeat * LANES, narrow), lambda j, _: (j, 0, 0)),
            pl.BlockSpec((None, full // step, repeat * step), lambda j, _: (j, 0, 0)),
            whole(cosine),
            whole(sine),
            pl.BlockSpec((pad.shape[0], group), lambda j, _: (0, j)),
            *[whole(x) for x in grads],
        ],
        out_specs=whole(out_shape),
        scratch=[
            pltpu.VMEM((full, LANES), F32),
            pltpu.VMEM((full, LANES), F32),
            pltpu.VMEM((len(grads), full // len(grads), narrow), BF16),
        ],
        cost_estimate=cost(2 * work * 640, 2 * proj.size * 4, work),
        name="attention_backward",
        waits=waits,
    )(me, proj, starts, place, lse, cosine, sine, pad, *grads)


def out_kernel(spans, me_ref, w_ref, tokens_ref, gain_ref, *rest):
    mixed, (resid_ref, *parts) = rest[:spans], rest[spans:]
    summed = tokens_ref[...].astype(F32)
    for at in range(spans):
        summed += dot(mixed[at][...], w_ref[jnp.bitwise_xor(me_ref[0], at)], 1, 0)
    resid_ref[...] = summed
    factor = lax.rsqrt(jnp.mean(summed * summed, axis=-1, keepdims=True) + epsilon)
    normed = (summed * factor * gain_ref[...]).astype(BF16)
    columns = parts[0].shape[1]
    for at, part in enumerate(parts):
        part[...] = normed[:, at * columns : (at + 1) * columns]


def project_out(seq, me, mixed, w_out, tokens, gain, ways, waits=()):
    _, span, width = tokens.shape
    out_shape = [shape(span, width, dtype=F32)] + [shape(span, width // len(ways))] * len(ways)
    return call(
        functools.partial(out_kernel, len(mixed)),
        out_shape=out_shape,
        prefetch=1,
        in_specs=[
            whole(w_out),
            pl.BlockSpec((None, span, width), lambda *_: (seq, 0, 0)),
            whole(gain),
            *[whole(x) for x in mixed],
        ],
        out_specs=[whole(x) for x in out_shape],
        cost_estimate=cost(2 * span * width * width, span * width * 10 + width * width * 2),
        name="project_out",
        waits=waits,
    )(me, w_out, tokens, gain, *mixed)


def assemble(held, core, near_ref, far_ref):
    for chip in range(near_ref.shape[0]):
        held[2 * chip + core] = near_ref[chip]
        held[2 * chip + 1 - core] = far_ref[chip]


def feed_kernel(
    visits, bits, ways, shard_ref, both_ref, near_ref, far_ref, cn_ref, cf_ref, *rest
):
    count = 2 * len(ways)
    rows, (hid_ref, dboth_ref, x_ref, *outs), held = rest[:count], rest[count:-1], rest[-1]
    inner = both_ref.shape[1] // 2

    @pl.when(pl.program_id(0) == 0)
    def _():
        assemble(held, shard_ref[0] % 2, near_ref, far_ref)

    down = held[...].reshape(inner, held.shape[2])
    columns = rows[0].shape[1]
    for at, way in enumerate(ways):
        x_ref[:, at * columns : (at + 1) * columns] = visits.load(way, rows[2 * at], rows[2 * at + 1])
    x = x_ref[...]
    gate = dot(x, both_ref[:, :inner], 1, 0)
    up = dot(x, both_ref[:, inner:], 1, 0)
    sig = jax.nn.sigmoid(gate)
    act = gate * sig
    hid_ref[...] = (act * up).astype(BF16)
    grad_hidden = dot(visits.load(bits, cn_ref, cf_ref), down, 1, 1)
    dboth_ref[:, :inner] = (grad_hidden * up * (sig * (1.0 + gate * (1.0 - sig)))).astype(BF16)
    dboth_ref[:, inner:] = (grad_hidden * act).astype(BF16)
    visits.store_halves(ways, outs, dot(dboth_ref[...], both_ref[...], 1, 1).astype(BF16))


def pairs_of(values):
    return list(zip(values[::2], values[1::2]))


def feed_forward(spans, me_shard, rows, cots, bits, ways, both_w, near, far, waits=()):
    width, inner = both_w.shape[0], both_w.shape[1] // 2
    half = cots[0].shape[0]
    span = 2 * half // spans
    visits = Visits(spans, span)
    one = pl.Buffered(1)
    total = 2 * half
    part = width // len(ways)
    flat = [x for pair in rows for x in pair]
    hidden, grads, x_all, *parts = call(
        functools.partial(feed_kernel, visits, bits, ways),
        out_shape=[shape(total, inner), shape(total, 2 * inner), shape(total, width)]
        + [shape(half, part)] * 2 * len(ways),
        prefetch=1,
        grid=(spans,),
        in_specs=[
            whole(both_w, pipeline_mode=one),
            whole(near, pipeline_mode=one),
            whole(far, pipeline_mode=one),
            *visits.specs(bits, width),
            *[spec for way in ways for spec in visits.specs(way, part)],
        ],
        out_specs=[
            visits.rows(bits, inner),
            visits.rows(bits, 2 * inner),
            visits.rows(bits, width),
            *[spec for way in ways for spec in visits.specs(way, part)],
        ],
        scratch=[pltpu.VMEM((2 * near.shape[0], *near.shape[1:]), BF16)],
        cost_estimate=cost(
            10 * total * width * inner, total * (6 * width + 6 * inner) + 6 * width * inner
        ),
        name="feed_forward",
        waits=waits,
    )(me_shard, both_w, near, far, *cots, *flat)
    return pairs_of(parts), hidden, grads, x_all


def feed_out_kernel(count, walk, shard_ref, near_ref, far_ref, *rest):
    hidden, outs, held = rest[:count], rest[count:-1], rest[-1]

    @pl.when(pl.program_id(0) == 0)
    def _():
        assemble(held, shard_ref[0] % 2, near_ref, far_ref)

    down = held[...].reshape(-1, held.shape[2])
    for at in range(count):
        walk.store(outs[2 * at], outs[2 * at + 1], dot(hidden[at][...], down, 1, 0).astype(BF16))


def feed_out(spans, me_shard, hidden, near, far, waits=()):
    total, inner = hidden[0].shape
    width = near.shape[2]
    walk = Walk(spans, total // spans, False)
    count = len(hidden)
    return pairs_of(
        call(
            functools.partial(feed_out_kernel, count, walk),
            out_shape=[shape(total // 2, width)] * 2 * count,
            prefetch=1,
            grid=(spans,),
            in_specs=[
                whole(near, pipeline_mode=pl.Buffered(1)),
                whole(far, pipeline_mode=pl.Buffered(1)),
                *[pl.BlockSpec((total // spans, inner), walk.both)] * count,
            ],
            out_specs=walk.specs(width) * count,
            scratch=[pltpu.VMEM((2 * near.shape[0], *near.shape[1:]), BF16)],
            cost_estimate=cost(
                2 * count * total * inner * width,
                2 * count * total * (inner + width) + 2 * inner * width,
            ),
            name="feed_out",
            waits=waits,
        )(me_shard, near, far, *hidden)
    )


def terms_of(*refs):
    sums = [a[...].astype(F32) + b[...].astype(F32) for a, b in zip(refs[::2], refs[1::2])]
    return sums[0] if len(sums) == 1 else jnp.concatenate(sums, axis=1)


def back_kernel(count, me_ref, resid_ref, cot_ref, gain_ref, w_ref, *rest):
    terms, (resid_grad_ref, branch_ref, *mixed) = rest[:count], rest[count:]
    rows = resid_ref[...]
    factor = lax.rsqrt(jnp.mean(rows * rows, axis=-1, keepdims=True) + epsilon)
    unit_rows = rows * factor
    scaled = terms_of(*terms) * gain_ref[...]
    mean_dot = jnp.mean(scaled * unit_rows, axis=-1, keepdims=True)
    grad = cot_ref[...].astype(F32) + factor * (scaled - unit_rows * mean_dot)
    resid_grad_ref[...] = grad
    branch = grad.astype(BF16)
    branch_ref[...] = branch
    for at, out in enumerate(mixed):
        out[...] = dot(branch, w_ref[jnp.bitwise_xor(me_ref[0], at)], 1, 1).astype(BF16)


def norm_out_back(seq, me, spans, parts, resid, cot, gain, w_out, waits=()):
    rows, width = resid.shape
    terms = [x for pair in parts for x in pair]
    out_shape = [shape(rows, width, dtype=F32), shape(rows, width)]
    out_shape += [shape(rows, w_out.shape[1])] * spans
    out = call(
        functools.partial(back_kernel, len(terms)),
        out_shape=out_shape,
        prefetch=1,
        in_specs=[whole(resid), pl.BlockSpec((None, rows, width), lambda *_: (seq, 0, 0))]
        + [whole(x) for x in (gain, w_out, *terms)],
        out_specs=[whole(x) for x in out_shape],
        cost_estimate=cost(2 * rows * width * width, rows * width * 16 + width * width * 2),
        name="norm_out_back",
        waits=waits,
    )(me, resid, cot, gain, w_out, *terms)
    return out[0], out[1], out[2:]


def grad_in_kernel(visits, ways, proj_ref, w_ref, *outs):
    visits.store_halves(ways, outs, dot(proj_ref[...], w_ref[...], 1, 1).astype(BF16))


def grad_into_rows(spans, proj_grad, bits, ways, w_in, waits=()):
    full, narrow = proj_grad.shape
    width = w_in.shape[0]
    visits = Visits(spans, full // spans)
    part = width // len(ways)
    parts = call(
        functools.partial(grad_in_kernel, visits, ways),
        out_shape=[shape(full // 2, part)] * 2 * len(ways),
        grid=(spans,),
        in_specs=[visits.rows(bits, narrow), whole(w_in, pipeline_mode=pl.Buffered(1))],
        out_specs=[spec for way in ways for spec in visits.specs(way, part)],
        cost_estimate=cost(2 * full * narrow * width, 2 * full * (narrow + width) + 2 * narrow * width),
        name="grad_into_rows",
        waits=waits,
    )(proj_grad, w_in)
    return pairs_of(parts)


def product_of(lefts, rights):
    total = None
    i = j = a = b = 0
    while i < len(lefts):
        size = min(lefts[i].shape[0] - a, rights[j].shape[0] - b)
        term = dot(lefts[i][a : a + size, :], rights[j][b : b + size, :], 0, 0)
        total = term if total is None else total + term
        a, b = a + size, b + size
        if a == lefts[i].shape[0]:
            i, a = i + 1, 0
        if b == rights[j].shape[0]:
            j, b = j + 1, 0
    return total


def weight_kernel(left_count, right_count, gain, *refs):
    lefts, rights = refs[:left_count], refs[left_count : left_count + right_count]
    rest = refs[left_count + right_count :]
    total = product_of(lefts, rights)
    if gain:
        w_ref, out_ref, gain_ref = rest
        gain_ref[...] = jnp.sum(total * w_ref[...].astype(F32), axis=1, keepdims=True)
    else:
        (out_ref,) = rest
    out_ref[...] = total.astype(BF16)


def weight_grad(lefts, rights, weight, name, waits=()):
    rows = lefts[0].shape[1]
    tile = 256
    columns = rights[0].shape[1]
    depth = sum(x.shape[0] for x in lefts)
    out_shape = [shape(rows, columns)]
    out_specs = [pl.BlockSpec((tile, columns), lambda i: (i, 0))]
    weights = () if weight is None else (weight,)
    if weights:
        out_shape.append(shape(rows, 1, dtype=F32))
        out_specs.append(pl.BlockSpec((tile, 1), lambda i: (i, 0)))
    return call(
        functools.partial(weight_kernel, len(lefts), len(rights), bool(weights)),
        out_shape=out_shape,
        grid=(rows // tile,),
        in_specs=[pl.BlockSpec((x.shape[0], tile), lambda i: (0, i)) for x in lefts]
        + [whole(x, pipeline_mode=pl.Buffered(1)) for x in rights]
        + [pl.BlockSpec((tile, x.shape[1]), lambda i: (i, 0)) for x in weights],
        out_specs=out_specs,
        cost_estimate=cost(
            2 * depth * rows * columns, 2 * depth * (rows + columns) + 2 * rows * columns
        ),
        name=name,
        waits=waits,
    )(*lefts, *rights, *weights)


def in_weight_kernel(own, shards, left_count, me_ref, *refs):
    lefts, (*rights, w_ref, near_ref, far_ref, gain_ref) = refs[:left_count], refs[left_count:]
    total = product_of(lefts, rights)
    gain_ref[...] = jnp.sum(total * w_ref[...].astype(F32), axis=1, keepdims=True)
    total = total.astype(BF16)
    steps = shards.bit_length() - 1
    count = total.shape[0] // own
    for at in range(count):
        apart = jnp.bitwise_xor(me_ref[0], pl.program_id(0) * count + at)
        where = 0
        for bit in range(steps):
            where = where * 2 + (apart >> bit) % 2
        piece = total[at * own : (at + 1) * own]

        @pl.when(where < shards // 2)
        def _():
            near_ref[where] = piece

        @pl.when(where >= shards // 2)
        def _():
            far_ref[where - shards // 2] = piece


def in_weight_grad(me, lefts, rights, weight, own, shards, waits=()):
    rows, columns = weight.shape
    tile = math.lcm(own, LANES)
    depth = sum(x.shape[0] for x in lefts)
    half = shape(shards // 2, own, columns)
    out_shape = (half, half, shape(rows, 1, dtype=F32))
    return call(
        functools.partial(in_weight_kernel, own, shards, len(lefts)),
        out_shape=out_shape,
        prefetch=1,
        grid=(rows // tile,),
        in_specs=[pl.BlockSpec((x.shape[0], tile), lambda i, _: (0, i)) for x in lefts]
        + [whole(x) for x in rights]
        + [pl.BlockSpec((tile, columns), lambda i, _: (i, 0))],
        out_specs=[whole(half), whole(half), pl.BlockSpec((tile, 1), lambda i, _: (i, 0))],
        cost_estimate=cost(
            2 * depth * rows * columns, 2 * depth * (rows + columns) + 2 * rows * columns
        ),
        name="in_weight_grad",
        waits=waits,
    )(me, *lefts, *rights, weight)


def add_pairs(left, right):
    return (left.astype(F32) + right.astype(F32)).astype(BF16)


def halve_kernel(near_ref, got_ref, *outs):
    total = (near_ref[...].astype(F32) + got_ref[...].astype(F32)).astype(BF16)
    cut = total.shape[0] // len(outs)
    for at, out in enumerate(outs):
        out[...] = total[at * cut : (at + 1) * cut]


def halve(near, got):
    parts = 2 if near.shape[0] > 1 else 1
    out_shape = [shape(near.shape[0] // parts, *near.shape[1:])] * parts
    return call(
        halve_kernel,
        out_shape=out_shape,
        in_specs=[whole(near), whole(got)],
        out_specs=[whole(x) for x in out_shape],
        cost_estimate=cost(0, 6 * near.size),
        name="halve",
    )(near, got)


def across(value, bit):
    size = lax.axis_size("fsdp")
    return lax.ppermute(value, "fsdp", [(i, i ^ bit) for i in range(size)])


def arrange_kernel(order, copies, outs_count, me_ref, *rest):
    blocks, outs, held = rest[: len(order)], rest[len(order) : -1], rest[-1]
    for at, owner in enumerate(order):
        held[jnp.bitwise_xor(me_ref[0], owner)] = blocks[at][...]
    for own in range(len(order)):
        for source, out, target, size in copies:
            begin = target(own)
            outs[out][:, begin : begin + size] = held[own, :, source : source + size].astype(F32)


def arrange(me, blocks, bits, copies, widths, name):
    rows, columns = blocks[0].shape
    tile = rows // 2
    order = order_of(bits)
    out_shape = [shape(rows, width, dtype=F32) for width in widths]
    return call(
        functools.partial(arrange_kernel, order, copies, len(widths)),
        out_shape=out_shape,
        prefetch=1,
        grid=(2,),
        in_specs=[pl.BlockSpec((tile, columns), lambda i, _: (i, 0))] * len(blocks),
        out_specs=[pl.BlockSpec((tile, width), lambda i, _: (i, 0)) for width in widths],
        scratch=[pltpu.VMEM((len(blocks), tile, columns), BF16)],
        cost_estimate=cost(0, 6 * rows * sum(widths)),
        name=name,
    )(me, *blocks)


def arrange_rows_kernel(order, me_ref, *rest):
    blocks, out_ref = rest[:-1], rest[-1]
    rows = blocks[0].shape[0]
    for at, owner in enumerate(order):
        begin = pl.multiple_of(jnp.bitwise_xor(me_ref[0], owner) * rows, rows)
        out_ref[pl.ds(begin, rows), :] = blocks[at][...].astype(F32)


def arrange_rows(me, blocks, bits):
    rows, width = blocks[0].shape
    out_shape = shape(len(blocks) * rows, width, dtype=F32)
    return call(
        functools.partial(arrange_rows_kernel, order_of(bits)),
        out_shape=out_shape,
        prefetch=1,
        in_specs=[whole(x) for x in blocks],
        out_specs=whole(out_shape),
        cost_estimate=cost(0, 6 * len(blocks) * rows * width),
        name="arrange_rows",
    )(me, *blocks)


def block_out_kernel(count, seqs, *refs):
    out_ref = refs[-1]
    for seq in range(seqs):
        resid_ref, *terms = refs[count * seq : count * (seq + 1)]
        out_ref[seq] = (resid_ref[...] + terms_of(*terms)).astype(BF16)


def finish_block_out(resid, terms, waits=()):
    rows, width = resid[0].shape
    out_shape = shape(len(resid), rows, width)
    flat = [y for q in range(len(resid)) for y in (resid[q], *[x for pair in terms[q] for x in pair])]
    count = len(flat) // len(resid)
    return call(
        functools.partial(block_out_kernel, count, len(resid)),
        out_shape=out_shape,
        in_specs=[whole(x) for x in flat],
        out_specs=whole(out_shape),
        cost_estimate=cost(0, 12 * out_shape.size),
        name="finish_block_out",
        waits=waits,
    )(*flat)


def tokens_grad_kernel(count, seqs, tokens_ref, gain_ref, *refs):
    out_ref = refs[-1]
    for seq in range(seqs):
        resid_ref, *terms = refs[count * seq : count * (seq + 1)]
        rows = tokens_ref[seq].astype(F32)
        factor = lax.rsqrt(jnp.mean(rows * rows, axis=-1, keepdims=True) + epsilon)
        unit_rows = rows * factor
        scaled = terms_of(*terms) * gain_ref[...]
        mean_dot = jnp.mean(scaled * unit_rows, axis=-1, keepdims=True)
        out_ref[seq] = (resid_ref[...] + factor * (scaled - unit_rows * mean_dot)).astype(BF16)


def finish_tokens_grad(tokens, gain, grad_resid, terms, waits=()):
    out_shape = shape(*tokens.shape)
    flat = [
        y for q in range(len(grad_resid)) for y in (grad_resid[q], *[x for pair in terms[q] for x in pair])
    ]
    count = len(flat) // len(grad_resid)
    return call(
        functools.partial(tokens_grad_kernel, count, len(grad_resid)),
        out_shape=out_shape,
        in_specs=[whole(x) for x in (tokens, gain, *flat)],
        out_specs=whole(out_shape),
        cost_estimate=cost(0, 12 * out_shape.size),
        name="finish_tokens_grad",
        waits=waits,
    )(tokens, gain, *flat)


def join_kernel(chips, me_ref, *refs):
    blocks, out_ref = refs[:-1], refs[-1]
    chip = me_ref[0] // 2
    for back in range(chips):
        out_ref[lax.rem(chip - back + chips, chips)] = blocks[back][...]


def join(me, blocks, waits=()):
    rows, width = blocks[0].shape
    out_shape = shape(len(blocks), rows, width)
    return call(
        functools.partial(join_kernel, len(blocks)),
        out_shape=out_shape,
        prefetch=1,
        in_specs=[whole(x) for x in blocks],
        out_specs=whole(out_shape),
        cost_estimate=cost(0, 4 * out_shape.size),
        name="join",
        waits=waits,
    )(me, *blocks)


def out_weight_kernel(spans, seqs, chips, own, me_ref, shard_ref, *refs):
    mixed, (*branches, near_ref, far_ref) = refs[: spans * seqs], refs[spans * seqs :]
    chip, core = shard_ref[0] // 2, shard_ref[0] % 2
    for at in range(spans):
        total = None
        for seq in range(seqs):
            term = dot(mixed[seq * spans + at][...], branches[seq][...], 0, 0)
            total = term if total is None else total + term
        total = total.astype(BF16)
        count = total.shape[0] // own
        for part in range(count):
            owner = jnp.bitwise_xor(me_ref[0], at) * count + part
            back = lax.rem(chip - owner // 2 + chips, chips)

            @pl.when(owner % 2 == core)
            def _():
                near_ref[back] = total[part * own : (part + 1) * own]

            @pl.when(owner % 2 != core)
            def _():
                far_ref[back] = total[part * own : (part + 1) * own]


def out_weight_grad(me, me_shard, mixed, branches, own, shards, waits=()):
    flat = [x for group in mixed for x in group]
    narrow, width = flat[0].shape[1], branches[0].shape[1]
    out_shape = [shape(shards // 2, own, width)] * 2
    return call(
        functools.partial(out_weight_kernel, len(mixed[0]), len(branches), shards // 2, own),
        out_shape=out_shape,
        prefetch=2,
        in_specs=[whole(x) for x in (*flat, *branches)],
        out_specs=[whole(x) for x in out_shape],
        cost_estimate=cost(
            2 * len(flat) * flat[0].size * width,
            2 * len(mixed[0]) * narrow * width,
        ),
        name="out_weight_grad",
        waits=waits,
    )(me, me_shard, *flat, *branches)


def turning_tables(positions):
    frequency = jnp.exp(
        jnp.arange(HALF, dtype=F32) * (-2.0 * math.log(rope_base) / HEAD_DIMENSION)
    )
    angles = positions.astype(F32)[:, :, None] * frequency
    cosine, sine = jnp.cos(angles), jnp.sin(angles)
    empty = jnp.zeros((*positions.shape, 64 - HALF), F32)
    return (
        jnp.concatenate([cosine, empty, cosine, empty], axis=-1),
        jnp.concatenate([-sine, empty, sine, empty], axis=-1),
    )


def sum_all(value):
    for axis in ("seq", "fsdp"):
        size = lax.axis_size(axis)
        bit = 1
        while bit < size:
            value = value + lax.ppermute(value, axis, [(i, i ^ bit) for i in range(size)])
            bit *= 2
    return value


def body(
    tokens,
    joined_input_weight,
    out_projection,
    gate_weight,
    up_weight,
    down_weight,
    norm_first,
    norm_second,
    positions,
    cotangent,
):
    seqs, span, width = tokens.shape
    spans = lax.axis_size("seq")
    shards = lax.axis_size("fsdp")
    chips = shards // 2
    me = jnp.full((1,), lax.axis_index("seq"), jnp.int32)
    me_shard = jnp.full((1,), lax.axis_index("fsdp"), jnp.int32)
    full = positions.shape[1]
    pairs = KEY_VALUE_HEADS // spans
    repeat = QUERY_HEAD_COUNT // KEY_VALUE_HEADS
    unit = repeat + 2
    query_columns = QUERY_HEAD_COUNT * HEAD_DIMENSION
    pair_columns = KEY_VALUE_HEADS * HEAD_DIMENSION
    query_slab = query_columns // spans
    pair_slab = pair_columns // spans
    own_rows = joined_input_weight.shape[0]
    piece = FF // (shards * spans)
    inner = shards * piece
    step = min(256, full)
    pad = jnp.asarray(pad_matrix(pairs, repeat), BF16)
    place = jnp.asarray(place_matrix(pairs, repeat), BF16)
    gain_in, gain_mid = norm_first[None, :], norm_second[None, :]
    upward = tuple(range(spans.bit_length() - 1))
    orders = [(upward[::-1], upward)[q % 2] for q in range(seqs)]
    both = range(seqs)
    del CHAIN[:]

    def gather(shard):
        return lax.all_gather(shard, "fsdp", axis=0, tiled=True)

    def owned(value):
        return lax.psum_scatter(value, "fsdp", scatter_dimension=0, tiled=True)

    ways = (upward[::-1], upward)

    def flat(pairs):
        return tuple(x for pair in pairs for x in pair)

    def copied(value, bits):
        held = [value]
        for bit in bits:
            held = held + [swap(x, bit) for x in held]
        return held

    in_shard = cut_in(me, joined_input_weight, spans, (query_slab, pair_slab, pair_slab))
    w_in = gather(in_shard)
    w_out = gather(out_projection).reshape(spans, query_slab, width)
    normed = norm_rows(tokens, gain_in)
    x_got = gather_start(normed, orders)
    both_shard, down_shard = cut_feed(
        me, gate_weight, up_weight, down_weight, spans, shards, piece, ()
    )
    w_both = gather(both_shard)
    down_blocks = [down_shard, around(down_shard)]

    def arrived():
        down_blocks[-1:] = pin(down_blocks[-1])

    def pass_on():
        if len(down_blocks) < chips:
            arrived()
            down_blocks.append(around(down_blocks[-1]))

    cosine, sine = turning_tables(positions)
    starts = (jnp.arange(full, dtype=jnp.int32)[None, :] - positions)[:, None, :]
    x_in = gather_end(normed, x_got, orders, "stack_in")
    arrived()
    w_wide = widen(w_in, pad)
    cot_rows = split_rows(cotangent)
    cot_got = gather_start(cot_rows, orders)

    projected, mixed, lse, resid, x_mid = [], [], [], [], []

    def project_rows(q):
        rows, *normed_mid = project_out(q, me, mixed[q], w_out, tokens, gain_mid, ways)
        resid.append(rows)
        return normed_mid, gather_start(normed_mid, ways)

    for q in both:
        projected.append(
            project_in(
                me, x_in[q], orders[q], w_wide, cosine[q], sine[q], unit, x_in[-1] if q == 0 else ()
            )
        )
        if q == 0:
            cots = gather_end(cot_rows, cot_got, orders, "stack_cot")
        if q == 1:
            pass_on()
            started = project_rows(0)
        heads, sums = attention_forward(me, projected[q], starts[q], place, spans, repeat, step)
        lse.append(sums)
        mixed.append(shared(heads))
        if q == 1:
            x_mid.append(gather_end(*started, ways, "stack_mid", flat(cots)))
    while len(down_blocks) < chips:
        pass_on()
    down_near = join(me_shard, down_blocks)
    down_far = beside(down_near)
    for q in both[1:]:
        x_mid.append(gather_end(*project_rows(q), ways, "stack_mid"))

    hidden, grad_both, grad_mid, x_all = [], [], [], []
    for q in both:
        parts, kept, grads, rows = feed_forward(
            spans, me_shard, x_mid[q], cots[q], orders[q], ways, w_both, down_near, down_far
        )
        hidden.append(kept)
        grad_both.append(grads)
        x_all.append(rows)
        grad_mid.append(scatter_start(parts, ways))

    grad_resid, branches, head_grads = [], [], []

    def norm_back(q, waits=()):
        rows, branch, heads = norm_out_back(
            q, me, spans, grad_mid[q], resid[q], cotangent, gain_mid, w_out, waits
        )
        grad_resid.append(rows)
        branches.append(branch)
        head_grads.append(shared(heads))

    grad_mid[0] = scatter_end(*grad_mid[0], ways)
    both_part, gain_second = weight_grad(x_all, grad_both, w_both, "gate_up_grad")
    both_own = owned(both_part)
    norm_back(0)
    for q in both[1:]:
        grad_mid[q] = scatter_end(*grad_mid[q], ways)
    outs = scatter_start(
        feed_out(spans, me_shard, hidden, down_near, down_far, tuple(head_grads[0][1:])), orders
    )
    for q in both[1:]:
        norm_back(q)
    (down_part,) = weight_grad(hidden, flat(cots), None, "down_grad")
    down_own = owned(down_part)
    out_near, out_far = out_weight_grad(me, me_shard, mixed, branches, own_rows, shards)
    out_got = beside(out_far)

    both_every = copied(both_own, ways[0])
    down_every = copied(down_own, ways[1])
    proj_grads, grad_in = [], []
    for q in both:
        proj_grads.append(
            attention_backward(
                me,
                projected[q],
                starts[q],
                place,
                head_grads[q],
                orders[q],
                lse[q],
                cosine[q],
                sine[q],
                pad,
                repeat,
                step,
                () if q == 0 else (both_own,),
            )
        )
        if q == 0:
            (out_got,) = pin(out_got)
            out_near = add_pairs(out_near, out_got)
            out_passing = around(out_near[1])
        if q == seqs - 1:
            for p in both[:-1]:
                grad_in[p] = scatter_end(*grad_in[p], ways)
            (out_passing,) = pin(out_passing)
            out_passing = around(add_pairs(out_near[2], out_passing))
            in_near, in_far, gain_first = in_weight_grad(
                me_shard,
                flat(x_in),
                proj_grads,
                w_in,
                own_rows,
                shards,
                both_every[1:2],
            )
            in_got = across(in_far, 1)
        waits = tuple(x for group in head_grads[1:] for x in group[1:]) if q == 0 else ()
        parts = grad_into_rows(spans, proj_grads[q], orders[q], ways, w_in, tuple(waits))
        grad_in.append(scatter_start(parts, ways))
        if q == 0:
            outs = scatter_end(*outs, orders)
    in_near, in_sent = halve(in_near, in_got)
    in_got = across(in_sent, 2)
    for back in range(3, chips):
        (out_passing,) = pin(out_passing)
        out_passing = around(add_pairs(out_near[back], out_passing))
    gains = sum_all(
        jnp.stack([gain_first.reshape(width) / norm_first, gain_second.reshape(width) / norm_second])
    )
    block_out = finish_block_out(resid, [[pair] for pair in outs])
    bit = 4
    while in_near.shape[0] > 1:
        in_near, in_sent = halve(in_near, in_got)
        in_got = across(in_sent, bit)
        bit *= 2
    out_total = add_pairs(out_near[0], out_passing)
    grad_in[-1] = scatter_end(*grad_in[-1], ways)
    copies = [
        (part * inner + shard * piece, part, lambda own, shard=shard: (shard * spans + own) * piece, piece)
        for part in range(2)
        for shard in range(shards)
    ]
    gate_grad, up_grad = arrange(me, both_every, ways[0], copies, (FF, FF), "arrange_gate_up")
    (in_own,) = halve(in_near, in_got)
    in_own = in_own[0]
    down_grad = arrange_rows(me, down_every, ways[1])
    tokens_grad = finish_tokens_grad(tokens, gain_in, grad_resid, grad_in)
    copies = [
        (0, 0, lambda own: own * query_slab, query_slab),
        (query_slab, 0, lambda own: query_columns + own * pair_slab, pair_slab),
        (
            query_slab + pair_slab,
            0,
            lambda own: query_columns + pair_columns + own * pair_slab,
            pair_slab,
        ),
    ]
    (in_grad,) = arrange(
        me,
        copied(in_own, upward),
        upward,
        copies,
        (query_columns + 2 * pair_columns,),
        "arrange_in",
    )
    for bit in upward:
        out_total = add_pairs(out_total, swap(out_total, bit))
    out_grad = out_total.astype(F32)
    return (
        block_out,
        tokens_grad,
        in_grad,
        out_grad,
        gate_grad,
        up_grad,
        down_grad,
        gains[0],
        gains[1],
    )


def solution(mesh):
    return jax.shard_map(
        body,
        mesh=mesh,
        in_specs=(
            P("fsdp", "seq", None),
            P("fsdp", None),
            P("fsdp", None),
            P("fsdp", None),
            P("fsdp", None),
            P("fsdp", None),
            P(),
            P(),
            P("fsdp", None),
            P("fsdp", "seq", None),
        ),
        out_specs=(
            P("fsdp", "seq", None),
            P("fsdp", "seq", None),
            P("fsdp", None),
            P("fsdp", None),
            P("fsdp", None),
            P("fsdp", None),
            P("fsdp", None),
            P(),
            P(),
        ),
        check_vma=False,
    )
```

time: 1120 us -> 594 us (0.53)
  waiting for transfers between devices: 673 us -> 135 us
  Pallas kernels: 132 us -> 312 us
  local copies, waits for them, and re-layouts: 108 us -> 21.5 us
  starting transfers between devices: 5.51 us -> 86.2 us
  blocking collectives: 74.7 us -> 0 us
  matrix products: 62.9 us -> 0 us
  other arithmetic: 42.4 us -> 16.8 us
    all_gather x7 -> x0, waiting for transfers between devices: 274 us -> none  [the longest x1 72.6 us: body(): lax.all_gather(normed_mid, 'seq', axis=0).reshape(spans * rows, width)]
    pallas_call x6 -> x48, Pallas kernels: 132 us -> 312 us  [the longest x42 312 us: made(): out = inner(*args, *waits)]
    unnamed x23 -> x5, waiting for transfers between devices: 154 us -> 0.76 us
    ppermute x0 -> x75, waiting for transfers between devices: none -> 126 us  [the longest x47 85.7 us: swap(): return lax.ppermute(value, 'seq', [(i, i ^ 1 << bit) for i in range(size)])]
    reduce_scatter x5 -> x2, waiting for transfers between devices: 122 us -> 0.01 us  [owned(): return lax.psum_scatter(value, 'fsdp', scatter_dimension=0, tiled=True)]
    all_gather x5 -> x3, waiting for transfers between devices: 111 us -> 7.84 us  [gather(): return lax.all_gather(shard, 'fsdp', axis=0, tiled=True)]
    ppermute x0 -> x75, starting transfers between devices: none -> 86 us  [the longest x47 54.9 us: swap(): return lax.ppermute(value, 'seq', [(i, i ^ 1 << bit) for i in range(size)])]
    dot_general x6 -> x0, matrix products: 62.9 us -> none  [the longest x4 47.1 us: product_of(): return jnp.einsum('rd,re->de', left, right, preferred_element_type=F32)]
  transfers between devices with their start and end apart: 21 -> 80, of which waited for: 19 -> 27; matrix products, arithmetic and copies ran while one was open for 16% -> 4% of each run, Pallas kernels for 7% -> 53%
where the time goes in v2:
time: 594 us; the launch traced here: 586 us
  Pallas kernels  312 us (53%)
  waiting for transfers between devices  135 us (23%)
  starting transfers between devices  86.2 us (15%)
  local copies, waits for them, and re-layouts  21.5 us (4%)
  other arithmetic  16.8 us (3%)
  between operations  14.8 us (2%)
    pallas_call x42, Pallas kernels, made(): out = inner(*args, *waits)  312 us
    ppermute x47, waiting for transfers between devices, swap(): return lax.ppermute(value, 'seq', [(i, i ^ 1 << bit) for i in range(size)])  85.7 us
    ppermute x47, starting transfers between devices, swap(): return lax.ppermute(value, 'seq', [(i, i ^ 1 << bit) for i in range(size)])  54.9 us
    ppermute x12, waiting for transfers between devices, exchange(): return lax.ppermute(value, 'seq', [(i, i ^ other) for i in range(size)])  16.6 us
    unnamed x110, local copies, waits for them, and re-layouts  16.1 us
    ppermute x12, starting transfers between devices, exchange(): return lax.ppermute(value, 'seq', [(i, i ^ other) for i in range(size)])  14 us
    ppermute x6, waiting for transfers between devices, around(): lax.ppermute(value, 'fsdp', [(i, (i + 2) % size) for i in range(size)])  11.9 us
  transfers between devices with their start and end apart: 80, of which 27 were waited for; matrix products, arithmetic and copies ran while one was open for 4% of the time, Pallas kernels for 53%

profile of v2, /device:TPU:0, one launch (start us, length us, event | category | flops | bytes accessed | tf_op | source)
XLA Modules:
  0.0 586.3 jit_solution(4027214035545917569)
XLA Ops:
  10.8 3.0 norm_rows.1
  13.8 3.0 collective-permute-start.1
  18.2 3.8 cut_feed.1
  24.9 3.7 fusion.6
  31.2 3.3 collective-permute-done.1.refs_1_
  36.9 3.6 stack_in.1
  44.6 7.8 %all-gather.6.cloned.1.call-done.refs_0_.refs_1_.refs_7_ = bf16[1536,768]{1,0:T(8,128)(2,1)} async-done(((bf16[192,768]{1,0:T(8,128)(2,1)}), bf16[1536,768]{1,0:T(8,128)(2,1)}) %all-gather.6.cloned.1.call-update) | async-done | bytes 2359312 | tf_op jit(solution)/shard_map/all_gather | solution.py:1275
  52.4 6.4 %widen.1.refs_1_ = bf16[1536,1024]{1,0:T(8,128)(2,1)} custom-call(bf16[1536,768]{1,0:T(8,128)(2,1)} %all-gather.6.cloned.1.call-done.refs_0_.refs_1_.refs_7_, bf16[768,1024]{1,0:T(8,128)(2,1)} %constant.16.clone.refs_1_.refs_7_, bf16[128,1536]{1,0:T(8,128)(2,1)} %pin.6.refs_2_.refs_0_), custom_call_target="tpu_custom_call" | custom-call | flops 48318382080 | bytes 110100480 | tf_op jit(solution)/shard_map/widen/pallas_call | solution.py:70
  58.8 2.7 split_rows.1
  64.7 13.3 %collective-permute-done.3.refs_5_.refs_2_ = bf16[512,1536]{1,0:T(8,128)(2,1)S(1)} collective-permute-done((bf16[512,1536]{1,0:T(8,128)(2,1)}, bf16[512,1536]{1,0:T(8,128)(2,1)S(1)}, u32[]{:S(2)}, u32[]{:S(2)}) %collective-permute-start.3) | collective-permute-done | bytes 1572896 | tf_op jit(solution)/shard_map/ppermute | solution.py:136
  79.6 8.4 %project_in.2.refs_4_.refs_1_ = bf16[1024,1024]{1,0:T(8,128)(2,1)} custom-call(s32[1]{0:T(128)} %bitcast.refs_0_, bf16[1536,1024]{1,0:T(8,128)(2,1)} %widen.1.refs_1_, f32[1024,128]{1,0:T(8,128)} %get-tuple-element.226.refs_2_.refs_5_, f32[1024,128]{1,0:T(8,128)} %get-tuple-element.214.refs_3_.refs_6_, bf16[512,1536]{1,0:T(8,128)(2,1)} %get-tuple-element.114.refs_4_.refs_1_, ...), custom_call_target="tpu_custom_call" | custom-call | flops 64424509440 | bytes 167772160 | tf_op jit(solution)/shard_map/project_in/pallas_call | solution.py:70
  88.0 5.8 collective-permute-done.5.refs_1_
  95.6 3.7 stack_cot.1
  100.7 10.0 %attention_forward.2 = (bf16[256,384]{1,0:T(8,128)(2,1)}, bf16[256,384]{1,0:T(8,128)(2,1)}, bf16[256,384]{1,0:T(8,128)(2,1)}, bf16[256,384]{1,0:T(8,128)(2,1)}, f32[2,4,512]{2,1,0:T(4,128)}) custom-call(s32[1]{0:T(128)} %bitcast.refs_0_, bf16[1024,1024]{1,0:T(8,128)(2,1)} %project_in.2.refs_4_.refs_1_, s32[1,1024]{1,0:T(1,128)} %get-tuple-element.223.refs_2_, ...), custom_call_target="tpu_custom_call" | custom-call | flops 42949672960 | bytes 83886080 | tf_op jit(solution)/shard_map/attention_forward/pallas_call | solution.py:70
  111.9 2.4 collective-permute-start.9
  114.2 8.7 %project_in.3.refs_1_ = bf16[1024,1024]{1,0:T(8,128)(2,1)} custom-call(s32[1]{0:T(128)} %bitcast.refs_0_, bf16[1536,1024]{1,0:T(8,128)(2,1)} %widen.1.refs_1_, f32[1024,128]{1,0:T(8,128)} %get-tuple-element.227.refs_2_.refs_5_, f32[1024,128]{1,0:T(8,128)} %get-tuple-element.213.refs_3_.refs_6_, ...), custom_call_target="tpu_custom_call" | custom-call | flops 64424509440 | bytes 167772160 | tf_op jit(solution)/shard_map/project_in/pallas_call | solution.py:70
  125.8 16.2 %collective-permute-done.8.refs_6_.refs_4_ = bf16[256,384]{1,0:T(8,128)(2,1)} collective-permute-done((bf16[256,384]{1,0:T(8,128)(2,1)}, bf16[256,384]{1,0:T(8,128)(2,1)}, u32[]{:S(2)}, u32[]{:S(2)}) %collective-permute-start.8) | collective-permute-done | bytes 196640 | tf_op jit(solution)/shard_map/ppermute | solution.py:141
  142.0 5.9 %project_out.2 = (f32[256,1536]{1,0:T(8,128)}, bf16[256,768]{1,0:T(8,128)(2,1)}, bf16[256,768]{1,0:T(8,128)(2,1)}) custom-call(s32[1]{0:T(128)} %bitcast.refs_0_, bf16[4,384,1536]{2,1,0:T(8,128)(2,1)} %bitcast.32, bf16[2,256,1536]{2,1,0:T(8,128)(2,1)} %refs_0_.5, f32[1,1536]{1,0:T(1,128)} %broadcast_in_dim.20.refs_3_, ...), custom_call_target="tpu_custom_call" | custom-call | flops 24159191040 | bytes 173015040 | tf_op jit(solution)/shard_map/project_out/pallas_call | solution.py:70
  150.2 10.0 %attention_forward.3 = (bf16[256,384]{1,0:T(8,128)(2,1)}, bf16[256,384]{1,0:T(8,128)(2,1)}, bf16[256,384]{1,0:T(8,128)(2,1)}, bf16[256,384]{1,0:T(8,128)(2,1)}, f32[2,4,512]{2,1,0:T(4,128)}) custom-call(s32[1]{0:T(128)} %bitcast.refs_0_, bf16[1024,1024]{1,0:T(8,128)(2,1)} %project_in.3.refs_1_, s32[1,1024]{1,0:T(1,128)} %get-tuple-element.222.refs_2_, ...), custom_call_target="tpu_custom_call" | custom-call | flops 42949672960 | bytes 83886080 | tf_op jit(solution)/shard_map/attention_forward/pallas_call | solution.py:70
  162.0 4.3 collective-permute-done.12.refs_3_
  166.3 2.6 stack_mid.2
  172.0 2.8 collective-permute-start.21
  175.1 11.2 %collective-permute-done.15.refs_4_ = bf16[128,1536]{1,0:T(8,128)(2,1)S(1)} collective-permute-done((bf16[128,1536]{1,0:T(8,128)(2,1)}, bf16[128,1536]{1,0:T(8,128)(2,1)S(1)}, u32[]{:S(2)}, u32[]{:S(2)}) %collective-permute-start.15) | collective-permute-done | bytes 393248 | tf_op jit(solution)/shard_map/ppermute | solution.py:150
  187.8 2.6 join.1.refs_8_.refs_2_.refs_1_
  190.4 5.9 %project_out.3 = (f32[256,1536]{1,0:T(8,128)}, bf16[256,768]{1,0:T(8,128)(2,1)}, bf16[256,768]{1,0:T(8,128)(2,1)}) custom-call(s32[1]{0:T(128)} %bitcast.refs_0_, bf16[4,384,1536]{2,1,0:T(8,128)(2,1)} %bitcast.33, bf16[2,256,1536]{2,1,0:T(8,128)(2,1)} %refs_0_.5, f32[1,1536]{1,0:T(1,128)} %broadcast_in_dim.20.refs_3_, ...), custom_call_target="tpu_custom_call" | custom-call | flops 24159191040 | bytes 173015040 | tf_op jit(solution)/shard_map/project_out/pallas_call | solution.py:70
  198.5 9.6 %collective-permute-done.22.refs_1_ = bf16[256,768]{1,0:T(8,128)(2,1)S(1)} collective-permute-done((bf16[256,768]{1,0:T(8,128)(2,1)}, bf16[256,768]{1,0:T(8,128)(2,1)S(1)}, u32[]{:S(2)}, u32[]{:S(2)}) %collective-permute-start.22) | collective-permute-done | bytes 393248 | tf_op jit(solution)/shard_map/ppermute | solution.py:136
  208.0 4.4 collective-permute-done.23.refs_3_
  213.2 2.6 stack_mid.3
  217.4 25.6 %feed_forward.2 = (bf16[1024,1024]{1,0:T(8,128)(2,1)}, bf16[1024,2048]{1,0:T(8,128)(2,1)}, bf16[1024,1536]{1,0:T(8,128)(2,1)}, bf16[512,768]{1,0:T(8,128)(2,1)},...) custom-call(s32[1]{0:T(128)} %bitcast.6.refs_0_.refs_1_, ...), custom_call_target="tpu_custom_call" | custom-call | flops 322122547200 | bytes 503316480 | tf_op jit(solution)/shard_map/feed_forward/pallas_call | solution.py:70
  246.7 25.2 %feed_forward.3 = (bf16[1024,1024]{1,0:T(8,128)(2,1)}, bf16[1024,2048]{1,0:T(8,128)(2,1)}, bf16[1024,1536]{1,0:T(8,128)(2,1)}, bf16[512,768]{1,0:T(8,128)(2,1)},...) custom-call(s32[1]{0:T(128)} %bitcast.6.refs_0_.refs_1_, ...), custom_call_target="tpu_custom_call" | custom-call | flops 322122547200 | bytes 503316480 | tf_op jit(solution)/shard_map/feed_forward/pallas_call | solution.py:70
  272.4 3.3 fold.5
  279.3 20.4 %gate_up_grad.1 = (bf16[1536,2048]{1,0:T(8,128)(2,1)}, f32[1536,1]{1,0:T(8,128)}) custom-call(bf16[1024,1536]{1,0:T(8,128)(2,1)} %get-tuple-element.150.refs_0_, bf16[1024,1536]{1,0:T(8,128)(2,1)} %get-tuple-element.151.refs_1_, bf16[1024,2048]{1,0:T(8,128)(2,1)} %get-tuple-element.152.refs_2_, bf16[1024,2048]{1,0:T(8,128)(2,1)} %get-tuple-element.153.refs_3_, ...), custom_call_target="tpu_custom_call" | custom-call | flops 257698037760 | bytes 419430400 | tf_op jit(solution)/shard_map/gate_up_grad/pallas_call | solution.py:70
  299.8 6.8 %norm_out_back.2 = (f32[256,1536]{1,0:T(8,128)}, bf16[256,1536]{1,0:T(8,128)(2,1)}, bf16[256,384]{1,0:T(8,128)(2,1)}, bf16[256,384]{1,0:T(8,128)(2,1)}, bf16[256...) custom-call(s32[1]{0:T(128)} %bitcast.refs_0_, f32[256,1536]{1,0:T(8,128)} %get-tuple-element.123.refs_1_.refs_0_, ...), custom_call_target="tpu_custom_call" | custom-call | flops 24159191040 | bytes 220200960 | tf_op jit(solution)/shard_map/norm_out_back/pallas_call | solution.py:70
  307.1 3.0 collective-permute-start.32
  312.1 3.3 fold.6
  316.8 12.8 %feed_out.1 = (bf16[512,1536]{1,0:T(8,128)(2,1)}, bf16[512,1536]{1,0:T(8,128)(2,1)}, bf16[512,1536]{1,0:T(8,128)(2,1)}, bf16[512,1536]{1,0:T(8,128)(2,1)}) custom-call(s32[1]{0:T(128)} %bitcast.6.refs_0_.refs_1_, bf16[4,128,1536]{2,1,0:T(8,128)(2,1)} %join.1.refs_8_.refs_2_.refs_1_, bf16[4,128,1536]{2,1,0:T(8,128)(2,1)} %copy-done.44, ...), custom_call_target="tpu_custom_call" | custom-call | flops 128849018880 | bytes 272629760 | tf_op jit(solution)/shard_map/feed_out/pallas_call | solution.py:70
  334.0 6.9 %norm_out_back.3 = (f32[256,1536]{1,0:T(8,128)}, bf16[256,1536]{1,0:T(8,128)(2,1)}, bf16[256,384]{1,0:T(8,128)(2,1)}, bf16[256,384]{1,0:T(8,128)(2,1)}, bf16[256...) custom-call(s32[1]{0:T(128)} %bitcast.refs_0_, f32[256,1536]{1,0:T(8,128)} %get-tuple-element.168.refs_1_.refs_3_, ...), custom_call_target="tpu_custom_call" | custom-call | flops 24159191040 | bytes 220200960 | tf_op jit(solution)/shard_map/norm_out_back/pallas_call | solution.py:70
  343.1 11.5 %down_grad.1.refs_12_ = bf16[1024,1536]{1,0:T(8,128)(2,1)} custom-call(bf16[1024,1024]{1,0:T(8,128)(2,1)} %get-tuple-element.138.refs_3_.refs_0_, bf16[1024,1024]{1,0:T(8,128)(2,1)} %get-tuple-element.141.refs_4_.refs_1_, bf16[512,1536]{1,0:T(8,128)(2,1)} %get-tuple-element.126.refs_4_.refs_2_, bf16[512,1536]{1,0:T(8,128)(2,1)} %copy-done.7, ...), custom_call_target="tpu_custom_call" | custom-call | flops 128849018880 | bytes 272629760 | tf_op jit(solution)/shard_map/down_grad/pallas_call | solution.py:70
  354.6 7.9 %out_weight_grad.1 = (bf16[4,192,1536]{2,1,0:T(8,128)(2,1)}, bf16[4,192,1536]{2,1,0:T(8,128)(2,1)}) custom-call(s32[1]{0:T(128)} %bitcast.refs_0_, s32[1]{0:T(128)} %bitcast.6.refs_0_.refs_1_, bf16[256,384]{1,0:T(8,128)(2,1)} %get-tuple-element.118.refs_4_.refs_2_, bf16[256,384]{1,0:T(8,128)(2,1)} %copy-done.48, ...), custom_call_target="tpu_custom_call" | custom-call | flops 48318382080 | bytes 94371840 | tf_op jit(solution)/shard_map/out_weight_grad/pallas_call | solution.py:70
  362.5 20.6 %attention_backward.2.refs_1_.refs_0_.refs_5_ = bf16[1024,768]{1,0:T(8,128)(2,1)} custom-call(s32[1]{0:T(128)} %bitcast.refs_0_, bf16[1024,1024]{1,0:T(8,128)(2,1)} %project_in.2.refs_4_.refs_1_, s32[1,1024]{1,0:T(1,128)} %get-tuple-element.223.refs_2_, bf16[2,256,384]{2,1,0:T(8,128)(2,1)} %constant.17.clone.refs_3_, ...), custom_call_target="tpu_custom_call" | custom-call | flops 107374182400 | bytes 167772160 | tf_op jit(solution)/shard_map/attention_backward/pallas_call | solution.py:70
  384.5 3.3 add_convert_fusion
  391.1 7.2 %grad_into_rows.2 = (bf16[512,768]{1,0:T(8,128)(2,1)}, bf16[512,768]{1,0:T(8,128)(2,1)}, bf16[512,768]{1,0:T(8,128)(2,1)}, bf16[512,768]{1,0:T(8,128)(2,1)}) custom-call(bf16[1024,768]{1,0:T(8,128)(2,1)} %attention_backward.2.refs_1_.refs_0_.refs_5_, bf16[1536,768]{1,0:T(8,128)(2,1)} %all-gather.6.cloned.1.call-done.refs_0_.refs_1_.refs_7_, ...), custom_call_target="tpu_custom_call" | custom-call | flops 48318382080 | bytes 141557760 | tf_op jit(solution)/shard_map/grad_into_rows/pallas_call | solution.py:70
  399.8 5.2 fold.7
  407.6 20.3 %attention_backward.3.refs_4_.refs_6_.refs_0_ = bf16[1024,768]{1,0:T(8,128)(2,1)} custom-call(s32[1]{0:T(128)} %bitcast.refs_0_, bf16[1024,1024]{1,0:T(8,128)(2,1)} %project_in.3.refs_1_, s32[1,1024]{1,0:T(1,128)} %get-tuple-element.222.refs_2_, bf16[2,256,384]{2,1,0:T(8,128)(2,1)} %constant.17.clone.refs_3_, ...), custom_call_target="tpu_custom_call" | custom-call | flops 107374182400 | bytes 167772160 | tf_op jit(solution)/shard_map/attention_backward/pallas_call | solution.py:70
  430.1 3.4 fold.8
  435.9 11.1 %in_weight_grad.1 = (bf16[4,192,768]{2,1,0:T(8,128)(2,1)}, bf16[4,192,768]{2,1,0:T(8,128)(2,1)}, f32[1536,1]{1,0:T(8,128)}) custom-call(s32[1]{0:T(128)} %bitcast.6.refs_0_.refs_1_, bf16[512,1536]{1,0:T(8,128)(2,1)} %get-tuple-element.114.refs_4_.refs_1_, bf16[512,1536]{1,0:T(8,128)(2,1)} %copy-done.43, ...), custom_call_target="tpu_custom_call" | custom-call | flops 96636764160 | bytes 235929600 | tf_op jit(solution)/shard_map/in_weight_grad/pallas_call | solution.py:70
  447.0 7.0 %grad_into_rows.3 = (bf16[512,768]{1,0:T(8,128)(2,1)}, bf16[512,768]{1,0:T(8,128)(2,1)}, bf16[512,768]{1,0:T(8,128)(2,1)}, bf16[512,768]{1,0:T(8,128)(2,1)}) custom-call(bf16[1024,768]{1,0:T(8,128)(2,1)} %attention_backward.3.refs_4_.refs_6_.refs_0_, bf16[1536,768]{1,0:T(8,128)(2,1)} %all-gather.6.cloned.1.call-done.refs_0_.refs_1_.refs_7_, ...), custom_call_target="tpu_custom_call" | custom-call | flops 48318382080 | bytes 141557760 | tf_op jit(solution)/shard_map/grad_into_rows/pallas_call | solution.py:70
  455.4 2.9 halve.3
  469.4 6.2 %collective-permute-done.58.refs_2_ = bf16[128,1536]{1,0:T(8,128)(2,1)S(1)} collective-permute-done((bf16[128,1536]{1,0:T(8,128)(2,1)}, bf16[128,1536]{1,0:T(8,128)(2,1)S(1)}, u32[]{:S(2)}, u32[]{:S(2)}) %collective-permute-start.58) | collective-permute-done | bytes 393248 | tf_op jit(solution)/shard_map/ppermute | solution.py:136
  476.8 7.2 %collective-permute-done.71 = f32[2,1536]{1,0:T(2,128)S(1)} collective-permute-done((f32[2,1536]{1,0:T(2,128)S(1)}, f32[2,1536]{1,0:T(2,128)S(1)}, u32[]{:S(2)}, u32[]{:S(2)}) %collective-permute-start.71) | collective-permute-done | bytes 12320 | tf_op jit(solution)/shard_map/ppermute | solution.py:1231
  487.4 2.6 collective-permute-done.55.refs_1_
  492.7 4.7 finish_block_out.1.refs_2_
  502.2 3.4 fold.9
  505.6 3.7 collective-permute-done.62.refs_3_
  510.6 15.6 %collective-permute-done.63.refs_4_ = bf16[192,2048]{1,0:T(8,128)(2,1)} collective-permute-done((bf16[192,2048]{1,0:T(8,128)(2,1)}, bf16[192,2048]{1,0:T(8,128)(2,1)}, u32[]{:S(2)}, u32[]{:S(2)}) %collective-permute-start.63) | collective-permute-done | bytes 786464 | tf_op jit(solution)/shard_map/ppermute | solution.py:136
  527.4 4.5 arrange_gate_up.1
  534.6 4.2 collective-permute-done.68
  540.9 2.3 collective-permute-start.73
  547.2 3.0 collective-permute-start.74
  555.5 3.2 arrange_rows.1.refs_12_
  558.7 6.1 %collective-permute-done.56.refs_9_ = bf16[256,768]{1,0:T(8,128)(2,1)S(1)} collective-permute-done((bf16[256,768]{1,0:T(8,128)(2,1)}, bf16[256,768]{1,0:T(8,128)(2,1)S(1)}, u32[]{:S(2)}, u32[]{:S(2)}) %collective-permute-start.56) | collective-permute-done | bytes 393248 | tf_op jit(solution)/shard_map/ppermute | solution.py:136
  565.7 6.4 %finish_tokens_grad.1.refs_5_ = bf16[2,256,1536]{2,1,0:T(8,128)(2,1)} custom-call(bf16[2,256,1536]{2,1,0:T(8,128)(2,1)} %refs_0_.5, f32[1,1536]{1,0:T(1,128)} %broadcast_in_dim.21.refs_1_, f32[256,1536]{1,0:T(8,128)} %get-tuple-element.194.refs_2_, f32[256,768]{1,0:T(8,128)} %get-tuple-element.195.refs_3_, bf16[256,768]{1,0:T(8,128)(2,1)} %copy-done.21, ...), custom_call_target="tpu_custom_call" | custom-call | bytes 188743680 | tf_op jit(solution)/shard_map/finish_tokens_grad/pallas_call | solution.py:70
  572.1 2.6 collective-permute-done.66.refs_4_
  575.4 2.7 arrange_in.1
  (288 shorter events, 118.0 us)
Async XLA Ops:
  7.2 45.3 %all-gather.6.cloned.1.call-start = ((), (), s32[]{:S(2)}) async-start(), calls=%async_computation.3 | async-start | bytes 2654208 | tf_op jit(solution)/shard_map/all_gather | solution.py:1275
  9.4 132.6 %all-gather.4.cloned.1.call-start = ((), (), s32[]{:S(2)}) async-start(), calls=%async_computation.2 | async-start | bytes 5308416 | tf_op jit(solution)/shard_map/all_gather | solution.py:1275
  10.1 206.2 %all-gather.8.cloned.1.call-start = ((), (), s32[]{:S(2)}) async-start(), calls=%async_computation.4 | async-start | bytes 7077888 | tf_op jit(solution)/shard_map/all_gather | solution.py:1275
  13.8 20.7 %collective-permute-start.1 = (bf16[256,1536]{1,0:T(8,128)(2,1)}, bf16[256,1536]{1,0:T(8,128)(2,1)S(1)}, u32[]{:S(2)}, u32[]{:S(2)}) collective-permute-start(bf16[256,1536]{1,0:T(8,128)(2,1)} %get-tuple-element.112.refs_0_), channel_id=1, source_target_pairs={{0,16},{8,24},{16,0},{24,8},{1,17},{9,25},{17,1},{25,9},{2,18},{10... | collective-permute-start | bytes 2359304 | tf_op jit(solution)/shard_map/ppermute | solution.py:136
  16.8 19.2 %collective-permute-start.2 = (bf16[256,1536]{1,0:T(8,128)(2,1)}, bf16[256,1536]{1,0:T(8,128)(2,1)S(1)}, u32[]{:S(2)}, u32[]{:S(2)}) collective-permute-start(bf16[256,1536]{1,0:T(8,128)(2,1)} %get-tuple-element.110.refs_4_.refs_2_), channel_id=1, source_target_pairs={{0,8},{8,0},{16,24},{24,16},{1,9},{9,1},{17,25},{25,17},{2,10},{10... | collective-permute-start | bytes 2359304 | tf_op jit(solution)/shard_map/ppermute | solution.py:136
  22.0 21.8 %collective-permute-start = (bf16[128,1536]{1,0:T(8,128)(2,1)}, bf16[128,1536]{1,0:T(8,128)(2,1)S(1)}, u32[]{:S(2)}, u32[]{:S(2)}) collective-permute-start(bf16[128,1536]{1,0:T(8,128)(2,1)} %get-tuple-element.111.refs_4_.refs_1_), channel_id=1, source_target_pairs={{0,2},{1,3},{2,4},{3,5},{4,6},{5,7},{6,0},{7,1},{8,10},{9,11},{10,... | collective-permute-start | bytes 1179656 | tf_op jit(solution)/shard_map/ppermute | solution.py:150
  23.6 383.2 %reduce-scatter.3.cloned.1.call-start = ((), (), s32[]{:S(2)}) async-start(), calls=%async_computation.5 | async-start | bytes 7077888 | tf_op jit(solution)/shard_map/reduce_scatter | solution.py:1278
  40.5 37.5 %collective-permute-start.3 = (bf16[512,1536]{1,0:T(8,128)(2,1)}, bf16[512,1536]{1,0:T(8,128)(2,1)S(1)}, u32[]{:S(2)}, u32[]{:S(2)}) collective-permute-start(bf16[512,1536]{1,0:T(8,128)(2,1)} %get-tuple-element.114.refs_4_.refs_1_), channel_id=1, source_target_pairs={{0,8},{8,0},{16,24},{24,16},{1,9},{9,1},{17,25},{25,17},{2,10},{10... | collective-permute-start | bytes 4718600 | tf_op jit(solution)/shard_map/ppermute | solution.py:136
  41.9 37.6 %collective-permute-start.4 = (bf16[512,1536]{1,0:T(8,128)(2,1)}, bf16[512,1536]{1,0:T(8,128)(2,1)}, u32[]{:S(2)}, u32[]{:S(2)}) collective-permute-start(bf16[512,1536]{1,0:T(8,128)(2,1)} %get-tuple-element.113.refs_1_.refs_6_.refs_4_.refs_3_), channel_id=1, source_target_pairs={{0,16},{8,24},{16,0},{24,8},{1,17},{9,25},{17,1},{25,9},{2,18},{10... | collective-permute-start | bytes 4718600 | tf_op jit(solution)/shard_map/ppermute | solution.py:136
  61.5 32.3 %collective-permute-start.5 = (bf16[256,1536]{1,0:T(8,128)(2,1)}, bf16[256,1536]{1,0:T(8,128)(2,1)S(1)}, u32[]{:S(2)}, u32[]{:S(2)}) collective-permute-start(bf16[256,1536]{1,0:T(8,128)(2,1)} %get-tuple-element.116.refs_0_), channel_id=1, source_target_pairs={{0,16},{8,24},{16,0},{24,8},{1,17},{9,25},{17,1},{25,9},{2,18},{10... | collective-permute-start | bytes 2359304 | tf_op jit(solution)/shard_map/ppermute | solution.py:136
  62.5 31.3 %collective-permute-start.6 = (bf16[256,1536]{1,0:T(8,128)(2,1)}, bf16[256,1536]{1,0:T(8,128)(2,1)S(1)}, u32[]{:S(2)}, u32[]{:S(2)}) collective-permute-start(bf16[256,1536]{1,0:T(8,128)(2,1)} %get-tuple-element.115.refs_8_.refs_2_), channel_id=1, source_target_pairs={{0,8},{8,0},{16,24},{24,16},{1,9},{9,1},{17,25},{25,17},{2,10},{10... | collective-permute-start | bytes 2359304 | tf_op jit(solution)/shard_map/ppermute | solution.py:136
  99.3 62.7 %collective-permute-start.14 = (bf16[512,1536]{1,0:T(8,128)(2,1)}, bf16[512,1536]{1,0:T(8,128)(2,1)}, u32[]{:S(2)}, u32[]{:S(2)}) collective-permute-start(bf16[512,1536]{1,0:T(8,128)(2,1)} %get-tuple-element.117.refs_4_.refs_6_), channel_id=1, source_target_pairs={{0,16},{8,24},{16,0},{24,8},{1,17},{9,25},{17,1},{25,9},{2,18},{10... | collective-permute-start | bytes 4718600 | tf_op jit(solution)/shard_map/ppermute | solution.py:136
  111.3 30.8 %collective-permute-start.8 = (bf16[256,384]{1,0:T(8,128)(2,1)}, bf16[256,384]{1,0:T(8,128)(2,1)}, u32[]{:S(2)}, u32[]{:S(2)}) collective-permute-start(bf16[256,384]{1,0:T(8,128)(2,1)} %get-tuple-element.120), channel_id=1, source_target_pairs={{0,16},{8,24},{16,0},{24,8},{1,17},{9,25},{17,1},{25,9},{2,18},{10... | collective-permute-start | bytes 589832 | tf_op jit(solution)/shard_map/ppermute | solution.py:141
  111.9 30.1 %collective-permute-start.9 = (bf16[256,384]{1,0:T(8,128)(2,1)}, bf16[256,384]{1,0:T(8,128)(2,1)}, u32[]{:S(2)}, u32[]{:S(2)}) collective-permute-start(bf16[256,384]{1,0:T(8,128)(2,1)} %get-tuple-element.121), channel_id=1, source_target_pairs={{0,24},{8,16},{16,8},{24,0},{1,25},{9,17},{17,9},{25,1},{2,26},{10... | collective-permute-start | bytes 589832 | tf_op jit(solution)/shard_map/ppermute | solution.py:141
  122.9 46.0 %collective-permute-start.10 = (bf16[128,1536]{1,0:T(8,128)(2,1)}, bf16[128,1536]{1,0:T(8,128)(2,1)S(1)}, u32[]{:S(2)}, u32[]{:S(2)}) collective-permute-start(bf16[128,1536]{1,0:T(8,128)(2,1)} %pin.7.refs_8_.refs_2_), channel_id=1, source_target_pairs={{0,2},{1,3},{2,4},{3,5},{4,6},{5,7},{6,0},{7,1},{8,10},{9,11},{10,... | collective-permute-start | bytes 1179656 | tf_op jit(solution)/shard_map/ppermute | solution.py:150
  125.2 36.8 %collective-permute-start.13 = (bf16[512,1536]{1,0:T(8,128)(2,1)S(1)}, bf16[512,1536]{1,0:T(8,128)(2,1)S(1)}, u32[]{:S(2)}, u32[]{:S(2)}) collective-permute-start(bf16[512,1536]{1,0:T(8,128)(2,1)S(1)} %copy-done.6), channel_id=1, source_target_pairs={{0,8},{8,0},{16,24},{24,16},{1,9},{9,1},{17,25},{25,17},{2,10},{10... | collective-permute-start | bytes 4718600 | tf_op jit(solution)/shard_map/ppermute | solution.py:136
  149.7 16.6 %collective-permute-start.12 = (bf16[256,768]{1,0:T(8,128)(2,1)}, bf16[256,768]{1,0:T(8,128)(2,1)}, u32[]{:S(2)}, u32[]{:S(2)}) collective-permute-start(bf16[256,768]{1,0:T(8,128)(2,1)} %get-tuple-element.125.refs_4_.refs_2_), channel_id=1, source_target_pairs={{0,8},{8,0},{16,24},{24,16},{1,9},{9,1},{17,25},{25,17},{2,10},{10... | collective-permute-start | bytes 1179656 | tf_op jit(solution)/shard_map/ppermute | solution.py:136
  169.7 16.6 %collective-permute-start.15 = (bf16[128,1536]{1,0:T(8,128)(2,1)}, bf16[128,1536]{1,0:T(8,128)(2,1)S(1)}, u32[]{:S(2)}, u32[]{:S(2)}) collective-permute-start(bf16[128,1536]{1,0:T(8,128)(2,1)} %pin.8.refs_3_.refs_5_), channel_id=1, source_target_pairs={{0,2},{1,3},{2,4},{3,5},{4,6},{5,7},{6,0},{7,1},{8,10},{9,11},{10,... | collective-permute-start | bytes 1179656 | tf_op jit(solution)/shard_map/ppermute | solution.py:150
  171.3 19.1 %collective-permute-start.19 = (bf16[256,384]{1,0:T(8,128)(2,1)S(1)}, bf16[256,384]{1,0:T(8,128)(2,1)}, u32[]{:S(2)}, u32[]{:S(2)}) collective-permute-start(bf16[256,384]{1,0:T(8,128)(2,1)S(1)} %copy-done.54), channel_id=1, source_target_pairs={{0,8},{8,0},{16,24},{24,16},{1,9},{9,1},{17,25},{25,17},{2,10},{10... | collective-permute-start | bytes 589832 | tf_op jit(solution)/shard_map/ppermute | solution.py:141
  171.6 18.8 %collective-permute-start.20 = (bf16[256,384]{1,0:T(8,128)(2,1)}, bf16[256,384]{1,0:T(8,128)(2,1)}, u32[]{:S(2)}, u32[]{:S(2)}) collective-permute-start(bf16[256,384]{1,0:T(8,128)(2,1)} %get-tuple-element.133), channel_id=1, source_target_pairs={{0,16},{8,24},{16,0},{24,8},{1,17},{9,25},{17,1},{25,9},{2,18},{10... | collective-permute-start | bytes 589832 | tf_op jit(solution)/shard_map/ppermute | solution.py:141
  172.0 18.4 %collective-permute-start.21 = (bf16[256,384]{1,0:T(8,128)(2,1)}, bf16[256,384]{1,0:T(8,128)(2,1)}, u32[]{:S(2)}, u32[]{:S(2)}) collective-permute-start(bf16[256,384]{1,0:T(8,128)(2,1)} %get-tuple-element.134), channel_id=1, source_target_pairs={{0,24},{8,16},{16,8},{24,0},{1,25},{9,17},{17,9},{25,1},{2,26},{10... | collective-permute-start | bytes 589832 | tf_op jit(solution)/shard_map/ppermute | solution.py:141
  174.8 41.5 %collective-permute-start.18 = (bf16[512,768]{1,0:T(8,128)(2,1)S(1)}, bf16[512,768]{1,0:T(8,128)(2,1)}, u32[]{:S(2)}, u32[]{:S(2)}) collective-permute-start(bf16[512,768]{1,0:T(8,128)(2,1)S(1)} %copy-done.15), channel_id=1, source_target_pairs={{0,16},{8,24},{16,0},{24,8},{1,17},{9,25},{17,1},{25,9},{2,18},{10... | collective-permute-start | bytes 2359304 | tf_op jit(solution)/shard_map/ppermute | solution.py:136
  186.3 30.0 %collective-permute-start.17 = (bf16[512,768]{1,0:T(8,128)(2,1)S(1)}, bf16[512,768]{1,0:T(8,128)(2,1)}, u32[]{:S(2)}, u32[]{:S(2)}) collective-permute-start(bf16[512,768]{1,0:T(8,128)(2,1)S(1)} %copy-done.45), channel_id=1, source_target_pairs={{0,8},{8,0},{16,24},{24,16},{1,9},{9,1},{17,25},{25,17},{2,10},{10... | collective-permute-start | bytes 2359304 | tf_op jit(solution)/shard_map/ppermute | solution.py:136
  190.4 25.9 %collective-permute-start.16 = (bf16[4,128,1536]{2,1,0:T(8,128)(2,1)}, bf16[4,128,1536]{2,1,0:T(8,128)(2,1)S(1)}, u32[]{:S(2)}, u32[]{:S(2)}) collective-permute-start(bf16[4,128,1536]{2,1,0:T(8,128)(2,1)} %join.1.refs_8_.refs_2_.refs_1_), channel_id=1, source_target_pairs={{0,1},{1,0},{2,3},{3,2},{4,5},{5,4},{6,7},{7,6},{8,9},{9,8},{10,11... | collective-permute-start | bytes 4718600 | tf_op jit(solution)/shard_map/ppermute | solution.py:155
  215.8 30.9 %collective-permute-start.24 = (bf16[512,768]{1,0:T(8,128)(2,1)}, bf16[512,768]{1,0:T(8,128)(2,1)}, u32[]{:S(2)}, u32[]{:S(2)}) collective-permute-start(bf16[512,768]{1,0:T(8,128)(2,1)} %get-tuple-element.139.refs_6_), channel_id=1, source_target_pairs={{0,8},{8,0},{16,24},{24,16},{1,9},{9,1},{17,25},{25,17},{2,10},{10... | collective-permute-start | bytes 2359304 | tf_op jit(solution)/shard_map/ppermute | solution.py:136
  216.0 30.6 %collective-permute-start.25 = (bf16[512,768]{1,0:T(8,128)(2,1)}, bf16[512,768]{1,0:T(8,128)(2,1)}, u32[]{:S(2)}, u32[]{:S(2)}) collective-permute-start(bf16[512,768]{1,0:T(8,128)(2,1)} %get-tuple-element.137.refs_10_.refs_8_), channel_id=1, source_target_pairs={{0,16},{8,24},{16,0},{24,8},{1,17},{9,25},{17,1},{25,9},{2,18},{10... | collective-permute-start | bytes 2359304 | tf_op jit(solution)/shard_map/ppermute | solution.py:136
  243.1 29.4 %collective-permute-start.26 = (bf16[512,768]{1,0:T(8,128)(2,1)}, bf16[512,768]{1,0:T(8,128)(2,1)}, u32[]{:S(2)}, u32[]{:S(2)}) collective-permute-start(bf16[512,768]{1,0:T(8,128)(2,1)} %get-tuple-element.144), channel_id=1, source_target_pairs={{0,8},{8,0},{16,24},{24,16},{1,9},{9,1},{17,25},{25,17},{2,10},{10... | collective-permute-start | bytes 2359304 | tf_op jit(solution)/shard_map/ppermute | solution.py:136
  244.7 27.7 %collective-permute-start.27 = (bf16[512,768]{1,0:T(8,128)(2,1)}, bf16[512,768]{1,0:T(8,128)(2,1)}, u32[]{:S(2)}, u32[]{:S(2)}) collective-permute-start(bf16[512,768]{1,0:T(8,128)(2,1)} %get-tuple-element.140.refs_10_), channel_id=1, source_target_pairs={{0,16},{8,24},{16,0},{24,8},{1,17},{9,25},{17,1},{25,9},{2,18},{10... | collective-permute-start | bytes 2359304 | tf_op jit(solution)/shard_map/ppermute | solution.py:136
  271.9 40.3 %collective-permute-start.33 = (bf16[512,768]{1,0:T(8,128)(2,1)}, bf16[512,768]{1,0:T(8,128)(2,1)}, u32[]{:S(2)}, u32[]{:S(2)}) collective-permute-start(bf16[512,768]{1,0:T(8,128)(2,1)} %get-tuple-element.160), channel_id=1, source_target_pairs={{0,8},{8,0},{16,24},{24,16},{1,9},{9,1},{17,25},{25,17},{2,10},{10... | collective-permute-start | bytes 2359304 | tf_op jit(solution)/shard_map/ppermute | solution.py:136
  272.2 39.9 %collective-permute-start.34 = (bf16[512,768]{1,0:T(8,128)(2,1)}, bf16[512,768]{1,0:T(8,128)(2,1)}, u32[]{:S(2)}, u32[]{:S(2)}) collective-permute-start(bf16[512,768]{1,0:T(8,128)(2,1)} %get-tuple-element.145.refs_4_), channel_id=1, source_target_pairs={{0,16},{8,24},{16,0},{24,8},{1,17},{9,25},{17,1},{25,9},{2,18},{10... | collective-permute-start | bytes 2359304 | tf_op jit(solution)/shard_map/ppermute | solution.py:136
  275.8 24.0 %collective-permute-start.28 = (bf16[256,768]{1,0:T(8,128)(2,1)}, bf16[256,768]{1,0:T(8,128)(2,1)}, u32[]{:S(2)}, u32[]{:S(2)}) collective-permute-start(bf16[256,768]{1,0:T(8,128)(2,1)} %get-tuple-element.147), channel_id=1, source_target_pairs={{0,16},{8,24},{16,0},{24,8},{1,17},{9,25},{17,1},{25,9},{2,18},{10... | collective-permute-start | bytes 1179656 | tf_op jit(solution)/shard_map/ppermute | solution.py:136
  277.6 22.2 %collective-permute-start.29 = (bf16[256,768]{1,0:T(8,128)(2,1)}, bf16[256,768]{1,0:T(8,128)(2,1)}, u32[]{:S(2)}, u32[]{:S(2)}) collective-permute-start(bf16[256,768]{1,0:T(8,128)(2,1)} %get-tuple-element.149.refs_5_), channel_id=1, source_target_pairs={{0,8},{8,0},{16,24},{24,16},{1,9},{9,1},{17,25},{25,17},{2,10},{10... | collective-permute-start | bytes 1179656 | tf_op jit(solution)/shard_map/ppermute | solution.py:136
  310.1 153.3 %reduce-scatter.5.cloned.1.call-start = ((), (), s32[]{:S(2)}) async-start(), calls=%async_computation.6 | async-start | bytes 3538944 | tf_op jit(solution)/shard_map/reduce_scatter | solution.py:1278
  315.4 17.6 %collective-permute-start.37 = (bf16[256,768]{1,0:T(8,128)(2,1)}, bf16[256,768]{1,0:T(8,128)(2,1)S(1)}, u32[]{:S(2)}, u32[]{:S(2)}) collective-permute-start(bf16[256,768]{1,0:T(8,128)(2,1)} %get-tuple-element.170), channel_id=1, source_target_pairs={{0,16},{8,24},{16,0},{24,8},{1,17},{9,25},{17,1},{25,9},{2,18},{10... | collective-permute-start | bytes 1179656 | tf_op jit(solution)/shard_map/ppermute | solution.py:136
  315.5 17.5 %collective-permute-start.38 = (bf16[256,768]{1,0:T(8,128)(2,1)}, bf16[256,768]{1,0:T(8,128)(2,1)S(1)}, u32[]{:S(2)}, u32[]{:S(2)}) collective-permute-start(bf16[256,768]{1,0:T(8,128)(2,1)} %get-tuple-element.161.refs_8_), channel_id=1, source_target_pairs={{0,8},{8,0},{16,24},{24,16},{1,9},{9,1},{17,25},{25,17},{2,10},{10... | collective-permute-start | bytes 1179656 | tf_op jit(solution)/shard_map/ppermute | solution.py:136
  329.6 70.2 %collective-permute-start.35 = (bf16[512,1536]{1,0:T(8,128)(2,1)}, bf16[512,1536]{1,0:T(8,128)(2,1)}, u32[]{:S(2)}, u32[]{:S(2)}) collective-permute-start(bf16[512,1536]{1,0:T(8,128)(2,1)} %get-tuple-element.164), channel_id=1, source_target_pairs={{0,8},{8,0},{16,24},{24,16},{1,9},{9,1},{17,25},{25,17},{2,10},{10... | collective-permute-start | bytes 4718600 | tf_op jit(solution)/shard_map/ppermute | solution.py:136
  331.8 68.0 %collective-permute-start.36 = (bf16[512,1536]{1,0:T(8,128)(2,1)}, bf16[512,1536]{1,0:T(8,128)(2,1)}, u32[]{:S(2)}, u32[]{:S(2)}) collective-permute-start(bf16[512,1536]{1,0:T(8,128)(2,1)} %get-tuple-element.165.refs_9_), channel_id=1, source_target_pairs={{0,16},{8,24},{16,0},{24,8},{1,17},{9,25},{17,1},{25,9},{2,18},{10... | collective-permute-start | bytes 4718600 | tf_op jit(solution)/shard_map/ppermute | solution.py:136
  340.9 49.2 %collective-permute-start.39 = (bf16[256,384]{1,0:T(8,128)(2,1)}, bf16[256,384]{1,0:T(8,128)(2,1)}, u32[]{:S(2)}, u32[]{:S(2)}) collective-permute-start(bf16[256,384]{1,0:T(8,128)(2,1)} %get-tuple-element.175), channel_id=1, source_target_pairs={{0,8},{8,0},{16,24},{24,16},{1,9},{9,1},{17,25},{25,17},{2,10},{10... | collective-permute-start | bytes 589832 | tf_op jit(solution)/shard_map/ppermute | solution.py:141
  341.2 49.2 %collective-permute-start.41 = (bf16[256,384]{1,0:T(8,128)(2,1)}, bf16[256,384]{1,0:T(8,128)(2,1)}, u32[]{:S(2)}, u32[]{:S(2)}) collective-permute-start(bf16[256,384]{1,0:T(8,128)(2,1)} %get-tuple-element.173.refs_6_), channel_id=1, source_target_pairs={{0,24},{8,16},{16,8},{24,0},{1,25},{9,17},{17,9},{25,1},{2,26},{10... | collective-permute-start | bytes 589832 | tf_op jit(solution)/shard_map/ppermute | solution.py:141
  362.5 20.6 %collective-permute-start.42 = (bf16[4,192,1536]{2,1,0:T(8,128)(2,1)}, bf16[4,192,1536]{2,1,0:T(8,128)(2,1)S(1)}, u32[]{:S(2)}, u32[]{:S(2)}) collective-permute-start(bf16[4,192,1536]{2,1,0:T(8,128)(2,1)} %get-tuple-element.174.refs_12_), channel_id=1, source_target_pairs={{0,1},{1,0},{2,3},{3,2},{4,5},{5,4},{6,7},{7,6},{8,9},{9,8},{10,11... | collective-permute-start | bytes 7077896 | tf_op jit(solution)/shard_map/ppermute | solution.py:155
  390.1 43.4 %collective-permute-start.45 = (bf16[192,1536]{1,0:T(8,128)(2,1)}, bf16[192,1536]{1,0:T(8,128)(2,1)}, u32[]{:S(2)}, u32[]{:S(2)}) collective-permute-start(bf16[192,1536]{1,0:T(8,128)(2,1)} %slice_bitcast_fusion.2), channel_id=1, source_target_pairs={{0,2},{1,3},{2,4},{3,5},{4,6},{5,7},{6,0},{7,1},{8,10},{9,11},{10,... | collective-permute-start | bytes 1769480 | tf_op jit(solution)/shard_map/ppermute | solution.py:150
  398.3 29.6 %collective-permute-start.46 = (bf16[512,768]{1,0:T(8,128)(2,1)}, bf16[512,768]{1,0:T(8,128)(2,1)S(1)}, u32[]{:S(2)}, u32[]{:S(2)}) collective-permute-start(bf16[512,768]{1,0:T(8,128)(2,1)} %get-tuple-element.185), channel_id=1, source_target_pairs={{0,8},{8,0},{16,24},{24,16},{1,9},{9,1},{17,25},{25,17},{2,10},{10... | collective-permute-start | bytes 2359304 | tf_op jit(solution)/shard_map/ppermute | solution.py:136
  398.3 30.9 %collective-permute-start.47 = (bf16[512,768]{1,0:T(8,128)(2,1)}, bf16[512,768]{1,0:T(8,128)(2,1)S(1)}, u32[]{:S(2)}, u32[]{:S(2)}) collective-permute-start(bf16[512,768]{1,0:T(8,128)(2,1)} %get-tuple-element.177.refs_4_), channel_id=1, source_target_pairs={{0,16},{8,24},{16,0},{24,8},{1,17},{9,25},{17,1},{25,9},{2,18},{10... | collective-permute-start | bytes 2359304 | tf_op jit(solution)/shard_map/ppermute | solution.py:136
  405.0 60.2 %collective-permute-start.44 = (bf16[256,1536]{1,0:T(8,128)(2,1)}, bf16[256,1536]{1,0:T(8,128)(2,1)}, u32[]{:S(2)}, u32[]{:S(2)}) collective-permute-start(bf16[256,1536]{1,0:T(8,128)(2,1)} %get-tuple-element.181.refs_13_), channel_id=1, source_target_pairs={{0,8},{8,0},{16,24},{24,16},{1,9},{9,1},{17,25},{25,17},{2,10},{10... | collective-permute-start | bytes 2359304 | tf_op jit(solution)/shard_map/ppermute | solution.py:136
  406.8 29.1 %collective-permute-start.49 = (bf16[192,2048]{1,0:T(8,128)(2,1)}, bf16[192,2048]{1,0:T(8,128)(2,1)}, u32[]{:S(2)}, u32[]{:S(2)}) collective-permute-start(bf16[192,2048]{1,0:T(8,128)(2,1)} %reduce-scatter.3.cloned.1.call-done.refs_12_.refs_1_), channel_id=1, source_target_pairs={{0,16},{8,24},{16,0},{24,8},{1,17},{9,25},{17,1},{25,9},{2,18},{10... | collective-permute-start | bytes 2359304 | tf_op jit(solution)/shard_map/ppermute | solution.py:136
  427.9 36.6 %collective-permute-start.43 = (bf16[256,1536]{1,0:T(8,128)(2,1)}, bf16[256,1536]{1,0:T(8,128)(2,1)}, u32[]{:S(2)}, u32[]{:S(2)}) collective-permute-start(bf16[256,1536]{1,0:T(8,128)(2,1)} %get-tuple-element.179), channel_id=1, source_target_pairs={{0,16},{8,24},{16,0},{24,8},{1,17},{9,25},{17,1},{25,9},{2,18},{10... | collective-permute-start | bytes 2359304 | tf_op jit(solution)/shard_map/ppermute | solution.py:136
  435.7 22.6 %collective-permute-start.48 = (bf16[192,1536]{1,0:T(8,128)(2,1)}, bf16[192,1536]{1,0:T(8,128)(2,1)}, u32[]{:S(2)}, u32[]{:S(2)}) collective-permute-start(bf16[192,1536]{1,0:T(8,128)(2,1)} %fusion.2), channel_id=1, source_target_pairs={{0,2},{1,3},{2,4},{3,5},{4,6},{5,7},{6,0},{7,1},{8,10},{9,11},{10,... | collective-permute-start | bytes 1769480 | tf_op jit(solution)/shard_map/ppermute | solution.py:150
  459.6 25.3 %collective-permute-start.67 = (bf16[192,1536]{1,0:T(8,128)(2,1)S(1)}, bf16[192,1536]{1,0:T(8,128)(2,1)}, u32[]{:S(2)}, u32[]{:S(2)}) collective-permute-start(bf16[192,1536]{1,0:T(8,128)(2,1)S(1)} %fusion), channel_id=1, source_target_pairs={{0,2},{1,3},{2,4},{3,5},{4,6},{5,7},{6,0},{7,1},{8,10},{9,11},{10,... | collective-permute-start | bytes 1769480 | tf_op jit(solution)/shard_map/ppermute | solution.py:150
  464.5 36.4 %collective-permute-start.54 = (bf16[512,768]{1,0:T(8,128)(2,1)}, bf16[512,768]{1,0:T(8,128)(2,1)}, u32[]{:S(2)}, u32[]{:S(2)}) collective-permute-start(bf16[512,768]{1,0:T(8,128)(2,1)} %get-tuple-element.192.refs_2_), channel_id=1, source_target_pairs={{0,16},{8,24},{16,0},{24,8},{1,17},{9,25},{17,1},{25,9},{2,18},{10... | collective-permute-start | bytes 2359304 | tf_op jit(solution)/shard_map/ppermute | solution.py:136
  465.3 34.3 %collective-permute-start.53 = (bf16[512,768]{1,0:T(8,128)(2,1)}, bf16[512,768]{1,0:T(8,128)(2,1)}, u32[]{:S(2)}, u32[]{:S(2)}) collective-permute-start(bf16[512,768]{1,0:T(8,128)(2,1)} %get-tuple-element.201), channel_id=1, source_target_pairs={{0,8},{8,0},{16,24},{24,16},{1,9},{9,1},{17,25},{25,17},{2,10},{10... | collective-permute-start | bytes 2359304 | tf_op jit(solution)/shard_map/ppermute | solution.py:136
  466.7 23.3 %collective-permute-start.55 = (bf16[2,192,768]{2,1,0:T(8,128)(2,1)S(1)}, bf16[2,192,768]{2,1,0:T(8,128)(2,1)S(1)}, u32[]{:S(2)}, u32[]{:S(2)}) collective-permute-start(bf16[2,192,768]{2,1,0:T(8,128)(2,1)S(1)} %copy-done.18), channel_id=1, source_target_pairs={{0,2},{1,3},{2,0},{3,1},{4,6},{5,7},{6,4},{7,5},{8,10},{9,11},{10,... | collective-permute-start | bytes 1769480 | tf_op jit(solution)/shard_map/ppermute | solution.py:1044
  484.1 25.3 %collective-permute-start.62 = (bf16[192,2048]{1,0:T(8,128)(2,1)}, bf16[192,2048]{1,0:T(8,128)(2,1)}, u32[]{:S(2)}, u32[]{:S(2)}) collective-permute-start(bf16[192,2048]{1,0:T(8,128)(2,1)} %reduce-scatter.3.cloned.1.call-done.refs_12_.refs_1_), channel_id=1, source_target_pairs={{0,8},{8,0},{16,24},{24,16},{1,9},{9,1},{17,25},{25,17},{2,10},{10... | collective-permute-start | bytes 2359304 | tf_op jit(solution)/shard_map/ppermute | solution.py:136
  485.0 41.3 %collective-permute-start.63 = (bf16[192,2048]{1,0:T(8,128)(2,1)}, bf16[192,2048]{1,0:T(8,128)(2,1)}, u32[]{:S(2)}, u32[]{:S(2)}) collective-permute-start(bf16[192,2048]{1,0:T(8,128)(2,1)} %collective-permute-done.49.refs_8_.refs_2_), channel_id=1, source_target_pairs={{0,8},{8,0},{16,24},{24,16},{1,9},{9,1},{17,25},{25,17},{2,10},{10... | collective-permute-start | bytes 2359304 | tf_op jit(solution)/shard_map/ppermute | solution.py:136
  490.7 48.0 %collective-permute-start.68 = (bf16[192,1536]{1,0:T(8,128)(2,1)S(1)}, bf16[192,1536]{1,0:T(8,128)(2,1)S(1)}, u32[]{:S(2)}, u32[]{:S(2)}) collective-permute-start(bf16[192,1536]{1,0:T(8,128)(2,1)S(1)} %fusion.1), channel_id=1, source_target_pairs={{0,8},{8,0},{16,24},{24,16},{1,9},{9,1},{17,25},{25,17},{2,10},{10... | collective-permute-start | bytes 1769480 | tf_op jit(solution)/shard_map/ppermute | solution.py:136
  499.6 35.0 %collective-permute-start.59 = (bf16[128,1536]{1,0:T(8,128)(2,1)S(1)}, bf16[128,1536]{1,0:T(8,128)(2,1)}, u32[]{:S(2)}, u32[]{:S(2)}) collective-permute-start(bf16[128,1536]{1,0:T(8,128)(2,1)S(1)} %copy-done.28), channel_id=1, source_target_pairs={{0,16},{8,24},{16,0},{24,8},{1,17},{9,25},{17,1},{25,9},{2,18},{10... | collective-permute-start | bytes 1179656 | tf_op jit(solution)/shard_map/ppermute | solution.py:136
  500.9 31.0 %collective-permute-start.61 = (bf16[1,192,768]{2,1,0:T(8,128)(2,1)}, bf16[1,192,768]{2,1,0:T(8,128)(2,1)S(1)}, u32[]{:S(2)}, u32[]{:S(2)}) collective-permute-start(bf16[1,192,768]{2,1,0:T(8,128)(2,1)} %get-tuple-element.203.refs_4_), channel_id=1, source_target_pairs={{0,4},{1,5},{2,6},{3,7},{4,0},{5,1},{6,2},{7,3},{8,12},{9,13},{10,... | collective-permute-start | bytes 884744 | tf_op jit(solution)/shard_map/ppermute | solution.py:1044
  509.4 31.5 %collective-permute-start.60 = (bf16[128,1536]{1,0:T(8,128)(2,1)S(1)}, bf16[128,1536]{1,0:T(8,128)(2,1)}, u32[]{:S(2)}, u32[]{:S(2)}) collective-permute-start(bf16[128,1536]{1,0:T(8,128)(2,1)S(1)} %copy-done.30), channel_id=1, source_target_pairs={{0,16},{8,24},{16,0},{24,8},{1,17},{9,25},{17,1},{25,9},{2,18},{10... | collective-permute-start | bytes 1179656 | tf_op jit(solution)/shard_map/ppermute | solution.py:136
  526.2 21.0 %collective-permute-start.52 = (bf16[256,768]{1,0:T(8,128)(2,1)S(1)}, bf16[256,768]{1,0:T(8,128)(2,1)S(1)}, u32[]{:S(2)}, u32[]{:S(2)}) collective-permute-start(bf16[256,768]{1,0:T(8,128)(2,1)S(1)} %copy-done.24), channel_id=1, source_target_pairs={{0,8},{8,0},{16,24},{24,16},{1,9},{9,1},{17,25},{25,17},{2,10},{10... | collective-permute-start | bytes 1179656 | tf_op jit(solution)/shard_map/ppermute | solution.py:136
  538.8 14.9 %collective-permute-start.64 = (bf16[192,768]{1,0:T(8,128)(2,1)}, bf16[192,768]{1,0:T(8,128)(2,1)}, u32[]{:S(2)}, u32[]{:S(2)}) collective-permute-start(bf16[192,768]{1,0:T(8,128)(2,1)} %bitcast.29), channel_id=1, source_target_pairs={{0,8},{8,0},{16,24},{24,16},{1,9},{9,1},{17,25},{25,17},{2,10},{10... | collective-permute-start | bytes 884744 | tf_op jit(solution)/shard_map/ppermute | solution.py:136
  540.1 38.1 %collective-permute-start.69 = (bf16[192,1536]{1,0:T(8,128)(2,1)S(1)}, bf16[192,1536]{1,0:T(8,128)(2,1)S(1)}, u32[]{:S(2)}, u32[]{:S(2)}) collective-permute-start(bf16[192,1536]{1,0:T(8,128)(2,1)S(1)} %add_convert_fusion.2), channel_id=1, source_target_pairs={{0,16},{8,24},{16,0},{24,8},{1,17},{9,25},{17,1},{25,9},{2,18},{10... | collective-permute-start | bytes 1769480 | tf_op jit(solution)/shard_map/ppermute | solution.py:136
  543.2 21.6 %collective-permute-start.56 = (bf16[256,768]{1,0:T(8,128)(2,1)}, bf16[256,768]{1,0:T(8,128)(2,1)S(1)}, u32[]{:S(2)}, u32[]{:S(2)}) collective-permute-start(bf16[256,768]{1,0:T(8,128)(2,1)} %get-tuple-element.205), channel_id=1, source_target_pairs={{0,16},{8,24},{16,0},{24,8},{1,17},{9,25},{17,1},{25,9},{2,18},{10... | collective-permute-start | bytes 1179656 | tf_op jit(solution)/shard_map/ppermute | solution.py:136
  544.8 20.0 %collective-permute-start.57 = (bf16[256,768]{1,0:T(8,128)(2,1)}, bf16[256,768]{1,0:T(8,128)(2,1)S(1)}, u32[]{:S(2)}, u32[]{:S(2)}) collective-permute-start(bf16[256,768]{1,0:T(8,128)(2,1)} %get-tuple-element.207.refs_5_), channel_id=1, source_target_pairs={{0,8},{8,0},{16,24},{24,16},{1,9},{9,1},{17,25},{25,17},{2,10},{10... | collective-permute-start | bytes 1179656 | tf_op jit(solution)/shard_map/ppermute | solution.py:136
  551.8 20.2 %collective-permute-start.65 = (bf16[192,768]{1,0:T(8,128)(2,1)S(1)}, bf16[192,768]{1,0:T(8,128)(2,1)S(1)}, u32[]{:S(2)}, u32[]{:S(2)}) collective-permute-start(bf16[192,768]{1,0:T(8,128)(2,1)S(1)} %bitcast.31), channel_id=1, source_target_pairs={{0,16},{8,24},{16,0},{24,8},{1,17},{9,25},{17,1},{25,9},{2,18},{10... | collective-permute-start | bytes 884744 | tf_op jit(solution)/shard_map/ppermute | solution.py:136
  553.6 21.1 %collective-permute-start.66 = (bf16[192,768]{1,0:T(8,128)(2,1)}, bf16[192,768]{1,0:T(8,128)(2,1)S(1)}, u32[]{:S(2)}, u32[]{:S(2)}) collective-permute-start(bf16[192,768]{1,0:T(8,128)(2,1)} %collective-permute-done.64.refs_2_), channel_id=1, source_target_pairs={{0,16},{8,24},{16,0},{24,8},{1,17},{9,25},{17,1},{25,9},{2,18},{10... | collective-permute-start | bytes 884744 | tf_op jit(solution)/shard_map/ppermute | solution.py:136
  (71 other events, 380.7 us)
Sparse Core Ops, SparseCore 0:
  9.7 42.7 all-gather.5
  54.1 50.7 all-gather.3
  107.1 77.6 all-gather.7
  310.2 68.4 reduce-scatter.2
  381.5 51.3 reduce-scatter.4

commit v3 on v2

--- a/solution.py
+++ b/solution.py
@@ -23,8 +23,10 @@
 BF16 = jnp.bfloat16
 F32 = jnp.float32
 MIB = 1024 * 1024
-VMEM_LIMIT = 60
+VMEM_LIMIT = 64
 COST_SCALE = 20
+WEIGHTS = {"norm_out_back": 2.5, "feed_out": 2.5}
+OPTIONS = (1, 0, 0, 0, 0, 0, 1, 0)
 
 
 def dot(a, b, ca, cb):
@@ -36,8 +38,13 @@
 
 
 def cost(flops, moved, trans=0):
+    return int(flops), int(moved)
+
+
+def weighted(estimate, name):
+    scale = WEIGHTS.get(name, COST_SCALE)
     return pl.CostEstimate(
-        flops=int(flops) * COST_SCALE, bytes_accessed=int(moved) * COST_SCALE, transcendentals=0
+        flops=int(estimate[0] * scale), bytes_accessed=int(estimate[1] * scale), transcendentals=0
     )
 
 
@@ -62,7 +69,7 @@
             scratch_shapes=list(scratch),
         ),
         compiler_params=params(VMEM_LIMIT),
-        cost_estimate=cost_estimate,
+        cost_estimate=weighted(cost_estimate, name),
         name=name,
     )
 
@@ -84,7 +91,7 @@
         in_specs=[hbm] * (count + len(waits)),
         out_specs=[hbm] * count,
         input_output_aliases={at: at for at in range(count)},
-        cost_estimate=cost(0, 0),
+        cost_estimate=weighted(cost(0, 0), "pin"),
         name="pin",
     )(*values, *waits)
     CHAIN.append(out[-1])
@@ -930,13 +937,18 @@
     return total
 
 
+def row_sums(product):
+    sums = jnp.sum(product, axis=1, keepdims=True)
+    return jnp.broadcast_to(sums, (product.shape[0], LANES)).T[:8]
+
+
 def weight_kernel(left_count, right_count, gain, *refs):
     lefts, rights = refs[:left_count], refs[left_count : left_count + right_count]
     rest = refs[left_count + right_count :]
     total = product_of(lefts, rights)
     if gain:
         w_ref, out_ref, gain_ref = rest
-        gain_ref[...] = jnp.sum(total * w_ref[...].astype(F32), axis=1, keepdims=True)
+        gain_ref[...] = row_sums(total * w_ref[...].astype(F32))
     else:
         (out_ref,) = rest
     out_ref[...] = total.astype(BF16)
@@ -951,8 +963,8 @@
     out_specs = [pl.BlockSpec((tile, columns), lambda i: (i, 0))]
     weights = () if weight is None else (weight,)
     if weights:
-        out_shape.append(shape(rows, 1, dtype=F32))
-        out_specs.append(pl.BlockSpec((tile, 1), lambda i: (i, 0)))
+        out_shape.append(shape(8, rows, dtype=F32))
+        out_specs.append(pl.BlockSpec((8, tile), lambda i: (0, i)))
     return call(
         functools.partial(weight_kernel, len(lefts), len(rights), bool(weights)),
         out_shape=out_shape,
@@ -970,9 +982,11 @@
 
 
 def in_weight_kernel(own, shards, left_count, me_ref, *refs):
-    lefts, (*rights, w_ref, near_ref, far_ref, gain_ref) = refs[:left_count], refs[left_count:]
+    lefts, (*rights, w_ref, other_ref, near_ref, far_ref, gain_ref) = refs[:left_count], refs[left_count:]
     total = product_of(lefts, rights)
-    gain_ref[...] = jnp.sum(total * w_ref[...].astype(F32), axis=1, keepdims=True)
+    gain = row_sums(total * w_ref[...].astype(F32))
+    first = lax.broadcasted_iota(jnp.int32, gain.shape, 0) < 4
+    gain_ref[...] = jnp.where(first, gain, other_ref[...])
     total = total.astype(BF16)
     steps = shards.bit_length() - 1
     count = total.shape[0] // own
@@ -992,12 +1006,12 @@
             far_ref[where - shards // 2] = piece
 
 
-def in_weight_grad(me, lefts, rights, weight, own, shards, waits=()):
+def in_weight_grad(me, lefts, rights, weight, other_gain, own, shards, waits=()):
     rows, columns = weight.shape
     tile = math.lcm(own, LANES)
     depth = sum(x.shape[0] for x in lefts)
     half = shape(shards // 2, own, columns)
-    out_shape = (half, half, shape(rows, 1, dtype=F32))
+    out_shape = (half, half, shape(8, rows, dtype=F32))
     return call(
         functools.partial(in_weight_kernel, own, shards, len(lefts)),
         out_shape=out_shape,
@@ -1005,38 +1019,41 @@
         grid=(rows // tile,),
         in_specs=[pl.BlockSpec((x.shape[0], tile), lambda i, _: (0, i)) for x in lefts]
         + [whole(x) for x in rights]
-        + [pl.BlockSpec((tile, columns), lambda i, _: (i, 0))],
-        out_specs=[whole(half), whole(half), pl.BlockSpec((tile, 1), lambda i, _: (i, 0))],
+        + [pl.BlockSpec((tile, columns), lambda i, _: (i, 0)), pl.BlockSpec((8, tile), lambda i, _: (0, i))],
+        out_specs=[whole(half), whole(half), pl.BlockSpec((8, tile), lambda i, _: (0, i))],
         cost_estimate=cost(
             2 * depth * rows * columns, 2 * depth * (rows + columns) + 2 * rows * columns
         ),
         name="in_weight_grad",
         waits=waits,
-    )(me, *lefts, *rights, weight)
+    )(me, *lefts, *rights, weight, other_gain)
 
 
 def add_pairs(left, right):
     return (left.astype(F32) + right.astype(F32)).astype(BF16)
 
 
-def halve_kernel(near_ref, got_ref, *outs):
+def halve_kernel(near_ref, got_ref, gain_ref, gain_got_ref, *rest):
+    outs, gain_out = rest[:-1], rest[-1]
     total = (near_ref[...].astype(F32) + got_ref[...].astype(F32)).astype(BF16)
     cut = total.shape[0] // len(outs)
     for at, out in enumerate(outs):
         out[...] = total[at * cut : (at + 1) * cut]
-
-
-def halve(near, got):
+    gain_out[...] = gain_ref[...] + gain_got_ref[...]
+
+
+def halve(near, got, gain, gain_got, waits=()):
     parts = 2 if near.shape[0] > 1 else 1
-    out_shape = [shape(near.shape[0] // parts, *near.shape[1:])] * parts
+    out_shape = [shape(near.shape[0] // parts, *near.shape[1:])] * parts + [gain]
     return call(
         halve_kernel,
-        out_shape=out_shape,
-        in_specs=[whole(near), whole(got)],
+        out_shape=[shape(*x.shape, dtype=x.dtype) for x in out_shape],
+        in_specs=[whole(x) for x in (near, got, gain, gain_got)],
         out_specs=[whole(x) for x in out_shape],
         cost_estimate=cost(0, 6 * near.size),
         name="halve",
-    )(near, got)
+        waits=waits,
+    )(near, got, gain, gain_got)
 
 
 def across(value, bit):
@@ -1044,23 +1061,57 @@
     return lax.ppermute(value, "fsdp", [(i, i ^ bit) for i in range(size)])
 
 
-def arrange_kernel(order, copies, outs_count, me_ref, *rest):
+def arrange_kernel(copies, every_ref, *outs):
+    for own in range(every_ref.shape[0]):
+        for source, out, target, size in copies:
+            begin = target(own)
+            outs[out][:, begin : begin + size] = every_ref[own, :, source : source + size].astype(F32)
+
+
+def arrange_halves_kernel(order, copies, me_ref, *rest):
+    blocks, (out_ref, held) = rest[:-2], rest[-2:]
+    for at, owner in enumerate(order):
+        held[jnp.bitwise_xor(me_ref[0], owner)] = blocks[at][...]
+    arrange_kernel(copies, held, out_ref)
+
+
+def arrange_halves(me, near, far, bits, copies, width, name):
+    order = order_of(bits)
+    count = len(order) // 2
+    rows, columns = near.shape[0] // count, near.shape[1]
+    tile = rows // 2
+    out_shape = shape(rows, width, dtype=F32)
+
+    def block(at):
+        return pl.BlockSpec((tile, columns), lambda i, _: (2 * at + i, 0))
+
+    return call(
+        functools.partial(arrange_halves_kernel, order, copies),
+        out_shape=out_shape,
+        prefetch=1,
+        grid=(2,),
+        in_specs=[block(at) for _ in range(2) for at in range(count)],
+        out_specs=pl.BlockSpec((tile, width), lambda i, _: (i, 0)),
+        scratch=[pltpu.VMEM((len(order), tile, columns), BF16)],
+        cost_estimate=cost(0, 6 * rows * width),
+        name=name,
+    )(me, *[near] * count, *[far] * count)
+
+
+def arrange_blocks_kernel(order, copies, me_ref, *rest):
     blocks, outs, held = rest[: len(order)], rest[len(order) : -1], rest[-1]
     for at, owner in enumerate(order):
         held[jnp.bitwise_xor(me_ref[0], owner)] = blocks[at][...]
-    for own in range(len(order)):
-        for source, out, target, size in copies:
-            begin = target(own)
-            outs[out][:, begin : begin + size] = held[own, :, source : source + size].astype(F32)
-
-
-def arrange(me, blocks, bits, copies, widths, name):
+    arrange_kernel(copies, held, *outs)
+
+
+def arrange_blocks(me, blocks, bits, copies, widths, name):
     rows, columns = blocks[0].shape
     tile = rows // 2
     order = order_of(bits)
     out_shape = [shape(rows, width, dtype=F32) for width in widths]
     return call(
-        functools.partial(arrange_kernel, order, copies, len(widths)),
+        functools.partial(arrange_blocks_kernel, order, copies),
         out_shape=out_shape,
         prefetch=1,
         grid=(2,),
@@ -1072,26 +1123,61 @@
     )(me, *blocks)
 
 
-def arrange_rows_kernel(order, me_ref, *rest):
-    blocks, out_ref = rest[:-1], rest[-1]
-    rows = blocks[0].shape[0]
-    for at, owner in enumerate(order):
-        begin = pl.multiple_of(jnp.bitwise_xor(me_ref[0], owner) * rows, rows)
-        out_ref[pl.ds(begin, rows), :] = blocks[at][...].astype(F32)
-
-
-def arrange_rows(me, blocks, bits):
-    rows, width = blocks[0].shape
-    out_shape = shape(len(blocks) * rows, width, dtype=F32)
-    return call(
-        functools.partial(arrange_rows_kernel, order_of(bits)),
-        out_shape=out_shape,
-        prefetch=1,
-        in_specs=[whole(x) for x in blocks],
-        out_specs=whole(out_shape),
-        cost_estimate=cost(0, 6 * len(blocks) * rows * width),
-        name="arrange_rows",
-    )(me, *blocks)
+def widen_rows_kernel(every_ref, out_ref):
+    out_ref[...] = every_ref[...].astype(F32)
+
+
+def to_float(value, name, waits=()):
+    rows, width = value.shape
+    tile = rows // 4 if rows % 64 == 0 else rows
+    spec = pl.BlockSpec((tile, width), lambda i: (i, 0))
+    return call(
+        widen_rows_kernel,
+        out_shape=shape(rows, width, dtype=F32),
+        grid=(rows // tile,),
+        in_specs=[spec],
+        out_specs=spec,
+        cost_estimate=cost(0, 6 * value.size),
+        name=name,
+        waits=waits,
+    )(value)
+
+
+def add_kernel(left_ref, right_ref, out_ref):
+    out_ref[...] = left_ref[...].astype(F32) + right_ref[...].astype(F32)
+
+
+def add_float(left, right):
+    rows, width = left.shape
+    tile = rows // 2
+    spec = pl.BlockSpec((tile, width), lambda i: (i, 0))
+    return call(
+        add_kernel,
+        out_shape=shape(rows, width, dtype=F32),
+        grid=(2,),
+        in_specs=[spec, spec],
+        out_specs=spec,
+        cost_estimate=cost(0, 8 * left.size),
+        name="add_float",
+    )(left, right)
+
+
+def gains_kernel(left_ref, right_ref, first_norm, second_norm, first_ref, second_ref):
+    total = left_ref[...] + right_ref[...]
+    first_ref[...] = total[0:1] / first_norm[...]
+    second_ref[...] = total[4:5] / second_norm[...]
+
+
+def finish_gains(left, right, first_norm, second_norm):
+    out_shape = [shape(1, left.shape[1], dtype=F32)] * 2
+    return call(
+        gains_kernel,
+        out_shape=out_shape,
+        in_specs=[whole(x) for x in (left, right, first_norm, second_norm)],
+        out_specs=[whole(x) for x in out_shape],
+        cost_estimate=cost(0, 8 * left.size),
+        name="finish_gains",
+    )(left, right, first_norm, second_norm)
 
 
 def block_out_kernel(count, seqs, *refs):
@@ -1168,46 +1254,30 @@
     )(me, *blocks)
 
 
-def out_weight_kernel(spans, seqs, chips, own, me_ref, shard_ref, *refs):
-    mixed, (*branches, near_ref, far_ref) = refs[: spans * seqs], refs[spans * seqs :]
-    chip, core = shard_ref[0] // 2, shard_ref[0] % 2
+def out_weight_kernel(spans, seqs, me_ref, *refs):
+    mixed, branches, out_ref = refs[: spans * seqs], refs[spans * seqs : -1], refs[-1]
     for at in range(spans):
         total = None
         for seq in range(seqs):
             term = dot(mixed[seq * spans + at][...], branches[seq][...], 0, 0)
             total = term if total is None else total + term
-        total = total.astype(BF16)
-        count = total.shape[0] // own
-        for part in range(count):
-            owner = jnp.bitwise_xor(me_ref[0], at) * count + part
-            back = lax.rem(chip - owner // 2 + chips, chips)
-
-            @pl.when(owner % 2 == core)
-            def _():
-                near_ref[back] = total[part * own : (part + 1) * own]
-
-            @pl.when(owner % 2 != core)
-            def _():
-                far_ref[back] = total[part * own : (part + 1) * own]
-
-
-def out_weight_grad(me, me_shard, mixed, branches, own, shards, waits=()):
+        out_ref[jnp.bitwise_xor(me_ref[0], at)] = total.astype(BF16)
+
+
+def out_weight_grad(me, mixed, branches, waits=()):
     flat = [x for group in mixed for x in group]
     narrow, width = flat[0].shape[1], branches[0].shape[1]
-    out_shape = [shape(shards // 2, own, width)] * 2
-    return call(
-        functools.partial(out_weight_kernel, len(mixed[0]), len(branches), shards // 2, own),
-        out_shape=out_shape,
-        prefetch=2,
+    out_shape = shape(len(mixed[0]), narrow, width)
+    return call(
+        functools.partial(out_weight_kernel, len(mixed[0]), len(branches)),
+        out_shape=out_shape,
+        prefetch=1,
         in_specs=[whole(x) for x in (*flat, *branches)],
-        out_specs=[whole(x) for x in out_shape],
-        cost_estimate=cost(
-            2 * len(flat) * flat[0].size * width,
-            2 * len(mixed[0]) * narrow * width,
-        ),
+        out_specs=whole(out_shape),
+        cost_estimate=cost(2 * len(flat) * flat[0].size * width, 2 * len(mixed[0]) * narrow * width),
         name="out_weight_grad",
         waits=waits,
-    )(me, me_shard, *flat, *branches)
+    )(me, *flat, *branches)
 
 
 def turning_tables(positions):
@@ -1221,16 +1291,6 @@
         jnp.concatenate([cosine, empty, cosine, empty], axis=-1),
         jnp.concatenate([-sine, empty, sine, empty], axis=-1),
     )
-
-
-def sum_all(value):
-    for axis in ("seq", "fsdp"):
-        size = lax.axis_size(axis)
-        bit = 1
-        while bit < size:
-            value = value + lax.ppermute(value, axis, [(i, i ^ bit) for i in range(size)])
-            bit *= 2
-    return value
 
 
 def body(
@@ -1291,6 +1351,8 @@
     in_shard = cut_in(me, joined_input_weight, spans, (query_slab, pair_slab, pair_slab))
     w_in = gather(in_shard)
     w_out = gather(out_projection).reshape(spans, query_slab, width)
+    cot_rows = split_rows(cotangent)
+    cot_got = gather_start(cot_rows, orders)
     normed = norm_rows(tokens, gain_in)
     x_got = gather_start(normed, orders)
     both_shard, down_shard = cut_feed(
@@ -1299,26 +1361,22 @@
     w_both = gather(both_shard)
     down_blocks = [down_shard, around(down_shard)]
 
-    def arrived():
-        down_blocks[-1:] = pin(down_blocks[-1])
-
     def pass_on():
         if len(down_blocks) < chips:
-            arrived()
+            down_blocks[-1:] = pin(down_blocks[-1])
             down_blocks.append(around(down_blocks[-1]))
 
     cosine, sine = turning_tables(positions)
     starts = (jnp.arange(full, dtype=jnp.int32)[None, :] - positions)[:, None, :]
     x_in = gather_end(normed, x_got, orders, "stack_in")
-    arrived()
+    pass_on()
     w_wide = widen(w_in, pad)
-    cot_rows = split_rows(cotangent)
-    cot_got = gather_start(cot_rows, orders)
+    pass_on()
 
     projected, mixed, lse, resid, x_mid = [], [], [], [], []
 
-    def project_rows(q):
-        rows, *normed_mid = project_out(q, me, mixed[q], w_out, tokens, gain_mid, ways)
+    def project_rows(q, waits=()):
+        rows, *normed_mid = project_out(q, me, mixed[q], w_out, tokens, gain_mid, ways, waits)
         resid.append(rows)
         return normed_mid, gather_start(normed_mid, ways)
 
@@ -1330,20 +1388,22 @@
         )
         if q == 0:
             cots = gather_end(cot_rows, cot_got, orders, "stack_cot")
+            pass_on()
         if q == 1:
-            pass_on()
-            started = project_rows(0)
+            started = [project_rows(0, flat(cots) if OPTIONS[0] == 0 else ())]
         heads, sums = attention_forward(me, projected[q], starts[q], place, spans, repeat, step)
         lse.append(sums)
         mixed.append(shared(heads))
-        if q == 1:
-            x_mid.append(gather_end(*started, ways, "stack_mid", flat(cots)))
-    while len(down_blocks) < chips:
-        pass_on()
-    down_near = join(me_shard, down_blocks)
-    down_far = beside(down_near)
+        if q == 0:
+            while len(down_blocks) < chips:
+                pass_on()
+            down_near = join(me_shard, down_blocks)
+            down_far = beside(down_near)
+    x_mid.append(gather_end(*started[0], ways, "stack_mid"))
     for q in both[1:]:
-        x_mid.append(gather_end(*project_rows(q), ways, "stack_mid"))
+        started.append(project_rows(q, (down_far,) if OPTIONS[0] != 1 else (down_far, *flat(cots))))
+    for q in both[1:]:
+        x_mid.append(gather_end(*started[q], ways, "stack_mid"))
 
     hidden, grad_both, grad_mid, x_all = [], [], [], []
     for q in both:
@@ -1376,13 +1436,14 @@
     )
     for q in both[1:]:
         norm_back(q)
-    (down_part,) = weight_grad(hidden, flat(cots), None, "down_grad")
-    down_own = owned(down_part)
-    out_near, out_far = out_weight_grad(me, me_shard, mixed, branches, own_rows, shards)
-    out_got = beside(out_far)
-
-    both_every = copied(both_own, ways[0])
-    down_every = copied(down_own, ways[1])
+    for at in (0, 1) if OPTIONS[5] == 0 else (1, 0):
+        if at == 0:
+            out_part = out_weight_grad(me, mixed, branches).reshape(query_columns, width)
+            out_own = owned(out_part)
+        else:
+            (down_part,) = weight_grad(hidden, flat(cots), None, "down_grad")
+            down_own = owned(down_part)
+
     proj_grads, grad_in = [], []
     for q in both:
         proj_grads.append(
@@ -1399,59 +1460,80 @@
                 pad,
                 repeat,
                 step,
-                () if q == 0 else (both_own,),
             )
         )
         if q == 0:
-            (out_got,) = pin(out_got)
-            out_near = add_pairs(out_near, out_got)
-            out_passing = around(out_near[1])
+            if OPTIONS[4] == 0:
+                outs = scatter_end(*outs, orders)
+            both_every = copied(both_own, ways[0])
         if q == seqs - 1:
             for p in both[:-1]:
                 grad_in[p] = scatter_end(*grad_in[p], ways)
-            (out_passing,) = pin(out_passing)
-            out_passing = around(add_pairs(out_near[2], out_passing))
-            in_near, in_far, gain_first = in_weight_grad(
+            in_near, in_far, in_gain = in_weight_grad(
                 me_shard,
                 flat(x_in),
                 proj_grads,
                 w_in,
+                gain_second,
                 own_rows,
                 shards,
-                both_every[1:2],
+                ((*flat(outs), both_every[1]), flat(outs), (both_every[1],), ())[OPTIONS[3]],
             )
-            in_got = across(in_far, 1)
-        waits = tuple(x for group in head_grads[1:] for x in group[1:]) if q == 0 else ()
-        parts = grad_into_rows(spans, proj_grads[q], orders[q], ways, w_in, tuple(waits))
+            in_got, gain_got = across(in_far, 1), across(in_gain, 1)
+        waits = tuple(x for group in head_grads[1:] for x in group[1:]) if q == 0 else (flat(grad_in[0]) if OPTIONS[2] == 0 else ())
+        parts = grad_into_rows(spans, proj_grads[q], orders[q], ways, w_in, waits)
         grad_in.append(scatter_start(parts, ways))
-        if q == 0:
+        if q == 0 and OPTIONS[4] == 1:
             outs = scatter_end(*outs, orders)
-    in_near, in_sent = halve(in_near, in_got)
-    in_got = across(in_sent, 2)
-    for back in range(3, chips):
-        (out_passing,) = pin(out_passing)
-        out_passing = around(add_pairs(out_near[back], out_passing))
-    gains = sum_all(
-        jnp.stack([gain_first.reshape(width) / norm_first, gain_second.reshape(width) / norm_second])
-    )
-    block_out = finish_block_out(resid, [[pair] for pair in outs])
-    bit = 4
-    while in_near.shape[0] > 1:
-        in_near, in_sent = halve(in_near, in_got)
-        in_got = across(in_sent, bit)
-        bit *= 2
-    out_total = add_pairs(out_near[0], out_passing)
-    grad_in[-1] = scatter_end(*grad_in[-1], ways)
+    (down_own,) = pin(down_own)
+    down_every = lax.all_gather(down_own, "seq", axis=0, tiled=True)
+    in_near, in_sent, in_gain = halve(in_near, in_got, in_gain, gain_got, tuple(both_every) if OPTIONS[1] == 0 else ())
+    in_got, gain_got = across(in_sent, 2), across(in_gain, 2)
     copies = [
         (part * inner + shard * piece, part, lambda own, shard=shard: (shard * spans + own) * piece, piece)
         for part in range(2)
         for shard in range(shards)
     ]
-    gate_grad, up_grad = arrange(me, both_every, ways[0], copies, (FF, FF), "arrange_gate_up")
-    (in_own,) = halve(in_near, in_got)
-    in_own = in_own[0]
-    down_grad = arrange_rows(me, down_every, ways[1])
-    tokens_grad = finish_tokens_grad(tokens, gain_in, grad_resid, grad_in)
+    sums = [out_own]
+
+    def out_start(bit):
+        sums[:] = pin(*sums)
+        total = sums[0] if len(sums) == 1 else add_pairs(*sums)
+        sums[:] = [total, swap(total, bit)]
+
+    if OPTIONS[7] == 0:
+        out_start(0)
+    block_out = finish_block_out(resid, [[pair] for pair in outs])
+    if OPTIONS[6] == 1:
+        grad_in[-1] = scatter_end(*grad_in[-1], ways)
+    bit = 4
+    while in_near.shape[0] > 1:
+        in_near, in_sent, in_gain = halve(in_near, in_got, in_gain, gain_got)
+        in_got, gain_got = across(in_sent, bit), across(in_gain, bit)
+        bit *= 2
+    if OPTIONS[6] == 0:
+        grad_in[-1] = scatter_end(*grad_in[-1], ways)
+    in_own, in_gain = halve(in_near, in_got, in_gain, gain_got)
+    in_every = [in_own[0]]
+    out_start(0 if OPTIONS[7] else 1)
+    for bit in upward:
+        got = [swap(x, bit) for x in in_every]
+        gain_got = swap(in_gain, bit)
+        if bit == 0:
+            tokens_grad = finish_tokens_grad(tokens, gain_in, grad_resid, grad_in)
+        if bit + 1 < len(upward):
+            *got, gain_got = pin(*got, gain_got)
+        in_every = in_every + got
+        if bit + 1 < len(upward):
+            in_gain = in_gain + gain_got
+    for bit in upward[1 if OPTIONS[7] else 2 :]:
+        out_start(bit)
+    if OPTIONS[7] == 0:
+        out_grad = add_float(*sums)
+    gate_grad, up_grad = arrange_blocks(me, both_every, ways[0], copies, (FF, FF), "arrange_gate_up")
+    down_grad = to_float(down_every, "down_to_float")
+    if OPTIONS[7]:
+        out_grad = add_float(*sums)
     copies = [
         (0, 0, lambda own: own * query_slab, query_slab),
         (query_slab, 0, lambda own: query_columns + own * pair_slab, pair_slab),
@@ -1462,17 +1544,15 @@
             pair_slab,
         ),
     ]
-    (in_grad,) = arrange(
+    (in_grad,) = arrange_blocks(
         me,
-        copied(in_own, upward),
+        in_every,
         upward,
         copies,
         (query_columns + 2 * pair_columns,),
         "arrange_in",
     )
-    for bit in upward:
-        out_total = add_pairs(out_total, swap(out_total, bit))
-    out_grad = out_total.astype(F32)
+    first_gain, second_gain = finish_gains(in_gain, gain_got, gain_in, gain_mid)
     return (
         block_out,
         tokens_grad,
@@ -1481,8 +1561,8 @@
         gate_grad,
         up_grad,
         down_grad,
-        gains[0],
-        gains[1],
+        first_gain.reshape(width),
+        second_gain.reshape(width),
     )
 
 

time: 594 us -> 564 us (0.949)
  local copies, waits for them, and re-layouts: 21.5 us -> 5.23 us
  starting transfers between devices: 86.2 us -> 77.6 us
    unnamed x110 -> x4, local copies, waits for them, and re-layouts: 16.1 us -> 0.62 us
    ppermute x3 -> x6, waiting for transfers between devices: 2.57 us -> 14.3 us  [across(): return lax.ppermute(value, 'fsdp', [(i, i ^ bit) for i in range(size)])]
    ppermute x5 -> x0, waiting for transfers between devices: 9.41 us -> none  [sum_all(): lax.ppermute(value, axis, [(i, i ^ bit) for i in range(size)])]
    all_gather x3, waiting for transfers between devices: 7.84 us -> 0.01 us  [gather(): return lax.all_gather(shard, 'fsdp', axis=0, tiled=True)]
    ppermute x5 -> x0, starting transfers between devices: 7.37 us -> none  [sum_all(): lax.ppermute(value, axis, [(i, i ^ bit) for i in range(size)])]
    ppermute x47 -> x46, starting transfers between devices: 54.9 us -> 47.8 us  [swap(): return lax.ppermute(value, 'seq', [(i, i ^ 1 << bit) for i in range(size)])]
    ppermute x6 -> x3, waiting for transfers between devices: 11.9 us -> 6.31 us  [around(): lax.ppermute(value, 'fsdp', [(i, (i + 2) % size) for i in range(size)])]
    pallas_call x42 -> x44, Pallas kernels: 312 us -> 316 us  [made(): out = inner(*args, *waits)]
  transfers between devices with their start and end apart: 80 -> 75, of which waited for: 27 -> 21; matrix products, arithmetic and copies ran while one was open for 4% -> 3% of each run, Pallas kernels for 53% -> 56%
where the time goes in v3:
time: 564 us; the launch traced here: 556 us
  Pallas kernels  316 us (56%)
  waiting for transfers between devices  130 us (23%)
  starting transfers between devices  77.6 us (14%)
  between operations  14.6 us (3%)
  other arithmetic  11.9 us (2%)
    pallas_call x44, Pallas kernels, made(): out = inner(*args, *waits)  316 us
    ppermute x46, waiting for transfers between devices, swap(): return lax.ppermute(value, 'seq', [(i, i ^ 1 << bit) for i in range(size)])  86.8 us
    ppermute x46, starting transfers between devices, swap(): return lax.ppermute(value, 'seq', [(i, i ^ 1 << bit) for i in range(size)])  47.8 us
    ppermute x12, waiting for transfers between devices, exchange(): return lax.ppermute(value, 'seq', [(i, i ^ other) for i in range(size)])  22.1 us
    ppermute x6, waiting for transfers between devices, across(): return lax.ppermute(value, 'fsdp', [(i, i ^ bit) for i in range(size)])  14.3 us
    ppermute x12, starting transfers between devices, exchange(): return lax.ppermute(value, 'seq', [(i, i ^ other) for i in range(size)])  13.9 us
  transfers between devices with their start and end apart: 75, of which 21 were waited for; matrix products, arithmetic and copies ran while one was open for 3% of the time, Pallas kernels for 56%

profile of v3, /device:TPU:0, one launch (start us, length us, event | category | flops | bytes accessed | tf_op | source)
XLA Modules:
  0.0 555.5 jit_solution(5074956664882782572)
XLA Ops:
  7.2 2.1 cut_in.1.refs_1_
  10.1 2.6 split_rows.1
  12.7 3.0 collective-permute-start.6
  18.5 3.1 norm_rows.1
  22.0 3.6 cut_feed.1
  25.6 2.1 collective-permute-start
  30.5 3.7 fusion.2
  36.8 13.7 %collective-permute-done.1.refs_1_ = bf16[256,1536]{1,0:T(8,128)(2,1)} collective-permute-done((bf16[256,1536]{1,0:T(8,128)(2,1)}, bf16[256,1536]{1,0:T(8,128)(2,1)}, u32[]{:S(2)}, u32[]{:S(2)}) %collective-permute-start.1) | collective-permute-done | bytes 786464 | tf_op jit(solution)/shard_map/ppermute | solution.py:143
  51.9 3.6 stack_in.1
  59.1 6.7 %widen.1.refs_1_ = bf16[1536,1024]{1,0:T(8,128)(2,1)} custom-call(bf16[1536,768]{1,0:T(8,128)(2,1)} %all-gather.7.cloned.1.call-done.refs_0_.refs_1_.refs_7_, bf16[768,1024]{1,0:T(8,128)(2,1)} %constant.16.clone.refs_1_.refs_7_, bf16[128,1536]{1,0:T(8,128)(2,1)} %pin.6.refs_2_), custom_call_target="tpu_custom_call" | custom-call | flops 48318382080 | bytes 110100480 | tf_op jit(solution)/shard_map/widen/pallas_call | solution.py:77
  65.8 6.3 %collective-permute-done.5.refs_0_ = bf16[128,1536]{1,0:T(8,128)(2,1)} collective-permute-done((bf16[128,1536]{1,0:T(8,128)(2,1)}, bf16[128,1536]{1,0:T(8,128)(2,1)}, u32[]{:S(2)}, u32[]{:S(2)}) %collective-permute-start.5) | collective-permute-done | bytes 393248 | tf_op jit(solution)/shard_map/ppermute | solution.py:157
  72.1 6.4 %collective-permute-start.11 = (bf16[128,1536]{1,0:T(8,128)(2,1)}, bf16[128,1536]{1,0:T(8,128)(2,1)}, u32[]{:S(2)}, u32[]{:S(2)}) collective-permute-start(bf16[128,1536]{1,0:T(8,128)(2,1)} %pin.7.refs_8_.refs_3_), channel_id=1, source_target_pairs={{0,2},{1,3},{2,4},{3,5},{4,6},{5,7},{6,0},{7,1},{8,10},{9,11},{10,... | collective-permute-start | bytes 1179656 | tf_op jit(solution)/shard_map/ppermute | solution.py:157
  78.5 13.9 %collective-permute-done.3.refs_5_.refs_2_ = bf16[512,1536]{1,0:T(8,128)(2,1)} collective-permute-done((bf16[512,1536]{1,0:T(8,128)(2,1)}, bf16[512,1536]{1,0:T(8,128)(2,1)}, u32[]{:S(2)}, u32[]{:S(2)}) %collective-permute-start.3) | collective-permute-done | bytes 1572896 | tf_op jit(solution)/shard_map/ppermute | solution.py:143
  92.4 8.2 %project_in.2.refs_4_.refs_1_ = bf16[1024,1024]{1,0:T(8,128)(2,1)} custom-call(s32[1]{0:T(128)} %bitcast.refs_0_, bf16[1536,1024]{1,0:T(8,128)(2,1)} %widen.1.refs_1_, f32[1024,128]{1,0:T(8,128)} %get-tuple-element.240.refs_2_.refs_5_, f32[1024,128]{1,0:T(8,128)} %get-tuple-element.228.refs_3_.refs_6_, bf16[512,1536]{1,0:T(8,128)(2,1)} %get-tuple-element.123.refs_4_.refs_1_, ...), custom_call_target="tpu_custom_call" | custom-call | flops 64424509440 | bytes 167772160 | tf_op jit(solution)/shard_map/project_in/pallas_call | solution.py:77
  100.6 3.6 stack_cot.1
  105.6 9.9 %attention_forward.2 = (bf16[256,384]{1,0:T(8,128)(2,1)}, bf16[256,384]{1,0:T(8,128)(2,1)}, bf16[256,384]{1,0:T(8,128)(2,1)}, bf16[256,384]{1,0:T(8,128)(2,1)}, f32[2,4,512]{2,1,0:T(4,128)}) custom-call(s32[1]{0:T(128)} %bitcast.refs_0_, bf16[1024,1024]{1,0:T(8,128)(2,1)} %project_in.2.refs_4_.refs_1_, s32[1,1024]{1,0:T(1,128)} %get-tuple-element.237.refs_2_, ...), custom_call_target="tpu_custom_call" | custom-call | flops 42949672960 | bytes 83886080 | tf_op jit(solution)/shard_map/attention_forward/pallas_call | solution.py:77
  120.5 2.6 join.1.refs_6_.refs_2_.refs_1_
  123.2 8.8 %project_in.3.refs_8_.refs_1_ = bf16[1024,1024]{1,0:T(8,128)(2,1)} custom-call(s32[1]{0:T(128)} %bitcast.refs_0_, bf16[1536,1024]{1,0:T(8,128)(2,1)} %widen.1.refs_1_, f32[1024,128]{1,0:T(8,128)} %get-tuple-element.241.refs_2_.refs_5_, f32[1024,128]{1,0:T(8,128)} %get-tuple-element.227.refs_3_.refs_6_, ...), custom_call_target="tpu_custom_call" | custom-call | flops 64424509440 | bytes 167772160 | tf_op jit(solution)/shard_map/project_in/pallas_call | solution.py:77
  132.0 14.5 %collective-permute-done.9.refs_6_.refs_3_ = bf16[256,384]{1,0:T(8,128)(2,1)} collective-permute-done((bf16[256,384]{1,0:T(8,128)(2,1)}, bf16[256,384]{1,0:T(8,128)(2,1)}, u32[]{:S(2)}, u32[]{:S(2)}) %collective-permute-start.9) | collective-permute-done | bytes 196640 | tf_op jit(solution)/shard_map/ppermute | solution.py:148
  146.5 6.0 %project_out.2 = (f32[256,1536]{1,0:T(8,128)}, bf16[256,768]{1,0:T(8,128)(2,1)}, bf16[256,768]{1,0:T(8,128)(2,1)}) custom-call(s32[1]{0:T(128)} %bitcast.refs_0_, bf16[4,384,1536]{2,1,0:T(8,128)(2,1)} %bitcast.13, bf16[2,256,1536]{2,1,0:T(8,128)(2,1)} %refs_0_.5, f32[1,1536]{1,0:T(1,128)} %broadcast_in_dim.20.refs_3_, ...), custom_call_target="tpu_custom_call" | custom-call | flops 24159191040 | bytes 173015040 | tf_op jit(solution)/shard_map/project_out/pallas_call | solution.py:77
  155.3 10.2 %attention_forward.3 = (bf16[256,384]{1,0:T(8,128)(2,1)}, bf16[256,384]{1,0:T(8,128)(2,1)}, bf16[256,384]{1,0:T(8,128)(2,1)}, bf16[256,384]{1,0:T(8,128)(2,1)}, f32[2,4,512]{2,1,0:T(4,128)}) custom-call(s32[1]{0:T(128)} %bitcast.refs_0_, bf16[1024,1024]{1,0:T(8,128)(2,1)} %project_in.3.refs_8_.refs_1_, s32[1,1024]{1,0:T(1,128)} %get-tuple-element.236.refs_2_, ...), custom_call_target="tpu_custom_call" | custom-call | flops 42949672960 | bytes 83886080 | tf_op jit(solution)/shard_map/attention_forward/pallas_call | solution.py:77
  168.3 2.1 collective-permute-start.20
  170.4 2.5 stack_mid.2
  176.2 1.9 collective-permute-done.20.refs_7_.refs_8_
  178.1 5.9 %project_out.3 = (f32[256,1536]{1,0:T(8,128)}, bf16[256,768]{1,0:T(8,128)(2,1)}, bf16[256,768]{1,0:T(8,128)(2,1)}) custom-call(s32[1]{0:T(128)} %bitcast.refs_0_, bf16[4,384,1536]{2,1,0:T(8,128)(2,1)} %bitcast.14, bf16[2,256,1536]{2,1,0:T(8,128)(2,1)} %refs_0_.5, f32[1,1536]{1,0:T(1,128)} %broadcast_in_dim.20.refs_3_, ...), custom_call_target="tpu_custom_call" | custom-call | flops 24159191040 | bytes 173015040 | tf_op jit(solution)/shard_map/project_out/pallas_call | solution.py:77
  186.0 14.3 %collective-permute-done.22.refs_1_ = bf16[256,768]{1,0:T(8,128)(2,1)} collective-permute-done((bf16[256,768]{1,0:T(8,128)(2,1)}, bf16[256,768]{1,0:T(8,128)(2,1)}, u32[]{:S(2)}, u32[]{:S(2)}) %collective-permute-start.22) | collective-permute-done | bytes 393248 | tf_op jit(solution)/shard_map/ppermute | solution.py:143
  200.3 2.6 stack_mid.3
  205.4 25.4 %feed_forward.2 = (bf16[1024,1024]{1,0:T(8,128)(2,1)}, bf16[1024,2048]{1,0:T(8,128)(2,1)}, bf16[1024,1536]{1,0:T(8,128)(2,1)}, bf16[512,768]{1,0:T(8,128)(2,1)},...) custom-call(s32[1]{0:T(128)} %bitcast.6.refs_0_, ...), custom_call_target="tpu_custom_call" | custom-call | flops 322122547200 | bytes 503316480 | tf_op jit(solution)/shard_map/feed_forward/pallas_call | solution.py:77
  232.4 25.2 %feed_forward.3 = (bf16[1024,1024]{1,0:T(8,128)(2,1)}, bf16[1024,2048]{1,0:T(8,128)(2,1)}, bf16[1024,1536]{1,0:T(8,128)(2,1)}, bf16[512,768]{1,0:T(8,128)(2,1)},...) custom-call(s32[1]{0:T(128)} %bitcast.6.refs_0_, ...), custom_call_target="tpu_custom_call" | custom-call | flops 322122547200 | bytes 503316480 | tf_op jit(solution)/shard_map/feed_forward/pallas_call | solution.py:77
  260.2 3.4 fold.5
  265.1 20.5 %gate_up_grad.1 = (bf16[1536,2048]{1,0:T(8,128)(2,1)}, f32[8,1536]{1,0:T(8,128)}) custom-call(bf16[1024,1536]{1,0:T(8,128)(2,1)} %get-tuple-element.158.refs_0_, bf16[1024,1536]{1,0:T(8,128)(2,1)} %get-tuple-element.159.refs_1_, bf16[1024,2048]{1,0:T(8,128)(2,1)} %get-tuple-element.160.refs_2_, bf16[1024,2048]{1,0:T(8,128)(2,1)} %get-tuple-element.161.refs_3_, ...), custom_call_target="tpu_custom_call" | custom-call | flops 257698037760 | bytes 419430400 | tf_op jit(solution)/shard_map/gate_up_grad/pallas_call | solution.py:77
  285.6 6.8 %norm_out_back.2 = (f32[256,1536]{1,0:T(8,128)}, bf16[256,1536]{1,0:T(8,128)(2,1)}, bf16[256,384]{1,0:T(8,128)(2,1)}, bf16[256,384]{1,0:T(8,128)(2,1)}, bf16[256...) custom-call(s32[1]{0:T(128)} %bitcast.refs_0_, f32[256,1536]{1,0:T(8,128)} %get-tuple-element.131.refs_1_.refs_0_, ...), custom_call_target="tpu_custom_call" | custom-call | flops 3019898880 | bytes 27525120 | tf_op jit(solution)/shard_map/norm_out_back/pallas_call | solution.py:77
  296.0 3.3 fold.6
  301.8 1.9 collective-permute-done.31.refs_6_.refs_10_
  304.3 12.8 %feed_out.1 = (bf16[512,1536]{1,0:T(8,128)(2,1)}, bf16[512,1536]{1,0:T(8,128)(2,1)}, bf16[512,1536]{1,0:T(8,128)(2,1)}, bf16[512,1536]{1,0:T(8,128)(2,1)}) custom-call(s32[1]{0:T(128)} %bitcast.6.refs_0_, bf16[4,128,1536]{2,1,0:T(8,128)(2,1)} %join.1.refs_6_.refs_2_.refs_1_, bf16[4,128,1536]{2,1,0:T(8,128)(2,1)} %collective-permute-done.12.refs_8_.refs_3_.refs_2_, ...), custom_call_target="tpu_custom_call" | custom-call | flops 16106127360 | bytes 34078720 | tf_op jit(solution)/shard_map/feed_out/pallas_call | solution.py:77
  317.1 6.9 %norm_out_back.3 = (f32[256,1536]{1,0:T(8,128)}, bf16[256,1536]{1,0:T(8,128)(2,1)}, bf16[256,384]{1,0:T(8,128)(2,1)}, bf16[256,384]{1,0:T(8,128)(2,1)}, bf16[256...) custom-call(s32[1]{0:T(128)} %bitcast.refs_0_, f32[256,1536]{1,0:T(8,128)} %get-tuple-element.176.refs_1_.refs_3_, ...), custom_call_target="tpu_custom_call" | custom-call | flops 3019898880 | bytes 27525120 | tf_op jit(solution)/shard_map/norm_out_back/pallas_call | solution.py:77
  324.0 6.8 %out_weight_grad.1.refs_6_ = bf16[4,384,1536]{2,1,0:T(8,128)(2,1)} custom-call(s32[1]{0:T(128)} %bitcast.refs_0_, bf16[256,384]{1,0:T(8,128)(2,1)} %get-tuple-element.126.refs_4_.refs_1_, bf16[256,384]{1,0:T(8,128)(2,1)} %collective-permute-done.8.refs_5_.refs_2_, bf16[256,384]{1,0:T(8,128)(2,1)} %collective-permute-done.9.refs_6_.refs_3_, ...), custom_call_target="tpu_custom_call" | custom-call | flops 48318382080 | bytes 94371840 | tf_op jit(solution)/shard_map/out_weight_grad/pallas_call | solution.py:77
  330.8 11.5 %down_grad.1.refs_12_ = bf16[1024,1536]{1,0:T(8,128)(2,1)} custom-call(bf16[1024,1024]{1,0:T(8,128)(2,1)} %get-tuple-element.146.refs_3_.refs_0_, bf16[1024,1024]{1,0:T(8,128)(2,1)} %get-tuple-element.149.refs_4_.refs_1_, bf16[512,1536]{1,0:T(8,128)(2,1)} %get-tuple-element.133.refs_9_.refs_4_.refs_2_, ...), custom_call_target="tpu_custom_call" | custom-call | flops 128849018880 | bytes 272629760 | tf_op jit(solution)/shard_map/down_grad/pallas_call | solution.py:77
  348.2 20.5 %attention_backward.2.refs_4_.refs_0_.refs_5_ = bf16[1024,768]{1,0:T(8,128)(2,1)} custom-call(s32[1]{0:T(128)} %bitcast.refs_0_, bf16[1024,1024]{1,0:T(8,128)(2,1)} %project_in.2.refs_4_.refs_1_, s32[1,1024]{1,0:T(1,128)} %get-tuple-element.237.refs_2_, bf16[2,256,384]{2,1,0:T(8,128)(2,1)} %constant.17.clone.refs_3_, ...), custom_call_target="tpu_custom_call" | custom-call | flops 107374182400 | bytes 167772160 | tf_op jit(solution)/shard_map/attention_backward/pallas_call | solution.py:77
  368.7 12.0 %collective-permute-done.35.refs_2_ = bf16[512,1536]{1,0:T(8,128)(2,1)} collective-permute-done((bf16[512,1536]{1,0:T(8,128)(2,1)}, bf16[512,1536]{1,0:T(8,128)(2,1)}, u32[]{:S(2)}, u32[]{:S(2)}) %collective-permute-start.35) | collective-permute-done | bytes 1572896 | tf_op jit(solution)/shard_map/ppermute | solution.py:143
  380.7 5.3 fold.7
  389.1 7.0 %grad_into_rows.2 = (bf16[512,768]{1,0:T(8,128)(2,1)}, bf16[512,768]{1,0:T(8,128)(2,1)}, bf16[512,768]{1,0:T(8,128)(2,1)}, bf16[512,768]{1,0:T(8,128)(2,1)}) custom-call(bf16[1024,768]{1,0:T(8,128)(2,1)} %attention_backward.2.refs_4_.refs_0_.refs_5_, bf16[1536,768]{1,0:T(8,128)(2,1)} %all-gather.7.cloned.1.call-done.refs_0_.refs_1_.refs_7_, ...), custom_call_target="tpu_custom_call" | custom-call | flops 48318382080 | bytes 141557760 | tf_op jit(solution)/shard_map/grad_into_rows/pallas_call | solution.py:77
  399.1 20.6 %attention_backward.3.refs_4_.refs_6_.refs_0_ = bf16[1024,768]{1,0:T(8,128)(2,1)} custom-call(s32[1]{0:T(128)} %bitcast.refs_0_, bf16[1024,1024]{1,0:T(8,128)(2,1)} %project_in.3.refs_8_.refs_1_, s32[1,1024]{1,0:T(1,128)} %get-tuple-element.236.refs_2_, bf16[2,256,384]{2,1,0:T(8,128)(2,1)} %constant.17.clone.refs_3_, ...), custom_call_target="tpu_custom_call" | custom-call | flops 107374182400 | bytes 167772160 | tf_op jit(solution)/shard_map/attention_backward/pallas_call | solution.py:77
  419.7 3.9 collective-permute-done.46.refs_3_
  423.6 3.4 fold.8
  429.5 4.2 collective-permute-done.44.refs_13_.refs_5_.refs_2_
  433.7 11.1 %in_weight_grad.1 = (bf16[4,192,768]{2,1,0:T(8,128)(2,1)}, bf16[4,192,768]{2,1,0:T(8,128)(2,1)}, f32[8,1536]{1,0:T(8,128)}) custom-call(s32[1]{0:T(128)} %bitcast.6.refs_0_, bf16[512,1536]{1,0:T(8,128)(2,1)} %get-tuple-element.123.refs_4_.refs_1_, bf16[512,1536]{1,0:T(8,128)(2,1)} %collective-permute-done.3.refs_5_.refs_2_, ...), custom_call_target="tpu_custom_call" | custom-call | flops 96636764160 | bytes 235929600 | tf_op jit(solution)/shard_map/in_weight_grad/pallas_call | solution.py:77
  445.8 7.2 %grad_into_rows.3 = (bf16[512,768]{1,0:T(8,128)(2,1)}, bf16[512,768]{1,0:T(8,128)(2,1)}, bf16[512,768]{1,0:T(8,128)(2,1)}, bf16[512,768]{1,0:T(8,128)(2,1)}) custom-call(bf16[1024,768]{1,0:T(8,128)(2,1)} %attention_backward.3.refs_4_.refs_6_.refs_0_, bf16[1536,768]{1,0:T(8,128)(2,1)} %all-gather.7.cloned.1.call-done.refs_0_.refs_1_.refs_7_, ...), custom_call_target="tpu_custom_call" | custom-call | flops 48318382080 | bytes 141557760 | tf_op jit(solution)/shard_map/grad_into_rows/pallas_call | solution.py:77
  457.3 8.3 %collective-permute-done.50.refs_7_.refs_4_ = bf16[192,2048]{1,0:T(8,128)(2,1)} collective-permute-done((bf16[192,2048]{1,0:T(8,128)(2,1)}, bf16[192,2048]{1,0:T(8,128)(2,1)}, u32[]{:S(2)}, u32[]{:S(2)}) %collective-permute-start.50) | collective-permute-done | bytes 786464 | tf_op jit(solution)/shard_map/ppermute | solution.py:143
  465.6 2.8 halve.3
  471.3 4.8 finish_block_out.1.refs_4_
  476.1 10.6 %collective-permute-done.53.refs_2_ = bf16[512,768]{1,0:T(8,128)(2,1)} collective-permute-done((bf16[512,768]{1,0:T(8,128)(2,1)}, bf16[512,768]{1,0:T(8,128)(2,1)}, u32[]{:S(2)}, u32[]{:S(2)}) %collective-permute-start.53) | collective-permute-done | bytes 786464 | tf_op jit(solution)/shard_map/ppermute | solution.py:143
  486.7 3.6 fold.9
  490.3 2.1 halve.4
  492.4 2.7 collective-permute-start.60
  496.9 13.1 %collective-permute-done.61.refs_3_ = f32[8,1536]{1,0:T(8,128)} collective-permute-done((f32[8,1536]{1,0:T(8,128)}, f32[8,1536]{1,0:T(8,128)}, u32[]{:S(2)}, u32[]{:S(2)}) %collective-permute-start.61) | collective-permute-done | bytes 49184 | tf_op jit(solution)/shard_map/ppermute | solution.py:1061
  510.0 1.9 halve.5
  511.9 2.2 add_convert_fusion.refs_0_
  518.1 6.4 %finish_tokens_grad.1.refs_2_ = bf16[2,256,1536]{2,1,0:T(8,128)(2,1)} custom-call(bf16[2,256,1536]{2,1,0:T(8,128)(2,1)} %refs_0_.5, f32[1,1536]{1,0:T(1,128)} %broadcast_in_dim.21.refs_1_.refs_2_, f32[256,1536]{1,0:T(8,128)} %get-tuple-element.203.refs_2_, f32[256,768]{1,0:T(8,128)} %get-tuple-element.198.refs_2_.refs_3_, ...), custom_call_target="tpu_custom_call" | custom-call | bytes 188743680 | tf_op jit(solution)/shard_map/finish_tokens_grad/pallas_call | solution.py:77
  528.0 2.6 collective-permute-done.66.refs_1_
  530.7 2.1 add_float.1.refs_5_
  532.8 4.5 arrange_gate_up.1
  537.3 3.9 down_to_float.1.refs_5_
  541.6 2.7 arrange_in.1.refs_4_
  (160 shorter events, 83.1 us)
Async XLA Ops:
  7.2 51.9 %all-gather.7.cloned.1.call-start = ((), (), s32[]{:S(2)}) async-start(), calls=%async_computation.4 | async-start | bytes 2654208 | tf_op jit(solution)/shard_map/all_gather | solution.py:1335
  9.3 137.2 %all-gather.5.cloned.1.call-start = ((), (), s32[]{:S(2)}) async-start(), calls=%async_computation.3 | async-start | bytes 5308416 | tf_op jit(solution)/shard_map/all_gather | solution.py:1335
  10.1 195.3 %all-gather.9.cloned.1.call-start = ((), (), s32[]{:S(2)}) async-start(), calls=%async_computation.5 | async-start | bytes 7077888 | tf_op jit(solution)/shard_map/all_gather | solution.py:1335
  12.7 87.8 %collective-permute-start.6 = (bf16[256,1536]{1,0:T(8,128)(2,1)}, bf16[256,1536]{1,0:T(8,128)(2,1)}, u32[]{:S(2)}, u32[]{:S(2)}) collective-permute-start(bf16[256,1536]{1,0:T(8,128)(2,1)} %get-tuple-element.124.refs_0_), channel_id=1, source_target_pairs={{0,16},{8,24},{16,0},{24,8},{1,17},{9,25},{17,1},{25,9},{2,18},{10... | collective-permute-start | bytes 2359304 | tf_op jit(solution)/shard_map/ppermute | solution.py:143
  15.7 84.9 %collective-permute-start.7 = (bf16[256,1536]{1,0:T(8,128)(2,1)}, bf16[256,1536]{1,0:T(8,128)(2,1)}, u32[]{:S(2)}, u32[]{:S(2)}) collective-permute-start(bf16[256,1536]{1,0:T(8,128)(2,1)} %get-tuple-element.118.refs_2_), channel_id=1, source_target_pairs={{0,8},{8,0},{16,24},{24,16},{1,9},{9,1},{17,25},{25,17},{2,10},{10... | collective-permute-start | bytes 2359304 | tf_op jit(solution)/shard_map/ppermute | solution.py:143
  21.6 28.9 %collective-permute-start.1 = (bf16[256,1536]{1,0:T(8,128)(2,1)}, bf16[256,1536]{1,0:T(8,128)(2,1)}, u32[]{:S(2)}, u32[]{:S(2)}) collective-permute-start(bf16[256,1536]{1,0:T(8,128)(2,1)} %get-tuple-element.121.refs_0_), channel_id=1, source_target_pairs={{0,16},{8,24},{16,0},{24,8},{1,17},{9,25},{17,1},{25,9},{2,18},{10... | collective-permute-start | bytes 2359304 | tf_op jit(solution)/shard_map/ppermute | solution.py:143
  22.0 29.9 %collective-permute-start.2 = (bf16[256,1536]{1,0:T(8,128)(2,1)}, bf16[256,1536]{1,0:T(8,128)(2,1)}, u32[]{:S(2)}, u32[]{:S(2)}) collective-permute-start(bf16[256,1536]{1,0:T(8,128)(2,1)} %get-tuple-element.119.refs_4_.refs_2_), channel_id=1, source_target_pairs={{0,8},{8,0},{16,24},{24,16},{1,9},{9,1},{17,25},{25,17},{2,10},{10... | collective-permute-start | bytes 2359304 | tf_op jit(solution)/shard_map/ppermute | solution.py:143
  25.6 30.2 %collective-permute-start = (bf16[128,1536]{1,0:T(8,128)(2,1)}, bf16[128,1536]{1,0:T(8,128)(2,1)}, u32[]{:S(2)}, u32[]{:S(2)}) collective-permute-start(bf16[128,1536]{1,0:T(8,128)(2,1)} %get-tuple-element.120.refs_4_.refs_1_), channel_id=1, source_target_pairs={{0,2},{1,3},{2,4},{3,5},{4,6},{5,7},{6,0},{7,1},{8,10},{9,11},{10,... | collective-permute-start | bytes 1179656 | tf_op jit(solution)/shard_map/ppermute | solution.py:157
  27.7 370.3 %reduce-scatter.6.cloned.1.call-start = ((), (), s32[]{:S(2)}) async-start(), calls=%async_computation.7 | async-start | bytes 7077888 | tf_op jit(solution)/shard_map/reduce_scatter | solution.py:1338
  55.5 36.9 %collective-permute-start.4 = (bf16[512,1536]{1,0:T(8,128)(2,1)}, bf16[512,1536]{1,0:T(8,128)(2,1)}, u32[]{:S(2)}, u32[]{:S(2)}) collective-permute-start(bf16[512,1536]{1,0:T(8,128)(2,1)} %get-tuple-element.122.refs_1_.refs_6_.refs_4_.refs_3_), channel_id=1, source_target_pairs={{0,16},{8,24},{16,0},{24,8},{1,17},{9,25},{17,1},{25,9},{2,18},{10... | collective-permute-start | bytes 4718600 | tf_op jit(solution)/shard_map/ppermute | solution.py:143
  55.8 16.3 %collective-permute-start.5 = (bf16[128,1536]{1,0:T(8,128)(2,1)}, bf16[128,1536]{1,0:T(8,128)(2,1)}, u32[]{:S(2)}, u32[]{:S(2)}) collective-permute-start(bf16[128,1536]{1,0:T(8,128)(2,1)} %pin.6.refs_2_), channel_id=1, source_target_pairs={{0,2},{1,3},{2,4},{3,5},{4,6},{5,7},{6,0},{7,1},{8,10},{9,11},{10,... | collective-permute-start | bytes 1179656 | tf_op jit(solution)/shard_map/ppermute | solution.py:157
  57.6 34.8 %collective-permute-start.3 = (bf16[512,1536]{1,0:T(8,128)(2,1)}, bf16[512,1536]{1,0:T(8,128)(2,1)}, u32[]{:S(2)}, u32[]{:S(2)}) collective-permute-start(bf16[512,1536]{1,0:T(8,128)(2,1)} %get-tuple-element.123.refs_4_.refs_1_), channel_id=1, source_target_pairs={{0,8},{8,0},{16,24},{24,16},{1,9},{9,1},{17,25},{25,17},{2,10},{10... | collective-permute-start | bytes 4718600 | tf_op jit(solution)/shard_map/ppermute | solution.py:143
  72.1 47.0 %collective-permute-start.11 = (bf16[128,1536]{1,0:T(8,128)(2,1)}, bf16[128,1536]{1,0:T(8,128)(2,1)}, u32[]{:S(2)}, u32[]{:S(2)}) collective-permute-start(bf16[128,1536]{1,0:T(8,128)(2,1)} %pin.7.refs_8_.refs_3_), channel_id=1, source_target_pairs={{0,2},{1,3},{2,4},{3,5},{4,6},{5,7},{6,0},{7,1},{8,10},{9,11},{10,... | collective-permute-start | bytes 1179656 | tf_op jit(solution)/shard_map/ppermute | solution.py:157
  104.2 68.7 %collective-permute-start.21 = (bf16[512,1536]{1,0:T(8,128)(2,1)}, bf16[512,1536]{1,0:T(8,128)(2,1)}, u32[]{:S(2)}, u32[]{:S(2)}) collective-permute-start(bf16[512,1536]{1,0:T(8,128)(2,1)} %get-tuple-element.125.refs_4_.refs_11_), channel_id=1, source_target_pairs={{0,16},{8,24},{16,0},{24,8},{1,17},{9,25},{17,1},{25,9},{2,18},{10... | collective-permute-start | bytes 4718600 | tf_op jit(solution)/shard_map/ppermute | solution.py:143
  115.5 16.5 %collective-permute-start.8 = (bf16[256,384]{1,0:T(8,128)(2,1)}, bf16[256,384]{1,0:T(8,128)(2,1)}, u32[]{:S(2)}, u32[]{:S(2)}) collective-permute-start(bf16[256,384]{1,0:T(8,128)(2,1)} %get-tuple-element.127), channel_id=1, source_target_pairs={{0,8},{8,0},{16,24},{24,16},{1,9},{9,1},{17,25},{25,17},{2,10},{10... | collective-permute-start | bytes 589832 | tf_op jit(solution)/shard_map/ppermute | solution.py:148
  117.0 29.5 %collective-permute-start.9 = (bf16[256,384]{1,0:T(8,128)(2,1)}, bf16[256,384]{1,0:T(8,128)(2,1)}, u32[]{:S(2)}, u32[]{:S(2)}) collective-permute-start(bf16[256,384]{1,0:T(8,128)(2,1)} %get-tuple-element.128), channel_id=1, source_target_pairs={{0,16},{8,24},{16,0},{24,8},{1,17},{9,25},{17,1},{25,9},{2,18},{10... | collective-permute-start | bytes 589832 | tf_op jit(solution)/shard_map/ppermute | solution.py:148
  117.7 28.8 %collective-permute-start.10 = (bf16[256,384]{1,0:T(8,128)(2,1)}, bf16[256,384]{1,0:T(8,128)(2,1)}, u32[]{:S(2)}, u32[]{:S(2)}) collective-permute-start(bf16[256,384]{1,0:T(8,128)(2,1)} %get-tuple-element.129), channel_id=1, source_target_pairs={{0,24},{8,16},{16,8},{24,0},{1,25},{9,17},{17,9},{25,1},{2,26},{10... | collective-permute-start | bytes 589832 | tf_op jit(solution)/shard_map/ppermute | solution.py:148
  119.1 46.5 %collective-permute-start.13 = (bf16[512,1536]{1,0:T(8,128)(2,1)}, bf16[512,1536]{1,0:T(8,128)(2,1)}, u32[]{:S(2)}, u32[]{:S(2)}) collective-permute-start(bf16[512,1536]{1,0:T(8,128)(2,1)} %get-tuple-element.133.refs_9_.refs_4_.refs_2_), channel_id=1, source_target_pairs={{0,8},{8,0},{16,24},{24,16},{1,9},{9,1},{17,25},{25,17},{2,10},{10... | collective-permute-start | bytes 4718600 | tf_op jit(solution)/shard_map/ppermute | solution.py:143
  132.0 41.1 %collective-permute-start.12 = (bf16[4,128,1536]{2,1,0:T(8,128)(2,1)}, bf16[4,128,1536]{2,1,0:T(8,128)(2,1)}, u32[]{:S(2)}, u32[]{:S(2)}) collective-permute-start(bf16[4,128,1536]{2,1,0:T(8,128)(2,1)} %join.1.refs_6_.refs_2_.refs_1_), channel_id=1, source_target_pairs={{0,1},{1,0},{2,3},{3,2},{4,5},{5,4},{6,7},{7,6},{8,9},{9,8},{10,11... | collective-permute-start | bytes 4718600 | tf_op jit(solution)/shard_map/ppermute | solution.py:162
  172.9 32.5 %collective-permute-start.16 = (bf16[512,768]{1,0:T(8,128)(2,1)}, bf16[512,768]{1,0:T(8,128)(2,1)}, u32[]{:S(2)}, u32[]{:S(2)}) collective-permute-start(bf16[512,768]{1,0:T(8,128)(2,1)} %get-tuple-element.137.refs_6_), channel_id=1, source_target_pairs={{0,8},{8,0},{16,24},{24,16},{1,9},{9,1},{17,25},{25,17},{2,10},{10... | collective-permute-start | bytes 2359304 | tf_op jit(solution)/shard_map/ppermute | solution.py:143
  173.1 32.3 %collective-permute-start.17 = (bf16[512,768]{1,0:T(8,128)(2,1)}, bf16[512,768]{1,0:T(8,128)(2,1)}, u32[]{:S(2)}, u32[]{:S(2)}) collective-permute-start(bf16[512,768]{1,0:T(8,128)(2,1)} %get-tuple-element.138.refs_13_.refs_8_), channel_id=1, source_target_pairs={{0,16},{8,24},{16,0},{24,8},{1,17},{9,25},{17,1},{25,9},{2,18},{10... | collective-permute-start | bytes 2359304 | tf_op jit(solution)/shard_map/ppermute | solution.py:143
  184.1 16.2 %collective-permute-start.22 = (bf16[256,768]{1,0:T(8,128)(2,1)}, bf16[256,768]{1,0:T(8,128)(2,1)}, u32[]{:S(2)}, u32[]{:S(2)}) collective-permute-start(bf16[256,768]{1,0:T(8,128)(2,1)} %get-tuple-element.143.refs_0_), channel_id=1, source_target_pairs={{0,16},{8,24},{16,0},{24,8},{1,17},{9,25},{17,1},{25,9},{2,18},{10... | collective-permute-start | bytes 1179656 | tf_op jit(solution)/shard_map/ppermute | solution.py:143
  185.3 14.9 %collective-permute-start.23 = (bf16[256,768]{1,0:T(8,128)(2,1)}, bf16[256,768]{1,0:T(8,128)(2,1)}, u32[]{:S(2)}, u32[]{:S(2)}) collective-permute-start(bf16[256,768]{1,0:T(8,128)(2,1)} %get-tuple-element.144.refs_2_.refs_4_), channel_id=1, source_target_pairs={{0,8},{8,0},{16,24},{24,16},{1,9},{9,1},{17,25},{25,17},{2,10},{10... | collective-permute-start | bytes 1179656 | tf_op jit(solution)/shard_map/ppermute | solution.py:143
  202.9 29.5 %collective-permute-start.24 = (bf16[512,768]{1,0:T(8,128)(2,1)}, bf16[512,768]{1,0:T(8,128)(2,1)}, u32[]{:S(2)}, u32[]{:S(2)}) collective-permute-start(bf16[512,768]{1,0:T(8,128)(2,1)} %get-tuple-element.147.refs_6_), channel_id=1, source_target_pairs={{0,8},{8,0},{16,24},{24,16},{1,9},{9,1},{17,25},{25,17},{2,10},{10... | collective-permute-start | bytes 2359304 | tf_op jit(solution)/shard_map/ppermute | solution.py:143
  204.3 28.0 %collective-permute-start.25 = (bf16[512,768]{1,0:T(8,128)(2,1)}, bf16[512,768]{1,0:T(8,128)(2,1)}, u32[]{:S(2)}, u32[]{:S(2)}) collective-permute-start(bf16[512,768]{1,0:T(8,128)(2,1)} %get-tuple-element.145.refs_10_.refs_8_), channel_id=1, source_target_pairs={{0,16},{8,24},{16,0},{24,8},{1,17},{9,25},{17,1},{25,9},{2,18},{10... | collective-permute-start | bytes 2359304 | tf_op jit(solution)/shard_map/ppermute | solution.py:143
  230.8 29.4 %collective-permute-start.26 = (bf16[512,768]{1,0:T(8,128)(2,1)}, bf16[512,768]{1,0:T(8,128)(2,1)}, u32[]{:S(2)}, u32[]{:S(2)}) collective-permute-start(bf16[512,768]{1,0:T(8,128)(2,1)} %get-tuple-element.152), channel_id=1, source_target_pairs={{0,8},{8,0},{16,24},{24,16},{1,9},{9,1},{17,25},{25,17},{2,10},{10... | collective-permute-start | bytes 2359304 | tf_op jit(solution)/shard_map/ppermute | solution.py:143
  231.5 28.6 %collective-permute-start.27 = (bf16[512,768]{1,0:T(8,128)(2,1)}, bf16[512,768]{1,0:T(8,128)(2,1)}, u32[]{:S(2)}, u32[]{:S(2)}) collective-permute-start(bf16[512,768]{1,0:T(8,128)(2,1)} %get-tuple-element.148.refs_10_), channel_id=1, source_target_pairs={{0,16},{8,24},{16,0},{24,8},{1,17},{9,25},{17,1},{25,9},{2,18},{10... | collective-permute-start | bytes 2359304 | tf_op jit(solution)/shard_map/ppermute | solution.py:143
  257.5 38.4 %collective-permute-start.33 = (bf16[512,768]{1,0:T(8,128)(2,1)}, bf16[512,768]{1,0:T(8,128)(2,1)}, u32[]{:S(2)}, u32[]{:S(2)}) collective-permute-start(bf16[512,768]{1,0:T(8,128)(2,1)} %get-tuple-element.168), channel_id=1, source_target_pairs={{0,8},{8,0},{16,24},{24,16},{1,9},{9,1},{17,25},{25,17},{2,10},{10... | collective-permute-start | bytes 2359304 | tf_op jit(solution)/shard_map/ppermute | solution.py:143
  259.1 36.9 %collective-permute-start.34 = (bf16[512,768]{1,0:T(8,128)(2,1)}, bf16[512,768]{1,0:T(8,128)(2,1)}, u32[]{:S(2)}, u32[]{:S(2)}) collective-permute-start(bf16[512,768]{1,0:T(8,128)(2,1)} %get-tuple-element.153.refs_4_), channel_id=1, source_target_pairs={{0,16},{8,24},{16,0},{24,8},{1,17},{9,25},{17,1},{25,9},{2,18},{10... | collective-permute-start | bytes 2359304 | tf_op jit(solution)/shard_map/ppermute | solution.py:143
  263.6 22.0 %collective-permute-start.28 = (bf16[256,768]{1,0:T(8,128)(2,1)}, bf16[256,768]{1,0:T(8,128)(2,1)}, u32[]{:S(2)}, u32[]{:S(2)}) collective-permute-start(bf16[256,768]{1,0:T(8,128)(2,1)} %get-tuple-element.155), channel_id=1, source_target_pairs={{0,16},{8,24},{16,0},{24,8},{1,17},{9,25},{17,1},{25,9},{2,18},{10... | collective-permute-start | bytes 1179656 | tf_op jit(solution)/shard_map/ppermute | solution.py:143
  264.5 21.0 %collective-permute-start.29 = (bf16[256,768]{1,0:T(8,128)(2,1)}, bf16[256,768]{1,0:T(8,128)(2,1)}, u32[]{:S(2)}, u32[]{:S(2)}) collective-permute-start(bf16[256,768]{1,0:T(8,128)(2,1)} %get-tuple-element.157.refs_5_), channel_id=1, source_target_pairs={{0,8},{8,0},{16,24},{24,16},{1,9},{9,1},{17,25},{25,17},{2,10},{10... | collective-permute-start | bytes 1179656 | tf_op jit(solution)/shard_map/ppermute | solution.py:143
  295.9 157.2 %reduce-scatter.8.cloned.1.call-start = ((), (), s32[]{:S(2)}) async-start(), calls=%async_computation.8 | async-start | bytes 3538944 | tf_op jit(solution)/shard_map/reduce_scatter | solution.py:1338
  299.3 17.8 %collective-permute-start.37 = (bf16[256,768]{1,0:T(8,128)(2,1)}, bf16[256,768]{1,0:T(8,128)(2,1)}, u32[]{:S(2)}, u32[]{:S(2)}) collective-permute-start(bf16[256,768]{1,0:T(8,128)(2,1)} %get-tuple-element.178), channel_id=1, source_target_pairs={{0,16},{8,24},{16,0},{24,8},{1,17},{9,25},{17,1},{25,9},{2,18},{10... | collective-permute-start | bytes 1179656 | tf_op jit(solution)/shard_map/ppermute | solution.py:143
  300.5 16.7 %collective-permute-start.38 = (bf16[256,768]{1,0:T(8,128)(2,1)}, bf16[256,768]{1,0:T(8,128)(2,1)}, u32[]{:S(2)}, u32[]{:S(2)}) collective-permute-start(bf16[256,768]{1,0:T(8,128)(2,1)} %get-tuple-element.169.refs_8_), channel_id=1, source_target_pairs={{0,8},{8,0},{16,24},{24,16},{1,9},{9,1},{17,25},{25,17},{2,10},{10... | collective-permute-start | bytes 1179656 | tf_op jit(solution)/shard_map/ppermute | solution.py:143
  342.3 127.8 %reduce-scatter.4.cloned.1.call-start = ((), (), s32[]{:S(2)}) async-start(), calls=%async_computation.6 | async-start | bytes 5308416 | tf_op jit(solution)/shard_map/reduce_scatter | solution.py:1338
  342.4 38.3 %collective-permute-start.36 = (bf16[512,1536]{1,0:T(8,128)(2,1)}, bf16[512,1536]{1,0:T(8,128)(2,1)}, u32[]{:S(2)}, u32[]{:S(2)}) collective-permute-start(bf16[512,1536]{1,0:T(8,128)(2,1)} %get-tuple-element.173.refs_9_), channel_id=1, source_target_pairs={{0,16},{8,24},{16,0},{24,8},{1,17},{9,25},{17,1},{25,9},{2,18},{10... | collective-permute-start | bytes 4718600 | tf_op jit(solution)/shard_map/ppermute | solution.py:143
  343.3 37.3 %collective-permute-start.35 = (bf16[512,1536]{1,0:T(8,128)(2,1)}, bf16[512,1536]{1,0:T(8,128)(2,1)}, u32[]{:S(2)}, u32[]{:S(2)}) collective-permute-start(bf16[512,1536]{1,0:T(8,128)(2,1)} %get-tuple-element.172), channel_id=1, source_target_pairs={{0,8},{8,0},{16,24},{24,16},{1,9},{9,1},{17,25},{25,17},{2,10},{10... | collective-permute-start | bytes 4718600 | tf_op jit(solution)/shard_map/ppermute | solution.py:143
  344.6 44.5 %collective-permute-start.43 = (bf16[256,384]{1,0:T(8,128)(2,1)}, bf16[256,384]{1,0:T(8,128)(2,1)}, u32[]{:S(2)}, u32[]{:S(2)}) collective-permute-start(bf16[256,384]{1,0:T(8,128)(2,1)} %get-tuple-element.181.refs_11_), channel_id=1, source_target_pairs={{0,24},{8,16},{16,8},{24,0},{1,25},{9,17},{17,9},{25,1},{2,26},{10... | collective-permute-start | bytes 589832 | tf_op jit(solution)/shard_map/ppermute | solution.py:148
  345.9 43.2 %collective-permute-start.41 = (bf16[256,384]{1,0:T(8,128)(2,1)}, bf16[256,384]{1,0:T(8,128)(2,1)}, u32[]{:S(2)}, u32[]{:S(2)}) collective-permute-start(bf16[256,384]{1,0:T(8,128)(2,1)} %get-tuple-element.187), channel_id=1, source_target_pairs={{0,8},{8,0},{16,24},{24,16},{1,9},{9,1},{17,25},{25,17},{2,10},{10... | collective-permute-start | bytes 589832 | tf_op jit(solution)/shard_map/ppermute | solution.py:148
  347.2 41.9 %collective-permute-start.42 = (bf16[256,384]{1,0:T(8,128)(2,1)}, bf16[256,384]{1,0:T(8,128)(2,1)}, u32[]{:S(2)}, u32[]{:S(2)}) collective-permute-start(bf16[256,384]{1,0:T(8,128)(2,1)} %get-tuple-element.188), channel_id=1, source_target_pairs={{0,16},{8,24},{16,0},{24,8},{1,17},{9,25},{17,1},{25,9},{2,18},{10... | collective-permute-start | bytes 589832 | tf_op jit(solution)/shard_map/ppermute | solution.py:148
  348.1 189.2 %all-gather.11.cloned.1.call-start = ((), (), s32[]{:S(2)}) async-start(), calls=%async_computation.9 | async-start | bytes 1966080 | tf_op jit(solution)/shard_map/all_gather | solution.py:1489
  385.9 42.9 %collective-permute-start.39 = (bf16[256,1536]{1,0:T(8,128)(2,1)}, bf16[256,1536]{1,0:T(8,128)(2,1)}, u32[]{:S(2)}, u32[]{:S(2)}) collective-permute-start(bf16[256,1536]{1,0:T(8,128)(2,1)} %get-tuple-element.183), channel_id=1, source_target_pairs={{0,16},{8,24},{16,0},{24,8},{1,17},{9,25},{17,1},{25,9},{2,18},{10... | collective-permute-start | bytes 2359304 | tf_op jit(solution)/shard_map/ppermute | solution.py:143
  386.4 43.1 %collective-permute-start.40 = (bf16[256,1536]{1,0:T(8,128)(2,1)}, bf16[256,1536]{1,0:T(8,128)(2,1)}, u32[]{:S(2)}, u32[]{:S(2)}) collective-permute-start(bf16[256,1536]{1,0:T(8,128)(2,1)} %get-tuple-element.185.refs_5_), channel_id=1, source_target_pairs={{0,8},{8,0},{16,24},{24,16},{1,9},{9,1},{17,25},{25,17},{2,10},{10... | collective-permute-start | bytes 2359304 | tf_op jit(solution)/shard_map/ppermute | solution.py:143
  396.1 23.6 %collective-permute-start.45 = (bf16[512,768]{1,0:T(8,128)(2,1)}, bf16[512,768]{1,0:T(8,128)(2,1)}, u32[]{:S(2)}, u32[]{:S(2)}) collective-permute-start(bf16[512,768]{1,0:T(8,128)(2,1)} %get-tuple-element.193), channel_id=1, source_target_pairs={{0,8},{8,0},{16,24},{24,16},{1,9},{9,1},{17,25},{25,17},{2,10},{10... | collective-permute-start | bytes 2359304 | tf_op jit(solution)/shard_map/ppermute | solution.py:143
  397.1 26.5 %collective-permute-start.46 = (bf16[512,768]{1,0:T(8,128)(2,1)}, bf16[512,768]{1,0:T(8,128)(2,1)}, u32[]{:S(2)}, u32[]{:S(2)}) collective-permute-start(bf16[512,768]{1,0:T(8,128)(2,1)} %get-tuple-element.189.refs_12_), channel_id=1, source_target_pairs={{0,16},{8,24},{16,0},{24,8},{1,17},{9,25},{17,1},{25,9},{2,18},{10... | collective-permute-start | bytes 2359304 | tf_op jit(solution)/shard_map/ppermute | solution.py:143
  398.0 35.7 %collective-permute-start.44 = (bf16[192,2048]{1,0:T(8,128)(2,1)}, bf16[192,2048]{1,0:T(8,128)(2,1)}, u32[]{:S(2)}, u32[]{:S(2)}) collective-permute-start(bf16[192,2048]{1,0:T(8,128)(2,1)} %reduce-scatter.6.cloned.1.call-done.refs_4_.refs_1_), channel_id=1, source_target_pairs={{0,16},{8,24},{16,0},{24,8},{1,17},{9,25},{17,1},{25,9},{2,18},{10... | collective-permute-start | bytes 2359304 | tf_op jit(solution)/shard_map/ppermute | solution.py:143
  427.0 18.9 %collective-permute-start.51 = (bf16[256,768]{1,0:T(8,128)(2,1)}, bf16[256,768]{1,0:T(8,128)(2,1)}, u32[]{:S(2)}, u32[]{:S(2)}) collective-permute-start(bf16[256,768]{1,0:T(8,128)(2,1)} %get-tuple-element.199), channel_id=1, source_target_pairs={{0,16},{8,24},{16,0},{24,8},{1,17},{9,25},{17,1},{25,9},{2,18},{10... | collective-permute-start | bytes 1179656 | tf_op jit(solution)/shard_map/ppermute | solution.py:143
  427.4 18.4 %collective-permute-start.52 = (bf16[256,768]{1,0:T(8,128)(2,1)}, bf16[256,768]{1,0:T(8,128)(2,1)}, u32[]{:S(2)}, u32[]{:S(2)}) collective-permute-start(bf16[256,768]{1,0:T(8,128)(2,1)} %get-tuple-element.194.refs_14_), channel_id=1, source_target_pairs={{0,8},{8,0},{16,24},{24,16},{1,9},{9,1},{17,25},{25,17},{2,10},{10... | collective-permute-start | bytes 1179656 | tf_op jit(solution)/shard_map/ppermute | solution.py:143
  428.9 26.6 %collective-permute-start.49 = (bf16[192,2048]{1,0:T(8,128)(2,1)}, bf16[192,2048]{1,0:T(8,128)(2,1)}, u32[]{:S(2)}, u32[]{:S(2)}) collective-permute-start(bf16[192,2048]{1,0:T(8,128)(2,1)} %reduce-scatter.6.cloned.1.call-done.refs_4_.refs_1_), channel_id=1, source_target_pairs={{0,8},{8,0},{16,24},{24,16},{1,9},{9,1},{17,25},{25,17},{2,10},{10... | collective-permute-start | bytes 2359304 | tf_op jit(solution)/shard_map/ppermute | solution.py:143
  444.8 20.8 %collective-permute-start.47 = (bf16[4,192,768]{2,1,0:T(8,128)(2,1)}, bf16[4,192,768]{2,1,0:T(8,128)(2,1)}, u32[]{:S(2)}, u32[]{:S(2)}) collective-permute-start(bf16[4,192,768]{2,1,0:T(8,128)(2,1)} %get-tuple-element.196), channel_id=1, source_target_pairs={{0,1},{1,0},{2,3},{3,2},{4,5},{5,4},{6,7},{7,6},{8,9},{9,8},{10,11... | collective-permute-start | bytes 3538952 | tf_op jit(solution)/shard_map/ppermute | solution.py:1061
  444.9 20.7 %collective-permute-start.50 = (bf16[192,2048]{1,0:T(8,128)(2,1)}, bf16[192,2048]{1,0:T(8,128)(2,1)}, u32[]{:S(2)}, u32[]{:S(2)}) collective-permute-start(bf16[192,2048]{1,0:T(8,128)(2,1)} %collective-permute-done.44.refs_13_.refs_5_.refs_2_), channel_id=1, source_target_pairs={{0,8},{8,0},{16,24},{24,16},{1,9},{9,1},{17,25},{25,17},{2,10},{10... | collective-permute-start | bytes 2359304 | tf_op jit(solution)/shard_map/ppermute | solution.py:143
  453.1 33.6 %collective-permute-start.53 = (bf16[512,768]{1,0:T(8,128)(2,1)}, bf16[512,768]{1,0:T(8,128)(2,1)}, u32[]{:S(2)}, u32[]{:S(2)}) collective-permute-start(bf16[512,768]{1,0:T(8,128)(2,1)} %get-tuple-element.207), channel_id=1, source_target_pairs={{0,8},{8,0},{16,24},{24,16},{1,9},{9,1},{17,25},{25,17},{2,10},{10... | collective-permute-start | bytes 2359304 | tf_op jit(solution)/shard_map/ppermute | solution.py:143
  454.3 32.3 %collective-permute-start.54 = (bf16[512,768]{1,0:T(8,128)(2,1)}, bf16[512,768]{1,0:T(8,128)(2,1)}, u32[]{:S(2)}, u32[]{:S(2)}) collective-permute-start(bf16[512,768]{1,0:T(8,128)(2,1)} %get-tuple-element.201.refs_1_), channel_id=1, source_target_pairs={{0,16},{8,24},{16,0},{24,8},{1,17},{9,25},{17,1},{25,9},{2,18},{10... | collective-permute-start | bytes 2359304 | tf_op jit(solution)/shard_map/ppermute | solution.py:143
  468.4 21.9 %collective-permute-start.58 = (bf16[2,192,768]{2,1,0:T(8,128)(2,1)}, bf16[2,192,768]{2,1,0:T(8,128)(2,1)}, u32[]{:S(2)}, u32[]{:S(2)}) collective-permute-start(bf16[2,192,768]{2,1,0:T(8,128)(2,1)} %get-tuple-element.213), channel_id=1, source_target_pairs={{0,2},{1,3},{2,0},{3,1},{4,6},{5,7},{6,4},{7,5},{8,10},{9,11},{10,... | collective-permute-start | bytes 1769480 | tf_op jit(solution)/shard_map/ppermute | solution.py:1061
  470.2 41.7 %collective-permute-start.57 = (bf16[192,1536]{1,0:T(8,128)(2,1)}, bf16[192,1536]{1,0:T(8,128)(2,1)}, u32[]{:S(2)}, u32[]{:S(2)}) collective-permute-start(bf16[192,1536]{1,0:T(8,128)(2,1)} %pin.9.refs_6_.refs_0_), channel_id=1, source_target_pairs={{0,8},{8,0},{16,24},{24,16},{1,9},{9,1},{17,25},{25,17},{2,10},{10... | collective-permute-start | bytes 1769480 | tf_op jit(solution)/shard_map/ppermute | solution.py:143
  470.8 19.5 %collective-permute-start.59 = (f32[8,1536]{1,0:T(8,128)}, f32[8,1536]{1,0:T(8,128)}, u32[]{:S(2)}, u32[]{:S(2)}) collective-permute-start(f32[8,1536]{1,0:T(8,128)} %get-tuple-element.202.refs_1_.refs_2_), channel_id=1, source_target_pairs={{0,2},{1,3},{2,0},{3,1},{4,6},{5,7},{6,4},{7,5},{8,10},{9,11},{10,... | collective-permute-start | bytes 147464 | tf_op jit(solution)/shard_map/ppermute | solution.py:1061
  492.4 17.6 %collective-permute-start.60 = (bf16[1,192,768]{2,1,0:T(8,128)(2,1)}, bf16[1,192,768]{2,1,0:T(8,128)(2,1)}, u32[]{:S(2)}, u32[]{:S(2)}) collective-permute-start(bf16[1,192,768]{2,1,0:T(8,128)(2,1)} %get-tuple-element.215), channel_id=1, source_target_pairs={{0,4},{1,5},{2,6},{3,7},{4,0},{5,1},{6,2},{7,3},{8,12},{9,13},{10,... | collective-permute-start | bytes 884744 | tf_op jit(solution)/shard_map/ppermute | solution.py:1061
  495.2 14.9 %collective-permute-start.61 = (f32[8,1536]{1,0:T(8,128)}, f32[8,1536]{1,0:T(8,128)}, u32[]{:S(2)}, u32[]{:S(2)}) collective-permute-start(f32[8,1536]{1,0:T(8,128)} %get-tuple-element.216.refs_2_.refs_4_), channel_id=1, source_target_pairs={{0,4},{1,5},{2,6},{3,7},{4,0},{5,1},{6,2},{7,3},{8,12},{9,13},{10,... | collective-permute-start | bytes 147464 | tf_op jit(solution)/shard_map/ppermute | solution.py:1061
  495.3 22.8 %collective-permute-start.56 = (bf16[256,768]{1,0:T(8,128)(2,1)}, bf16[256,768]{1,0:T(8,128)(2,1)}, u32[]{:S(2)}, u32[]{:S(2)}) collective-permute-start(bf16[256,768]{1,0:T(8,128)(2,1)} %get-tuple-element.211.refs_4_), channel_id=1, source_target_pairs={{0,8},{8,0},{16,24},{24,16},{1,9},{9,1},{17,25},{25,17},{2,10},{10... | collective-permute-start | bytes 1179656 | tf_op jit(solution)/shard_map/ppermute | solution.py:143
  495.9 21.2 %collective-permute-start.55 = (bf16[256,768]{1,0:T(8,128)(2,1)}, bf16[256,768]{1,0:T(8,128)(2,1)}, u32[]{:S(2)}, u32[]{:S(2)}) collective-permute-start(bf16[256,768]{1,0:T(8,128)(2,1)} %get-tuple-element.209), channel_id=1, source_target_pairs={{0,16},{8,24},{16,0},{24,8},{1,17},{9,25},{17,1},{25,9},{2,18},{10... | collective-permute-start | bytes 1179656 | tf_op jit(solution)/shard_map/ppermute | solution.py:143
  514.1 16.6 %collective-permute-start.66 = (bf16[192,1536]{1,0:T(8,128)(2,1)}, bf16[192,1536]{1,0:T(8,128)(2,1)}, u32[]{:S(2)}, u32[]{:S(2)}) collective-permute-start(bf16[192,1536]{1,0:T(8,128)(2,1)} %add_convert_fusion.refs_0_), channel_id=1, source_target_pairs={{0,16},{8,24},{16,0},{24,8},{1,17},{9,25},{17,1},{25,9},{2,18},{10... | collective-permute-start | bytes 1769480 | tf_op jit(solution)/shard_map/ppermute | solution.py:143
  517.1 24.1 %collective-permute-start.64 = (bf16[192,768]{1,0:T(8,128)(2,1)}, bf16[192,768]{1,0:T(8,128)(2,1)}, u32[]{:S(2)}, u32[]{:S(2)}) collective-permute-start(bf16[192,768]{1,0:T(8,128)(2,1)} %bitcast.8.refs_1_), channel_id=1, source_target_pairs={{0,16},{8,24},{16,0},{24,8},{1,17},{9,25},{17,1},{25,9},{2,18},{10... | collective-permute-start | bytes 884744 | tf_op jit(solution)/shard_map/ppermute | solution.py:143
  524.5 17.1 %collective-permute-start.65 = (bf16[192,768]{1,0:T(8,128)(2,1)}, bf16[192,768]{1,0:T(8,128)(2,1)}, u32[]{:S(2)}, u32[]{:S(2)}) collective-permute-start(bf16[192,768]{1,0:T(8,128)(2,1)} %get-tuple-element.220.refs_2_), channel_id=1, source_target_pairs={{0,16},{8,24},{16,0},{24,8},{1,17},{9,25},{17,1},{25,9},{2,18},{10... | collective-permute-start | bytes 884744 | tf_op jit(solution)/shard_map/ppermute | solution.py:143
  527.0 17.3 %collective-permute-start.67 = (f32[8,1536]{1,0:T(8,128)}, f32[8,1536]{1,0:T(8,128)}, u32[]{:S(2)}, u32[]{:S(2)}) collective-permute-start(f32[8,1536]{1,0:T(8,128)} %add.13.refs_0_), channel_id=1, source_target_pairs={{0,16},{8,24},{16,0},{24,8},{1,17},{9,25},{17,1},{25,9},{2,18},{10... | collective-permute-start | bytes 147464 | tf_op jit(solution)/shard_map/ppermute | solution.py:143
  (13 other events, 107.9 us)
Sparse Core Ops, SparseCore 0:
  9.6 42.6 all-gather.6
  54.0 61.6 all-gather.4
  117.3 63.8 all-gather.8
  296.0 69.5 reduce-scatter.5
  368.3 38.6 reduce-scatter.7
  409.2 54.0 reduce-scatter.3
  465.2 42.0 all-gather.10

commit v4 on v3

--- a/solution.py
+++ b/solution.py
@@ -26,7 +26,6 @@
 VMEM_LIMIT = 64
 COST_SCALE = 20
 WEIGHTS = {"norm_out_back": 2.5, "feed_out": 2.5}
-OPTIONS = (1, 0, 0, 0, 0, 0, 1, 0)
 
 
 def dot(a, b, ca, cb):
@@ -1390,7 +1389,7 @@
             cots = gather_end(cot_rows, cot_got, orders, "stack_cot")
             pass_on()
         if q == 1:
-            started = [project_rows(0, flat(cots) if OPTIONS[0] == 0 else ())]
+            started = [project_rows(0)]
         heads, sums = attention_forward(me, projected[q], starts[q], place, spans, repeat, step)
         lse.append(sums)
         mixed.append(shared(heads))
@@ -1401,7 +1400,7 @@
             down_far = beside(down_near)
     x_mid.append(gather_end(*started[0], ways, "stack_mid"))
     for q in both[1:]:
-        started.append(project_rows(q, (down_far,) if OPTIONS[0] != 1 else (down_far, *flat(cots))))
+        started.append(project_rows(q, (down_far, *flat(cots))))
     for q in both[1:]:
         x_mid.append(gather_end(*started[q], ways, "stack_mid"))
 
@@ -1436,13 +1435,10 @@
     )
     for q in both[1:]:
         norm_back(q)
-    for at in (0, 1) if OPTIONS[5] == 0 else (1, 0):
-        if at == 0:
-            out_part = out_weight_grad(me, mixed, branches).reshape(query_columns, width)
-            out_own = owned(out_part)
-        else:
-            (down_part,) = weight_grad(hidden, flat(cots), None, "down_grad")
-            down_own = owned(down_part)
+    (down_part,) = weight_grad(hidden, flat(cots), None, "down_grad")
+    down_own = owned(down_part)
+    out_part = out_weight_grad(me, mixed, branches).reshape(query_columns, width)
+    out_own = owned(out_part)
 
     proj_grads, grad_in = [], []
     for q in both:
@@ -1463,8 +1459,7 @@
             )
         )
         if q == 0:
-            if OPTIONS[4] == 0:
-                outs = scatter_end(*outs, orders)
+            outs = scatter_end(*outs, orders)
             both_every = copied(both_own, ways[0])
         if q == seqs - 1:
             for p in both[:-1]:
@@ -1477,17 +1472,15 @@
                 gain_second,
                 own_rows,
                 shards,
-                ((*flat(outs), both_every[1]), flat(outs), (both_every[1],), ())[OPTIONS[3]],
+                (*flat(outs), both_every[1]),
             )
             in_got, gain_got = across(in_far, 1), across(in_gain, 1)
-        waits = tuple(x for group in head_grads[1:] for x in group[1:]) if q == 0 else (flat(grad_in[0]) if OPTIONS[2] == 0 else ())
+        waits = tuple(x for group in head_grads[1:] for x in group[1:]) if q == 0 else flat(grad_in[0])
         parts = grad_into_rows(spans, proj_grads[q], orders[q], ways, w_in, waits)
         grad_in.append(scatter_start(parts, ways))
-        if q == 0 and OPTIONS[4] == 1:
-            outs = scatter_end(*outs, orders)
     (down_own,) = pin(down_own)
     down_every = lax.all_gather(down_own, "seq", axis=0, tiled=True)
-    in_near, in_sent, in_gain = halve(in_near, in_got, in_gain, gain_got, tuple(both_every) if OPTIONS[1] == 0 else ())
+    in_near, in_sent, in_gain = halve(in_near, in_got, in_gain, gain_got, tuple(both_every))
     in_got, gain_got = across(in_sent, 2), across(in_gain, 2)
     copies = [
         (part * inner + shard * piece, part, lambda own, shard=shard: (shard * spans + own) * piece, piece)
@@ -1501,21 +1494,17 @@
         total = sums[0] if len(sums) == 1 else add_pairs(*sums)
         sums[:] = [total, swap(total, bit)]
 
-    if OPTIONS[7] == 0:
-        out_start(0)
+    out_start(0)
     block_out = finish_block_out(resid, [[pair] for pair in outs])
-    if OPTIONS[6] == 1:
-        grad_in[-1] = scatter_end(*grad_in[-1], ways)
+    grad_in[-1] = scatter_end(*grad_in[-1], ways)
     bit = 4
     while in_near.shape[0] > 1:
         in_near, in_sent, in_gain = halve(in_near, in_got, in_gain, gain_got)
         in_got, gain_got = across(in_sent, bit), across(in_gain, bit)
         bit *= 2
-    if OPTIONS[6] == 0:
-        grad_in[-1] = scatter_end(*grad_in[-1], ways)
     in_own, in_gain = halve(in_near, in_got, in_gain, gain_got)
     in_every = [in_own[0]]
-    out_start(0 if OPTIONS[7] else 1)
+    out_start(1)
     for bit in upward:
         got = [swap(x, bit) for x in in_every]
         gain_got = swap(in_gain, bit)
@@ -1526,14 +1515,11 @@
         in_every = in_every + got
         if bit + 1 < len(upward):
             in_gain = in_gain + gain_got
-    for bit in upward[1 if OPTIONS[7] else 2 :]:
+    for bit in upward[2:]:
         out_start(bit)
-    if OPTIONS[7] == 0:
-        out_grad = add_float(*sums)
+    out_grad = add_float(*sums)
     gate_grad, up_grad = arrange_blocks(me, both_every, ways[0], copies, (FF, FF), "arrange_gate_up")
     down_grad = to_float(down_every, "down_to_float")
-    if OPTIONS[7]:
-        out_grad = add_float(*sums)
     copies = [
         (0, 0, lambda own: own * query_slab, query_slab),
         (query_slab, 0, lambda own: query_columns + own * pair_slab, pair_slab),

time: 564 us -> 554 us (0.982)
  waiting for transfers between devices: 130 us -> 122 us
    ppermute x46, waiting for transfers between devices: 86.8 us -> 78.1 us  [swap(): return lax.ppermute(value, 'seq', [(i, i ^ 1 << bit) for i in range(size)])]
  transfers between devices with their start and end apart: 75 -> 75, of which waited for: 21 -> 23; matrix products, arithmetic and copies ran while one was open for 3% -> 3% of each run, Pallas kernels for 56% -> 57%
where the time goes in v4:
time: 554 us; the launch traced here: 546 us
  Pallas kernels  316 us (57%)
  waiting for transfers between devices  122 us (22%)
  starting transfers between devices  75.4 us (14%)
  between operations  14.6 us (3%)
  other arithmetic  11.9 us (2%)
    pallas_call x44, Pallas kernels, made(): out = inner(*args, *waits)  316 us
    ppermute x46, waiting for transfers between devices, swap(): return lax.ppermute(value, 'seq', [(i, i ^ 1 << bit) for i in range(size)])  78.1 us
    ppermute x46, starting transfers between devices, swap(): return lax.ppermute(value, 'seq', [(i, i ^ 1 << bit) for i in range(size)])  45.8 us
    ppermute x12, waiting for transfers between devices, exchange(): return lax.ppermute(value, 'seq', [(i, i ^ other) for i in range(size)])  23.1 us
    ppermute x6, waiting for transfers between devices, across(): return lax.ppermute(value, 'fsdp', [(i, i ^ bit) for i in range(size)])  14.1 us
    ppermute x12, starting transfers between devices, exchange(): return lax.ppermute(value, 'seq', [(i, i ^ other) for i in range(size)])  13.9 us
  transfers between devices with their start and end apart: 75, of which 23 were waited for; matrix products, arithmetic and copies ran while one was open for 3% of the time, Pallas kernels for 57%

profile of v4, /device:TPU:0, one launch (start us, length us, event | category | flops | bytes accessed | tf_op | source)
XLA Modules:
  0.0 545.7 jit_solution(14233692507304432295)
XLA Ops:
  7.2 2.1 cut_in.1.refs_1_
  10.2 2.6 split_rows.1
  12.8 3.0 collective-permute-start.6
  18.5 3.1 norm_rows.1
  22.0 3.6 cut_feed.1
  25.6 2.1 collective-permute-start
  30.5 3.7 fusion.2
  36.8 13.6 %collective-permute-done.1.refs_1_ = bf16[256,1536]{1,0:T(8,128)(2,1)} collective-permute-done((bf16[256,1536]{1,0:T(8,128)(2,1)}, bf16[256,1536]{1,0:T(8,128)(2,1)}, u32[]{:S(2)}, u32[]{:S(2)}) %collective-permute-start.1) | collective-permute-done | bytes 786464 | tf_op jit(solution)/shard_map/ppermute | solution.py:142
  51.9 3.6 stack_in.1
  59.1 6.7 %widen.1.refs_1_ = bf16[1536,1024]{1,0:T(8,128)(2,1)} custom-call(bf16[1536,768]{1,0:T(8,128)(2,1)} %all-gather.7.cloned.1.call-done.refs_0_.refs_1_.refs_7_, bf16[768,1024]{1,0:T(8,128)(2,1)} %constant.16.clone.refs_1_.refs_7_, bf16[128,1536]{1,0:T(8,128)(2,1)} %pin.6.refs_2_), custom_call_target="tpu_custom_call" | custom-call | flops 48318382080 | bytes 110100480 | tf_op jit(solution)/shard_map/widen/pallas_call | solution.py:76
  65.8 6.3 %collective-permute-done.5.refs_0_ = bf16[128,1536]{1,0:T(8,128)(2,1)} collective-permute-done((bf16[128,1536]{1,0:T(8,128)(2,1)}, bf16[128,1536]{1,0:T(8,128)(2,1)}, u32[]{:S(2)}, u32[]{:S(2)}) %collective-permute-start.5) | collective-permute-done | bytes 393248 | tf_op jit(solution)/shard_map/ppermute | solution.py:156
  72.1 6.4 %collective-permute-start.11 = (bf16[128,1536]{1,0:T(8,128)(2,1)}, bf16[128,1536]{1,0:T(8,128)(2,1)}, u32[]{:S(2)}, u32[]{:S(2)}) collective-permute-start(bf16[128,1536]{1,0:T(8,128)(2,1)} %pin.7.refs_8_.refs_3_), channel_id=1, source_target_pairs={{0,2},{1,3},{2,4},{3,5},{4,6},{5,7},{6,0},{7,1},{8,10},{9,11},{10,... | collective-permute-start | bytes 1179656 | tf_op jit(solution)/shard_map/ppermute | solution.py:156
  78.5 13.9 %collective-permute-done.3.refs_5_.refs_2_ = bf16[512,1536]{1,0:T(8,128)(2,1)} collective-permute-done((bf16[512,1536]{1,0:T(8,128)(2,1)}, bf16[512,1536]{1,0:T(8,128)(2,1)}, u32[]{:S(2)}, u32[]{:S(2)}) %collective-permute-start.3) | collective-permute-done | bytes 1572896 | tf_op jit(solution)/shard_map/ppermute | solution.py:142
  92.4 8.2 %project_in.2.refs_4_.refs_1_ = bf16[1024,1024]{1,0:T(8,128)(2,1)} custom-call(s32[1]{0:T(128)} %bitcast.refs_0_, bf16[1536,1024]{1,0:T(8,128)(2,1)} %widen.1.refs_1_, f32[1024,128]{1,0:T(8,128)} %get-tuple-element.240.refs_2_.refs_5_, f32[1024,128]{1,0:T(8,128)} %get-tuple-element.228.refs_3_.refs_6_, bf16[512,1536]{1,0:T(8,128)(2,1)} %get-tuple-element.123.refs_4_.refs_1_, ...), custom_call_target="tpu_custom_call" | custom-call | flops 64424509440 | bytes 167772160 | tf_op jit(solution)/shard_map/project_in/pallas_call | solution.py:76
  100.6 3.7 stack_cot.1
  105.7 9.9 %attention_forward.2 = (bf16[256,384]{1,0:T(8,128)(2,1)}, bf16[256,384]{1,0:T(8,128)(2,1)}, bf16[256,384]{1,0:T(8,128)(2,1)}, bf16[256,384]{1,0:T(8,128)(2,1)}, f32[2,4,512]{2,1,0:T(4,128)}) custom-call(s32[1]{0:T(128)} %bitcast.refs_0_, bf16[1024,1024]{1,0:T(8,128)(2,1)} %project_in.2.refs_4_.refs_1_, s32[1,1024]{1,0:T(1,128)} %get-tuple-element.237.refs_2_, ...), custom_call_target="tpu_custom_call" | custom-call | flops 42949672960 | bytes 83886080 | tf_op jit(solution)/shard_map/attention_forward/pallas_call | solution.py:76
  120.6 2.6 join.1.refs_6_.refs_2_.refs_1_
  123.2 8.8 %project_in.3.refs_8_.refs_1_ = bf16[1024,1024]{1,0:T(8,128)(2,1)} custom-call(s32[1]{0:T(128)} %bitcast.refs_0_, bf16[1536,1024]{1,0:T(8,128)(2,1)} %widen.1.refs_1_, f32[1024,128]{1,0:T(8,128)} %get-tuple-element.241.refs_2_.refs_5_, f32[1024,128]{1,0:T(8,128)} %get-tuple-element.227.refs_3_.refs_6_, ...), custom_call_target="tpu_custom_call" | custom-call | flops 64424509440 | bytes 167772160 | tf_op jit(solution)/shard_map/project_in/pallas_call | solution.py:76
  132.0 14.6 %collective-permute-done.9.refs_6_.refs_3_ = bf16[256,384]{1,0:T(8,128)(2,1)} collective-permute-done((bf16[256,384]{1,0:T(8,128)(2,1)}, bf16[256,384]{1,0:T(8,128)(2,1)}, u32[]{:S(2)}, u32[]{:S(2)}) %collective-permute-start.9) | collective-permute-done | bytes 196640 | tf_op jit(solution)/shard_map/ppermute | solution.py:147
  146.6 6.0 %project_out.2 = (f32[256,1536]{1,0:T(8,128)}, bf16[256,768]{1,0:T(8,128)(2,1)}, bf16[256,768]{1,0:T(8,128)(2,1)}) custom-call(s32[1]{0:T(128)} %bitcast.refs_0_, bf16[4,384,1536]{2,1,0:T(8,128)(2,1)} %bitcast.13, bf16[2,256,1536]{2,1,0:T(8,128)(2,1)} %refs_0_.5, f32[1,1536]{1,0:T(1,128)} %broadcast_in_dim.20.refs_3_, ...), custom_call_target="tpu_custom_call" | custom-call | flops 24159191040 | bytes 173015040 | tf_op jit(solution)/shard_map/project_out/pallas_call | solution.py:76
  155.4 10.2 %attention_forward.3 = (bf16[256,384]{1,0:T(8,128)(2,1)}, bf16[256,384]{1,0:T(8,128)(2,1)}, bf16[256,384]{1,0:T(8,128)(2,1)}, bf16[256,384]{1,0:T(8,128)(2,1)}, f32[2,4,512]{2,1,0:T(4,128)}) custom-call(s32[1]{0:T(128)} %bitcast.refs_0_, bf16[1024,1024]{1,0:T(8,128)(2,1)} %project_in.3.refs_8_.refs_1_, s32[1,1024]{1,0:T(1,128)} %get-tuple-element.236.refs_2_, ...), custom_call_target="tpu_custom_call" | custom-call | flops 42949672960 | bytes 83886080 | tf_op jit(solution)/shard_map/attention_forward/pallas_call | solution.py:76
  168.3 2.1 collective-permute-start.20
  170.4 2.5 stack_mid.2
  176.2 2.1 collective-permute-done.20.refs_7_.refs_8_
  178.2 5.9 %project_out.3 = (f32[256,1536]{1,0:T(8,128)}, bf16[256,768]{1,0:T(8,128)(2,1)}, bf16[256,768]{1,0:T(8,128)(2,1)}) custom-call(s32[1]{0:T(128)} %bitcast.refs_0_, bf16[4,384,1536]{2,1,0:T(8,128)(2,1)} %bitcast.14, bf16[2,256,1536]{2,1,0:T(8,128)(2,1)} %refs_0_.5, f32[1,1536]{1,0:T(1,128)} %broadcast_in_dim.20.refs_3_, ...), custom_call_target="tpu_custom_call" | custom-call | flops 24159191040 | bytes 173015040 | tf_op jit(solution)/shard_map/project_out/pallas_call | solution.py:76
  186.0 14.3 %collective-permute-done.22.refs_1_ = bf16[256,768]{1,0:T(8,128)(2,1)} collective-permute-done((bf16[256,768]{1,0:T(8,128)(2,1)}, bf16[256,768]{1,0:T(8,128)(2,1)}, u32[]{:S(2)}, u32[]{:S(2)}) %collective-permute-start.22) | collective-permute-done | bytes 393248 | tf_op jit(solution)/shard_map/ppermute | solution.py:142
  200.3 2.6 stack_mid.3
  205.5 25.4 %feed_forward.2 = (bf16[1024,1024]{1,0:T(8,128)(2,1)}, bf16[1024,2048]{1,0:T(8,128)(2,1)}, bf16[1024,1536]{1,0:T(8,128)(2,1)}, bf16[512,768]{1,0:T(8,128)(2,1)},...) custom-call(s32[1]{0:T(128)} %bitcast.6.refs_0_, ...), custom_call_target="tpu_custom_call" | custom-call | flops 322122547200 | bytes 503316480 | tf_op jit(solution)/shard_map/feed_forward/pallas_call | solution.py:76
  232.4 25.2 %feed_forward.3 = (bf16[1024,1024]{1,0:T(8,128)(2,1)}, bf16[1024,2048]{1,0:T(8,128)(2,1)}, bf16[1024,1536]{1,0:T(8,128)(2,1)}, bf16[512,768]{1,0:T(8,128)(2,1)},...) custom-call(s32[1]{0:T(128)} %bitcast.6.refs_0_, ...), custom_call_target="tpu_custom_call" | custom-call | flops 322122547200 | bytes 503316480 | tf_op jit(solution)/shard_map/feed_forward/pallas_call | solution.py:76
  260.3 3.4 fold.5
  265.0 20.5 %gate_up_grad.1 = (bf16[1536,2048]{1,0:T(8,128)(2,1)}, f32[8,1536]{1,0:T(8,128)}) custom-call(bf16[1024,1536]{1,0:T(8,128)(2,1)} %get-tuple-element.158.refs_0_, bf16[1024,1536]{1,0:T(8,128)(2,1)} %get-tuple-element.159.refs_1_, bf16[1024,2048]{1,0:T(8,128)(2,1)} %get-tuple-element.160.refs_2_, bf16[1024,2048]{1,0:T(8,128)(2,1)} %get-tuple-element.161.refs_3_, ...), custom_call_target="tpu_custom_call" | custom-call | flops 257698037760 | bytes 419430400 | tf_op jit(solution)/shard_map/gate_up_grad/pallas_call | solution.py:76
  285.5 6.8 %norm_out_back.2 = (f32[256,1536]{1,0:T(8,128)}, bf16[256,1536]{1,0:T(8,128)(2,1)}, bf16[256,384]{1,0:T(8,128)(2,1)}, bf16[256,384]{1,0:T(8,128)(2,1)}, bf16[256...) custom-call(s32[1]{0:T(128)} %bitcast.refs_0_, f32[256,1536]{1,0:T(8,128)} %get-tuple-element.131.refs_1_.refs_0_, ...), custom_call_target="tpu_custom_call" | custom-call | flops 3019898880 | bytes 27525120 | tf_op jit(solution)/shard_map/norm_out_back/pallas_call | solution.py:76
  295.9 3.3 fold.6
  301.9 2.0 collective-permute-done.31.refs_6_.refs_10_
  304.4 12.8 %feed_out.1 = (bf16[512,1536]{1,0:T(8,128)(2,1)}, bf16[512,1536]{1,0:T(8,128)(2,1)}, bf16[512,1536]{1,0:T(8,128)(2,1)}, bf16[512,1536]{1,0:T(8,128)(2,1)}) custom-call(s32[1]{0:T(128)} %bitcast.6.refs_0_, bf16[4,128,1536]{2,1,0:T(8,128)(2,1)} %join.1.refs_6_.refs_2_.refs_1_, bf16[4,128,1536]{2,1,0:T(8,128)(2,1)} %collective-permute-done.12.refs_8_.refs_3_.refs_2_, ...), custom_call_target="tpu_custom_call" | custom-call | flops 16106127360 | bytes 34078720 | tf_op jit(solution)/shard_map/feed_out/pallas_call | solution.py:76
  317.2 6.9 %norm_out_back.3 = (f32[256,1536]{1,0:T(8,128)}, bf16[256,1536]{1,0:T(8,128)(2,1)}, bf16[256,384]{1,0:T(8,128)(2,1)}, bf16[256,384]{1,0:T(8,128)(2,1)}, bf16[256...) custom-call(s32[1]{0:T(128)} %bitcast.refs_0_, f32[256,1536]{1,0:T(8,128)} %get-tuple-element.176.refs_1_.refs_3_, ...), custom_call_target="tpu_custom_call" | custom-call | flops 3019898880 | bytes 27525120 | tf_op jit(solution)/shard_map/norm_out_back/pallas_call | solution.py:76
  324.1 11.5 %down_grad.1.refs_11_ = bf16[1024,1536]{1,0:T(8,128)(2,1)} custom-call(bf16[1024,1024]{1,0:T(8,128)(2,1)} %get-tuple-element.146.refs_3_.refs_0_, bf16[1024,1024]{1,0:T(8,128)(2,1)} %get-tuple-element.149.refs_4_.refs_1_, bf16[512,1536]{1,0:T(8,128)(2,1)} %get-tuple-element.133.refs_9_.refs_4_.refs_2_, ...), custom_call_target="tpu_custom_call" | custom-call | flops 128849018880 | bytes 272629760 | tf_op jit(solution)/shard_map/down_grad/pallas_call | solution.py:76
  341.3 6.8 %out_weight_grad.1.refs_12_ = bf16[4,384,1536]{2,1,0:T(8,128)(2,1)} custom-call(s32[1]{0:T(128)} %bitcast.refs_0_, bf16[256,384]{1,0:T(8,128)(2,1)} %get-tuple-element.126.refs_4_.refs_1_, bf16[256,384]{1,0:T(8,128)(2,1)} %collective-permute-done.8.refs_5_.refs_2_, bf16[256,384]{1,0:T(8,128)(2,1)} %collective-permute-done.9.refs_6_.refs_3_, ...), custom_call_target="tpu_custom_call" | custom-call | flops 48318382080 | bytes 94371840 | tf_op jit(solution)/shard_map/out_weight_grad/pallas_call | solution.py:76
  348.2 20.5 %attention_backward.2.refs_4_.refs_0_.refs_5_ = bf16[1024,768]{1,0:T(8,128)(2,1)} custom-call(s32[1]{0:T(128)} %bitcast.refs_0_, bf16[1024,1024]{1,0:T(8,128)(2,1)} %project_in.2.refs_4_.refs_1_, s32[1,1024]{1,0:T(1,128)} %get-tuple-element.237.refs_2_, bf16[2,256,384]{2,1,0:T(8,128)(2,1)} %constant.17.clone.refs_3_, ...), custom_call_target="tpu_custom_call" | custom-call | flops 107374182400 | bytes 167772160 | tf_op jit(solution)/shard_map/attention_backward/pallas_call | solution.py:76
  370.2 5.4 fold.7
  376.6 2.0 collective-permute-done.41.refs_2_.refs_9_
  378.7 7.0 %grad_into_rows.2 = (bf16[512,768]{1,0:T(8,128)(2,1)}, bf16[512,768]{1,0:T(8,128)(2,1)}, bf16[512,768]{1,0:T(8,128)(2,1)}, bf16[512,768]{1,0:T(8,128)(2,1)}) custom-call(bf16[1024,768]{1,0:T(8,128)(2,1)} %attention_backward.2.refs_4_.refs_0_.refs_5_, bf16[1536,768]{1,0:T(8,128)(2,1)} %all-gather.7.cloned.1.call-done.refs_0_.refs_1_.refs_7_, ...), custom_call_target="tpu_custom_call" | custom-call | flops 48318382080 | bytes 141557760 | tf_op jit(solution)/shard_map/grad_into_rows/pallas_call | solution.py:76
  387.8 20.5 %attention_backward.3.refs_4_.refs_6_.refs_0_ = bf16[1024,768]{1,0:T(8,128)(2,1)} custom-call(s32[1]{0:T(128)} %bitcast.refs_0_, bf16[1024,1024]{1,0:T(8,128)(2,1)} %project_in.3.refs_8_.refs_1_, s32[1,1024]{1,0:T(1,128)} %get-tuple-element.236.refs_2_, bf16[2,256,384]{2,1,0:T(8,128)(2,1)} %constant.17.clone.refs_3_, ...), custom_call_target="tpu_custom_call" | custom-call | flops 107374182400 | bytes 167772160 | tf_op jit(solution)/shard_map/attention_backward/pallas_call | solution.py:76
  408.4 4.9 collective-permute-done.46.refs_3_
  413.3 3.8 fold.8
  419.4 7.6 %collective-permute-done.44.refs_13_.refs_5_.refs_2_ = bf16[192,2048]{1,0:T(8,128)(2,1)} collective-permute-done((bf16[192,2048]{1,0:T(8,128)(2,1)}, bf16[192,2048]{1,0:T(8,128)(2,1)}, u32[]{:S(2)}, u32[]{:S(2)}) %collective-permute-start.44) | collective-permute-done | bytes 786464 | tf_op jit(solution)/shard_map/ppermute | solution.py:142
  427.1 11.1 %in_weight_grad.1 = (bf16[4,192,768]{2,1,0:T(8,128)(2,1)}, bf16[4,192,768]{2,1,0:T(8,128)(2,1)}, f32[8,1536]{1,0:T(8,128)}) custom-call(s32[1]{0:T(128)} %bitcast.6.refs_0_, bf16[512,1536]{1,0:T(8,128)(2,1)} %get-tuple-element.123.refs_4_.refs_1_, bf16[512,1536]{1,0:T(8,128)(2,1)} %collective-permute-done.3.refs_5_.refs_2_, ...), custom_call_target="tpu_custom_call" | custom-call | flops 96636764160 | bytes 235929600 | tf_op jit(solution)/shard_map/in_weight_grad/pallas_call | solution.py:76
  439.1 7.2 %grad_into_rows.3 = (bf16[512,768]{1,0:T(8,128)(2,1)}, bf16[512,768]{1,0:T(8,128)(2,1)}, bf16[512,768]{1,0:T(8,128)(2,1)}, bf16[512,768]{1,0:T(8,128)(2,1)}) custom-call(bf16[1024,768]{1,0:T(8,128)(2,1)} %attention_backward.3.refs_4_.refs_6_.refs_0_, bf16[1536,768]{1,0:T(8,128)(2,1)} %all-gather.7.cloned.1.call-done.refs_0_.refs_1_.refs_7_, ...), custom_call_target="tpu_custom_call" | custom-call | flops 48318382080 | bytes 141557760 | tf_op jit(solution)/shard_map/grad_into_rows/pallas_call | solution.py:76
  450.7 8.3 %collective-permute-done.50.refs_7_.refs_4_ = bf16[192,2048]{1,0:T(8,128)(2,1)} collective-permute-done((bf16[192,2048]{1,0:T(8,128)(2,1)}, bf16[192,2048]{1,0:T(8,128)(2,1)}, u32[]{:S(2)}, u32[]{:S(2)}) %collective-permute-start.50) | collective-permute-done | bytes 786464 | tf_op jit(solution)/shard_map/ppermute | solution.py:142
  459.0 2.8 halve.3
  461.8 2.0 collective-permute-start.58
  464.8 4.7 finish_block_out.1.refs_4_
  469.6 8.2 %collective-permute-done.53.refs_2_ = bf16[512,768]{1,0:T(8,128)(2,1)} collective-permute-done((bf16[512,768]{1,0:T(8,128)(2,1)}, bf16[512,768]{1,0:T(8,128)(2,1)}, u32[]{:S(2)}, u32[]{:S(2)}) %collective-permute-start.53) | collective-permute-done | bytes 786464 | tf_op jit(solution)/shard_map/ppermute | solution.py:142
  477.7 3.3 fold.9
  481.1 2.1 halve.4
  483.2 3.1 collective-permute-start.60
  487.7 12.9 %collective-permute-done.61.refs_3_ = f32[8,1536]{1,0:T(8,128)} collective-permute-done((f32[8,1536]{1,0:T(8,128)}, f32[8,1536]{1,0:T(8,128)}, u32[]{:S(2)}, u32[]{:S(2)}) %collective-permute-start.61) | collective-permute-done | bytes 49184 | tf_op jit(solution)/shard_map/ppermute | solution.py:1060
  500.5 1.9 halve.5
  502.4 2.2 add_convert_fusion.refs_0_
  509.6 6.4 %finish_tokens_grad.1.refs_2_ = bf16[2,256,1536]{2,1,0:T(8,128)(2,1)} custom-call(bf16[2,256,1536]{2,1,0:T(8,128)(2,1)} %refs_0_.5, f32[1,1536]{1,0:T(1,128)} %broadcast_in_dim.21.refs_1_.refs_2_, f32[256,1536]{1,0:T(8,128)} %get-tuple-element.203.refs_2_, f32[256,768]{1,0:T(8,128)} %get-tuple-element.198.refs_2_.refs_3_, ...), custom_call_target="tpu_custom_call" | custom-call | bytes 188743680 | tf_op jit(solution)/shard_map/finish_tokens_grad/pallas_call | solution.py:76
  521.2 2.1 add_float.1.refs_5_
  523.3 4.5 arrange_gate_up.1
  527.8 3.9 down_to_float.1.refs_5_
  531.8 2.7 arrange_in.1.refs_4_
  (160 shorter events, 81.2 us)
Async XLA Ops:
  7.2 51.9 %all-gather.7.cloned.1.call-start = ((), (), s32[]{:S(2)}) async-start(), calls=%async_computation.4 | async-start | bytes 2654208 | tf_op jit(solution)/shard_map/all_gather | solution.py:1334
  9.4 137.2 %all-gather.5.cloned.1.call-start = ((), (), s32[]{:S(2)}) async-start(), calls=%async_computation.3 | async-start | bytes 5308416 | tf_op jit(solution)/shard_map/all_gather | solution.py:1334
  10.1 195.4 %all-gather.9.cloned.1.call-start = ((), (), s32[]{:S(2)}) async-start(), calls=%async_computation.5 | async-start | bytes 7077888 | tf_op jit(solution)/shard_map/all_gather | solution.py:1334
  12.8 87.8 %collective-permute-start.6 = (bf16[256,1536]{1,0:T(8,128)(2,1)}, bf16[256,1536]{1,0:T(8,128)(2,1)}, u32[]{:S(2)}, u32[]{:S(2)}) collective-permute-start(bf16[256,1536]{1,0:T(8,128)(2,1)} %get-tuple-element.124.refs_0_), channel_id=1, source_target_pairs={{0,16},{8,24},{16,0},{24,8},{1,17},{9,25},{17,1},{25,9},{2,18},{10... | collective-permute-start | bytes 2359304 | tf_op jit(solution)/shard_map/ppermute | solution.py:142
  15.7 84.9 %collective-permute-start.7 = (bf16[256,1536]{1,0:T(8,128)(2,1)}, bf16[256,1536]{1,0:T(8,128)(2,1)}, u32[]{:S(2)}, u32[]{:S(2)}) collective-permute-start(bf16[256,1536]{1,0:T(8,128)(2,1)} %get-tuple-element.118.refs_2_), channel_id=1, source_target_pairs={{0,8},{8,0},{16,24},{24,16},{1,9},{9,1},{17,25},{25,17},{2,10},{10... | collective-permute-start | bytes 2359304 | tf_op jit(solution)/shard_map/ppermute | solution.py:142
  21.6 28.9 %collective-permute-start.1 = (bf16[256,1536]{1,0:T(8,128)(2,1)}, bf16[256,1536]{1,0:T(8,128)(2,1)}, u32[]{:S(2)}, u32[]{:S(2)}) collective-permute-start(bf16[256,1536]{1,0:T(8,128)(2,1)} %get-tuple-element.121.refs_0_), channel_id=1, source_target_pairs={{0,16},{8,24},{16,0},{24,8},{1,17},{9,25},{17,1},{25,9},{2,18},{10... | collective-permute-start | bytes 2359304 | tf_op jit(solution)/shard_map/ppermute | solution.py:142
  22.0 29.9 %collective-permute-start.2 = (bf16[256,1536]{1,0:T(8,128)(2,1)}, bf16[256,1536]{1,0:T(8,128)(2,1)}, u32[]{:S(2)}, u32[]{:S(2)}) collective-permute-start(bf16[256,1536]{1,0:T(8,128)(2,1)} %get-tuple-element.119.refs_4_.refs_2_), channel_id=1, source_target_pairs={{0,8},{8,0},{16,24},{24,16},{1,9},{9,1},{17,25},{25,17},{2,10},{10... | collective-permute-start | bytes 2359304 | tf_op jit(solution)/shard_map/ppermute | solution.py:142
  25.6 30.2 %collective-permute-start = (bf16[128,1536]{1,0:T(8,128)(2,1)}, bf16[128,1536]{1,0:T(8,128)(2,1)}, u32[]{:S(2)}, u32[]{:S(2)}) collective-permute-start(bf16[128,1536]{1,0:T(8,128)(2,1)} %get-tuple-element.120.refs_4_.refs_1_), channel_id=1, source_target_pairs={{0,2},{1,3},{2,4},{3,5},{4,6},{5,7},{6,0},{7,1},{8,10},{9,11},{10,... | collective-permute-start | bytes 1179656 | tf_op jit(solution)/shard_map/ppermute | solution.py:156
  27.7 359.1 %reduce-scatter.6.cloned.1.call-start = ((), (), s32[]{:S(2)}) async-start(), calls=%async_computation.7 | async-start | bytes 7077888 | tf_op jit(solution)/shard_map/reduce_scatter | solution.py:1337
  55.5 36.9 %collective-permute-start.4 = (bf16[512,1536]{1,0:T(8,128)(2,1)}, bf16[512,1536]{1,0:T(8,128)(2,1)}, u32[]{:S(2)}, u32[]{:S(2)}) collective-permute-start(bf16[512,1536]{1,0:T(8,128)(2,1)} %get-tuple-element.122.refs_1_.refs_6_.refs_4_.refs_3_), channel_id=1, source_target_pairs={{0,16},{8,24},{16,0},{24,8},{1,17},{9,25},{17,1},{25,9},{2,18},{10... | collective-permute-start | bytes 4718600 | tf_op jit(solution)/shard_map/ppermute | solution.py:142
  55.8 16.3 %collective-permute-start.5 = (bf16[128,1536]{1,0:T(8,128)(2,1)}, bf16[128,1536]{1,0:T(8,128)(2,1)}, u32[]{:S(2)}, u32[]{:S(2)}) collective-permute-start(bf16[128,1536]{1,0:T(8,128)(2,1)} %pin.6.refs_2_), channel_id=1, source_target_pairs={{0,2},{1,3},{2,4},{3,5},{4,6},{5,7},{6,0},{7,1},{8,10},{9,11},{10,... | collective-permute-start | bytes 1179656 | tf_op jit(solution)/shard_map/ppermute | solution.py:156
  57.6 34.8 %collective-permute-start.3 = (bf16[512,1536]{1,0:T(8,128)(2,1)}, bf16[512,1536]{1,0:T(8,128)(2,1)}, u32[]{:S(2)}, u32[]{:S(2)}) collective-permute-start(bf16[512,1536]{1,0:T(8,128)(2,1)} %get-tuple-element.123.refs_4_.refs_1_), channel_id=1, source_target_pairs={{0,8},{8,0},{16,24},{24,16},{1,9},{9,1},{17,25},{25,17},{2,10},{10... | collective-permute-start | bytes 4718600 | tf_op jit(solution)/shard_map/ppermute | solution.py:142
  72.1 47.0 %collective-permute-start.11 = (bf16[128,1536]{1,0:T(8,128)(2,1)}, bf16[128,1536]{1,0:T(8,128)(2,1)}, u32[]{:S(2)}, u32[]{:S(2)}) collective-permute-start(bf16[128,1536]{1,0:T(8,128)(2,1)} %pin.7.refs_8_.refs_3_), channel_id=1, source_target_pairs={{0,2},{1,3},{2,4},{3,5},{4,6},{5,7},{6,0},{7,1},{8,10},{9,11},{10,... | collective-permute-start | bytes 1179656 | tf_op jit(solution)/shard_map/ppermute | solution.py:156
  104.3 68.7 %collective-permute-start.21 = (bf16[512,1536]{1,0:T(8,128)(2,1)}, bf16[512,1536]{1,0:T(8,128)(2,1)}, u32[]{:S(2)}, u32[]{:S(2)}) collective-permute-start(bf16[512,1536]{1,0:T(8,128)(2,1)} %get-tuple-element.125.refs_4_.refs_11_), channel_id=1, source_target_pairs={{0,16},{8,24},{16,0},{24,8},{1,17},{9,25},{17,1},{25,9},{2,18},{10... | collective-permute-start | bytes 4718600 | tf_op jit(solution)/shard_map/ppermute | solution.py:142
  115.6 16.4 %collective-permute-start.8 = (bf16[256,384]{1,0:T(8,128)(2,1)}, bf16[256,384]{1,0:T(8,128)(2,1)}, u32[]{:S(2)}, u32[]{:S(2)}) collective-permute-start(bf16[256,384]{1,0:T(8,128)(2,1)} %get-tuple-element.127), channel_id=1, source_target_pairs={{0,8},{8,0},{16,24},{24,16},{1,9},{9,1},{17,25},{25,17},{2,10},{10... | collective-permute-start | bytes 589832 | tf_op jit(solution)/shard_map/ppermute | solution.py:147
  117.1 29.5 %collective-permute-start.9 = (bf16[256,384]{1,0:T(8,128)(2,1)}, bf16[256,384]{1,0:T(8,128)(2,1)}, u32[]{:S(2)}, u32[]{:S(2)}) collective-permute-start(bf16[256,384]{1,0:T(8,128)(2,1)} %get-tuple-element.128), channel_id=1, source_target_pairs={{0,16},{8,24},{16,0},{24,8},{1,17},{9,25},{17,1},{25,9},{2,18},{10... | collective-permute-start | bytes 589832 | tf_op jit(solution)/shard_map/ppermute | solution.py:147
  117.8 28.8 %collective-permute-start.10 = (bf16[256,384]{1,0:T(8,128)(2,1)}, bf16[256,384]{1,0:T(8,128)(2,1)}, u32[]{:S(2)}, u32[]{:S(2)}) collective-permute-start(bf16[256,384]{1,0:T(8,128)(2,1)} %get-tuple-element.129), channel_id=1, source_target_pairs={{0,24},{8,16},{16,8},{24,0},{1,25},{9,17},{17,9},{25,1},{2,26},{10... | collective-permute-start | bytes 589832 | tf_op jit(solution)/shard_map/ppermute | solution.py:147
  119.1 46.5 %collective-permute-start.13 = (bf16[512,1536]{1,0:T(8,128)(2,1)}, bf16[512,1536]{1,0:T(8,128)(2,1)}, u32[]{:S(2)}, u32[]{:S(2)}) collective-permute-start(bf16[512,1536]{1,0:T(8,128)(2,1)} %get-tuple-element.133.refs_9_.refs_4_.refs_2_), channel_id=1, source_target_pairs={{0,8},{8,0},{16,24},{24,16},{1,9},{9,1},{17,25},{25,17},{2,10},{10... | collective-permute-start | bytes 4718600 | tf_op jit(solution)/shard_map/ppermute | solution.py:142
  132.0 41.1 %collective-permute-start.12 = (bf16[4,128,1536]{2,1,0:T(8,128)(2,1)}, bf16[4,128,1536]{2,1,0:T(8,128)(2,1)}, u32[]{:S(2)}, u32[]{:S(2)}) collective-permute-start(bf16[4,128,1536]{2,1,0:T(8,128)(2,1)} %join.1.refs_6_.refs_2_.refs_1_), channel_id=1, source_target_pairs={{0,1},{1,0},{2,3},{3,2},{4,5},{5,4},{6,7},{7,6},{8,9},{9,8},{10,11... | collective-permute-start | bytes 4718600 | tf_op jit(solution)/shard_map/ppermute | solution.py:161
  153.9 14.4 %collective-permute-start.15 = (bf16[256,768]{1,0:T(8,128)(2,1)}, bf16[256,768]{1,0:T(8,128)(2,1)}, u32[]{:S(2)}, u32[]{:S(2)}) collective-permute-start(bf16[256,768]{1,0:T(8,128)(2,1)} %get-tuple-element.135.refs_4_.refs_2_), channel_id=1, source_target_pairs={{0,8},{8,0},{16,24},{24,16},{1,9},{9,1},{17,25},{25,17},{2,10},{10... | collective-permute-start | bytes 1179656 | tf_op jit(solution)/shard_map/ppermute | solution.py:142
  172.9 32.5 %collective-permute-start.16 = (bf16[512,768]{1,0:T(8,128)(2,1)}, bf16[512,768]{1,0:T(8,128)(2,1)}, u32[]{:S(2)}, u32[]{:S(2)}) collective-permute-start(bf16[512,768]{1,0:T(8,128)(2,1)} %get-tuple-element.137.refs_6_), channel_id=1, source_target_pairs={{0,8},{8,0},{16,24},{24,16},{1,9},{9,1},{17,25},{25,17},{2,10},{10... | collective-permute-start | bytes 2359304 | tf_op jit(solution)/shard_map/ppermute | solution.py:142
  173.1 32.4 %collective-permute-start.17 = (bf16[512,768]{1,0:T(8,128)(2,1)}, bf16[512,768]{1,0:T(8,128)(2,1)}, u32[]{:S(2)}, u32[]{:S(2)}) collective-permute-start(bf16[512,768]{1,0:T(8,128)(2,1)} %get-tuple-element.138.refs_13_.refs_8_), channel_id=1, source_target_pairs={{0,16},{8,24},{16,0},{24,8},{1,17},{9,25},{17,1},{25,9},{2,18},{10... | collective-permute-start | bytes 2359304 | tf_op jit(solution)/shard_map/ppermute | solution.py:142
  184.2 16.1 %collective-permute-start.22 = (bf16[256,768]{1,0:T(8,128)(2,1)}, bf16[256,768]{1,0:T(8,128)(2,1)}, u32[]{:S(2)}, u32[]{:S(2)}) collective-permute-start(bf16[256,768]{1,0:T(8,128)(2,1)} %get-tuple-element.143.refs_0_), channel_id=1, source_target_pairs={{0,16},{8,24},{16,0},{24,8},{1,17},{9,25},{17,1},{25,9},{2,18},{10... | collective-permute-start | bytes 1179656 | tf_op jit(solution)/shard_map/ppermute | solution.py:142
  185.4 14.8 %collective-permute-start.23 = (bf16[256,768]{1,0:T(8,128)(2,1)}, bf16[256,768]{1,0:T(8,128)(2,1)}, u32[]{:S(2)}, u32[]{:S(2)}) collective-permute-start(bf16[256,768]{1,0:T(8,128)(2,1)} %get-tuple-element.144.refs_2_.refs_4_), channel_id=1, source_target_pairs={{0,8},{8,0},{16,24},{24,16},{1,9},{9,1},{17,25},{25,17},{2,10},{10... | collective-permute-start | bytes 1179656 | tf_op jit(solution)/shard_map/ppermute | solution.py:142
  202.8 29.5 %collective-permute-start.24 = (bf16[512,768]{1,0:T(8,128)(2,1)}, bf16[512,768]{1,0:T(8,128)(2,1)}, u32[]{:S(2)}, u32[]{:S(2)}) collective-permute-start(bf16[512,768]{1,0:T(8,128)(2,1)} %get-tuple-element.147.refs_6_), channel_id=1, source_target_pairs={{0,8},{8,0},{16,24},{24,16},{1,9},{9,1},{17,25},{25,17},{2,10},{10... | collective-permute-start | bytes 2359304 | tf_op jit(solution)/shard_map/ppermute | solution.py:142
  204.4 28.0 %collective-permute-start.25 = (bf16[512,768]{1,0:T(8,128)(2,1)}, bf16[512,768]{1,0:T(8,128)(2,1)}, u32[]{:S(2)}, u32[]{:S(2)}) collective-permute-start(bf16[512,768]{1,0:T(8,128)(2,1)} %get-tuple-element.145.refs_10_.refs_8_), channel_id=1, source_target_pairs={{0,16},{8,24},{16,0},{24,8},{1,17},{9,25},{17,1},{25,9},{2,18},{10... | collective-permute-start | bytes 2359304 | tf_op jit(solution)/shard_map/ppermute | solution.py:142
  230.9 29.4 %collective-permute-start.26 = (bf16[512,768]{1,0:T(8,128)(2,1)}, bf16[512,768]{1,0:T(8,128)(2,1)}, u32[]{:S(2)}, u32[]{:S(2)}) collective-permute-start(bf16[512,768]{1,0:T(8,128)(2,1)} %get-tuple-element.152), channel_id=1, source_target_pairs={{0,8},{8,0},{16,24},{24,16},{1,9},{9,1},{17,25},{25,17},{2,10},{10... | collective-permute-start | bytes 2359304 | tf_op jit(solution)/shard_map/ppermute | solution.py:142
  231.6 28.7 %collective-permute-start.27 = (bf16[512,768]{1,0:T(8,128)(2,1)}, bf16[512,768]{1,0:T(8,128)(2,1)}, u32[]{:S(2)}, u32[]{:S(2)}) collective-permute-start(bf16[512,768]{1,0:T(8,128)(2,1)} %get-tuple-element.148.refs_10_), channel_id=1, source_target_pairs={{0,16},{8,24},{16,0},{24,8},{1,17},{9,25},{17,1},{25,9},{2,18},{10... | collective-permute-start | bytes 2359304 | tf_op jit(solution)/shard_map/ppermute | solution.py:142
  257.6 38.3 %collective-permute-start.33 = (bf16[512,768]{1,0:T(8,128)(2,1)}, bf16[512,768]{1,0:T(8,128)(2,1)}, u32[]{:S(2)}, u32[]{:S(2)}) collective-permute-start(bf16[512,768]{1,0:T(8,128)(2,1)} %get-tuple-element.168), channel_id=1, source_target_pairs={{0,8},{8,0},{16,24},{24,16},{1,9},{9,1},{17,25},{25,17},{2,10},{10... | collective-permute-start | bytes 2359304 | tf_op jit(solution)/shard_map/ppermute | solution.py:142
  259.2 36.7 %collective-permute-start.34 = (bf16[512,768]{1,0:T(8,128)(2,1)}, bf16[512,768]{1,0:T(8,128)(2,1)}, u32[]{:S(2)}, u32[]{:S(2)}) collective-permute-start(bf16[512,768]{1,0:T(8,128)(2,1)} %get-tuple-element.153.refs_4_), channel_id=1, source_target_pairs={{0,16},{8,24},{16,0},{24,8},{1,17},{9,25},{17,1},{25,9},{2,18},{10... | collective-permute-start | bytes 2359304 | tf_op jit(solution)/shard_map/ppermute | solution.py:142
  263.6 21.9 %collective-permute-start.28 = (bf16[256,768]{1,0:T(8,128)(2,1)}, bf16[256,768]{1,0:T(8,128)(2,1)}, u32[]{:S(2)}, u32[]{:S(2)}) collective-permute-start(bf16[256,768]{1,0:T(8,128)(2,1)} %get-tuple-element.155), channel_id=1, source_target_pairs={{0,16},{8,24},{16,0},{24,8},{1,17},{9,25},{17,1},{25,9},{2,18},{10... | collective-permute-start | bytes 1179656 | tf_op jit(solution)/shard_map/ppermute | solution.py:142
  264.6 20.9 %collective-permute-start.29 = (bf16[256,768]{1,0:T(8,128)(2,1)}, bf16[256,768]{1,0:T(8,128)(2,1)}, u32[]{:S(2)}, u32[]{:S(2)}) collective-permute-start(bf16[256,768]{1,0:T(8,128)(2,1)} %get-tuple-element.157.refs_5_), channel_id=1, source_target_pairs={{0,8},{8,0},{16,24},{24,16},{1,9},{9,1},{17,25},{25,17},{2,10},{10... | collective-permute-start | bytes 1179656 | tf_op jit(solution)/shard_map/ppermute | solution.py:142
  295.9 150.5 %reduce-scatter.8.cloned.1.call-start = ((), (), s32[]{:S(2)}) async-start(), calls=%async_computation.8 | async-start | bytes 3538944 | tf_op jit(solution)/shard_map/reduce_scatter | solution.py:1337
  299.3 17.9 %collective-permute-start.37 = (bf16[256,768]{1,0:T(8,128)(2,1)}, bf16[256,768]{1,0:T(8,128)(2,1)}, u32[]{:S(2)}, u32[]{:S(2)}) collective-permute-start(bf16[256,768]{1,0:T(8,128)(2,1)} %get-tuple-element.178), channel_id=1, source_target_pairs={{0,16},{8,24},{16,0},{24,8},{1,17},{9,25},{17,1},{25,9},{2,18},{10... | collective-permute-start | bytes 1179656 | tf_op jit(solution)/shard_map/ppermute | solution.py:142
  300.5 16.7 %collective-permute-start.38 = (bf16[256,768]{1,0:T(8,128)(2,1)}, bf16[256,768]{1,0:T(8,128)(2,1)}, u32[]{:S(2)}, u32[]{:S(2)}) collective-permute-start(bf16[256,768]{1,0:T(8,128)(2,1)} %get-tuple-element.169.refs_8_), channel_id=1, source_target_pairs={{0,8},{8,0},{16,24},{24,16},{1,9},{9,1},{17,25},{25,17},{2,10},{10... | collective-permute-start | bytes 1179656 | tf_op jit(solution)/shard_map/ppermute | solution.py:142
  335.6 128.2 %reduce-scatter.4.cloned.1.call-start = ((), (), s32[]{:S(2)}) async-start(), calls=%async_computation.6 | async-start | bytes 5308416 | tf_op jit(solution)/shard_map/reduce_scatter | solution.py:1337
  335.6 34.6 %collective-permute-start.36 = (bf16[512,1536]{1,0:T(8,128)(2,1)}, bf16[512,1536]{1,0:T(8,128)(2,1)}, u32[]{:S(2)}, u32[]{:S(2)}) collective-permute-start(bf16[512,1536]{1,0:T(8,128)(2,1)} %get-tuple-element.173.refs_9_), channel_id=1, source_target_pairs={{0,16},{8,24},{16,0},{24,8},{1,17},{9,25},{17,1},{25,9},{2,18},{10... | collective-permute-start | bytes 4718600 | tf_op jit(solution)/shard_map/ppermute | solution.py:142
  336.6 33.7 %collective-permute-start.35 = (bf16[512,1536]{1,0:T(8,128)(2,1)}, bf16[512,1536]{1,0:T(8,128)(2,1)}, u32[]{:S(2)}, u32[]{:S(2)}) collective-permute-start(bf16[512,1536]{1,0:T(8,128)(2,1)} %get-tuple-element.172), channel_id=1, source_target_pairs={{0,8},{8,0},{16,24},{24,16},{1,9},{9,1},{17,25},{25,17},{2,10},{10... | collective-permute-start | bytes 4718600 | tf_op jit(solution)/shard_map/ppermute | solution.py:142
  337.8 40.9 %collective-permute-start.43 = (bf16[256,384]{1,0:T(8,128)(2,1)}, bf16[256,384]{1,0:T(8,128)(2,1)}, u32[]{:S(2)}, u32[]{:S(2)}) collective-permute-start(bf16[256,384]{1,0:T(8,128)(2,1)} %get-tuple-element.181.refs_6_), channel_id=1, source_target_pairs={{0,24},{8,16},{16,8},{24,0},{1,25},{9,17},{17,9},{25,1},{2,26},{10... | collective-permute-start | bytes 589832 | tf_op jit(solution)/shard_map/ppermute | solution.py:147
  339.2 39.5 %collective-permute-start.41 = (bf16[256,384]{1,0:T(8,128)(2,1)}, bf16[256,384]{1,0:T(8,128)(2,1)}, u32[]{:S(2)}, u32[]{:S(2)}) collective-permute-start(bf16[256,384]{1,0:T(8,128)(2,1)} %get-tuple-element.187), channel_id=1, source_target_pairs={{0,8},{8,0},{16,24},{24,16},{1,9},{9,1},{17,25},{25,17},{2,10},{10... | collective-permute-start | bytes 589832 | tf_op jit(solution)/shard_map/ppermute | solution.py:147
  340.3 38.3 %collective-permute-start.42 = (bf16[256,384]{1,0:T(8,128)(2,1)}, bf16[256,384]{1,0:T(8,128)(2,1)}, u32[]{:S(2)}, u32[]{:S(2)}) collective-permute-start(bf16[256,384]{1,0:T(8,128)(2,1)} %get-tuple-element.188), channel_id=1, source_target_pairs={{0,16},{8,24},{16,0},{24,8},{1,17},{9,25},{17,1},{25,9},{2,18},{10... | collective-permute-start | bytes 589832 | tf_op jit(solution)/shard_map/ppermute | solution.py:147
  348.1 179.7 %all-gather.11.cloned.1.call-start = ((), (), s32[]{:S(2)}) async-start(), calls=%async_computation.9 | async-start | bytes 1966080 | tf_op jit(solution)/shard_map/all_gather | solution.py:1482
  375.6 42.0 %collective-permute-start.39 = (bf16[256,1536]{1,0:T(8,128)(2,1)}, bf16[256,1536]{1,0:T(8,128)(2,1)}, u32[]{:S(2)}, u32[]{:S(2)}) collective-permute-start(bf16[256,1536]{1,0:T(8,128)(2,1)} %get-tuple-element.183), channel_id=1, source_target_pairs={{0,16},{8,24},{16,0},{24,8},{1,17},{9,25},{17,1},{25,9},{2,18},{10... | collective-permute-start | bytes 2359304 | tf_op jit(solution)/shard_map/ppermute | solution.py:142
  376.4 43.0 %collective-permute-start.40 = (bf16[256,1536]{1,0:T(8,128)(2,1)}, bf16[256,1536]{1,0:T(8,128)(2,1)}, u32[]{:S(2)}, u32[]{:S(2)}) collective-permute-start(bf16[256,1536]{1,0:T(8,128)(2,1)} %get-tuple-element.185.refs_5_), channel_id=1, source_target_pairs={{0,8},{8,0},{16,24},{24,16},{1,9},{9,1},{17,25},{25,17},{2,10},{10... | collective-permute-start | bytes 2359304 | tf_op jit(solution)/shard_map/ppermute | solution.py:142
  385.7 22.7 %collective-permute-start.45 = (bf16[512,768]{1,0:T(8,128)(2,1)}, bf16[512,768]{1,0:T(8,128)(2,1)}, u32[]{:S(2)}, u32[]{:S(2)}) collective-permute-start(bf16[512,768]{1,0:T(8,128)(2,1)} %get-tuple-element.193), channel_id=1, source_target_pairs={{0,8},{8,0},{16,24},{24,16},{1,9},{9,1},{17,25},{25,17},{2,10},{10... | collective-permute-start | bytes 2359304 | tf_op jit(solution)/shard_map/ppermute | solution.py:142
  385.8 27.5 %collective-permute-start.46 = (bf16[512,768]{1,0:T(8,128)(2,1)}, bf16[512,768]{1,0:T(8,128)(2,1)}, u32[]{:S(2)}, u32[]{:S(2)}) collective-permute-start(bf16[512,768]{1,0:T(8,128)(2,1)} %get-tuple-element.189.refs_12_), channel_id=1, source_target_pairs={{0,16},{8,24},{16,0},{24,8},{1,17},{9,25},{17,1},{25,9},{2,18},{10... | collective-permute-start | bytes 2359304 | tf_op jit(solution)/shard_map/ppermute | solution.py:142
  386.8 40.2 %collective-permute-start.44 = (bf16[192,2048]{1,0:T(8,128)(2,1)}, bf16[192,2048]{1,0:T(8,128)(2,1)}, u32[]{:S(2)}, u32[]{:S(2)}) collective-permute-start(bf16[192,2048]{1,0:T(8,128)(2,1)} %reduce-scatter.6.cloned.1.call-done.refs_4_.refs_1_), channel_id=1, source_target_pairs={{0,16},{8,24},{16,0},{24,8},{1,17},{9,25},{17,1},{25,9},{2,18},{10... | collective-permute-start | bytes 2359304 | tf_op jit(solution)/shard_map/ppermute | solution.py:142
  417.0 22.1 %collective-permute-start.51 = (bf16[256,768]{1,0:T(8,128)(2,1)}, bf16[256,768]{1,0:T(8,128)(2,1)}, u32[]{:S(2)}, u32[]{:S(2)}) collective-permute-start(bf16[256,768]{1,0:T(8,128)(2,1)} %get-tuple-element.199), channel_id=1, source_target_pairs={{0,16},{8,24},{16,0},{24,8},{1,17},{9,25},{17,1},{25,9},{2,18},{10... | collective-permute-start | bytes 1179656 | tf_op jit(solution)/shard_map/ppermute | solution.py:142
  417.4 21.8 %collective-permute-start.52 = (bf16[256,768]{1,0:T(8,128)(2,1)}, bf16[256,768]{1,0:T(8,128)(2,1)}, u32[]{:S(2)}, u32[]{:S(2)}) collective-permute-start(bf16[256,768]{1,0:T(8,128)(2,1)} %get-tuple-element.194.refs_14_), channel_id=1, source_target_pairs={{0,8},{8,0},{16,24},{24,16},{1,9},{9,1},{17,25},{25,17},{2,10},{10... | collective-permute-start | bytes 1179656 | tf_op jit(solution)/shard_map/ppermute | solution.py:142
  417.6 31.2 %collective-permute-start.49 = (bf16[192,2048]{1,0:T(8,128)(2,1)}, bf16[192,2048]{1,0:T(8,128)(2,1)}, u32[]{:S(2)}, u32[]{:S(2)}) collective-permute-start(bf16[192,2048]{1,0:T(8,128)(2,1)} %reduce-scatter.6.cloned.1.call-done.refs_4_.refs_1_), channel_id=1, source_target_pairs={{0,8},{8,0},{16,24},{24,16},{1,9},{9,1},{17,25},{25,17},{2,10},{10... | collective-permute-start | bytes 2359304 | tf_op jit(solution)/shard_map/ppermute | solution.py:142
  438.2 20.8 %collective-permute-start.47 = (bf16[4,192,768]{2,1,0:T(8,128)(2,1)}, bf16[4,192,768]{2,1,0:T(8,128)(2,1)}, u32[]{:S(2)}, u32[]{:S(2)}) collective-permute-start(bf16[4,192,768]{2,1,0:T(8,128)(2,1)} %get-tuple-element.196), channel_id=1, source_target_pairs={{0,1},{1,0},{2,3},{3,2},{4,5},{5,4},{6,7},{7,6},{8,9},{9,8},{10,11... | collective-permute-start | bytes 3538952 | tf_op jit(solution)/shard_map/ppermute | solution.py:1060
  438.3 20.7 %collective-permute-start.50 = (bf16[192,2048]{1,0:T(8,128)(2,1)}, bf16[192,2048]{1,0:T(8,128)(2,1)}, u32[]{:S(2)}, u32[]{:S(2)}) collective-permute-start(bf16[192,2048]{1,0:T(8,128)(2,1)} %collective-permute-done.44.refs_13_.refs_5_.refs_2_), channel_id=1, source_target_pairs={{0,8},{8,0},{16,24},{24,16},{1,9},{9,1},{17,25},{25,17},{2,10},{10... | collective-permute-start | bytes 2359304 | tf_op jit(solution)/shard_map/ppermute | solution.py:142
  446.4 31.3 %collective-permute-start.53 = (bf16[512,768]{1,0:T(8,128)(2,1)}, bf16[512,768]{1,0:T(8,128)(2,1)}, u32[]{:S(2)}, u32[]{:S(2)}) collective-permute-start(bf16[512,768]{1,0:T(8,128)(2,1)} %get-tuple-element.207), channel_id=1, source_target_pairs={{0,8},{8,0},{16,24},{24,16},{1,9},{9,1},{17,25},{25,17},{2,10},{10... | collective-permute-start | bytes 2359304 | tf_op jit(solution)/shard_map/ppermute | solution.py:142
  447.7 30.0 %collective-permute-start.54 = (bf16[512,768]{1,0:T(8,128)(2,1)}, bf16[512,768]{1,0:T(8,128)(2,1)}, u32[]{:S(2)}, u32[]{:S(2)}) collective-permute-start(bf16[512,768]{1,0:T(8,128)(2,1)} %get-tuple-element.201.refs_1_), channel_id=1, source_target_pairs={{0,16},{8,24},{16,0},{24,8},{1,17},{9,25},{17,1},{25,9},{2,18},{10... | collective-permute-start | bytes 2359304 | tf_op jit(solution)/shard_map/ppermute | solution.py:142
  461.8 19.3 %collective-permute-start.58 = (bf16[2,192,768]{2,1,0:T(8,128)(2,1)}, bf16[2,192,768]{2,1,0:T(8,128)(2,1)}, u32[]{:S(2)}, u32[]{:S(2)}) collective-permute-start(bf16[2,192,768]{2,1,0:T(8,128)(2,1)} %get-tuple-element.213), channel_id=1, source_target_pairs={{0,2},{1,3},{2,0},{3,1},{4,6},{5,7},{6,4},{7,5},{8,10},{9,11},{10,... | collective-permute-start | bytes 1769480 | tf_op jit(solution)/shard_map/ppermute | solution.py:1060
  463.8 38.6 %collective-permute-start.57 = (bf16[192,1536]{1,0:T(8,128)(2,1)}, bf16[192,1536]{1,0:T(8,128)(2,1)}, u32[]{:S(2)}, u32[]{:S(2)}) collective-permute-start(bf16[192,1536]{1,0:T(8,128)(2,1)} %pin.9.refs_6_.refs_0_), channel_id=1, source_target_pairs={{0,8},{8,0},{16,24},{24,16},{1,9},{9,1},{17,25},{25,17},{2,10},{10... | collective-permute-start | bytes 1769480 | tf_op jit(solution)/shard_map/ppermute | solution.py:142
  464.8 16.3 %collective-permute-start.59 = (f32[8,1536]{1,0:T(8,128)}, f32[8,1536]{1,0:T(8,128)}, u32[]{:S(2)}, u32[]{:S(2)}) collective-permute-start(f32[8,1536]{1,0:T(8,128)} %get-tuple-element.202.refs_1_.refs_2_), channel_id=1, source_target_pairs={{0,2},{1,3},{2,0},{3,1},{4,6},{5,7},{6,4},{7,5},{8,10},{9,11},{10,... | collective-permute-start | bytes 147464 | tf_op jit(solution)/shard_map/ppermute | solution.py:1060
  483.2 17.3 %collective-permute-start.60 = (bf16[1,192,768]{2,1,0:T(8,128)(2,1)}, bf16[1,192,768]{2,1,0:T(8,128)(2,1)}, u32[]{:S(2)}, u32[]{:S(2)}) collective-permute-start(bf16[1,192,768]{2,1,0:T(8,128)(2,1)} %get-tuple-element.215), channel_id=1, source_target_pairs={{0,4},{1,5},{2,6},{3,7},{4,0},{5,1},{6,2},{7,3},{8,12},{9,13},{10,... | collective-permute-start | bytes 884744 | tf_op jit(solution)/shard_map/ppermute | solution.py:1060
  486.3 23.2 %collective-permute-start.56 = (bf16[256,768]{1,0:T(8,128)(2,1)}, bf16[256,768]{1,0:T(8,128)(2,1)}, u32[]{:S(2)}, u32[]{:S(2)}) collective-permute-start(bf16[256,768]{1,0:T(8,128)(2,1)} %get-tuple-element.211.refs_4_), channel_id=1, source_target_pairs={{0,8},{8,0},{16,24},{24,16},{1,9},{9,1},{17,25},{25,17},{2,10},{10... | collective-permute-start | bytes 1179656 | tf_op jit(solution)/shard_map/ppermute | solution.py:142
  487.4 19.5 %collective-permute-start.55 = (bf16[256,768]{1,0:T(8,128)(2,1)}, bf16[256,768]{1,0:T(8,128)(2,1)}, u32[]{:S(2)}, u32[]{:S(2)}) collective-permute-start(bf16[256,768]{1,0:T(8,128)(2,1)} %get-tuple-element.209), channel_id=1, source_target_pairs={{0,16},{8,24},{16,0},{24,8},{1,17},{9,25},{17,1},{25,9},{2,18},{10... | collective-permute-start | bytes 1179656 | tf_op jit(solution)/shard_map/ppermute | solution.py:142
  504.6 16.6 %collective-permute-start.66 = (bf16[192,1536]{1,0:T(8,128)(2,1)}, bf16[192,1536]{1,0:T(8,128)(2,1)}, u32[]{:S(2)}, u32[]{:S(2)}) collective-permute-start(bf16[192,1536]{1,0:T(8,128)(2,1)} %add_convert_fusion.refs_0_), channel_id=1, source_target_pairs={{0,16},{8,24},{16,0},{24,8},{1,17},{9,25},{17,1},{25,9},{2,18},{10... | collective-permute-start | bytes 1769480 | tf_op jit(solution)/shard_map/ppermute | solution.py:142
  506.9 24.8 %collective-permute-start.64 = (bf16[192,768]{1,0:T(8,128)(2,1)}, bf16[192,768]{1,0:T(8,128)(2,1)}, u32[]{:S(2)}, u32[]{:S(2)}) collective-permute-start(bf16[192,768]{1,0:T(8,128)(2,1)} %bitcast.8.refs_1_), channel_id=1, source_target_pairs={{0,16},{8,24},{16,0},{24,8},{1,17},{9,25},{17,1},{25,9},{2,18},{10... | collective-permute-start | bytes 884744 | tf_op jit(solution)/shard_map/ppermute | solution.py:142
  516.5 15.4 %collective-permute-start.65 = (bf16[192,768]{1,0:T(8,128)(2,1)}, bf16[192,768]{1,0:T(8,128)(2,1)}, u32[]{:S(2)}, u32[]{:S(2)}) collective-permute-start(bf16[192,768]{1,0:T(8,128)(2,1)} %get-tuple-element.220.refs_2_), channel_id=1, source_target_pairs={{0,16},{8,24},{16,0},{24,8},{1,17},{9,25},{17,1},{25,9},{2,18},{10... | collective-permute-start | bytes 884744 | tf_op jit(solution)/shard_map/ppermute | solution.py:142
  519.0 15.5 %collective-permute-start.67 = (f32[8,1536]{1,0:T(8,128)}, f32[8,1536]{1,0:T(8,128)}, u32[]{:S(2)}, u32[]{:S(2)}) collective-permute-start(f32[8,1536]{1,0:T(8,128)} %add.13.refs_0_), channel_id=1, source_target_pairs={{0,16},{8,24},{16,0},{24,8},{1,17},{9,25},{17,1},{25,9},{2,18},{10... | collective-permute-start | bytes 147464 | tf_op jit(solution)/shard_map/ppermute | solution.py:142
  (13 other events, 111.9 us)
Sparse Core Ops, SparseCore 0:
  9.6 42.6 all-gather.6
  54.0 61.6 all-gather.4
  117.4 63.8 all-gather.8
  296.0 69.6 reduce-scatter.5
  368.4 38.7 reduce-scatter.7
  409.3 54.0 reduce-scatter.3
  465.2 41.9 all-gather.10

commit v5 on v4

--- a/solution.py
+++ b/solution.py
@@ -1163,12 +1163,12 @@
 
 def gains_kernel(left_ref, right_ref, first_norm, second_norm, first_ref, second_ref):
     total = left_ref[...] + right_ref[...]
-    first_ref[...] = total[0:1] / first_norm[...]
-    second_ref[...] = total[4:5] / second_norm[...]
+    first_ref[...] = (total[0:1] / first_norm[...])[0]
+    second_ref[...] = (total[4:5] / second_norm[...])[0]
 
 
 def finish_gains(left, right, first_norm, second_norm):
-    out_shape = [shape(1, left.shape[1], dtype=F32)] * 2
+    out_shape = [shape(left.shape[1], dtype=F32)] * 2
     return call(
         gains_kernel,
         out_shape=out_shape,
@@ -1547,8 +1547,8 @@
         gate_grad,
         up_grad,
         down_grad,
-        first_gain.reshape(width),
-        second_gain.reshape(width),
+        first_gain,
+        second_gain,
     )
 
 

time: 554 us -> 552 us (level)
  no operation moved by 1% of the time
where the time goes in v5:
time: 552 us; the launch traced here: 544 us
  Pallas kernels  316 us (57%)
  waiting for transfers between devices  123 us (22%)
  starting transfers between devices  75.4 us (14%)
  between operations  14.6 us (3%)
  other arithmetic  9.3 us (2%)
    pallas_call x44, Pallas kernels, made(): out = inner(*args, *waits)  316 us
    ppermute x46, waiting for transfers between devices, swap(): return lax.ppermute(value, 'seq', [(i, i ^ 1 << bit) for i in range(size)])  78.5 us
    ppermute x46, starting transfers between devices, swap(): return lax.ppermute(value, 'seq', [(i, i ^ 1 << bit) for i in range(size)])  45.1 us
    ppermute x12, waiting for transfers between devices, exchange(): return lax.ppermute(value, 'seq', [(i, i ^ other) for i in range(size)])  23.1 us
    ppermute x6, waiting for transfers between devices, across(): return lax.ppermute(value, 'fsdp', [(i, i ^ bit) for i in range(size)])  14.7 us
    ppermute x12, starting transfers between devices, exchange(): return lax.ppermute(value, 'seq', [(i, i ^ other) for i in range(size)])  13.9 us
  transfers between devices with their start and end apart: 75, of which 23 were waited for; matrix products, arithmetic and copies ran while one was open for 3% of the time, Pallas kernels for 57%

profile of v5, /device:TPU:0, one launch (start us, length us, event | category | flops | bytes accessed | tf_op | source)
XLA Modules:
  0.0 544.0 jit_solution(2749663353137648640)
XLA Ops:
  7.2 2.1 cut_in.1.refs_1_
  10.2 2.6 split_rows.1
  12.8 3.0 collective-permute-start.6
  18.5 3.1 norm_rows.1
  22.0 3.6 cut_feed.1
  25.6 2.1 collective-permute-start
  30.5 3.7 fusion.2
  36.8 13.6 %collective-permute-done.1.refs_1_ = bf16[256,1536]{1,0:T(8,128)(2,1)} collective-permute-done((bf16[256,1536]{1,0:T(8,128)(2,1)}, bf16[256,1536]{1,0:T(8,128)(2,1)}, u32[]{:S(2)}, u32[]{:S(2)}) %collective-permute-start.1) | collective-permute-done | bytes 786464 | tf_op jit(solution)/shard_map/ppermute | solution.py:142
  51.9 3.6 stack_in.1
  59.1 6.7 %widen.1.refs_1_ = bf16[1536,1024]{1,0:T(8,128)(2,1)} custom-call(bf16[1536,768]{1,0:T(8,128)(2,1)} %all-gather.7.cloned.1.call-done.refs_0_.refs_1_.refs_7_, bf16[768,1024]{1,0:T(8,128)(2,1)} %constant.16.clone.refs_1_.refs_7_, bf16[128,1536]{1,0:T(8,128)(2,1)} %pin.6.refs_2_), custom_call_target="tpu_custom_call" | custom-call | flops 48318382080 | bytes 110100480 | tf_op jit(solution)/shard_map/widen/pallas_call | solution.py:76
  65.8 6.3 %collective-permute-done.5.refs_0_ = bf16[128,1536]{1,0:T(8,128)(2,1)} collective-permute-done((bf16[128,1536]{1,0:T(8,128)(2,1)}, bf16[128,1536]{1,0:T(8,128)(2,1)}, u32[]{:S(2)}, u32[]{:S(2)}) %collective-permute-start.5) | collective-permute-done | bytes 393248 | tf_op jit(solution)/shard_map/ppermute | solution.py:156
  72.1 6.4 %collective-permute-start.11 = (bf16[128,1536]{1,0:T(8,128)(2,1)}, bf16[128,1536]{1,0:T(8,128)(2,1)}, u32[]{:S(2)}, u32[]{:S(2)}) collective-permute-start(bf16[128,1536]{1,0:T(8,128)(2,1)} %pin.7.refs_8_.refs_3_), channel_id=1, source_target_pairs={{0,2},{1,3},{2,4},{3,5},{4,6},{5,7},{6,0},{7,1},{8,10},{9,11},{10,... | collective-permute-start | bytes 1179656 | tf_op jit(solution)/shard_map/ppermute | solution.py:156
  78.5 13.9 %collective-permute-done.3.refs_5_.refs_2_ = bf16[512,1536]{1,0:T(8,128)(2,1)} collective-permute-done((bf16[512,1536]{1,0:T(8,128)(2,1)}, bf16[512,1536]{1,0:T(8,128)(2,1)}, u32[]{:S(2)}, u32[]{:S(2)}) %collective-permute-start.3) | collective-permute-done | bytes 1572896 | tf_op jit(solution)/shard_map/ppermute | solution.py:142
  92.4 8.2 %project_in.2.refs_4_.refs_1_ = bf16[1024,1024]{1,0:T(8,128)(2,1)} custom-call(s32[1]{0:T(128)} %bitcast.refs_0_, bf16[1536,1024]{1,0:T(8,128)(2,1)} %widen.1.refs_1_, f32[1024,128]{1,0:T(8,128)} %get-tuple-element.240.refs_2_.refs_5_, f32[1024,128]{1,0:T(8,128)} %get-tuple-element.228.refs_3_.refs_6_, bf16[512,1536]{1,0:T(8,128)(2,1)} %get-tuple-element.123.refs_4_.refs_1_, ...), custom_call_target="tpu_custom_call" | custom-call | flops 64424509440 | bytes 167772160 | tf_op jit(solution)/shard_map/project_in/pallas_call | solution.py:76
  100.6 3.7 stack_cot.1
  105.7 9.9 %attention_forward.2 = (bf16[256,384]{1,0:T(8,128)(2,1)}, bf16[256,384]{1,0:T(8,128)(2,1)}, bf16[256,384]{1,0:T(8,128)(2,1)}, bf16[256,384]{1,0:T(8,128)(2,1)}, f32[2,4,512]{2,1,0:T(4,128)}) custom-call(s32[1]{0:T(128)} %bitcast.refs_0_, bf16[1024,1024]{1,0:T(8,128)(2,1)} %project_in.2.refs_4_.refs_1_, s32[1,1024]{1,0:T(1,128)} %get-tuple-element.237.refs_2_, ...), custom_call_target="tpu_custom_call" | custom-call | flops 42949672960 | bytes 83886080 | tf_op jit(solution)/shard_map/attention_forward/pallas_call | solution.py:76
  120.6 2.6 join.1.refs_6_.refs_2_.refs_1_
  123.2 8.8 %project_in.3.refs_8_.refs_1_ = bf16[1024,1024]{1,0:T(8,128)(2,1)} custom-call(s32[1]{0:T(128)} %bitcast.refs_0_, bf16[1536,1024]{1,0:T(8,128)(2,1)} %widen.1.refs_1_, f32[1024,128]{1,0:T(8,128)} %get-tuple-element.241.refs_2_.refs_5_, f32[1024,128]{1,0:T(8,128)} %get-tuple-element.227.refs_3_.refs_6_, ...), custom_call_target="tpu_custom_call" | custom-call | flops 64424509440 | bytes 167772160 | tf_op jit(solution)/shard_map/project_in/pallas_call | solution.py:76
  132.0 14.6 %collective-permute-done.9.refs_6_.refs_3_ = bf16[256,384]{1,0:T(8,128)(2,1)} collective-permute-done((bf16[256,384]{1,0:T(8,128)(2,1)}, bf16[256,384]{1,0:T(8,128)(2,1)}, u32[]{:S(2)}, u32[]{:S(2)}) %collective-permute-start.9) | collective-permute-done | bytes 196640 | tf_op jit(solution)/shard_map/ppermute | solution.py:147
  146.6 6.0 %project_out.2 = (f32[256,1536]{1,0:T(8,128)}, bf16[256,768]{1,0:T(8,128)(2,1)}, bf16[256,768]{1,0:T(8,128)(2,1)}) custom-call(s32[1]{0:T(128)} %bitcast.refs_0_, bf16[4,384,1536]{2,1,0:T(8,128)(2,1)} %bitcast.13, bf16[2,256,1536]{2,1,0:T(8,128)(2,1)} %refs_0_.5, f32[1,1536]{1,0:T(1,128)} %broadcast_in_dim.20.refs_3_, ...), custom_call_target="tpu_custom_call" | custom-call | flops 24159191040 | bytes 173015040 | tf_op jit(solution)/shard_map/project_out/pallas_call | solution.py:76
  155.4 10.2 %attention_forward.3 = (bf16[256,384]{1,0:T(8,128)(2,1)}, bf16[256,384]{1,0:T(8,128)(2,1)}, bf16[256,384]{1,0:T(8,128)(2,1)}, bf16[256,384]{1,0:T(8,128)(2,1)}, f32[2,4,512]{2,1,0:T(4,128)}) custom-call(s32[1]{0:T(128)} %bitcast.refs_0_, bf16[1024,1024]{1,0:T(8,128)(2,1)} %project_in.3.refs_8_.refs_1_, s32[1,1024]{1,0:T(1,128)} %get-tuple-element.236.refs_2_, ...), custom_call_target="tpu_custom_call" | custom-call | flops 42949672960 | bytes 83886080 | tf_op jit(solution)/shard_map/attention_forward/pallas_call | solution.py:76
  168.3 2.1 collective-permute-start.20
  170.4 2.5 stack_mid.2
  176.1 2.1 collective-permute-done.20.refs_7_.refs_8_
  178.2 6.0 %project_out.3 = (f32[256,1536]{1,0:T(8,128)}, bf16[256,768]{1,0:T(8,128)(2,1)}, bf16[256,768]{1,0:T(8,128)(2,1)}) custom-call(s32[1]{0:T(128)} %bitcast.refs_0_, bf16[4,384,1536]{2,1,0:T(8,128)(2,1)} %bitcast.14, bf16[2,256,1536]{2,1,0:T(8,128)(2,1)} %refs_0_.5, f32[1,1536]{1,0:T(1,128)} %broadcast_in_dim.20.refs_3_, ...), custom_call_target="tpu_custom_call" | custom-call | flops 24159191040 | bytes 173015040 | tf_op jit(solution)/shard_map/project_out/pallas_call | solution.py:76
  186.0 14.3 %collective-permute-done.22.refs_1_ = bf16[256,768]{1,0:T(8,128)(2,1)} collective-permute-done((bf16[256,768]{1,0:T(8,128)(2,1)}, bf16[256,768]{1,0:T(8,128)(2,1)}, u32[]{:S(2)}, u32[]{:S(2)}) %collective-permute-start.22) | collective-permute-done | bytes 393248 | tf_op jit(solution)/shard_map/ppermute | solution.py:142
  200.3 2.6 stack_mid.3
  205.5 25.4 %feed_forward.2 = (bf16[1024,1024]{1,0:T(8,128)(2,1)}, bf16[1024,2048]{1,0:T(8,128)(2,1)}, bf16[1024,1536]{1,0:T(8,128)(2,1)}, bf16[512,768]{1,0:T(8,128)(2,1)},...) custom-call(s32[1]{0:T(128)} %bitcast.6.refs_0_, ...), custom_call_target="tpu_custom_call" | custom-call | flops 322122547200 | bytes 503316480 | tf_op jit(solution)/shard_map/feed_forward/pallas_call | solution.py:76
  232.4 25.2 %feed_forward.3 = (bf16[1024,1024]{1,0:T(8,128)(2,1)}, bf16[1024,2048]{1,0:T(8,128)(2,1)}, bf16[1024,1536]{1,0:T(8,128)(2,1)}, bf16[512,768]{1,0:T(8,128)(2,1)},...) custom-call(s32[1]{0:T(128)} %bitcast.6.refs_0_, ...), custom_call_target="tpu_custom_call" | custom-call | flops 322122547200 | bytes 503316480 | tf_op jit(solution)/shard_map/feed_forward/pallas_call | solution.py:76
  260.3 3.4 fold.5
  265.1 20.5 %gate_up_grad.1 = (bf16[1536,2048]{1,0:T(8,128)(2,1)}, f32[8,1536]{1,0:T(8,128)}) custom-call(bf16[1024,1536]{1,0:T(8,128)(2,1)} %get-tuple-element.158.refs_0_, bf16[1024,1536]{1,0:T(8,128)(2,1)} %get-tuple-element.159.refs_1_, bf16[1024,2048]{1,0:T(8,128)(2,1)} %get-tuple-element.160.refs_2_, bf16[1024,2048]{1,0:T(8,128)(2,1)} %get-tuple-element.161.refs_3_, ...), custom_call_target="tpu_custom_call" | custom-call | flops 257698037760 | bytes 419430400 | tf_op jit(solution)/shard_map/gate_up_grad/pallas_call | solution.py:76
  285.6 6.8 %norm_out_back.2 = (f32[256,1536]{1,0:T(8,128)}, bf16[256,1536]{1,0:T(8,128)(2,1)}, bf16[256,384]{1,0:T(8,128)(2,1)}, bf16[256,384]{1,0:T(8,128)(2,1)}, bf16[256...) custom-call(s32[1]{0:T(128)} %bitcast.refs_0_, f32[256,1536]{1,0:T(8,128)} %get-tuple-element.131.refs_1_.refs_0_, ...), custom_call_target="tpu_custom_call" | custom-call | flops 3019898880 | bytes 27525120 | tf_op jit(solution)/shard_map/norm_out_back/pallas_call | solution.py:76
  295.9 3.3 fold.6
  301.9 2.0 collective-permute-done.31.refs_6_.refs_10_
  304.4 12.8 %feed_out.1 = (bf16[512,1536]{1,0:T(8,128)(2,1)}, bf16[512,1536]{1,0:T(8,128)(2,1)}, bf16[512,1536]{1,0:T(8,128)(2,1)}, bf16[512,1536]{1,0:T(8,128)(2,1)}) custom-call(s32[1]{0:T(128)} %bitcast.6.refs_0_, bf16[4,128,1536]{2,1,0:T(8,128)(2,1)} %join.1.refs_6_.refs_2_.refs_1_, bf16[4,128,1536]{2,1,0:T(8,128)(2,1)} %collective-permute-done.12.refs_8_.refs_3_.refs_2_, ...), custom_call_target="tpu_custom_call" | custom-call | flops 16106127360 | bytes 34078720 | tf_op jit(solution)/shard_map/feed_out/pallas_call | solution.py:76
  317.2 6.9 %norm_out_back.3 = (f32[256,1536]{1,0:T(8,128)}, bf16[256,1536]{1,0:T(8,128)(2,1)}, bf16[256,384]{1,0:T(8,128)(2,1)}, bf16[256,384]{1,0:T(8,128)(2,1)}, bf16[256...) custom-call(s32[1]{0:T(128)} %bitcast.refs_0_, f32[256,1536]{1,0:T(8,128)} %get-tuple-element.176.refs_1_.refs_3_, ...), custom_call_target="tpu_custom_call" | custom-call | flops 3019898880 | bytes 27525120 | tf_op jit(solution)/shard_map/norm_out_back/pallas_call | solution.py:76
  324.1 11.5 %down_grad.1.refs_11_ = bf16[1024,1536]{1,0:T(8,128)(2,1)} custom-call(bf16[1024,1024]{1,0:T(8,128)(2,1)} %get-tuple-element.146.refs_3_.refs_0_, bf16[1024,1024]{1,0:T(8,128)(2,1)} %get-tuple-element.149.refs_4_.refs_1_, bf16[512,1536]{1,0:T(8,128)(2,1)} %get-tuple-element.133.refs_9_.refs_4_.refs_2_, ...), custom_call_target="tpu_custom_call" | custom-call | flops 128849018880 | bytes 272629760 | tf_op jit(solution)/shard_map/down_grad/pallas_call | solution.py:76
  341.2 6.8 %out_weight_grad.1.refs_12_ = bf16[4,384,1536]{2,1,0:T(8,128)(2,1)} custom-call(s32[1]{0:T(128)} %bitcast.refs_0_, bf16[256,384]{1,0:T(8,128)(2,1)} %get-tuple-element.126.refs_4_.refs_1_, bf16[256,384]{1,0:T(8,128)(2,1)} %collective-permute-done.8.refs_5_.refs_2_, bf16[256,384]{1,0:T(8,128)(2,1)} %collective-permute-done.9.refs_6_.refs_3_, ...), custom_call_target="tpu_custom_call" | custom-call | flops 48318382080 | bytes 94371840 | tf_op jit(solution)/shard_map/out_weight_grad/pallas_call | solution.py:76
  348.1 20.5 %attention_backward.2.refs_4_.refs_0_.refs_5_ = bf16[1024,768]{1,0:T(8,128)(2,1)} custom-call(s32[1]{0:T(128)} %bitcast.refs_0_, bf16[1024,1024]{1,0:T(8,128)(2,1)} %project_in.2.refs_4_.refs_1_, s32[1,1024]{1,0:T(1,128)} %get-tuple-element.237.refs_2_, bf16[2,256,384]{2,1,0:T(8,128)(2,1)} %constant.17.clone.refs_3_, ...), custom_call_target="tpu_custom_call" | custom-call | flops 107374182400 | bytes 167772160 | tf_op jit(solution)/shard_map/attention_backward/pallas_call | solution.py:76
  370.2 5.4 fold.7
  376.6 2.0 collective-permute-done.41.refs_2_.refs_9_
  378.7 7.0 %grad_into_rows.2 = (bf16[512,768]{1,0:T(8,128)(2,1)}, bf16[512,768]{1,0:T(8,128)(2,1)}, bf16[512,768]{1,0:T(8,128)(2,1)}, bf16[512,768]{1,0:T(8,128)(2,1)}) custom-call(bf16[1024,768]{1,0:T(8,128)(2,1)} %attention_backward.2.refs_4_.refs_0_.refs_5_, bf16[1536,768]{1,0:T(8,128)(2,1)} %all-gather.7.cloned.1.call-done.refs_0_.refs_1_.refs_7_, ...), custom_call_target="tpu_custom_call" | custom-call | flops 48318382080 | bytes 141557760 | tf_op jit(solution)/shard_map/grad_into_rows/pallas_call | solution.py:76
  387.8 20.5 %attention_backward.3.refs_4_.refs_6_.refs_0_ = bf16[1024,768]{1,0:T(8,128)(2,1)} custom-call(s32[1]{0:T(128)} %bitcast.refs_0_, bf16[1024,1024]{1,0:T(8,128)(2,1)} %project_in.3.refs_8_.refs_1_, s32[1,1024]{1,0:T(1,128)} %get-tuple-element.236.refs_2_, bf16[2,256,384]{2,1,0:T(8,128)(2,1)} %constant.17.clone.refs_3_, ...), custom_call_target="tpu_custom_call" | custom-call | flops 107374182400 | bytes 167772160 | tf_op jit(solution)/shard_map/attention_backward/pallas_call | solution.py:76
  408.4 5.0 collective-permute-done.46.refs_3_
  413.3 3.8 fold.8
  419.4 7.6 %collective-permute-done.44.refs_13_.refs_5_.refs_2_ = bf16[192,2048]{1,0:T(8,128)(2,1)} collective-permute-done((bf16[192,2048]{1,0:T(8,128)(2,1)}, bf16[192,2048]{1,0:T(8,128)(2,1)}, u32[]{:S(2)}, u32[]{:S(2)}) %collective-permute-start.44) | collective-permute-done | bytes 786464 | tf_op jit(solution)/shard_map/ppermute | solution.py:142
  427.0 11.1 %in_weight_grad.1 = (bf16[4,192,768]{2,1,0:T(8,128)(2,1)}, bf16[4,192,768]{2,1,0:T(8,128)(2,1)}, f32[8,1536]{1,0:T(8,128)}) custom-call(s32[1]{0:T(128)} %bitcast.6.refs_0_, bf16[512,1536]{1,0:T(8,128)(2,1)} %get-tuple-element.123.refs_4_.refs_1_, bf16[512,1536]{1,0:T(8,128)(2,1)} %collective-permute-done.3.refs_5_.refs_2_, ...), custom_call_target="tpu_custom_call" | custom-call | flops 96636764160 | bytes 235929600 | tf_op jit(solution)/shard_map/in_weight_grad/pallas_call | solution.py:76
  439.2 7.2 %grad_into_rows.3 = (bf16[512,768]{1,0:T(8,128)(2,1)}, bf16[512,768]{1,0:T(8,128)(2,1)}, bf16[512,768]{1,0:T(8,128)(2,1)}, bf16[512,768]{1,0:T(8,128)(2,1)}) custom-call(bf16[1024,768]{1,0:T(8,128)(2,1)} %attention_backward.3.refs_4_.refs_6_.refs_0_, bf16[1536,768]{1,0:T(8,128)(2,1)} %all-gather.7.cloned.1.call-done.refs_0_.refs_1_.refs_7_, ...), custom_call_target="tpu_custom_call" | custom-call | flops 48318382080 | bytes 141557760 | tf_op jit(solution)/shard_map/grad_into_rows/pallas_call | solution.py:76
  450.7 8.3 %collective-permute-done.50.refs_7_.refs_4_ = bf16[192,2048]{1,0:T(8,128)(2,1)} collective-permute-done((bf16[192,2048]{1,0:T(8,128)(2,1)}, bf16[192,2048]{1,0:T(8,128)(2,1)}, u32[]{:S(2)}, u32[]{:S(2)}) %collective-permute-start.50) | collective-permute-done | bytes 786464 | tf_op jit(solution)/shard_map/ppermute | solution.py:142
  459.0 2.8 halve.3
  461.8 2.0 collective-permute-start.58
  464.9 4.7 finish_block_out.1.refs_4_
  469.6 8.0 %collective-permute-done.53.refs_2_ = bf16[512,768]{1,0:T(8,128)(2,1)} collective-permute-done((bf16[512,768]{1,0:T(8,128)(2,1)}, bf16[512,768]{1,0:T(8,128)(2,1)}, u32[]{:S(2)}, u32[]{:S(2)}) %collective-permute-start.53) | collective-permute-done | bytes 786464 | tf_op jit(solution)/shard_map/ppermute | solution.py:142
  477.6 3.3 fold.9
  481.0 2.1 halve.4
  483.1 3.6 collective-permute-start.60
  487.5 13.4 %collective-permute-done.61.refs_3_ = f32[8,1536]{1,0:T(8,128)} collective-permute-done((f32[8,1536]{1,0:T(8,128)}, f32[8,1536]{1,0:T(8,128)}, u32[]{:S(2)}, u32[]{:S(2)}) %collective-permute-start.61) | collective-permute-done | bytes 49184 | tf_op jit(solution)/shard_map/ppermute | solution.py:1060
  502.8 2.2 add_convert_fusion.refs_0_
  507.1 2.0 collective-permute-start.64
  509.5 6.4 %finish_tokens_grad.1.refs_2_ = bf16[2,256,1536]{2,1,0:T(8,128)(2,1)} custom-call(bf16[2,256,1536]{2,1,0:T(8,128)(2,1)} %refs_0_.5, f32[1,1536]{1,0:T(1,128)} %broadcast_in_dim.21.refs_1_.refs_2_, f32[256,1536]{1,0:T(8,128)} %get-tuple-element.203.refs_2_, f32[256,768]{1,0:T(8,128)} %get-tuple-element.198.refs_2_.refs_3_, ...), custom_call_target="tpu_custom_call" | custom-call | bytes 188743680 | tf_op jit(solution)/shard_map/finish_tokens_grad/pallas_call | solution.py:76
  521.6 2.1 add_float.1.refs_5_
  523.7 4.5 arrange_gate_up.1
  528.3 3.9 down_to_float.1.refs_5_
  532.8 2.7 arrange_in.1.refs_4_
  (158 shorter events, 78.5 us)
Async XLA Ops:
  7.2 51.9 %all-gather.7.cloned.1.call-start = ((), (), s32[]{:S(2)}) async-start(), calls=%async_computation.4 | async-start | bytes 2654208 | tf_op jit(solution)/shard_map/all_gather | solution.py:1334
  9.4 137.2 %all-gather.5.cloned.1.call-start = ((), (), s32[]{:S(2)}) async-start(), calls=%async_computation.3 | async-start | bytes 5308416 | tf_op jit(solution)/shard_map/all_gather | solution.py:1334
  10.1 195.4 %all-gather.9.cloned.1.call-start = ((), (), s32[]{:S(2)}) async-start(), calls=%async_computation.5 | async-start | bytes 7077888 | tf_op jit(solution)/shard_map/all_gather | solution.py:1334
  12.8 87.8 %collective-permute-start.6 = (bf16[256,1536]{1,0:T(8,128)(2,1)}, bf16[256,1536]{1,0:T(8,128)(2,1)}, u32[]{:S(2)}, u32[]{:S(2)}) collective-permute-start(bf16[256,1536]{1,0:T(8,128)(2,1)} %get-tuple-element.124.refs_0_), channel_id=1, source_target_pairs={{0,16},{8,24},{16,0},{24,8},{1,17},{9,25},{17,1},{25,9},{2,18},{10... | collective-permute-start | bytes 2359304 | tf_op jit(solution)/shard_map/ppermute | solution.py:142
  15.7 84.9 %collective-permute-start.7 = (bf16[256,1536]{1,0:T(8,128)(2,1)}, bf16[256,1536]{1,0:T(8,128)(2,1)}, u32[]{:S(2)}, u32[]{:S(2)}) collective-permute-start(bf16[256,1536]{1,0:T(8,128)(2,1)} %get-tuple-element.118.refs_2_), channel_id=1, source_target_pairs={{0,8},{8,0},{16,24},{24,16},{1,9},{9,1},{17,25},{25,17},{2,10},{10... | collective-permute-start | bytes 2359304 | tf_op jit(solution)/shard_map/ppermute | solution.py:142
  21.6 28.9 %collective-permute-start.1 = (bf16[256,1536]{1,0:T(8,128)(2,1)}, bf16[256,1536]{1,0:T(8,128)(2,1)}, u32[]{:S(2)}, u32[]{:S(2)}) collective-permute-start(bf16[256,1536]{1,0:T(8,128)(2,1)} %get-tuple-element.121.refs_0_), channel_id=1, source_target_pairs={{0,16},{8,24},{16,0},{24,8},{1,17},{9,25},{17,1},{25,9},{2,18},{10... | collective-permute-start | bytes 2359304 | tf_op jit(solution)/shard_map/ppermute | solution.py:142
  22.0 29.9 %collective-permute-start.2 = (bf16[256,1536]{1,0:T(8,128)(2,1)}, bf16[256,1536]{1,0:T(8,128)(2,1)}, u32[]{:S(2)}, u32[]{:S(2)}) collective-permute-start(bf16[256,1536]{1,0:T(8,128)(2,1)} %get-tuple-element.119.refs_4_.refs_2_), channel_id=1, source_target_pairs={{0,8},{8,0},{16,24},{24,16},{1,9},{9,1},{17,25},{25,17},{2,10},{10... | collective-permute-start | bytes 2359304 | tf_op jit(solution)/shard_map/ppermute | solution.py:142
  25.6 30.2 %collective-permute-start = (bf16[128,1536]{1,0:T(8,128)(2,1)}, bf16[128,1536]{1,0:T(8,128)(2,1)}, u32[]{:S(2)}, u32[]{:S(2)}) collective-permute-start(bf16[128,1536]{1,0:T(8,128)(2,1)} %get-tuple-element.120.refs_4_.refs_1_), channel_id=1, source_target_pairs={{0,2},{1,3},{2,4},{3,5},{4,6},{5,7},{6,0},{7,1},{8,10},{9,11},{10,... | collective-permute-start | bytes 1179656 | tf_op jit(solution)/shard_map/ppermute | solution.py:156
  27.7 359.1 %reduce-scatter.6.cloned.1.call-start = ((), (), s32[]{:S(2)}) async-start(), calls=%async_computation.7 | async-start | bytes 7077888 | tf_op jit(solution)/shard_map/reduce_scatter | solution.py:1337
  55.5 36.9 %collective-permute-start.4 = (bf16[512,1536]{1,0:T(8,128)(2,1)}, bf16[512,1536]{1,0:T(8,128)(2,1)}, u32[]{:S(2)}, u32[]{:S(2)}) collective-permute-start(bf16[512,1536]{1,0:T(8,128)(2,1)} %get-tuple-element.122.refs_1_.refs_6_.refs_4_.refs_3_), channel_id=1, source_target_pairs={{0,16},{8,24},{16,0},{24,8},{1,17},{9,25},{17,1},{25,9},{2,18},{10... | collective-permute-start | bytes 4718600 | tf_op jit(solution)/shard_map/ppermute | solution.py:142
  55.8 16.3 %collective-permute-start.5 = (bf16[128,1536]{1,0:T(8,128)(2,1)}, bf16[128,1536]{1,0:T(8,128)(2,1)}, u32[]{:S(2)}, u32[]{:S(2)}) collective-permute-start(bf16[128,1536]{1,0:T(8,128)(2,1)} %pin.6.refs_2_), channel_id=1, source_target_pairs={{0,2},{1,3},{2,4},{3,5},{4,6},{5,7},{6,0},{7,1},{8,10},{9,11},{10,... | collective-permute-start | bytes 1179656 | tf_op jit(solution)/shard_map/ppermute | solution.py:156
  57.6 34.8 %collective-permute-start.3 = (bf16[512,1536]{1,0:T(8,128)(2,1)}, bf16[512,1536]{1,0:T(8,128)(2,1)}, u32[]{:S(2)}, u32[]{:S(2)}) collective-permute-start(bf16[512,1536]{1,0:T(8,128)(2,1)} %get-tuple-element.123.refs_4_.refs_1_), channel_id=1, source_target_pairs={{0,8},{8,0},{16,24},{24,16},{1,9},{9,1},{17,25},{25,17},{2,10},{10... | collective-permute-start | bytes 4718600 | tf_op jit(solution)/shard_map/ppermute | solution.py:142
  72.1 47.0 %collective-permute-start.11 = (bf16[128,1536]{1,0:T(8,128)(2,1)}, bf16[128,1536]{1,0:T(8,128)(2,1)}, u32[]{:S(2)}, u32[]{:S(2)}) collective-permute-start(bf16[128,1536]{1,0:T(8,128)(2,1)} %pin.7.refs_8_.refs_3_), channel_id=1, source_target_pairs={{0,2},{1,3},{2,4},{3,5},{4,6},{5,7},{6,0},{7,1},{8,10},{9,11},{10,... | collective-permute-start | bytes 1179656 | tf_op jit(solution)/shard_map/ppermute | solution.py:156
  104.3 68.7 %collective-permute-start.21 = (bf16[512,1536]{1,0:T(8,128)(2,1)}, bf16[512,1536]{1,0:T(8,128)(2,1)}, u32[]{:S(2)}, u32[]{:S(2)}) collective-permute-start(bf16[512,1536]{1,0:T(8,128)(2,1)} %get-tuple-element.125.refs_4_.refs_11_), channel_id=1, source_target_pairs={{0,16},{8,24},{16,0},{24,8},{1,17},{9,25},{17,1},{25,9},{2,18},{10... | collective-permute-start | bytes 4718600 | tf_op jit(solution)/shard_map/ppermute | solution.py:142
  115.6 16.4 %collective-permute-start.8 = (bf16[256,384]{1,0:T(8,128)(2,1)}, bf16[256,384]{1,0:T(8,128)(2,1)}, u32[]{:S(2)}, u32[]{:S(2)}) collective-permute-start(bf16[256,384]{1,0:T(8,128)(2,1)} %get-tuple-element.127), channel_id=1, source_target_pairs={{0,8},{8,0},{16,24},{24,16},{1,9},{9,1},{17,25},{25,17},{2,10},{10... | collective-permute-start | bytes 589832 | tf_op jit(solution)/shard_map/ppermute | solution.py:147
  117.1 29.5 %collective-permute-start.9 = (bf16[256,384]{1,0:T(8,128)(2,1)}, bf16[256,384]{1,0:T(8,128)(2,1)}, u32[]{:S(2)}, u32[]{:S(2)}) collective-permute-start(bf16[256,384]{1,0:T(8,128)(2,1)} %get-tuple-element.128), channel_id=1, source_target_pairs={{0,16},{8,24},{16,0},{24,8},{1,17},{9,25},{17,1},{25,9},{2,18},{10... | collective-permute-start | bytes 589832 | tf_op jit(solution)/shard_map/ppermute | solution.py:147
  117.8 28.8 %collective-permute-start.10 = (bf16[256,384]{1,0:T(8,128)(2,1)}, bf16[256,384]{1,0:T(8,128)(2,1)}, u32[]{:S(2)}, u32[]{:S(2)}) collective-permute-start(bf16[256,384]{1,0:T(8,128)(2,1)} %get-tuple-element.129), channel_id=1, source_target_pairs={{0,24},{8,16},{16,8},{24,0},{1,25},{9,17},{17,9},{25,1},{2,26},{10... | collective-permute-start | bytes 589832 | tf_op jit(solution)/shard_map/ppermute | solution.py:147
  119.1 46.5 %collective-permute-start.13 = (bf16[512,1536]{1,0:T(8,128)(2,1)}, bf16[512,1536]{1,0:T(8,128)(2,1)}, u32[]{:S(2)}, u32[]{:S(2)}) collective-permute-start(bf16[512,1536]{1,0:T(8,128)(2,1)} %get-tuple-element.133.refs_9_.refs_4_.refs_2_), channel_id=1, source_target_pairs={{0,8},{8,0},{16,24},{24,16},{1,9},{9,1},{17,25},{25,17},{2,10},{10... | collective-permute-start | bytes 4718600 | tf_op jit(solution)/shard_map/ppermute | solution.py:142
  132.0 41.0 %collective-permute-start.12 = (bf16[4,128,1536]{2,1,0:T(8,128)(2,1)}, bf16[4,128,1536]{2,1,0:T(8,128)(2,1)}, u32[]{:S(2)}, u32[]{:S(2)}) collective-permute-start(bf16[4,128,1536]{2,1,0:T(8,128)(2,1)} %join.1.refs_6_.refs_2_.refs_1_), channel_id=1, source_target_pairs={{0,1},{1,0},{2,3},{3,2},{4,5},{5,4},{6,7},{7,6},{8,9},{9,8},{10,11... | collective-permute-start | bytes 4718600 | tf_op jit(solution)/shard_map/ppermute | solution.py:161
  153.9 14.4 %collective-permute-start.15 = (bf16[256,768]{1,0:T(8,128)(2,1)}, bf16[256,768]{1,0:T(8,128)(2,1)}, u32[]{:S(2)}, u32[]{:S(2)}) collective-permute-start(bf16[256,768]{1,0:T(8,128)(2,1)} %get-tuple-element.135.refs_4_.refs_2_), channel_id=1, source_target_pairs={{0,8},{8,0},{16,24},{24,16},{1,9},{9,1},{17,25},{25,17},{2,10},{10... | collective-permute-start | bytes 1179656 | tf_op jit(solution)/shard_map/ppermute | solution.py:142
  172.9 32.6 %collective-permute-start.16 = (bf16[512,768]{1,0:T(8,128)(2,1)}, bf16[512,768]{1,0:T(8,128)(2,1)}, u32[]{:S(2)}, u32[]{:S(2)}) collective-permute-start(bf16[512,768]{1,0:T(8,128)(2,1)} %get-tuple-element.137.refs_6_), channel_id=1, source_target_pairs={{0,8},{8,0},{16,24},{24,16},{1,9},{9,1},{17,25},{25,17},{2,10},{10... | collective-permute-start | bytes 2359304 | tf_op jit(solution)/shard_map/ppermute | solution.py:142
  173.1 32.4 %collective-permute-start.17 = (bf16[512,768]{1,0:T(8,128)(2,1)}, bf16[512,768]{1,0:T(8,128)(2,1)}, u32[]{:S(2)}, u32[]{:S(2)}) collective-permute-start(bf16[512,768]{1,0:T(8,128)(2,1)} %get-tuple-element.138.refs_13_.refs_8_), channel_id=1, source_target_pairs={{0,16},{8,24},{16,0},{24,8},{1,17},{9,25},{17,1},{25,9},{2,18},{10... | collective-permute-start | bytes 2359304 | tf_op jit(solution)/shard_map/ppermute | solution.py:142
  184.2 16.1 %collective-permute-start.22 = (bf16[256,768]{1,0:T(8,128)(2,1)}, bf16[256,768]{1,0:T(8,128)(2,1)}, u32[]{:S(2)}, u32[]{:S(2)}) collective-permute-start(bf16[256,768]{1,0:T(8,128)(2,1)} %get-tuple-element.143.refs_0_), channel_id=1, source_target_pairs={{0,16},{8,24},{16,0},{24,8},{1,17},{9,25},{17,1},{25,9},{2,18},{10... | collective-permute-start | bytes 1179656 | tf_op jit(solution)/shard_map/ppermute | solution.py:142
  185.4 14.8 %collective-permute-start.23 = (bf16[256,768]{1,0:T(8,128)(2,1)}, bf16[256,768]{1,0:T(8,128)(2,1)}, u32[]{:S(2)}, u32[]{:S(2)}) collective-permute-start(bf16[256,768]{1,0:T(8,128)(2,1)} %get-tuple-element.144.refs_2_.refs_4_), channel_id=1, source_target_pairs={{0,8},{8,0},{16,24},{24,16},{1,9},{9,1},{17,25},{25,17},{2,10},{10... | collective-permute-start | bytes 1179656 | tf_op jit(solution)/shard_map/ppermute | solution.py:142
  202.9 29.5 %collective-permute-start.24 = (bf16[512,768]{1,0:T(8,128)(2,1)}, bf16[512,768]{1,0:T(8,128)(2,1)}, u32[]{:S(2)}, u32[]{:S(2)}) collective-permute-start(bf16[512,768]{1,0:T(8,128)(2,1)} %get-tuple-element.147.refs_6_), channel_id=1, source_target_pairs={{0,8},{8,0},{16,24},{24,16},{1,9},{9,1},{17,25},{25,17},{2,10},{10... | collective-permute-start | bytes 2359304 | tf_op jit(solution)/shard_map/ppermute | solution.py:142
  204.4 28.0 %collective-permute-start.25 = (bf16[512,768]{1,0:T(8,128)(2,1)}, bf16[512,768]{1,0:T(8,128)(2,1)}, u32[]{:S(2)}, u32[]{:S(2)}) collective-permute-start(bf16[512,768]{1,0:T(8,128)(2,1)} %get-tuple-element.145.refs_10_.refs_8_), channel_id=1, source_target_pairs={{0,16},{8,24},{16,0},{24,8},{1,17},{9,25},{17,1},{25,9},{2,18},{10... | collective-permute-start | bytes 2359304 | tf_op jit(solution)/shard_map/ppermute | solution.py:142
  230.9 29.4 %collective-permute-start.26 = (bf16[512,768]{1,0:T(8,128)(2,1)}, bf16[512,768]{1,0:T(8,128)(2,1)}, u32[]{:S(2)}, u32[]{:S(2)}) collective-permute-start(bf16[512,768]{1,0:T(8,128)(2,1)} %get-tuple-element.152), channel_id=1, source_target_pairs={{0,8},{8,0},{16,24},{24,16},{1,9},{9,1},{17,25},{25,17},{2,10},{10... | collective-permute-start | bytes 2359304 | tf_op jit(solution)/shard_map/ppermute | solution.py:142
  231.6 28.7 %collective-permute-start.27 = (bf16[512,768]{1,0:T(8,128)(2,1)}, bf16[512,768]{1,0:T(8,128)(2,1)}, u32[]{:S(2)}, u32[]{:S(2)}) collective-permute-start(bf16[512,768]{1,0:T(8,128)(2,1)} %get-tuple-element.148.refs_10_), channel_id=1, source_target_pairs={{0,16},{8,24},{16,0},{24,8},{1,17},{9,25},{17,1},{25,9},{2,18},{10... | collective-permute-start | bytes 2359304 | tf_op jit(solution)/shard_map/ppermute | solution.py:142
  257.6 38.4 %collective-permute-start.33 = (bf16[512,768]{1,0:T(8,128)(2,1)}, bf16[512,768]{1,0:T(8,128)(2,1)}, u32[]{:S(2)}, u32[]{:S(2)}) collective-permute-start(bf16[512,768]{1,0:T(8,128)(2,1)} %get-tuple-element.168), channel_id=1, source_target_pairs={{0,8},{8,0},{16,24},{24,16},{1,9},{9,1},{17,25},{25,17},{2,10},{10... | collective-permute-start | bytes 2359304 | tf_op jit(solution)/shard_map/ppermute | solution.py:142
  259.2 36.7 %collective-permute-start.34 = (bf16[512,768]{1,0:T(8,128)(2,1)}, bf16[512,768]{1,0:T(8,128)(2,1)}, u32[]{:S(2)}, u32[]{:S(2)}) collective-permute-start(bf16[512,768]{1,0:T(8,128)(2,1)} %get-tuple-element.153.refs_4_), channel_id=1, source_target_pairs={{0,16},{8,24},{16,0},{24,8},{1,17},{9,25},{17,1},{25,9},{2,18},{10... | collective-permute-start | bytes 2359304 | tf_op jit(solution)/shard_map/ppermute | solution.py:142
  263.6 21.9 %collective-permute-start.28 = (bf16[256,768]{1,0:T(8,128)(2,1)}, bf16[256,768]{1,0:T(8,128)(2,1)}, u32[]{:S(2)}, u32[]{:S(2)}) collective-permute-start(bf16[256,768]{1,0:T(8,128)(2,1)} %get-tuple-element.155), channel_id=1, source_target_pairs={{0,16},{8,24},{16,0},{24,8},{1,17},{9,25},{17,1},{25,9},{2,18},{10... | collective-permute-start | bytes 1179656 | tf_op jit(solution)/shard_map/ppermute | solution.py:142
  264.6 21.0 %collective-permute-start.29 = (bf16[256,768]{1,0:T(8,128)(2,1)}, bf16[256,768]{1,0:T(8,128)(2,1)}, u32[]{:S(2)}, u32[]{:S(2)}) collective-permute-start(bf16[256,768]{1,0:T(8,128)(2,1)} %get-tuple-element.157.refs_5_), channel_id=1, source_target_pairs={{0,8},{8,0},{16,24},{24,16},{1,9},{9,1},{17,25},{25,17},{2,10},{10... | collective-permute-start | bytes 1179656 | tf_op jit(solution)/shard_map/ppermute | solution.py:142
  295.9 150.5 %reduce-scatter.8.cloned.1.call-start = ((), (), s32[]{:S(2)}) async-start(), calls=%async_computation.8 | async-start | bytes 3538944 | tf_op jit(solution)/shard_map/reduce_scatter | solution.py:1337
  299.3 17.9 %collective-permute-start.37 = (bf16[256,768]{1,0:T(8,128)(2,1)}, bf16[256,768]{1,0:T(8,128)(2,1)}, u32[]{:S(2)}, u32[]{:S(2)}) collective-permute-start(bf16[256,768]{1,0:T(8,128)(2,1)} %get-tuple-element.178), channel_id=1, source_target_pairs={{0,16},{8,24},{16,0},{24,8},{1,17},{9,25},{17,1},{25,9},{2,18},{10... | collective-permute-start | bytes 1179656 | tf_op jit(solution)/shard_map/ppermute | solution.py:142
  300.5 16.7 %collective-permute-start.38 = (bf16[256,768]{1,0:T(8,128)(2,1)}, bf16[256,768]{1,0:T(8,128)(2,1)}, u32[]{:S(2)}, u32[]{:S(2)}) collective-permute-start(bf16[256,768]{1,0:T(8,128)(2,1)} %get-tuple-element.169.refs_8_), channel_id=1, source_target_pairs={{0,8},{8,0},{16,24},{24,16},{1,9},{9,1},{17,25},{25,17},{2,10},{10... | collective-permute-start | bytes 1179656 | tf_op jit(solution)/shard_map/ppermute | solution.py:142
  335.6 128.2 %reduce-scatter.4.cloned.1.call-start = ((), (), s32[]{:S(2)}) async-start(), calls=%async_computation.6 | async-start | bytes 5308416 | tf_op jit(solution)/shard_map/reduce_scatter | solution.py:1337
  335.6 34.6 %collective-permute-start.36 = (bf16[512,1536]{1,0:T(8,128)(2,1)}, bf16[512,1536]{1,0:T(8,128)(2,1)}, u32[]{:S(2)}, u32[]{:S(2)}) collective-permute-start(bf16[512,1536]{1,0:T(8,128)(2,1)} %get-tuple-element.173.refs_9_), channel_id=1, source_target_pairs={{0,16},{8,24},{16,0},{24,8},{1,17},{9,25},{17,1},{25,9},{2,18},{10... | collective-permute-start | bytes 4718600 | tf_op jit(solution)/shard_map/ppermute | solution.py:142
  336.5 33.7 %collective-permute-start.35 = (bf16[512,1536]{1,0:T(8,128)(2,1)}, bf16[512,1536]{1,0:T(8,128)(2,1)}, u32[]{:S(2)}, u32[]{:S(2)}) collective-permute-start(bf16[512,1536]{1,0:T(8,128)(2,1)} %get-tuple-element.172), channel_id=1, source_target_pairs={{0,8},{8,0},{16,24},{24,16},{1,9},{9,1},{17,25},{25,17},{2,10},{10... | collective-permute-start | bytes 4718600 | tf_op jit(solution)/shard_map/ppermute | solution.py:142
  337.7 41.0 %collective-permute-start.43 = (bf16[256,384]{1,0:T(8,128)(2,1)}, bf16[256,384]{1,0:T(8,128)(2,1)}, u32[]{:S(2)}, u32[]{:S(2)}) collective-permute-start(bf16[256,384]{1,0:T(8,128)(2,1)} %get-tuple-element.181.refs_6_), channel_id=1, source_target_pairs={{0,24},{8,16},{16,8},{24,0},{1,25},{9,17},{17,9},{25,1},{2,26},{10... | collective-permute-start | bytes 589832 | tf_op jit(solution)/shard_map/ppermute | solution.py:147
  339.2 39.5 %collective-permute-start.41 = (bf16[256,384]{1,0:T(8,128)(2,1)}, bf16[256,384]{1,0:T(8,128)(2,1)}, u32[]{:S(2)}, u32[]{:S(2)}) collective-permute-start(bf16[256,384]{1,0:T(8,128)(2,1)} %get-tuple-element.187), channel_id=1, source_target_pairs={{0,8},{8,0},{16,24},{24,16},{1,9},{9,1},{17,25},{25,17},{2,10},{10... | collective-permute-start | bytes 589832 | tf_op jit(solution)/shard_map/ppermute | solution.py:147
  340.3 38.3 %collective-permute-start.42 = (bf16[256,384]{1,0:T(8,128)(2,1)}, bf16[256,384]{1,0:T(8,128)(2,1)}, u32[]{:S(2)}, u32[]{:S(2)}) collective-permute-start(bf16[256,384]{1,0:T(8,128)(2,1)} %get-tuple-element.188), channel_id=1, source_target_pairs={{0,16},{8,24},{16,0},{24,8},{1,17},{9,25},{17,1},{25,9},{2,18},{10... | collective-permute-start | bytes 589832 | tf_op jit(solution)/shard_map/ppermute | solution.py:147
  348.0 180.2 %all-gather.11.cloned.1.call-start = ((), (), s32[]{:S(2)}) async-start(), calls=%async_computation.9 | async-start | bytes 1966080 | tf_op jit(solution)/shard_map/all_gather | solution.py:1482
  375.7 42.0 %collective-permute-start.39 = (bf16[256,1536]{1,0:T(8,128)(2,1)}, bf16[256,1536]{1,0:T(8,128)(2,1)}, u32[]{:S(2)}, u32[]{:S(2)}) collective-permute-start(bf16[256,1536]{1,0:T(8,128)(2,1)} %get-tuple-element.183), channel_id=1, source_target_pairs={{0,16},{8,24},{16,0},{24,8},{1,17},{9,25},{17,1},{25,9},{2,18},{10... | collective-permute-start | bytes 2359304 | tf_op jit(solution)/shard_map/ppermute | solution.py:142
  376.4 43.0 %collective-permute-start.40 = (bf16[256,1536]{1,0:T(8,128)(2,1)}, bf16[256,1536]{1,0:T(8,128)(2,1)}, u32[]{:S(2)}, u32[]{:S(2)}) collective-permute-start(bf16[256,1536]{1,0:T(8,128)(2,1)} %get-tuple-element.185.refs_5_), channel_id=1, source_target_pairs={{0,8},{8,0},{16,24},{24,16},{1,9},{9,1},{17,25},{25,17},{2,10},{10... | collective-permute-start | bytes 2359304 | tf_op jit(solution)/shard_map/ppermute | solution.py:142
  385.7 22.6 %collective-permute-start.45 = (bf16[512,768]{1,0:T(8,128)(2,1)}, bf16[512,768]{1,0:T(8,128)(2,1)}, u32[]{:S(2)}, u32[]{:S(2)}) collective-permute-start(bf16[512,768]{1,0:T(8,128)(2,1)} %get-tuple-element.193), channel_id=1, source_target_pairs={{0,8},{8,0},{16,24},{24,16},{1,9},{9,1},{17,25},{25,17},{2,10},{10... | collective-permute-start | bytes 2359304 | tf_op jit(solution)/shard_map/ppermute | solution.py:142
  385.8 27.5 %collective-permute-start.46 = (bf16[512,768]{1,0:T(8,128)(2,1)}, bf16[512,768]{1,0:T(8,128)(2,1)}, u32[]{:S(2)}, u32[]{:S(2)}) collective-permute-start(bf16[512,768]{1,0:T(8,128)(2,1)} %get-tuple-element.189.refs_12_), channel_id=1, source_target_pairs={{0,16},{8,24},{16,0},{24,8},{1,17},{9,25},{17,1},{25,9},{2,18},{10... | collective-permute-start | bytes 2359304 | tf_op jit(solution)/shard_map/ppermute | solution.py:142
  386.8 40.2 %collective-permute-start.44 = (bf16[192,2048]{1,0:T(8,128)(2,1)}, bf16[192,2048]{1,0:T(8,128)(2,1)}, u32[]{:S(2)}, u32[]{:S(2)}) collective-permute-start(bf16[192,2048]{1,0:T(8,128)(2,1)} %reduce-scatter.6.cloned.1.call-done.refs_4_.refs_1_), channel_id=1, source_target_pairs={{0,16},{8,24},{16,0},{24,8},{1,17},{9,25},{17,1},{25,9},{2,18},{10... | collective-permute-start | bytes 2359304 | tf_op jit(solution)/shard_map/ppermute | solution.py:142
  417.1 22.1 %collective-permute-start.51 = (bf16[256,768]{1,0:T(8,128)(2,1)}, bf16[256,768]{1,0:T(8,128)(2,1)}, u32[]{:S(2)}, u32[]{:S(2)}) collective-permute-start(bf16[256,768]{1,0:T(8,128)(2,1)} %get-tuple-element.199), channel_id=1, source_target_pairs={{0,16},{8,24},{16,0},{24,8},{1,17},{9,25},{17,1},{25,9},{2,18},{10... | collective-permute-start | bytes 1179656 | tf_op jit(solution)/shard_map/ppermute | solution.py:142
  417.4 21.8 %collective-permute-start.52 = (bf16[256,768]{1,0:T(8,128)(2,1)}, bf16[256,768]{1,0:T(8,128)(2,1)}, u32[]{:S(2)}, u32[]{:S(2)}) collective-permute-start(bf16[256,768]{1,0:T(8,128)(2,1)} %get-tuple-element.194.refs_14_), channel_id=1, source_target_pairs={{0,8},{8,0},{16,24},{24,16},{1,9},{9,1},{17,25},{25,17},{2,10},{10... | collective-permute-start | bytes 1179656 | tf_op jit(solution)/shard_map/ppermute | solution.py:142
  417.6 31.2 %collective-permute-start.49 = (bf16[192,2048]{1,0:T(8,128)(2,1)}, bf16[192,2048]{1,0:T(8,128)(2,1)}, u32[]{:S(2)}, u32[]{:S(2)}) collective-permute-start(bf16[192,2048]{1,0:T(8,128)(2,1)} %reduce-scatter.6.cloned.1.call-done.refs_4_.refs_1_), channel_id=1, source_target_pairs={{0,8},{8,0},{16,24},{24,16},{1,9},{9,1},{17,25},{25,17},{2,10},{10... | collective-permute-start | bytes 2359304 | tf_op jit(solution)/shard_map/ppermute | solution.py:142
  438.2 20.8 %collective-permute-start.47 = (bf16[4,192,768]{2,1,0:T(8,128)(2,1)}, bf16[4,192,768]{2,1,0:T(8,128)(2,1)}, u32[]{:S(2)}, u32[]{:S(2)}) collective-permute-start(bf16[4,192,768]{2,1,0:T(8,128)(2,1)} %get-tuple-element.196), channel_id=1, source_target_pairs={{0,1},{1,0},{2,3},{3,2},{4,5},{5,4},{6,7},{7,6},{8,9},{9,8},{10,11... | collective-permute-start | bytes 3538952 | tf_op jit(solution)/shard_map/ppermute | solution.py:1060
  438.2 20.7 %collective-permute-start.50 = (bf16[192,2048]{1,0:T(8,128)(2,1)}, bf16[192,2048]{1,0:T(8,128)(2,1)}, u32[]{:S(2)}, u32[]{:S(2)}) collective-permute-start(bf16[192,2048]{1,0:T(8,128)(2,1)} %collective-permute-done.44.refs_13_.refs_5_.refs_2_), channel_id=1, source_target_pairs={{0,8},{8,0},{16,24},{24,16},{1,9},{9,1},{17,25},{25,17},{2,10},{10... | collective-permute-start | bytes 2359304 | tf_op jit(solution)/shard_map/ppermute | solution.py:142
  446.4 31.2 %collective-permute-start.53 = (bf16[512,768]{1,0:T(8,128)(2,1)}, bf16[512,768]{1,0:T(8,128)(2,1)}, u32[]{:S(2)}, u32[]{:S(2)}) collective-permute-start(bf16[512,768]{1,0:T(8,128)(2,1)} %get-tuple-element.207), channel_id=1, source_target_pairs={{0,8},{8,0},{16,24},{24,16},{1,9},{9,1},{17,25},{25,17},{2,10},{10... | collective-permute-start | bytes 2359304 | tf_op jit(solution)/shard_map/ppermute | solution.py:142
  447.7 29.9 %collective-permute-start.54 = (bf16[512,768]{1,0:T(8,128)(2,1)}, bf16[512,768]{1,0:T(8,128)(2,1)}, u32[]{:S(2)}, u32[]{:S(2)}) collective-permute-start(bf16[512,768]{1,0:T(8,128)(2,1)} %get-tuple-element.201.refs_1_), channel_id=1, source_target_pairs={{0,16},{8,24},{16,0},{24,8},{1,17},{9,25},{17,1},{25,9},{2,18},{10... | collective-permute-start | bytes 2359304 | tf_op jit(solution)/shard_map/ppermute | solution.py:142
  461.8 19.2 %collective-permute-start.58 = (bf16[2,192,768]{2,1,0:T(8,128)(2,1)}, bf16[2,192,768]{2,1,0:T(8,128)(2,1)}, u32[]{:S(2)}, u32[]{:S(2)}) collective-permute-start(bf16[2,192,768]{2,1,0:T(8,128)(2,1)} %get-tuple-element.213), channel_id=1, source_target_pairs={{0,2},{1,3},{2,0},{3,1},{4,6},{5,7},{6,4},{7,5},{8,10},{9,11},{10,... | collective-permute-start | bytes 1769480 | tf_op jit(solution)/shard_map/ppermute | solution.py:1060
  463.8 39.1 %collective-permute-start.57 = (bf16[192,1536]{1,0:T(8,128)(2,1)}, bf16[192,1536]{1,0:T(8,128)(2,1)}, u32[]{:S(2)}, u32[]{:S(2)}) collective-permute-start(bf16[192,1536]{1,0:T(8,128)(2,1)} %pin.9.refs_6_.refs_0_), channel_id=1, source_target_pairs={{0,8},{8,0},{16,24},{24,16},{1,9},{9,1},{17,25},{25,17},{2,10},{10... | collective-permute-start | bytes 1769480 | tf_op jit(solution)/shard_map/ppermute | solution.py:142
  464.9 16.1 %collective-permute-start.59 = (f32[8,1536]{1,0:T(8,128)}, f32[8,1536]{1,0:T(8,128)}, u32[]{:S(2)}, u32[]{:S(2)}) collective-permute-start(f32[8,1536]{1,0:T(8,128)} %get-tuple-element.202.refs_1_.refs_2_), channel_id=1, source_target_pairs={{0,2},{1,3},{2,0},{3,1},{4,6},{5,7},{6,4},{7,5},{8,10},{9,11},{10,... | collective-permute-start | bytes 147464 | tf_op jit(solution)/shard_map/ppermute | solution.py:1060
  483.1 17.9 %collective-permute-start.60 = (bf16[1,192,768]{2,1,0:T(8,128)(2,1)}, bf16[1,192,768]{2,1,0:T(8,128)(2,1)}, u32[]{:S(2)}, u32[]{:S(2)}) collective-permute-start(bf16[1,192,768]{2,1,0:T(8,128)(2,1)} %get-tuple-element.215), channel_id=1, source_target_pairs={{0,4},{1,5},{2,6},{3,7},{4,0},{5,1},{6,2},{7,3},{8,12},{9,13},{10,... | collective-permute-start | bytes 884744 | tf_op jit(solution)/shard_map/ppermute | solution.py:1060
  486.8 22.7 %collective-permute-start.56 = (bf16[256,768]{1,0:T(8,128)(2,1)}, bf16[256,768]{1,0:T(8,128)(2,1)}, u32[]{:S(2)}, u32[]{:S(2)}) collective-permute-start(bf16[256,768]{1,0:T(8,128)(2,1)} %get-tuple-element.211.refs_4_), channel_id=1, source_target_pairs={{0,8},{8,0},{16,24},{24,16},{1,9},{9,1},{17,25},{25,17},{2,10},{10... | collective-permute-start | bytes 1179656 | tf_op jit(solution)/shard_map/ppermute | solution.py:142
  487.4 19.7 %collective-permute-start.55 = (bf16[256,768]{1,0:T(8,128)(2,1)}, bf16[256,768]{1,0:T(8,128)(2,1)}, u32[]{:S(2)}, u32[]{:S(2)}) collective-permute-start(bf16[256,768]{1,0:T(8,128)(2,1)} %get-tuple-element.209), channel_id=1, source_target_pairs={{0,16},{8,24},{16,0},{24,8},{1,17},{9,25},{17,1},{25,9},{2,18},{10... | collective-permute-start | bytes 1179656 | tf_op jit(solution)/shard_map/ppermute | solution.py:142
  505.0 16.6 %collective-permute-start.66 = (bf16[192,1536]{1,0:T(8,128)(2,1)}, bf16[192,1536]{1,0:T(8,128)(2,1)}, u32[]{:S(2)}, u32[]{:S(2)}) collective-permute-start(bf16[192,1536]{1,0:T(8,128)(2,1)} %add_convert_fusion.refs_0_), channel_id=1, source_target_pairs={{0,16},{8,24},{16,0},{24,8},{1,17},{9,25},{17,1},{25,9},{2,18},{10... | collective-permute-start | bytes 1769480 | tf_op jit(solution)/shard_map/ppermute | solution.py:142
  507.1 25.1 %collective-permute-start.64 = (bf16[192,768]{1,0:T(8,128)(2,1)}, bf16[192,768]{1,0:T(8,128)(2,1)}, u32[]{:S(2)}, u32[]{:S(2)}) collective-permute-start(bf16[192,768]{1,0:T(8,128)(2,1)} %bitcast.8.refs_1_), channel_id=1, source_target_pairs={{0,16},{8,24},{16,0},{24,8},{1,17},{9,25},{17,1},{25,9},{2,18},{10... | collective-permute-start | bytes 884744 | tf_op jit(solution)/shard_map/ppermute | solution.py:142
  516.5 16.3 %collective-permute-start.65 = (bf16[192,768]{1,0:T(8,128)(2,1)}, bf16[192,768]{1,0:T(8,128)(2,1)}, u32[]{:S(2)}, u32[]{:S(2)}) collective-permute-start(bf16[192,768]{1,0:T(8,128)(2,1)} %get-tuple-element.220.refs_2_), channel_id=1, source_target_pairs={{0,16},{8,24},{16,0},{24,8},{1,17},{9,25},{17,1},{25,9},{2,18},{10... | collective-permute-start | bytes 884744 | tf_op jit(solution)/shard_map/ppermute | solution.py:142
  519.0 16.5 %collective-permute-start.67 = (f32[8,1536]{1,0:T(8,128)}, f32[8,1536]{1,0:T(8,128)}, u32[]{:S(2)}, u32[]{:S(2)}) collective-permute-start(f32[8,1536]{1,0:T(8,128)} %add.13.refs_0_), channel_id=1, source_target_pairs={{0,16},{8,24},{16,0},{24,8},{1,17},{9,25},{17,1},{25,9},{2,18},{10... | collective-permute-start | bytes 147464 | tf_op jit(solution)/shard_map/ppermute | solution.py:142
  (13 other events, 111.7 us)
Sparse Core Ops, SparseCore 0:
  9.6 42.6 all-gather.6
  54.0 61.6 all-gather.4
  117.4 63.7 all-gather.8
  296.0 69.6 reduce-scatter.5
  368.4 38.6 reduce-scatter.7
  409.3 54.0 reduce-scatter.3
  465.3 41.9 all-gather.10
